TPU v7x, 32 devices: a whole 2x2x4 slice. The times are simulated.
32 devices in a mesh: img: 4 (over z), gx: 4 (over y, core), gy: 2 (over x).
Axes of the slice: x: 2, y: 2, z: 4, core: 2. Of those that a mesh axis runs over, the one named last changes fastest.
Arguments:
- magnetization: float32 [4, 3, 16, 32, 512], P('img', None, None, 'gy', 'gx'), may hold values from -1 to 1, as said below
- lower_image: int32 [4], replicated, may hold values from 0 to 2, as said below
- image_weights: float32 [3], replicated, may hold values from 0.5 to 2
- regions: int32 [16, 32, 512], P(None, 'gy', 'gx'), may hold values from 0 to 7
- anisotropy: float32 [8], replicated, may hold values from 0.5 to 4
- damping: float32 [8], replicated, may hold values from 0.05 to 0.5
Outputs:
- evolved: float32 [4, 3, 16, 32, 512], P('img', None, None, 'gy', 'gx')
Inputs may be any that keep to these rules, and one draw needn't show every extreme that they name: `lower_image`: lower_image_j is j - 1 or j; it is 0 for image 0 and 2 for the last image. `magnetization`: every cell holds a unit vector, and in every cell neighbouring images make an angle under 90 degrees.
All inputs are finite; a program needn't handle non-finite values.
Results may differ from a plain program's by a relative error of at most 0.000024.
Values sent between devices are 32-bit elements; how exact they have to be, the bound alone decides.
No kernel may reach another device: no remote copies, remote signals or barrier semaphores. Data moves between devices by JAX's collectives and lax.ppermute only.
A program may use at most 64 MiB of HBM per device.

v0:
```python
import functools

import jax
import jax.numpy as jnp
from jax import lax
from jax.experimental import pallas as pl
from jax.experimental.pallas import tpu as pltpu
from jax.sharding import PartitionSpec as P

STEPS = 4
DEPTH = 2 * STEPS

eps = 1e-06
time_step = 0.05

SUB = 8
LANES = 128
COMPS = 3


def lane_iota():
    return lax.broadcasted_iota(jnp.int32, (SUB, LANES), 1)


def sub_iota():
    return lax.broadcasted_iota(jnp.int32, (SUB, LANES), 0)


def rows_at(ny, tiles, y, t):
    return pl.ds(y + ny * t, SUB, stride=ny * tiles)


def gather_kernel(ny, tiles, lower_ref, m_ref, up_ref, down_ref, reg_ref, part_ref, near_ref, left_ref, right_ref):
    here = lax.axis_index("img")
    take_up = lower_ref[here] < here
    lane = lane_iota()

    near_ref[...] = jnp.where(take_up, up_ref[...], down_ref[...])
    diff = m_ref[...] - up_ref[...]
    total = jnp.sum(jnp.sum(diff * diff, axis=(0, 1), keepdims=True)[0], axis=1, keepdims=True)
    slot = lax.broadcasted_iota(jnp.int32, (1, LANES), 1)
    part_ref[...] = jnp.where((slot == here) & (here > 0), total, 0.0)

    for t in range(tiles):
        for c in range(2 * COMPS + 1):
            left = jnp.zeros((SUB, LANES), jnp.float32)
            right = jnp.zeros((SUB, LANES), jnp.float32)
            for y in range(ny):
                rows = rows_at(ny, tiles, y, t)
                if c < COMPS:
                    cells = m_ref[c, rows, :]
                elif c < 2 * COMPS:
                    cells = near_ref[c - COMPS, rows, :]
                else:
                    cells = reg_ref[rows, :].astype(jnp.float32)
                cells = pltpu.roll(cells, (DEPTH * (y + 1)) % LANES, 1)
                left = jnp.where(lane // DEPTH == (y + 1) % ny, cells, left)
                right = jnp.where(lane // DEPTH == y, cells, right)
            left_ref[c, t] = left
            right_ref[c, t] = right


def turn(m, h, a2, b, sc):
    mx, my, mz = m
    hx, hy, hz = h
    hz = hz + a2 * mz
    gx = hx + b * (my * hz - mz * hy)
    gy = hy + b * (mz * hx - mx * hz)
    gz = hz + b * (mx * hy - my * hx)
    return (
        sc * (my * gz - mz * gy),
        sc * (mz * gx - mx * gz),
        sc * (mx * gy - my * gx),
    )


def normal(v):
    scale = lax.rsqrt(v[0] * v[0] + v[1] * v[1] + v[2] * v[2])
    return tuple(x * scale for x in v)


def evolve_kernel(
    ny,
    tiles,
    images,
    regions,
    lower_ref,
    aniso_ref,
    damp_ref,
    sq_ref,
    share_ref,
    m_ref,
    mp_ref,
    n_ref,
    np_ref,
    reg_ref,
    regp_ref,
    left_ref,
    right_ref,
    leftp_ref,
    rightp_ref,
    out_ref,
    main,
    strip,
    edge,
    seam,
    par,
    spar,
):
    window = ny + 2 * DEPTH
    here = lax.axis_index("img")
    lane = lane_iota()
    sub = sub_iota()
    block = lane // DEPTH
    first_lane = lane == 0
    last_lane = lane == LANES - 1
    head_lane = lane % DEPTH == 0
    tail_lane = lane % DEPTH == DEPTH - 1
    top = sub == SUB - 1
    bottom = sub == 0

    lo = lower_ref[here]
    slot = lax.broadcasted_iota(jnp.int32, (1, LANES), 1)
    lengths = jnp.where((slot >= 1) & (slot < images), jnp.sqrt(sq_ref[...] + eps), 0.0)
    total = jnp.sum(lengths, axis=1, keepdims=True)
    arc = jnp.sum(jnp.where(slot <= lo, lengths, 0.0), axis=1, keepdims=True)
    gap = jnp.sum(jnp.where(slot == lo + 1, lengths, 0.0), axis=1, keepdims=True)
    share = share_ref[...]
    spot = lax.broadcasted_iota(jnp.int32, share.shape, 1)
    target = jnp.sum(jnp.where(spot < here, share, 0.0), axis=1, keepdims=True) / jnp.sum(
        share, axis=1, keepdims=True
    )
    weight = jnp.clip((target * total - arc) / gap, -0.5, 1.5)
    weight = jnp.broadcast_to(weight, (SUB, LANES))
    below = lo < here
    w_own = jnp.where(below, weight, 1.0 - weight)
    w_near = jnp.where(below, 1.0 - weight, weight)

    def params(region):
        a = jnp.full((SUB, LANES), aniso_ref[0], jnp.float32)
        d = jnp.full((SUB, LANES), damp_ref[0], jnp.float32)
        for i in range(1, regions):
            inside = region == i
            a = jnp.where(inside, aniso_ref[i], a)
            d = jnp.where(inside, damp_ref[i], d)
        return 2.0 * a, d, -time_step / (1.0 + d * d)

    def merge(old, new, k):
        mask = ((lane - (DEPTH * k + DEPTH - 1)) & (LANES - 1)) < 2
        shift = (DEPTH * (k + 1)) & (LANES - 1)
        return jnp.where(mask, pltpu.roll(new, shift, 1), old)

    zero = jnp.zeros((SUB, LANES), jnp.float32)
    zeros = tuple(zero for _ in range(COMPS * tiles))
    for g, (own, near, reg) in enumerate(((m_ref, n_ref, reg_ref), (mp_ref, np_ref, regp_ref))):

        def fill(k, edges, g=g, own=own, near=near, reg=reg):
            edges = list(edges)
            for t in range(tiles):
                rows = rows_at(ny, tiles, k, t)
                v = normal(
                    [w_own * own[c, rows, :] + w_near * near[c, rows, :] for c in range(COMPS)]
                )
                for c in range(COMPS):
                    main[0, c, g * ny + k, t] = v[c]
                    edges[c * tiles + t] = merge(edges[c * tiles + t], v[c], k)
                p = params(reg[rows, :])
                for i in range(3):
                    par[i, g * ny + k, t] = p[i]
            return tuple(edges)

        edges = lax.fori_loop(0, ny, fill, zeros)
        for c in range(COMPS):
            for t in range(tiles):
                edge[0, c, g, t] = edges[c * tiles + t]
    for side, pair in enumerate(((left_ref, leftp_ref), (right_ref, rightp_ref))):
        for g in range(2):
            for t in range(tiles):
                v = normal(
                    [w_own * pair[g][c, t] + w_near * pair[g][COMPS + c, t] for c in range(COMPS)]
                )
                for c in range(COMPS):
                    strip[0, c, side, g, t] = v[c]
                p = params(pair[g][2 * COMPS, t].astype(jnp.int32))
                for i in range(3):
                    spar[i, side, g, t] = p[i]

    def seams(state):
        for c in range(COMPS):
            for g in range(2):
                for t in range(tiles):
                    seam[state, c, g, t] = jnp.where(
                        tail_lane, strip[state, c, 0, g, t], strip[state, c, 1, g, t]
                    )

    seams(0)

    def around_z(cells, t):
        if t + 1 < tiles:
            above = cells[t + 1]
        else:
            above = jnp.where(top, 0.0, pltpu.roll(cells[0], SUB - 1, 0))
        if t > 0:
            under = cells[t - 1]
        else:
            under = jnp.where(bottom, 0.0, pltpu.roll(cells[tiles - 1], 1, 0))
        return above + under

    def main_row(state, g, k):
        r = g * ny + k
        after = (r + 1) & (window - 1)
        before = (r - 1) & (window - 1)
        shift = (LANES - DEPTH * (k + 1)) & (LANES - 1)
        center = [[main[state, c, r, t] for t in range(tiles)] for c in range(COMPS)]
        result = []
        for t in range(tiles):
            h = []
            for c in range(COMPS):
                cells = center[c][t]
                ends = pltpu.roll(seam[state, c, g, t], shift, 1)
                s = pltpu.roll(jnp.where(last_lane, ends, cells), 1, 1)
                s = s + pltpu.roll(jnp.where(first_lane, ends, cells), LANES - 1, 1)
                s = s + (main[state, c, after, t] + main[state, c, before, t])
                h.append(s + around_z(center[c], t))
            m = [center[c][t] for c in range(COMPS)]
            rate = turn(m, h, par[0, r, t], par[1, r, t], par[2, r, t])
            if state == 0:
                new = [m[c] + rate[c] for c in range(COMPS)]
            else:
                new = normal([main[0, c, r, t] + (m[c] + rate[c]) for c in range(COMPS)])
            result.append(new)
        return r, result

    def strip_rows(state):
        for side in range(2):
            for g in range(2):
                center = [[strip[state, c, side, g, t] for t in range(tiles)] for c in range(COMPS)]
                for t in range(tiles):
                    h = []
                    for c in range(COMPS):
                        cells = center[c][t]
                        inner = edge[state, c, g, t]
                        other = strip[state, c, side, 1 - g, t]
                        if side == 0:
                            s = pltpu.roll(cells, 1, 1)
                            s = s + pltpu.roll(jnp.where(head_lane, inner, cells), LANES - 1, 1)
                        else:
                            s = pltpu.roll(jnp.where(tail_lane, inner, cells), 1, 1)
                            s = s + pltpu.roll(cells, LANES - 1, 1)
                        start = block == side
                        stop = block == (side + ny - 1) % ny
                        s = s + pltpu.roll(jnp.where(start, other, cells), LANES - DEPTH, 1)
                        s = s + pltpu.roll(jnp.where(stop, other, cells), DEPTH, 1)
                        h.append(s + around_z(center[c], t))
                    m = [center[c][t] for c in range(COMPS)]
                    rate = turn(
                        m, h, spar[0, side, g, t], spar[1, side, g, t], spar[2, side, g, t]
                    )
                    if state == 0:
                        new = [m[c] + rate[c] for c in range(COMPS)]
                    else:
                        new = normal(
                            [strip[0, c, side, g, t] + (m[c] + rate[c]) for c in range(COMPS)]
                        )
                    for c in range(COMPS):
                        strip[1 - state, c, side, g, t] = new[c]
        seams(1 - state)

    def main_rows(state, g, count, pick):
        def body(i, edges):
            edges = list(edges)
            for k in pick(i):
                r, result = main_row(state, g, k)
                for t in range(tiles):
                    for c in range(COMPS):
                        main[1 - state, c, r, t] = result[t][c]
                        edges[c * tiles + t] = merge(edges[c * tiles + t], result[t][c], k)
            return tuple(edges)

        edges = lax.fori_loop(0, count, body, zeros)
        for c in range(COMPS):
            for t in range(tiles):
                edge[1 - state, c, g, t] = edges[c * tiles + t]

    for stage in range(1, 2 * STEPS + 1):
        state = (stage + 1) % 2
        if stage == 2 * STEPS:

            def last(i, carry):
                for k in (i, i + ny // 2):
                    _, result = main_row(1, 0, k)
                    for t in range(tiles):
                        for c in range(COMPS):
                            out_ref[c, rows_at(ny, tiles, k, t), :] = result[t][c]
                return carry

            lax.fori_loop(0, ny // 2, last, 0)
        else:
            main_rows(state, 0, ny // 2, lambda i: (i, i + ny // 2))
            main_rows(state, 1, DEPTH - stage, lambda i: (i, ny - 1 - i))
            strip_rows(state)


def shifted(cells, axis, step, closed):
    count = lax.axis_size(axis)
    pairs = [(i, (i + step) % count) for i in range(count) if closed or 0 <= i + step < count]
    return lax.ppermute(cells, axis, pairs)


def around(cells, dim):
    ny = cells.shape[dim]
    if lax.axis_size("gy") == 2:
        return shifted(cells, "gy", 1, True)
    head = lax.slice_in_dim(cells, 0, DEPTH, axis=dim)
    tail = lax.slice_in_dim(cells, ny - DEPTH, ny, axis=dim)
    return jnp.concatenate([shifted(head, "gy", -1, True), shifted(tail, "gy", 1, True)], axis=dim)


def around_strip(cells, side):
    if lax.axis_size("gy") == 2:
        return shifted(cells, "gy", 1, True)
    block = (lax.broadcasted_iota(jnp.int32, cells.shape, cells.ndim - 1) // DEPTH - side) % (LANES // DEPTH)
    return jnp.where(block < DEPTH, shifted(cells, "gy", -1, True), shifted(cells, "gy", 1, True))


def body(magnetization, lower_image, image_weights, regions, anisotropy, damping):
    local, comps, nz, ny, nx = magnetization.shape
    images = local * lax.axis_size("img")
    tiles = nz // SUB
    assert local == 1 and comps == COMPS and nx == LANES
    assert ny == 2 * DEPTH and ny * DEPTH == LANES and tiles >= 2
    flat = (comps, nz * ny, nx)
    own = magnetization[0]
    up = shifted(own, "img", 1, False)
    down = shifted(own, "img", -1, False)
    own_p = around(own, 2)
    reg_p = around(regions, 1)

    smem = pl.BlockSpec(memory_space=pltpu.SMEM)
    vmem = pl.BlockSpec(memory_space=pltpu.VMEM)
    f32 = jnp.float32
    limit = pltpu.CompilerParams(vmem_limit_bytes=32 * 1024 * 1024)
    packed = jax.ShapeDtypeStruct((2 * comps + 1, tiles, SUB, LANES), f32)
    part, near, left, right = pl.pallas_call(
        functools.partial(gather_kernel, ny, tiles),
        out_shape=(
            jax.ShapeDtypeStruct((1, LANES), f32),
            jax.ShapeDtypeStruct(flat, f32),
            packed,
            packed,
        ),
        in_specs=[smem] + [vmem] * 4,
        out_specs=(vmem,) * 4,
        compiler_params=limit,
        name="gather_images",
    )(lower_image, own.reshape(flat), up.reshape(flat), down.reshape(flat), regions.reshape(flat[1:]))
    near_p = around(near.reshape(own.shape), 2)
    strip_r = shifted(left, "gx", -1, True)
    strip_l = shifted(right, "gx", 1, True)
    strip_lp = around_strip(strip_l, 0)
    strip_rp = around_strip(strip_r, 1)
    squares = lax.psum(part, ("img", "gx", "gy"))

    window = ny + 2 * DEPTH
    vreg = (SUB, LANES)
    out = pl.pallas_call(
        functools.partial(evolve_kernel, ny, tiles, images, anisotropy.shape[0]),
        out_shape=jax.ShapeDtypeStruct(flat, f32),
        in_specs=[smem] * 3 + [vmem] * 12,
        out_specs=vmem,
        scratch_shapes=[
            pltpu.VMEM((2, comps, window, tiles) + vreg, f32),
            pltpu.VMEM((2, comps, 2, 2, tiles) + vreg, f32),
            pltpu.VMEM((2, comps, 2, tiles) + vreg, f32),
            pltpu.VMEM((2, comps, 2, tiles) + vreg, f32),
            pltpu.VMEM((3, window, tiles) + vreg, f32),
            pltpu.VMEM((3, 2, 2, tiles) + vreg, f32),
        ],
        compiler_params=limit,
        name="evolve",
    )(
        lower_image,
        anisotropy,
        damping,
        squares,
        image_weights.reshape(1, -1),
        own.reshape(flat),
        own_p.reshape(flat),
        near,
        near_p.reshape(flat),
        regions.reshape(flat[1:]),
        reg_p.reshape(flat[1:]),
        strip_l,
        strip_r,
        strip_lp,
        strip_rp,
    )
    return out.reshape(magnetization.shape)


def solution(mesh):
    placed = (P("img", None, None, "gy", "gx"), P(), P(), P(None, "gy", "gx"), P(), P())
    return jax.shard_map(
        body,
        mesh=mesh,
        in_specs=placed,
        out_specs=P("img", None, None, "gy", "gx"),
        check_vma=False,
    )
```

profile of v0, /device:TPU:0, one launch (start us, length us, event | category | flops | bytes accessed | tf_op | source)
XLA Modules:
  0.0 102.8 jit_solution(2760567307362348107)
XLA Ops:
  0.0 1.3 %collective-permute-start.1 = (f32[3,16,16,128]{3,2,1,0:T(8,128)}, f32[3,16,16,128]{3,2,1,0:T(8,128)S(1)}, u32[]{:S(2)}, u32[]{:S(2)}) collective-permute-start(f32[3,16,16,128]{3,2,1,0:T(8,128)} %bitcast.11), channel_id=1, source_target_pairs={{8,0},{16,8},{24,16},{9,1},{17,9},{25,17},{10,2},{18,10},{26,18},{... | collective-permute-start | bytes 1179656 | tf_op jit(solution)/shard_map/ppermute | solution.py:307
  1.3 5.6 %collective-permute-start = (f32[3,16,16,128]{3,2,1,0:T(8,128)}, f32[3,16,16,128]{3,2,1,0:T(8,128)S(1)}, u32[]{:S(2)}, u32[]{:S(2)}) collective-permute-start(f32[3,16,16,128]{3,2,1,0:T(8,128)} %bitcast.12), channel_id=1, source_target_pairs={{0,8},{8,16},{16,24},{1,9},{9,17},{17,25},{2,10},{10,18},{18,26},{... | collective-permute-start | bytes 1179656 | tf_op jit(solution)/shard_map/ppermute | solution.py:307
  6.9 2.0 %collective-permute-start.2 = (f32[3,16,16,128]{3,2,1,0:T(8,128)}, f32[3,16,16,128]{3,2,1,0:T(8,128)S(1)}, u32[]{:S(2)}, u32[]{:S(2)}) collective-permute-start(f32[3,16,16,128]{3,2,1,0:T(8,128)} %bitcast.13), channel_id=1, source_target_pairs={{0,1},{1,0},{2,3},{3,2},{4,5},{5,4},{6,7},{7,6},{8,9},{9,8},{10,11... | collective-permute-start | bytes 1179656 | tf_op jit(solution)/shard_map/ppermute | solution.py:307
  8.9 5.4 %collective-permute-done.1 = f32[3,16,16,128]{3,2,1,0:T(8,128)S(1)} collective-permute-done((f32[3,16,16,128]{3,2,1,0:T(8,128)}, f32[3,16,16,128]{3,2,1,0:T(8,128)S(1)}, u32[]{:S(2)}, u32[]{:S(2)}) %collective-permute-start.1) | collective-permute-done | bytes 393248 | tf_op jit(solution)/shard_map/ppermute | solution.py:307
  14.2 1.3 %collective-permute-done = f32[3,16,16,128]{3,2,1,0:T(8,128)S(1)} collective-permute-done((f32[3,16,16,128]{3,2,1,0:T(8,128)}, f32[3,16,16,128]{3,2,1,0:T(8,128)S(1)}, u32[]{:S(2)}, u32[]{:S(2)}) %collective-permute-start) | collective-permute-done | bytes 393248 | tf_op jit(solution)/shard_map/ppermute | solution.py:307
  15.5 0.0 copy-start.2
  15.5 0.7 copy-done.2
  16.2 0.0 copy-start
  16.2 1.0 copy-done
  17.2 0.0 copy-start.1
  17.2 1.7 %gather_images.1 = (f32[1,128]{1,0:T(1,128)S(1)}, f32[3,256,128]{2,1,0:T(8,128)S(1)}, f32[7,2,8,128]{3,2,1,0:T(8,128)S(1)}, f32[7,2,8,128]{3,2,1,0:T(8,128)S(1)}) custom-call(s32[4]{0:T(128)S(1)} %copy-done.2, f32[3,256,128]{2,1,0:T(8,128)S(1)} %bitcast.14, f32[3,256,128]{2,1,0:T(8,128)S(1)} %bitcast.20, f32[3,256,128]{2,1,0:T(8,128)S(1)} %bitcast.19, ...), custom_call_target="tpu_custom_call" | custom-call | tf_op jit(solution)/shard_map/gather_images/pallas_call | solution.py:344
  18.8 1.7 %collective-permute-start.3 = (f32[3,16,16,128]{3,2,1,0:T(8,128)S(1)}, f32[3,16,16,128]{3,2,1,0:T(8,128)S(1)}, u32[]{:S(2)}, u32[]{:S(2)}) collective-permute-start(f32[3,16,16,128]{3,2,1,0:T(8,128)S(1)} %bitcast.17), channel_id=1, source_target_pairs={{0,1},{1,0},{2,3},{3,2},{4,5},{5,4},{6,7},{7,6},{8,9},{9,8},{10,11... | collective-permute-start | bytes 1179656 | tf_op jit(solution)/shard_map/ppermute | solution.py:307
  20.6 0.4 collective-permute-start.4
  20.9 0.0 collective-permute-start.5
  20.9 1.7 %collective-permute-start.6 = (f32[7,2,8,128]{3,2,1,0:T(8,128)S(1)}, f32[7,2,8,128]{3,2,1,0:T(8,128)S(1)}, u32[]{:S(2)}, u32[]{:S(2)}) collective-permute-start(f32[7,2,8,128]{3,2,1,0:T(8,128)S(1)} %get-tuple-element.12), channel_id=1, source_target_pairs={{0,6},{2,0},{4,2},{6,4},{1,7},{3,1},{5,3},{7,5},{8,14},{10,8},{12,... | collective-permute-start | bytes 172040 | tf_op jit(solution)/shard_map/ppermute | solution.py:307
  22.7 1.9 %collective-permute-done.5.left_ref = f32[7,2,8,128]{3,2,1,0:T(8,128)S(1)} collective-permute-done((f32[7,2,8,128]{3,2,1,0:T(8,128)S(1)}, f32[7,2,8,128]{3,2,1,0:T(8,128)S(1)}, u32[]{:S(2)}, u32[]{:S(2)}) %collective-permute-start.5) | collective-permute-done | bytes 57376 | tf_op jit(solution)/shard_map/ppermute | solution.py:307
  24.5 1.6 %collective-permute-start.7 = (f32[7,2,8,128]{3,2,1,0:T(8,128)S(1)}, f32[7,2,8,128]{3,2,1,0:T(8,128)S(1)}, u32[]{:S(2)}, u32[]{:S(2)}) collective-permute-start(f32[7,2,8,128]{3,2,1,0:T(8,128)S(1)} %collective-permute-done.5.left_ref), channel_id=1, source_target_pairs={{0,1},{1,0},{2,3},{3,2},{4,5},{5,4},{6,7},{7,6},{8,9},{9,8},{10,11... | collective-permute-start | bytes 172040 | tf_op jit(solution)/shard_map/ppermute | solution.py:307
  26.2 0.0 collective-permute-done.6.right_ref
  26.2 0.4 collective-permute-start.8
  26.6 42.7 %psum.7.sq_ref = f32[1,128]{1,0:T(1,128)S(1)} all-reduce(f32[1,128]{1,0:T(1,128)S(1)} %get-tuple-element.9), channel_id=1, replica_groups=mesh['img'=4,'gx'=4,'gy'=2] {'img','gx','gy'}, use_global_device_ids=true, to_apply=%region_0.0 | all-reduce | flops 128 | bytes 1024 | tf_op jit(solution)/shard_map/psum | solution.py:362
  69.2 0.0 collective-permute-done.4
  69.2 0.0 collective-permute-done.2
  69.2 0.0 collective-permute-done.7.leftp_ref
  69.3 0.0 collective-permute-done.8.rightp_ref
  69.3 0.0 collective-permute-done.3
  69.3 0.0 copy-start.3
  69.3 0.0 copy-start.4
  69.3 0.0 copy-start.5
  69.3 0.0 copy-done.1
  69.3 0.6 copy-done.3
  69.9 0.0 copy-done.4
  70.0 0.0 copy-done.5
  70.0 32.8 %evolve.1 = f32[3,256,128]{2,1,0:T(8,128)} custom-call(s32[4]{0:T(128)S(1)} %copy-done.2, f32[8]{0:T(128)S(1)} %copy-done.3, f32[8]{0:T(128)S(1)} %copy-done.4, f32[1,128]{1,0:T(1,128)S(1)} %psum.7.sq_ref, f32[1,3]{1,0:T(1,128)S(1)} %bitcast.22, f32[3,256,128]{2,1,0:T(8,128)S(1)} %bitcast.15, f32[3,256,128]{2,1,0:T(8,128)S(1)} %bitcast.16, ...), custom_call_target="tpu_custom_call" | custom-call | tf_op jit(solution)/shard_map/evolve/pallas_call | solution.py:366
Async XLA Ops:
  0.0 14.2 %collective-permute-start.1 = (f32[3,16,16,128]{3,2,1,0:T(8,128)}, f32[3,16,16,128]{3,2,1,0:T(8,128)S(1)}, u32[]{:S(2)}, u32[]{:S(2)}) collective-permute-start(f32[3,16,16,128]{3,2,1,0:T(8,128)} %bitcast.11), channel_id=1, source_target_pairs={{8,0},{16,8},{24,16},{9,1},{17,9},{25,17},{10,2},{18,10},{26,18},{... | collective-permute-start | bytes 1179656 | tf_op jit(solution)/shard_map/ppermute | solution.py:307
  1.3 14.2 %collective-permute-start = (f32[3,16,16,128]{3,2,1,0:T(8,128)}, f32[3,16,16,128]{3,2,1,0:T(8,128)S(1)}, u32[]{:S(2)}, u32[]{:S(2)}) collective-permute-start(f32[3,16,16,128]{3,2,1,0:T(8,128)} %bitcast.12), channel_id=1, source_target_pairs={{0,8},{8,16},{16,24},{1,9},{9,17},{17,25},{2,10},{10,18},{18,26},{... | collective-permute-start | bytes 1179656 | tf_op jit(solution)/shard_map/ppermute | solution.py:307
  6.9 62.4 %collective-permute-start.2 = (f32[3,16,16,128]{3,2,1,0:T(8,128)}, f32[3,16,16,128]{3,2,1,0:T(8,128)S(1)}, u32[]{:S(2)}, u32[]{:S(2)}) collective-permute-start(f32[3,16,16,128]{3,2,1,0:T(8,128)} %bitcast.13), channel_id=1, source_target_pairs={{0,1},{1,0},{2,3},{3,2},{4,5},{5,4},{6,7},{7,6},{8,9},{9,8},{10,11... | collective-permute-start | bytes 1179656 | tf_op jit(solution)/shard_map/ppermute | solution.py:307
  15.5 0.7 copy-start.2
  16.2 1.0 copy-start
  17.2 52.1 %copy-start.1 = (f32[1,3,16,16,128]{4,3,2,1,0:T(8,128)S(1)}, f32[1,3,16,16,128]{4,3,2,1,0:T(8,128)}, u32[]{:S(2)}) copy-start(f32[1,3,16,16,128]{4,3,2,1,0:T(8,128)} %param.6) | copy-start | bytes 1179652
  18.8 50.4 %collective-permute-start.3 = (f32[3,16,16,128]{3,2,1,0:T(8,128)S(1)}, f32[3,16,16,128]{3,2,1,0:T(8,128)S(1)}, u32[]{:S(2)}, u32[]{:S(2)}) collective-permute-start(f32[3,16,16,128]{3,2,1,0:T(8,128)S(1)} %bitcast.17), channel_id=1, source_target_pairs={{0,1},{1,0},{2,3},{3,2},{4,5},{5,4},{6,7},{7,6},{8,9},{9,8},{10,11... | collective-permute-start | bytes 1179656 | tf_op jit(solution)/shard_map/ppermute | solution.py:307
  20.6 48.7 %collective-permute-start.4 = (s32[16,16,128]{2,1,0:T(8,128)}, s32[16,16,128]{2,1,0:T(8,128)S(1)}, u32[]{:S(2)}, u32[]{:S(2)}) collective-permute-start(s32[16,16,128]{2,1,0:T(8,128)} %param.9), channel_id=1, source_target_pairs={{0,1},{1,0},{2,3},{3,2},{4,5},{5,4},{6,7},{7,6},{8,9},{9,8},{10,11... | collective-permute-start | bytes 393224 | tf_op jit(solution)/shard_map/ppermute | solution.py:307
  20.9 3.6 %collective-permute-start.5 = (f32[7,2,8,128]{3,2,1,0:T(8,128)S(1)}, f32[7,2,8,128]{3,2,1,0:T(8,128)S(1)}, u32[]{:S(2)}, u32[]{:S(2)}) collective-permute-start(f32[7,2,8,128]{3,2,1,0:T(8,128)S(1)} %get-tuple-element.11), channel_id=1, source_target_pairs={{0,2},{2,4},{4,6},{6,0},{1,3},{3,5},{5,7},{7,1},{8,10},{10,12},{12... | collective-permute-start | bytes 172040 | tf_op jit(solution)/shard_map/ppermute | solution.py:307
  20.9 5.3 %collective-permute-start.6 = (f32[7,2,8,128]{3,2,1,0:T(8,128)S(1)}, f32[7,2,8,128]{3,2,1,0:T(8,128)S(1)}, u32[]{:S(2)}, u32[]{:S(2)}) collective-permute-start(f32[7,2,8,128]{3,2,1,0:T(8,128)S(1)} %get-tuple-element.12), channel_id=1, source_target_pairs={{0,6},{2,0},{4,2},{6,4},{1,7},{3,1},{5,3},{7,5},{8,14},{10,8},{12,... | collective-permute-start | bytes 172040 | tf_op jit(solution)/shard_map/ppermute | solution.py:307
  24.5 44.7 %collective-permute-start.7 = (f32[7,2,8,128]{3,2,1,0:T(8,128)S(1)}, f32[7,2,8,128]{3,2,1,0:T(8,128)S(1)}, u32[]{:S(2)}, u32[]{:S(2)}) collective-permute-start(f32[7,2,8,128]{3,2,1,0:T(8,128)S(1)} %collective-permute-done.5.left_ref), channel_id=1, source_target_pairs={{0,1},{1,0},{2,3},{3,2},{4,5},{5,4},{6,7},{7,6},{8,9},{9,8},{10,11... | collective-permute-start | bytes 172040 | tf_op jit(solution)/shard_map/ppermute | solution.py:307
  26.2 43.1 %collective-permute-start.8 = (f32[7,2,8,128]{3,2,1,0:T(8,128)S(1)}, f32[7,2,8,128]{3,2,1,0:T(8,128)S(1)}, u32[]{:S(2)}, u32[]{:S(2)}) collective-permute-start(f32[7,2,8,128]{3,2,1,0:T(8,128)S(1)} %collective-permute-done.6.right_ref), channel_id=1, source_target_pairs={{0,1},{1,0},{2,3},{3,2},{4,5},{5,4},{6,7},{7,6},{8,9},{9,8},{10,11... | collective-permute-start | bytes 172040 | tf_op jit(solution)/shard_map/ppermute | solution.py:307
  69.3 0.7 copy-start.3
  69.3 0.7 copy-start.4
  69.3 0.7 copy-start.5
where the time goes:
time: 103 us
  blocking collectives  42.7 us (41%)
  Pallas kernels  34.5 us (33%)
  starting transfers between devices  14.7 us (14%)
  waiting for transfers between devices  8.52 us (8%)
  local copies, waits for them, and re-layouts  2.31 us (2%)
    psum x1, blocking collectives, body(): squares = lax.psum(part, ('img', 'gx', 'gy'))  42.7 us
    pallas_call x1, Pallas kernels, body(): pl.pallas_call(functools.partial(evolve_kernel, ny, tiles, images, anisot...  32.8 us
    ppermute x9, starting transfers between devices, shifted(): return lax.ppermute(cells, axis, pairs)  14.7 us
    ppermute x9, waiting for transfers between devices, shifted(): return lax.ppermute(cells, axis, pairs)  8.52 us
    unnamed x12, local copies, waits for them, and re-layouts  2.31 us
  transfers between devices with their start and end apart: 9, of which 3 were waited for; matrix products, arithmetic and copies ran while one was open for 0% of the time, Pallas kernels for 2%

commit v1 on v0

--- a/solution.py
+++ b/solution.py
@@ -38,7 +38,7 @@
     near_ref[...] = jnp.where(take_up, up_ref[...], down_ref[...])
     diff = m_ref[...] - up_ref[...]
     total = jnp.sum(jnp.sum(diff * diff, axis=(0, 1), keepdims=True)[0], axis=1, keepdims=True)
-    slot = lax.broadcasted_iota(jnp.int32, (1, LANES), 1)
+    slot = lax.broadcasted_iota(jnp.int32, part_ref.shape, 1)
     part_ref[...] = jnp.where((slot == here) & (here > 0), total, 0.0)
 
     for t in range(tiles):
@@ -82,7 +82,6 @@
 def evolve_kernel(
     ny,
     tiles,
-    images,
     regions,
     lower_ref,
     aniso_ref,
@@ -120,8 +119,8 @@
     bottom = sub == 0
 
     lo = lower_ref[here]
-    slot = lax.broadcasted_iota(jnp.int32, (1, LANES), 1)
-    lengths = jnp.where((slot >= 1) & (slot < images), jnp.sqrt(sq_ref[...] + eps), 0.0)
+    slot = lax.broadcasted_iota(jnp.int32, sq_ref.shape, 1)
+    lengths = jnp.where(slot >= 1, jnp.sqrt(sq_ref[...] + eps), 0.0)
     total = jnp.sum(lengths, axis=1, keepdims=True)
     arc = jnp.sum(jnp.where(slot <= lo, lengths, 0.0), axis=1, keepdims=True)
     gap = jnp.sum(jnp.where(slot == lo + 1, lengths, 0.0), axis=1, keepdims=True)
@@ -154,8 +153,8 @@
     zeros = tuple(zero for _ in range(COMPS * tiles))
     for g, (own, near, reg) in enumerate(((m_ref, n_ref, reg_ref), (mp_ref, np_ref, regp_ref))):
 
-        def fill(k, edges, g=g, own=own, near=near, reg=reg):
-            edges = list(edges)
+        edges = list(zeros)
+        for k in range(ny):
             for t in range(tiles):
                 rows = rows_at(ny, tiles, k, t)
                 v = normal(
@@ -167,9 +166,6 @@
                 p = params(reg[rows, :])
                 for i in range(3):
                     par[i, g * ny + k, t] = p[i]
-            return tuple(edges)
-
-        edges = lax.fori_loop(0, ny, fill, zeros)
         for c in range(COMPS):
             for t in range(tiles):
                 edge[0, c, g, t] = edges[c * tiles + t]
@@ -266,39 +262,28 @@
                         strip[1 - state, c, side, g, t] = new[c]
         seams(1 - state)
 
-    def main_rows(state, g, count, pick):
-        def body(i, edges):
-            edges = list(edges)
-            for k in pick(i):
-                r, result = main_row(state, g, k)
-                for t in range(tiles):
-                    for c in range(COMPS):
-                        main[1 - state, c, r, t] = result[t][c]
-                        edges[c * tiles + t] = merge(edges[c * tiles + t], result[t][c], k)
-            return tuple(edges)
-
-        edges = lax.fori_loop(0, count, body, zeros)
+    def main_rows(state, g, rows):
+        edges = list(zeros)
+        for k in rows:
+            r, result = main_row(state, g, k)
+            for t in range(tiles):
+                for c in range(COMPS):
+                    main[1 - state, c, r, t] = result[t][c]
+                    edges[c * tiles + t] = merge(edges[c * tiles + t], result[t][c], k)
         for c in range(COMPS):
             for t in range(tiles):
                 edge[1 - state, c, g, t] = edges[c * tiles + t]
 
-    for stage in range(1, 2 * STEPS + 1):
+    for stage in range(1, 2 * STEPS):
         state = (stage + 1) % 2
-        if stage == 2 * STEPS:
-
-            def last(i, carry):
-                for k in (i, i + ny // 2):
-                    _, result = main_row(1, 0, k)
-                    for t in range(tiles):
-                        for c in range(COMPS):
-                            out_ref[c, rows_at(ny, tiles, k, t), :] = result[t][c]
-                return carry
-
-            lax.fori_loop(0, ny // 2, last, 0)
-        else:
-            main_rows(state, 0, ny // 2, lambda i: (i, i + ny // 2))
-            main_rows(state, 1, DEPTH - stage, lambda i: (i, ny - 1 - i))
-            strip_rows(state)
+        main_rows(state, 0, range(ny))
+        main_rows(state, 1, [k for k in range(ny) if not DEPTH - stage <= k < DEPTH + stage])
+        strip_rows(state)
+    for k in range(ny):
+        _, result = main_row(1, 0, k)
+        for t in range(tiles):
+            for c in range(COMPS):
+                out_ref[c, rows_at(ny, tiles, k, t), :] = result[t][c]
 
 
 def shifted(cells, axis, step, closed):
@@ -344,7 +329,7 @@
     part, near, left, right = pl.pallas_call(
         functools.partial(gather_kernel, ny, tiles),
         out_shape=(
-            jax.ShapeDtypeStruct((1, LANES), f32),
+            jax.ShapeDtypeStruct((1, images), f32),
             jax.ShapeDtypeStruct(flat, f32),
             packed,
             packed,
@@ -359,12 +344,12 @@
     strip_l = shifted(right, "gx", 1, True)
     strip_lp = around_strip(strip_l, 0)
     strip_rp = around_strip(strip_r, 1)
-    squares = lax.psum(part, ("img", "gx", "gy"))
+    squares = lax.psum(part.reshape(images), ("img", "gx", "gy"))
 
     window = ny + 2 * DEPTH
     vreg = (SUB, LANES)
     out = pl.pallas_call(
-        functools.partial(evolve_kernel, ny, tiles, images, anisotropy.shape[0]),
+        functools.partial(evolve_kernel, ny, tiles, anisotropy.shape[0]),
         out_shape=jax.ShapeDtypeStruct(flat, f32),
         in_specs=[smem] * 3 + [vmem] * 12,
         out_specs=vmem,
@@ -382,7 +367,7 @@
         lower_image,
         anisotropy,
         damping,
-        squares,
+        squares.reshape(1, images),
         image_weights.reshape(1, -1),
         own.reshape(flat),
         own_p.reshape(flat),

time: 103 us -> 155 us (1.50)
  Pallas kernels: 34.5 us -> 86.6 us
    pallas_call x1, Pallas kernels: 32.8 us -> 84.9 us  [body(): pl.pallas_call(functools.partial(evolve_kernel, ny, tiles, anisotropy.sha...]
  transfers between devices with their start and end apart: 9 -> 9, of which waited for: 3 -> 3; matrix products, arithmetic and copies ran while one was open for 0% -> 0% of each run, Pallas kernels for 2% -> 1%
where the time goes in v1:
time: 155 us
  Pallas kernels  86.6 us (56%)
  blocking collectives  42.7 us (28%)
  starting transfers between devices  14.7 us (9%)
  waiting for transfers between devices  8.52 us (5%)
  local copies, waits for them, and re-layouts  2.31 us (1%)
    pallas_call x1, Pallas kernels, body(): pl.pallas_call(functools.partial(evolve_kernel, ny, tiles, anisotropy.sha...  84.9 us
    psum x1, blocking collectives, body(): squares = lax.psum(part.reshape(images), ('img', 'gx', 'gy'))  42.7 us
    ppermute x9, starting transfers between devices, shifted(): return lax.ppermute(cells, axis, pairs)  14.7 us
    ppermute x9, waiting for transfers between devices, shifted(): return lax.ppermute(cells, axis, pairs)  8.52 us
  transfers between devices with their start and end apart: 9, of which 3 were waited for; matrix products, arithmetic and copies ran while one was open for 0% of the time, Pallas kernels for 1%

profile of v1, /device:TPU:0, one launch (start us, length us, event | category | flops | bytes accessed | tf_op | source)
XLA Modules:
  0.0 154.9 jit_solution(16625067512879813380)
XLA Ops:
  0.0 1.3 collective-permute-start.1
  1.3 5.6 %collective-permute-start = (f32[3,16,16,128]{3,2,1,0:T(8,128)}, f32[3,16,16,128]{3,2,1,0:T(8,128)S(1)}, u32[]{:S(2)}, u32[]{:S(2)}) collective-permute-start(f32[3,16,16,128]{3,2,1,0:T(8,128)} %bitcast.12), channel_id=1, source_target_pairs={{0,8},{8,16},{16,24},{1,9},{9,17},{17,25},{2,10},{10,18},{18,26},{... | collective-permute-start | bytes 1179656 | tf_op jit(solution)/shard_map/ppermute | solution.py:292
  6.9 2.0 %collective-permute-start.2 = (f32[3,16,16,128]{3,2,1,0:T(8,128)}, f32[3,16,16,128]{3,2,1,0:T(8,128)S(1)}, u32[]{:S(2)}, u32[]{:S(2)}) collective-permute-start(f32[3,16,16,128]{3,2,1,0:T(8,128)} %bitcast.13), channel_id=1, source_target_pairs={{0,1},{1,0},{2,3},{3,2},{4,5},{5,4},{6,7},{7,6},{8,9},{9,8},{10,11... | collective-permute-start | bytes 1179656 | tf_op jit(solution)/shard_map/ppermute | solution.py:292
  8.9 5.4 %collective-permute-done.1 = f32[3,16,16,128]{3,2,1,0:T(8,128)S(1)} collective-permute-done((f32[3,16,16,128]{3,2,1,0:T(8,128)}, f32[3,16,16,128]{3,2,1,0:T(8,128)S(1)}, u32[]{:S(2)}, u32[]{:S(2)}) %collective-permute-start.1) | collective-permute-done | bytes 393248 | tf_op jit(solution)/shard_map/ppermute | solution.py:292
  14.2 1.3 collective-permute-done
  15.5 0.0 copy-start.2
  15.5 0.7 copy-done.2
  16.2 0.0 copy-start
  16.2 1.0 copy-done
  17.2 0.0 copy-start.1
  17.2 1.7 %gather_images.1 = (f32[1,4]{1,0:T(1,128)S(1)}, f32[3,256,128]{2,1,0:T(8,128)S(1)}, f32[7,2,8,128]{3,2,1,0:T(8,128)S(1)}, f32[7,2,8,128]{3,2,1,0:T(8,128)S(1)}) custom-call(s32[4]{0:T(128)S(1)} %copy-done.2, f32[3,256,128]{2,1,0:T(8,128)S(1)} %bitcast.14, f32[3,256,128]{2,1,0:T(8,128)S(1)} %bitcast.20, f32[3,256,128]{2,1,0:T(8,128)S(1)} %bitcast.19, ...), custom_call_target="tpu_custom_call" | custom-call | tf_op jit(solution)/shard_map/gather_images/pallas_call | solution.py:329
  18.8 1.7 %collective-permute-start.3 = (f32[3,16,16,128]{3,2,1,0:T(8,128)S(1)}, f32[3,16,16,128]{3,2,1,0:T(8,128)S(1)}, u32[]{:S(2)}, u32[]{:S(2)}) collective-permute-start(f32[3,16,16,128]{3,2,1,0:T(8,128)S(1)} %bitcast.17), channel_id=1, source_target_pairs={{0,1},{1,0},{2,3},{3,2},{4,5},{5,4},{6,7},{7,6},{8,9},{9,8},{10,11... | collective-permute-start | bytes 1179656 | tf_op jit(solution)/shard_map/ppermute | solution.py:292
  20.6 0.4 collective-permute-start.4
  20.9 0.0 collective-permute-start.5
  20.9 1.7 %collective-permute-start.6 = (f32[7,2,8,128]{3,2,1,0:T(8,128)S(1)}, f32[7,2,8,128]{3,2,1,0:T(8,128)S(1)}, u32[]{:S(2)}, u32[]{:S(2)}) collective-permute-start(f32[7,2,8,128]{3,2,1,0:T(8,128)S(1)} %get-tuple-element.12), channel_id=1, source_target_pairs={{0,6},{2,0},{4,2},{6,4},{1,7},{3,1},{5,3},{7,5},{8,14},{10,8},{12,... | collective-permute-start | bytes 172040 | tf_op jit(solution)/shard_map/ppermute | solution.py:292
  22.7 1.9 %collective-permute-done.5.left_ref = f32[7,2,8,128]{3,2,1,0:T(8,128)S(1)} collective-permute-done((f32[7,2,8,128]{3,2,1,0:T(8,128)S(1)}, f32[7,2,8,128]{3,2,1,0:T(8,128)S(1)}, u32[]{:S(2)}, u32[]{:S(2)}) %collective-permute-start.5) | collective-permute-done | bytes 57376 | tf_op jit(solution)/shard_map/ppermute | solution.py:292
  24.5 1.6 %collective-permute-start.7 = (f32[7,2,8,128]{3,2,1,0:T(8,128)S(1)}, f32[7,2,8,128]{3,2,1,0:T(8,128)S(1)}, u32[]{:S(2)}, u32[]{:S(2)}) collective-permute-start(f32[7,2,8,128]{3,2,1,0:T(8,128)S(1)} %collective-permute-done.5.left_ref), channel_id=1, source_target_pairs={{0,1},{1,0},{2,3},{3,2},{4,5},{5,4},{6,7},{7,6},{8,9},{9,8},{10,11... | collective-permute-start | bytes 172040 | tf_op jit(solution)/shard_map/ppermute | solution.py:292
  26.2 0.0 collective-permute-done.6.right_ref
  26.2 0.4 collective-permute-start.8
  26.6 42.7 %psum.7.sq_ref = f32[1,4]{1,0:T(1,128)S(1)} all-reduce(f32[1,4]{1,0:T(1,128)S(1)} %get-tuple-element.9), channel_id=1, replica_groups=mesh['img'=4,'gx'=4,'gy'=2] {'img','gx','gy'}, use_global_device_ids=true, to_apply=%region_0.0 | all-reduce | flops 4 | bytes 32 | tf_op jit(solution)/shard_map/psum | solution.py:347
  69.2 0.0 collective-permute-done.4
  69.2 0.0 collective-permute-done.2
  69.2 0.0 collective-permute-done.7.leftp_ref
  69.3 0.0 collective-permute-done.8.rightp_ref
  69.3 0.0 collective-permute-done.3
  69.3 0.0 copy-start.3
  69.3 0.0 copy-start.4
  69.3 0.0 copy-start.5
  69.3 0.0 copy-done.1
  69.3 0.6 copy-done.3
  69.9 0.0 copy-done.4
  70.0 0.0 copy-done.5
  70.0 84.9 %evolve.1 = f32[3,256,128]{2,1,0:T(8,128)} custom-call(s32[4]{0:T(128)S(1)} %copy-done.2, f32[8]{0:T(128)S(1)} %copy-done.3, f32[8]{0:T(128)S(1)} %copy-done.4, f32[1,4]{1,0:T(1,128)S(1)} %psum.7.sq_ref, f32[1,3]{1,0:T(1,128)S(1)} %bitcast.22, f32[3,256,128]{2,1,0:T(8,128)S(1)} %bitcast.15, f32[3,256,128]{2,1,0:T(8,128)S(1)} %bitcast.16, ...), custom_call_target="tpu_custom_call" | custom-call | tf_op jit(solution)/shard_map/evolve/pallas_call | solution.py:351
Async XLA Ops:
  0.0 14.2 %collective-permute-start.1 = (f32[3,16,16,128]{3,2,1,0:T(8,128)}, f32[3,16,16,128]{3,2,1,0:T(8,128)S(1)}, u32[]{:S(2)}, u32[]{:S(2)}) collective-permute-start(f32[3,16,16,128]{3,2,1,0:T(8,128)} %bitcast.11), channel_id=1, source_target_pairs={{8,0},{16,8},{24,16},{9,1},{17,9},{25,17},{10,2},{18,10},{26,18},{... | collective-permute-start | bytes 1179656 | tf_op jit(solution)/shard_map/ppermute | solution.py:292
  1.3 14.2 %collective-permute-start = (f32[3,16,16,128]{3,2,1,0:T(8,128)}, f32[3,16,16,128]{3,2,1,0:T(8,128)S(1)}, u32[]{:S(2)}, u32[]{:S(2)}) collective-permute-start(f32[3,16,16,128]{3,2,1,0:T(8,128)} %bitcast.12), channel_id=1, source_target_pairs={{0,8},{8,16},{16,24},{1,9},{9,17},{17,25},{2,10},{10,18},{18,26},{... | collective-permute-start | bytes 1179656 | tf_op jit(solution)/shard_map/ppermute | solution.py:292
  6.9 62.4 %collective-permute-start.2 = (f32[3,16,16,128]{3,2,1,0:T(8,128)}, f32[3,16,16,128]{3,2,1,0:T(8,128)S(1)}, u32[]{:S(2)}, u32[]{:S(2)}) collective-permute-start(f32[3,16,16,128]{3,2,1,0:T(8,128)} %bitcast.13), channel_id=1, source_target_pairs={{0,1},{1,0},{2,3},{3,2},{4,5},{5,4},{6,7},{7,6},{8,9},{9,8},{10,11... | collective-permute-start | bytes 1179656 | tf_op jit(solution)/shard_map/ppermute | solution.py:292
  15.5 0.7 copy-start.2
  16.2 1.0 copy-start
  17.2 52.1 %copy-start.1 = (f32[1,3,16,16,128]{4,3,2,1,0:T(8,128)S(1)}, f32[1,3,16,16,128]{4,3,2,1,0:T(8,128)}, u32[]{:S(2)}) copy-start(f32[1,3,16,16,128]{4,3,2,1,0:T(8,128)} %param.6) | copy-start | bytes 1179652
  18.8 50.4 %collective-permute-start.3 = (f32[3,16,16,128]{3,2,1,0:T(8,128)S(1)}, f32[3,16,16,128]{3,2,1,0:T(8,128)S(1)}, u32[]{:S(2)}, u32[]{:S(2)}) collective-permute-start(f32[3,16,16,128]{3,2,1,0:T(8,128)S(1)} %bitcast.17), channel_id=1, source_target_pairs={{0,1},{1,0},{2,3},{3,2},{4,5},{5,4},{6,7},{7,6},{8,9},{9,8},{10,11... | collective-permute-start | bytes 1179656 | tf_op jit(solution)/shard_map/ppermute | solution.py:292
  20.6 48.7 %collective-permute-start.4 = (s32[16,16,128]{2,1,0:T(8,128)}, s32[16,16,128]{2,1,0:T(8,128)S(1)}, u32[]{:S(2)}, u32[]{:S(2)}) collective-permute-start(s32[16,16,128]{2,1,0:T(8,128)} %param.9), channel_id=1, source_target_pairs={{0,1},{1,0},{2,3},{3,2},{4,5},{5,4},{6,7},{7,6},{8,9},{9,8},{10,11... | collective-permute-start | bytes 393224 | tf_op jit(solution)/shard_map/ppermute | solution.py:292
  20.9 3.6 %collective-permute-start.5 = (f32[7,2,8,128]{3,2,1,0:T(8,128)S(1)}, f32[7,2,8,128]{3,2,1,0:T(8,128)S(1)}, u32[]{:S(2)}, u32[]{:S(2)}) collective-permute-start(f32[7,2,8,128]{3,2,1,0:T(8,128)S(1)} %get-tuple-element.11), channel_id=1, source_target_pairs={{0,2},{2,4},{4,6},{6,0},{1,3},{3,5},{5,7},{7,1},{8,10},{10,12},{12... | collective-permute-start | bytes 172040 | tf_op jit(solution)/shard_map/ppermute | solution.py:292
  20.9 5.3 %collective-permute-start.6 = (f32[7,2,8,128]{3,2,1,0:T(8,128)S(1)}, f32[7,2,8,128]{3,2,1,0:T(8,128)S(1)}, u32[]{:S(2)}, u32[]{:S(2)}) collective-permute-start(f32[7,2,8,128]{3,2,1,0:T(8,128)S(1)} %get-tuple-element.12), channel_id=1, source_target_pairs={{0,6},{2,0},{4,2},{6,4},{1,7},{3,1},{5,3},{7,5},{8,14},{10,8},{12,... | collective-permute-start | bytes 172040 | tf_op jit(solution)/shard_map/ppermute | solution.py:292
  24.5 44.7 %collective-permute-start.7 = (f32[7,2,8,128]{3,2,1,0:T(8,128)S(1)}, f32[7,2,8,128]{3,2,1,0:T(8,128)S(1)}, u32[]{:S(2)}, u32[]{:S(2)}) collective-permute-start(f32[7,2,8,128]{3,2,1,0:T(8,128)S(1)} %collective-permute-done.5.left_ref), channel_id=1, source_target_pairs={{0,1},{1,0},{2,3},{3,2},{4,5},{5,4},{6,7},{7,6},{8,9},{9,8},{10,11... | collective-permute-start | bytes 172040 | tf_op jit(solution)/shard_map/ppermute | solution.py:292
  26.2 43.1 %collective-permute-start.8 = (f32[7,2,8,128]{3,2,1,0:T(8,128)S(1)}, f32[7,2,8,128]{3,2,1,0:T(8,128)S(1)}, u32[]{:S(2)}, u32[]{:S(2)}) collective-permute-start(f32[7,2,8,128]{3,2,1,0:T(8,128)S(1)} %collective-permute-done.6.right_ref), channel_id=1, source_target_pairs={{0,1},{1,0},{2,3},{3,2},{4,5},{5,4},{6,7},{7,6},{8,9},{9,8},{10,11... | collective-permute-start | bytes 172040 | tf_op jit(solution)/shard_map/ppermute | solution.py:292
  69.3 0.7 copy-start.3
  69.3 0.7 copy-start.4
  69.3 0.7 copy-start.5

commit v2 on v1

--- a/solution.py
+++ b/solution.py
@@ -16,6 +16,7 @@
 SUB = 8
 LANES = 128
 COMPS = 3
+ROWS = 2
 
 
 def lane_iota():
@@ -33,31 +34,44 @@
 def gather_kernel(ny, tiles, lower_ref, m_ref, up_ref, down_ref, reg_ref, part_ref, near_ref, left_ref, right_ref):
     here = lax.axis_index("img")
     take_up = lower_ref[here] < here
-    lane = lane_iota()
-
-    near_ref[...] = jnp.where(take_up, up_ref[...], down_ref[...])
-    diff = m_ref[...] - up_ref[...]
-    total = jnp.sum(jnp.sum(diff * diff, axis=(0, 1), keepdims=True)[0], axis=1, keepdims=True)
+    block = lane_iota() // DEPTH
+
+    def squares(i, sums):
+        sums = list(sums)
+        for u in range(2):
+            rows = pl.ds(pl.multiple_of((2 * i + u) * SUB, SUB), SUB)
+            for c in range(COMPS):
+                up = up_ref[c, rows, :]
+                near_ref[c, rows, :] = jnp.where(take_up, up, down_ref[c, rows, :])
+                diff = m_ref[c, rows, :] - up
+                sums[c + COMPS * u] = sums[c + COMPS * u] + diff * diff
+        return tuple(sums)
+
+    zero = jnp.zeros((SUB, LANES), jnp.float32)
+    sums = lax.fori_loop(0, m_ref.shape[1] // (2 * SUB), squares, (zero,) * (2 * COMPS))
+    total = jnp.sum(functools.reduce(jnp.add, sums), axis=(0, 1), keepdims=True)
     slot = lax.broadcasted_iota(jnp.int32, part_ref.shape, 1)
     part_ref[...] = jnp.where((slot == here) & (here > 0), total, 0.0)
 
-    for t in range(tiles):
-        for c in range(2 * COMPS + 1):
-            left = jnp.zeros((SUB, LANES), jnp.float32)
-            right = jnp.zeros((SUB, LANES), jnp.float32)
-            for y in range(ny):
-                rows = rows_at(ny, tiles, y, t)
+    def pack(y, carry):
+        shift = (DEPTH * (y + 1)) & (LANES - 1)
+        left = block == ((y + 1) & (ny - 1))
+        right = block == y
+        for t in range(tiles):
+            rows = rows_at(ny, tiles, y, t)
+            for c in range(2 * COMPS + 1):
                 if c < COMPS:
                     cells = m_ref[c, rows, :]
                 elif c < 2 * COMPS:
                     cells = near_ref[c - COMPS, rows, :]
                 else:
                     cells = reg_ref[rows, :].astype(jnp.float32)
-                cells = pltpu.roll(cells, (DEPTH * (y + 1)) % LANES, 1)
-                left = jnp.where(lane // DEPTH == (y + 1) % ny, cells, left)
-                right = jnp.where(lane // DEPTH == y, cells, right)
-            left_ref[c, t] = left
-            right_ref[c, t] = right
+                cells = pltpu.roll(cells, shift, 1)
+                pltpu.store(left_ref.at[c, t], cells, mask=left)
+                pltpu.store(right_ref.at[c, t], cells, mask=right)
+        return carry
+
+    lax.fori_loop(0, ny, pack, 0)
 
 
 def turn(m, h, a2, b, sc):
@@ -82,6 +96,7 @@
 def evolve_kernel(
     ny,
     tiles,
+    images,
     regions,
     lower_ref,
     aniso_ref,
@@ -119,8 +134,9 @@
     bottom = sub == 0
 
     lo = lower_ref[here]
-    slot = lax.broadcasted_iota(jnp.int32, sq_ref.shape, 1)
-    lengths = jnp.where(slot >= 1, jnp.sqrt(sq_ref[...] + eps), 0.0)
+    slot = lax.broadcasted_iota(jnp.int32, (1, LANES), 1)
+    squares = jnp.sum(sq_ref[...], axis=0, keepdims=True)
+    lengths = jnp.where((slot >= 1) & (slot < images), jnp.sqrt(squares + eps), 0.0)
     total = jnp.sum(lengths, axis=1, keepdims=True)
     arc = jnp.sum(jnp.where(slot <= lo, lengths, 0.0), axis=1, keepdims=True)
     gap = jnp.sum(jnp.where(slot == lo + 1, lengths, 0.0), axis=1, keepdims=True)
@@ -135,26 +151,24 @@
     w_own = jnp.where(below, weight, 1.0 - weight)
     w_near = jnp.where(below, 1.0 - weight, weight)
 
+    table_a = jnp.zeros((SUB, LANES), jnp.float32)
+    table_d = jnp.zeros((SUB, LANES), jnp.float32)
+    for i in range(regions):
+        table_a = jnp.where(lane == i, 2.0 * aniso_ref[i], table_a)
+        table_d = jnp.where(lane == i, damp_ref[i], table_d)
+    tables = (table_a, table_d, -time_step / (1.0 + table_d * table_d))
+
     def params(region):
-        a = jnp.full((SUB, LANES), aniso_ref[0], jnp.float32)
-        d = jnp.full((SUB, LANES), damp_ref[0], jnp.float32)
-        for i in range(1, regions):
-            inside = region == i
-            a = jnp.where(inside, aniso_ref[i], a)
-            d = jnp.where(inside, damp_ref[i], d)
-        return 2.0 * a, d, -time_step / (1.0 + d * d)
-
-    def merge(old, new, k):
+        return [jnp.take_along_axis(table, region, axis=1) for table in tables]
+
+    def keep_ends(state, g, k, t, new):
         mask = ((lane - (DEPTH * k + DEPTH - 1)) & (LANES - 1)) < 2
         shift = (DEPTH * (k + 1)) & (LANES - 1)
-        return jnp.where(mask, pltpu.roll(new, shift, 1), old)
-
-    zero = jnp.zeros((SUB, LANES), jnp.float32)
-    zeros = tuple(zero for _ in range(COMPS * tiles))
-    for g, (own, near, reg) in enumerate(((m_ref, n_ref, reg_ref), (mp_ref, np_ref, regp_ref))):
-
-        edges = list(zeros)
-        for k in range(ny):
+        for c in range(COMPS):
+            pltpu.store(edge.at[state, c, g, t], pltpu.roll(new[c], shift, 1), mask=mask)
+
+    def fill(k, carry):
+        for g, (own, near, reg) in enumerate(((m_ref, n_ref, reg_ref), (mp_ref, np_ref, regp_ref))):
             for t in range(tiles):
                 rows = rows_at(ny, tiles, k, t)
                 v = normal(
@@ -162,34 +176,33 @@
                 )
                 for c in range(COMPS):
                     main[0, c, g * ny + k, t] = v[c]
-                    edges[c * tiles + t] = merge(edges[c * tiles + t], v[c], k)
+                keep_ends(0, g, k, t, v)
                 p = params(reg[rows, :])
                 for i in range(3):
                     par[i, g * ny + k, t] = p[i]
-        for c in range(COMPS):
-            for t in range(tiles):
-                edge[0, c, g, t] = edges[c * tiles + t]
-    for side, pair in enumerate(((left_ref, leftp_ref), (right_ref, rightp_ref))):
-        for g in range(2):
-            for t in range(tiles):
+        return carry
+
+    lax.fori_loop(0, ny, fill, 0)
+
+    def fill_strips(t, carry):
+        for g, pair in enumerate(((left_ref, right_ref), (leftp_ref, rightp_ref))):
+            ends = []
+            for side in range(2):
+                cells = pair[side]
                 v = normal(
-                    [w_own * pair[g][c, t] + w_near * pair[g][COMPS + c, t] for c in range(COMPS)]
+                    [w_own * cells[c, t] + w_near * cells[COMPS + c, t] for c in range(COMPS)]
                 )
                 for c in range(COMPS):
                     strip[0, c, side, g, t] = v[c]
-                p = params(pair[g][2 * COMPS, t].astype(jnp.int32))
+                p = params(cells[2 * COMPS, t].astype(jnp.int32))
                 for i in range(3):
                     spar[i, side, g, t] = p[i]
-
-    def seams(state):
-        for c in range(COMPS):
-            for g in range(2):
-                for t in range(tiles):
-                    seam[state, c, g, t] = jnp.where(
-                        tail_lane, strip[state, c, 0, g, t], strip[state, c, 1, g, t]
-                    )
-
-    seams(0)
+                ends.append(v)
+            for c in range(COMPS):
+                seam[0, c, g, t] = jnp.where(tail_lane, ends[0][c], ends[1][c])
+        return carry
+
+    lax.fori_loop(0, tiles, fill_strips, 0)
 
     def around_z(cells, t):
         if t + 1 < tiles:
@@ -202,13 +215,13 @@
             under = jnp.where(bottom, 0.0, pltpu.roll(cells[tiles - 1], 1, 0))
         return above + under
 
-    def main_row(state, g, k):
-        r = g * ny + k
+    def main_row(state, r):
+        g = r // ny
+        k = r & (ny - 1)
         after = (r + 1) & (window - 1)
         before = (r - 1) & (window - 1)
         shift = (LANES - DEPTH * (k + 1)) & (LANES - 1)
         center = [[main[state, c, r, t] for t in range(tiles)] for c in range(COMPS)]
-        result = []
         for t in range(tiles):
             h = []
             for c in range(COMPS):
@@ -224,12 +237,16 @@
                 new = [m[c] + rate[c] for c in range(COMPS)]
             else:
                 new = normal([main[0, c, r, t] + (m[c] + rate[c]) for c in range(COMPS)])
-            result.append(new)
-        return r, result
+            for c in range(COMPS):
+                main[1 - state, c, r, t] = new[c]
+            keep_ends(1 - state, g, k, t, new)
 
     def strip_rows(state):
-        for side in range(2):
-            for g in range(2):
+        def group(g, carry):
+            ends = [[None] * tiles, [None] * tiles]
+            for side in range(2):
+                start = block == side
+                stop = block == (side + ny - 1) % ny
                 center = [[strip[state, c, side, g, t] for t in range(tiles)] for c in range(COMPS)]
                 for t in range(tiles):
                     h = []
@@ -243,8 +260,6 @@
                         else:
                             s = pltpu.roll(jnp.where(tail_lane, inner, cells), 1, 1)
                             s = s + pltpu.roll(cells, LANES - 1, 1)
-                        start = block == side
-                        stop = block == (side + ny - 1) % ny
                         s = s + pltpu.roll(jnp.where(start, other, cells), LANES - DEPTH, 1)
                         s = s + pltpu.roll(jnp.where(stop, other, cells), DEPTH, 1)
                         h.append(s + around_z(center[c], t))
@@ -260,30 +275,38 @@
                         )
                     for c in range(COMPS):
                         strip[1 - state, c, side, g, t] = new[c]
-        seams(1 - state)
-
-    def main_rows(state, g, rows):
-        edges = list(zeros)
-        for k in rows:
-            r, result = main_row(state, g, k)
+                    ends[side][t] = new
             for t in range(tiles):
                 for c in range(COMPS):
-                    main[1 - state, c, r, t] = result[t][c]
-                    edges[c * tiles + t] = merge(edges[c * tiles + t], result[t][c], k)
-        for c in range(COMPS):
-            for t in range(tiles):
-                edge[1 - state, c, g, t] = edges[c * tiles + t]
-
-    for stage in range(1, 2 * STEPS):
-        state = (stage + 1) % 2
-        main_rows(state, 0, range(ny))
-        main_rows(state, 1, [k for k in range(ny) if not DEPTH - stage <= k < DEPTH + stage])
-        strip_rows(state)
-    for k in range(ny):
-        _, result = main_row(1, 0, k)
+                    seam[1 - state, c, g, t] = jnp.where(tail_lane, ends[0][t][c], ends[1][t][c])
+            return carry
+
+        lax.fori_loop(0, 2, group, 0)
+
+    def main_rows(state, first, count):
+        def rows(i, carry):
+            for u in range(ROWS):
+                main_row(state, (first + ROWS * i + u) & (window - 1))
+            return carry
+
+        lax.fori_loop(0, count // ROWS, rows, 0)
+
+    def step(i, carry):
+        for state in range(2):
+            margin = DEPTH - 1 - state - 2 * i
+            main_rows(state, -margin, ny + 2 * margin)
+            strip_rows(state)
+        return carry
+
+    lax.fori_loop(0, STEPS, step, 0)
+
+    def hand_out(k, carry):
         for t in range(tiles):
             for c in range(COMPS):
-                out_ref[c, rows_at(ny, tiles, k, t), :] = result[t][c]
+                out_ref[c, rows_at(ny, tiles, k, t), :] = main[0, c, k, t]
+        return carry
+
+    lax.fori_loop(0, ny, hand_out, 0)
 
 
 def shifted(cells, axis, step, closed):
@@ -301,17 +324,26 @@
     return jnp.concatenate([shifted(head, "gy", -1, True), shifted(tail, "gy", 1, True)], axis=dim)
 
 
-def around_strip(cells, side):
+def diagonal(cells, step_x, step_y):
+    nx, ny = lax.axis_size("gx"), lax.axis_size("gy")
+    pairs = [
+        (x * ny + y, (x + step_x) % nx * ny + (y + step_y) % ny) for x in range(nx) for y in range(ny)
+    ]
+    return lax.ppermute(cells, ("gx", "gy"), pairs)
+
+
+def around_strip(cells, step_x, side):
     if lax.axis_size("gy") == 2:
-        return shifted(cells, "gy", 1, True)
+        return diagonal(cells, step_x, 1)
     block = (lax.broadcasted_iota(jnp.int32, cells.shape, cells.ndim - 1) // DEPTH - side) % (LANES // DEPTH)
-    return jnp.where(block < DEPTH, shifted(cells, "gy", -1, True), shifted(cells, "gy", 1, True))
+    return jnp.where(block < DEPTH, diagonal(cells, step_x, -1), diagonal(cells, step_x, 1))
 
 
 def body(magnetization, lower_image, image_weights, regions, anisotropy, damping):
     local, comps, nz, ny, nx = magnetization.shape
     images = local * lax.axis_size("img")
     tiles = nz // SUB
+    devices = lax.axis_size(("img", "gx", "gy"))
     assert local == 1 and comps == COMPS and nx == LANES
     assert ny == 2 * DEPTH and ny * DEPTH == LANES and tiles >= 2
     flat = (comps, nz * ny, nx)
@@ -329,7 +361,7 @@
     part, near, left, right = pl.pallas_call(
         functools.partial(gather_kernel, ny, tiles),
         out_shape=(
-            jax.ShapeDtypeStruct((1, images), f32),
+            jax.ShapeDtypeStruct((devices, LANES), f32),
             jax.ShapeDtypeStruct(flat, f32),
             packed,
             packed,
@@ -342,14 +374,14 @@
     near_p = around(near.reshape(own.shape), 2)
     strip_r = shifted(left, "gx", -1, True)
     strip_l = shifted(right, "gx", 1, True)
-    strip_lp = around_strip(strip_l, 0)
-    strip_rp = around_strip(strip_r, 1)
-    squares = lax.psum(part.reshape(images), ("img", "gx", "gy"))
+    strip_lp = around_strip(right, 1, 0)
+    strip_rp = around_strip(left, -1, 1)
+    squares = lax.all_to_all(part, ("img", "gx", "gy"), 0, 0, tiled=True)
 
     window = ny + 2 * DEPTH
     vreg = (SUB, LANES)
     out = pl.pallas_call(
-        functools.partial(evolve_kernel, ny, tiles, anisotropy.shape[0]),
+        functools.partial(evolve_kernel, ny, tiles, images, anisotropy.shape[0]),
         out_shape=jax.ShapeDtypeStruct(flat, f32),
         in_specs=[smem] * 3 + [vmem] * 12,
         out_specs=vmem,
@@ -367,7 +399,7 @@
         lower_image,
         anisotropy,
         damping,
-        squares.reshape(1, images),
+        squares,
         image_weights.reshape(1, -1),
         own.reshape(flat),
         own_p.reshape(flat),

time: 155 us -> 93.2 us (0.60)
  Pallas kernels: 86.6 us -> 46.3 us
  blocking collectives: 42.7 us -> 11.8 us
  waiting for transfers between devices: 8.52 us -> 15.3 us
    psum x1 -> x0, blocking collectives: 42.7 us -> none  [body(): squares = lax.psum(part.reshape(images), ('img', 'gx', 'gy'))]
    pallas_call x1, Pallas kernels: 84.9 us -> 43.7 us  [body(): pl.pallas_call(functools.partial(evolve_kernel, ny, tiles, images, anisot...]
    all_to_all x0 -> x1, blocking collectives: none -> 11.8 us  [body(): squares = lax.all_to_all(part, ('img', 'gx', 'gy'), 0, 0, tiled=True)]
    ppermute x9 -> x7, waiting for transfers between devices: 8.52 us -> 15.3 us  [shifted(): return lax.ppermute(cells, axis, pairs)]
    ppermute x9 -> x7, starting transfers between devices: 14.7 us -> 16.2 us  [shifted(): return lax.ppermute(cells, axis, pairs)]
    unnamed x12 -> x14, local copies, waits for them, and re-layouts: 2.31 us -> 3.21 us
  transfers between devices with their start and end apart: 9 -> 9, of which waited for: 3 -> 3; matrix products, arithmetic and copies ran while one was open for 0% -> 0% of each run, Pallas kernels for 1% -> 3%
where the time goes in v2:
time: 93.2 us; the launch traced here: 92.9 us
  Pallas kernels  46.3 us (50%)
  starting transfers between devices  16.2 us (17%)
  waiting for transfers between devices  15.3 us (16%)
  blocking collectives  11.8 us (13%)
  local copies, waits for them, and re-layouts  3.21 us (3%)
    pallas_call x1, Pallas kernels, body(): pl.pallas_call(functools.partial(evolve_kernel, ny, tiles, images, anisot...  43.7 us
    ppermute x7, starting transfers between devices, shifted(): return lax.ppermute(cells, axis, pairs)  16.2 us
    ppermute x7, waiting for transfers between devices, shifted(): return lax.ppermute(cells, axis, pairs)  15.3 us
    all_to_all x1, blocking collectives, body(): squares = lax.all_to_all(part, ('img', 'gx', 'gy'), 0, 0, tiled=True)  11.8 us
    unnamed x14, local copies, waits for them, and re-layouts  3.21 us
    pallas_call x1, Pallas kernels, body(): pl.pallas_call(functools.partial(gather_kernel, ny, tiles), out_shape=(ja...  2.54 us
  transfers between devices with their start and end apart: 9, of which 3 were waited for; matrix products, arithmetic and copies ran while one was open for 0% of the time, Pallas kernels for 3%

profile of v2, /device:TPU:0, one launch (start us, length us, event | category | flops | bytes accessed | tf_op | source)
XLA Modules:
  0.0 92.9 jit_solution(17562232579784521528)
XLA Ops:
  0.0 1.3 %collective-permute-start.1 = (f32[3,16,16,128]{3,2,1,0:T(8,128)}, f32[3,16,16,128]{3,2,1,0:T(8,128)S(1)}, u32[]{:S(2)}, u32[]{:S(2)}) collective-permute-start(f32[3,16,16,128]{3,2,1,0:T(8,128)} %bitcast.15), channel_id=1, source_target_pairs={{8,0},{16,8},{24,16},{9,1},{17,9},{25,17},{10,2},{18,10},{26,18},{... | collective-permute-start | bytes 1179656 | tf_op jit(solution)/shard_map/ppermute | solution.py:315
  1.3 5.6 %collective-permute-start = (f32[3,16,16,128]{3,2,1,0:T(8,128)}, f32[3,16,16,128]{3,2,1,0:T(8,128)S(1)}, u32[]{:S(2)}, u32[]{:S(2)}) collective-permute-start(f32[3,16,16,128]{3,2,1,0:T(8,128)} %bitcast.16), channel_id=1, source_target_pairs={{0,8},{8,16},{16,24},{1,9},{9,17},{17,25},{2,10},{10,18},{18,26},{... | collective-permute-start | bytes 1179656 | tf_op jit(solution)/shard_map/ppermute | solution.py:315
  6.9 2.0 %collective-permute-start.2 = (f32[3,16,16,128]{3,2,1,0:T(8,128)}, f32[3,16,16,128]{3,2,1,0:T(8,128)S(1)}, u32[]{:S(2)}, u32[]{:S(2)}) collective-permute-start(f32[3,16,16,128]{3,2,1,0:T(8,128)} %bitcast.17), channel_id=1, source_target_pairs={{0,1},{1,0},{2,3},{3,2},{4,5},{5,4},{6,7},{7,6},{8,9},{9,8},{10,11... | collective-permute-start | bytes 1179656 | tf_op jit(solution)/shard_map/ppermute | solution.py:315
  8.9 5.4 %collective-permute-done.1 = f32[3,16,16,128]{3,2,1,0:T(8,128)S(1)} collective-permute-done((f32[3,16,16,128]{3,2,1,0:T(8,128)}, f32[3,16,16,128]{3,2,1,0:T(8,128)S(1)}, u32[]{:S(2)}, u32[]{:S(2)}) %collective-permute-start.1) | collective-permute-done | bytes 393248 | tf_op jit(solution)/shard_map/ppermute | solution.py:315
  14.2 1.3 %collective-permute-done = f32[3,16,16,128]{3,2,1,0:T(8,128)S(1)} collective-permute-done((f32[3,16,16,128]{3,2,1,0:T(8,128)}, f32[3,16,16,128]{3,2,1,0:T(8,128)S(1)}, u32[]{:S(2)}, u32[]{:S(2)}) %collective-permute-start) | collective-permute-done | bytes 393248 | tf_op jit(solution)/shard_map/ppermute | solution.py:315
  15.5 0.0 copy-start.3
  15.5 0.7 copy-done.3
  16.2 0.0 copy-start
  16.2 1.0 %copy-done = f32[1,3,16,16,128]{4,3,2,1,0:T(8,128)S(1)} copy-done((f32[1,3,16,16,128]{4,3,2,1,0:T(8,128)S(1)}, f32[1,3,16,16,128]{4,3,2,1,0:T(8,128)}, u32[]{:S(2)}) %copy-start) | copy-done | bytes 393240
  17.2 0.0 copy-start.1
  17.2 0.9 copy-done.1
  18.1 0.0 copy-start.2
  18.1 2.5 %gather_images.1 = (f32[32,128]{1,0:T(8,128)S(1)}, f32[3,256,128]{2,1,0:T(8,128)S(1)}, f32[7,2,8,128]{3,2,1,0:T(8,128)S(1)}, f32[7,2,8,128]{3,2,1,0:T(8,128)S(1)}) custom-call(s32[4]{0:T(128)S(1)} %copy-done.3, f32[3,256,128]{2,1,0:T(8,128)S(1)} %bitcast.18, f32[3,256,128]{2,1,0:T(8,128)S(1)} %bitcast.23, f32[3,256,128]{2,1,0:T(8,128)S(1)} %bitcast.22, ...), custom_call_target="tpu_custom_call" | custom-call | tf_op jit(solution)/shard_map/gather_images/pallas_call | solution.py:361
  20.6 1.7 %collective-permute-start.3 = (f32[3,16,16,128]{3,2,1,0:T(8,128)S(1)}, f32[3,16,16,128]{3,2,1,0:T(8,128)S(1)}, u32[]{:S(2)}, u32[]{:S(2)}) collective-permute-start(f32[3,16,16,128]{3,2,1,0:T(8,128)S(1)} %bitcast.25), channel_id=1, source_target_pairs={{0,1},{1,0},{2,3},{3,2},{4,5},{5,4},{6,7},{7,6},{8,9},{9,8},{10,11... | collective-permute-start | bytes 1179656 | tf_op jit(solution)/shard_map/ppermute | solution.py:315
  22.3 0.4 collective-permute-start.4
  22.7 0.0 collective-permute-start.7
  22.7 2.7 %collective-permute-start.5 = (f32[7,2,8,128]{3,2,1,0:T(8,128)S(1)}, f32[7,2,8,128]{3,2,1,0:T(8,128)S(1)}, u32[]{:S(2)}, u32[]{:S(2)}) collective-permute-start(f32[7,2,8,128]{3,2,1,0:T(8,128)S(1)} %get-tuple-element.11), channel_id=1, source_target_pairs={{0,2},{2,4},{4,6},{6,0},{1,3},{3,5},{5,7},{7,1},{8,10},{10,12},{12... | collective-permute-start | bytes 172040 | tf_op jit(solution)/shard_map/ppermute | solution.py:315
  25.4 8.7 %collective-permute-done.4 = s32[16,16,128]{2,1,0:T(8,128)S(1)} collective-permute-done((s32[16,16,128]{2,1,0:T(8,128)S(1)}, s32[16,16,128]{2,1,0:T(8,128)S(1)}, u32[]{:S(2)}, u32[]{:S(2)}) %collective-permute-start.4) | collective-permute-done | bytes 131104 | tf_op jit(solution)/shard_map/ppermute | solution.py:315
  34.1 0.0 collective-permute-start.8
  34.1 0.0 collective-permute-done.2
  34.1 2.6 %collective-permute-start.6 = (f32[7,2,8,128]{3,2,1,0:T(8,128)S(1)}, f32[7,2,8,128]{3,2,1,0:T(8,128)S(1)}, u32[]{:S(2)}, u32[]{:S(2)}) collective-permute-start(f32[7,2,8,128]{3,2,1,0:T(8,128)S(1)} %get-tuple-element.12), channel_id=1, source_target_pairs={{0,6},{2,0},{4,2},{6,4},{1,7},{3,1},{5,3},{7,5},{8,14},{10,8},{12,... | collective-permute-start | bytes 172040 | tf_op jit(solution)/shard_map/ppermute | solution.py:315
  36.7 11.8 %all_to_all.11 = f32[32,1,128]{2,1,0:T(1,128)S(1)} all-to-all(f32[32,1,128]{2,1,0:T(1,128)S(1)} %bitcast.29), channel_id=1, replica_groups=mesh['img'=4,'gx'=4,'gy'=2] {'img','gx','gy'}, dimensions={0} | all-to-all | bytes 32768 | tf_op jit(solution)/shard_map/all_to_all | solution.py:379
  48.5 0.0 collective-permute-done.7.leftp_ref
  48.5 0.0 collective-permute-done.5.left_ref
  48.5 0.0 collective-permute-done.8.rightp_ref
  48.5 0.0 collective-permute-done.6.right_ref
  48.5 0.0 collective-permute-done.3
  48.5 0.0 copy-start.4
  48.5 0.0 copy-start.5
  48.5 0.0 copy-start.6
  48.5 0.0 copy-done.2
  48.5 0.6 copy-done.4
  49.2 0.0 copy-done.5
  49.2 0.0 copy-done.6
  49.2 43.7 %evolve.1 = f32[3,256,128]{2,1,0:T(8,128)} custom-call(s32[4]{0:T(128)S(1)} %copy-done.3, f32[8]{0:T(128)S(1)} %copy-done.4, f32[8]{0:T(128)S(1)} %copy-done.5, f32[32,128]{1,0:T(8,128)S(1)} %bitcast.28, f32[1,3]{1,0:T(1,128)S(1)} %bitcast.30, f32[3,256,128]{2,1,0:T(8,128)S(1)} %bitcast.19, f32[3,256,128]{2,1,0:T(8,128)S(1)} %bitcast.24, ...), custom_call_target="tpu_custom_call" | custom-call | tf_op jit(solution)/shard_map/evolve/pallas_call | solution.py:383
Async XLA Ops:
  0.0 14.2 %collective-permute-start.1 = (f32[3,16,16,128]{3,2,1,0:T(8,128)}, f32[3,16,16,128]{3,2,1,0:T(8,128)S(1)}, u32[]{:S(2)}, u32[]{:S(2)}) collective-permute-start(f32[3,16,16,128]{3,2,1,0:T(8,128)} %bitcast.15), channel_id=1, source_target_pairs={{8,0},{16,8},{24,16},{9,1},{17,9},{25,17},{10,2},{18,10},{26,18},{... | collective-permute-start | bytes 1179656 | tf_op jit(solution)/shard_map/ppermute | solution.py:315
  1.3 14.2 %collective-permute-start = (f32[3,16,16,128]{3,2,1,0:T(8,128)}, f32[3,16,16,128]{3,2,1,0:T(8,128)S(1)}, u32[]{:S(2)}, u32[]{:S(2)}) collective-permute-start(f32[3,16,16,128]{3,2,1,0:T(8,128)} %bitcast.16), channel_id=1, source_target_pairs={{0,8},{8,16},{16,24},{1,9},{9,17},{17,25},{2,10},{10,18},{18,26},{... | collective-permute-start | bytes 1179656 | tf_op jit(solution)/shard_map/ppermute | solution.py:315
  6.9 27.2 %collective-permute-start.2 = (f32[3,16,16,128]{3,2,1,0:T(8,128)}, f32[3,16,16,128]{3,2,1,0:T(8,128)S(1)}, u32[]{:S(2)}, u32[]{:S(2)}) collective-permute-start(f32[3,16,16,128]{3,2,1,0:T(8,128)} %bitcast.17), channel_id=1, source_target_pairs={{0,1},{1,0},{2,3},{3,2},{4,5},{5,4},{6,7},{7,6},{8,9},{9,8},{10,11... | collective-permute-start | bytes 1179656 | tf_op jit(solution)/shard_map/ppermute | solution.py:315
  15.5 0.7 copy-start.3
  16.2 1.0 %copy-start = (f32[1,3,16,16,128]{4,3,2,1,0:T(8,128)S(1)}, f32[1,3,16,16,128]{4,3,2,1,0:T(8,128)}, u32[]{:S(2)}) copy-start(f32[1,3,16,16,128]{4,3,2,1,0:T(8,128)} %param.6) | copy-start | bytes 1179652
  17.2 0.9 copy-start.1
  18.1 30.5 %copy-start.2 = (s32[16,16,128]{2,1,0:T(8,128)S(1)}, s32[16,16,128]{2,1,0:T(8,128)}, u32[]{:S(2)}) copy-start(s32[16,16,128]{2,1,0:T(8,128)} %param.9) | copy-start | bytes 393220
  20.6 27.9 %collective-permute-start.3 = (f32[3,16,16,128]{3,2,1,0:T(8,128)S(1)}, f32[3,16,16,128]{3,2,1,0:T(8,128)S(1)}, u32[]{:S(2)}, u32[]{:S(2)}) collective-permute-start(f32[3,16,16,128]{3,2,1,0:T(8,128)S(1)} %bitcast.25), channel_id=1, source_target_pairs={{0,1},{1,0},{2,3},{3,2},{4,5},{5,4},{6,7},{7,6},{8,9},{9,8},{10,11... | collective-permute-start | bytes 1179656 | tf_op jit(solution)/shard_map/ppermute | solution.py:315
  22.3 11.8 %collective-permute-start.4 = (s32[16,16,128]{2,1,0:T(8,128)S(1)}, s32[16,16,128]{2,1,0:T(8,128)S(1)}, u32[]{:S(2)}, u32[]{:S(2)}) collective-permute-start(s32[16,16,128]{2,1,0:T(8,128)S(1)} %copy-done.1), channel_id=1, source_target_pairs={{0,1},{1,0},{2,3},{3,2},{4,5},{5,4},{6,7},{7,6},{8,9},{9,8},{10,11... | collective-permute-start | bytes 393224 | tf_op jit(solution)/shard_map/ppermute | solution.py:315
  22.7 25.7 %collective-permute-start.7 = (f32[7,2,8,128]{3,2,1,0:T(8,128)S(1)}, f32[7,2,8,128]{3,2,1,0:T(8,128)S(1)}, u32[]{:S(2)}, u32[]{:S(2)}) collective-permute-start(f32[7,2,8,128]{3,2,1,0:T(8,128)S(1)} %get-tuple-element.11), channel_id=1, source_target_pairs={{0,3},{1,2},{2,5},{3,4},{4,7},{5,6},{6,1},{7,0},{8,11},{9,10},{10,... | collective-permute-start | bytes 172040 | tf_op jit(solution)/shard_map/ppermute | solution.py:332
  22.7 25.7 %collective-permute-start.5 = (f32[7,2,8,128]{3,2,1,0:T(8,128)S(1)}, f32[7,2,8,128]{3,2,1,0:T(8,128)S(1)}, u32[]{:S(2)}, u32[]{:S(2)}) collective-permute-start(f32[7,2,8,128]{3,2,1,0:T(8,128)S(1)} %get-tuple-element.11), channel_id=1, source_target_pairs={{0,2},{2,4},{4,6},{6,0},{1,3},{3,5},{5,7},{7,1},{8,10},{10,12},{12... | collective-permute-start | bytes 172040 | tf_op jit(solution)/shard_map/ppermute | solution.py:315
  34.1 14.4 %collective-permute-start.8 = (f32[7,2,8,128]{3,2,1,0:T(8,128)S(1)}, f32[7,2,8,128]{3,2,1,0:T(8,128)S(1)}, u32[]{:S(2)}, u32[]{:S(2)}) collective-permute-start(f32[7,2,8,128]{3,2,1,0:T(8,128)S(1)} %get-tuple-element.12), channel_id=1, source_target_pairs={{0,7},{1,6},{2,1},{3,0},{4,3},{5,2},{6,5},{7,4},{8,15},{9,14},{10,... | collective-permute-start | bytes 172040 | tf_op jit(solution)/shard_map/ppermute | solution.py:332
  34.1 14.4 %collective-permute-start.6 = (f32[7,2,8,128]{3,2,1,0:T(8,128)S(1)}, f32[7,2,8,128]{3,2,1,0:T(8,128)S(1)}, u32[]{:S(2)}, u32[]{:S(2)}) collective-permute-start(f32[7,2,8,128]{3,2,1,0:T(8,128)S(1)} %get-tuple-element.12), channel_id=1, source_target_pairs={{0,6},{2,0},{4,2},{6,4},{1,7},{3,1},{5,3},{7,5},{8,14},{10,8},{12,... | collective-permute-start | bytes 172040 | tf_op jit(solution)/shard_map/ppermute | solution.py:315
  48.5 0.7 copy-start.4
  48.5 0.7 copy-start.5
  48.5 0.7 copy-start.6

commit v3 on v2

--- a/solution.py
+++ b/solution.py
@@ -16,7 +16,7 @@
 SUB = 8
 LANES = 128
 COMPS = 3
-ROWS = 2
+ROWS = 4
 
 
 def lane_iota():
@@ -57,6 +57,7 @@
         shift = (DEPTH * (y + 1)) & (LANES - 1)
         left = block == ((y + 1) & (ny - 1))
         right = block == y
+        done = []
         for t in range(tiles):
             rows = rows_at(ny, tiles, y, t)
             for c in range(2 * COMPS + 1):
@@ -66,9 +67,10 @@
                     cells = near_ref[c - COMPS, rows, :]
                 else:
                     cells = reg_ref[rows, :].astype(jnp.float32)
-                cells = pltpu.roll(cells, shift, 1)
-                pltpu.store(left_ref.at[c, t], cells, mask=left)
-                pltpu.store(right_ref.at[c, t], cells, mask=right)
+                done.append((c, t, pltpu.roll(cells, shift, 1)))
+        for c, t, cells in done:
+            pltpu.store(left_ref.at[c, t], cells, mask=left)
+            pltpu.store(right_ref.at[c, t], cells, mask=right)
         return carry
 
     lax.fori_loop(0, ny, pack, 0)
@@ -114,13 +116,18 @@
     leftp_ref,
     rightp_ref,
     out_ref,
-    main,
-    strip,
-    edge,
-    seam,
+    main0,
+    main1,
+    strip0,
+    strip1,
+    edge0,
+    edge1,
+    seam0,
+    seam1,
     par,
     spar,
 ):
+    main, strip, edge, seam = (main0, main1), (strip0, strip1), (edge0, edge1), (seam0, seam1)
     window = ny + 2 * DEPTH
     here = lax.axis_index("img")
     lane = lane_iota()
@@ -161,25 +168,30 @@
     def params(region):
         return [jnp.take_along_axis(table, region, axis=1) for table in tables]
 
-    def keep_ends(state, g, k, t, new):
+    def ends_of(k, new):
+        shift = (DEPTH * (k + 1)) & (LANES - 1)
+        return [pltpu.roll(new[c], shift, 1) for c in range(COMPS)]
+
+    def keep(state, r, t, new, ends):
+        k = r & (ny - 1)
         mask = ((lane - (DEPTH * k + DEPTH - 1)) & (LANES - 1)) < 2
-        shift = (DEPTH * (k + 1)) & (LANES - 1)
         for c in range(COMPS):
-            pltpu.store(edge.at[state, c, g, t], pltpu.roll(new[c], shift, 1), mask=mask)
+            main[state][c, r, t] = new[c]
+            pltpu.store(edge[state].at[c, r // ny, t], ends[c], mask=mask)
 
     def fill(k, carry):
+        done = []
         for g, (own, near, reg) in enumerate(((m_ref, n_ref, reg_ref), (mp_ref, np_ref, regp_ref))):
             for t in range(tiles):
                 rows = rows_at(ny, tiles, k, t)
                 v = normal(
                     [w_own * own[c, rows, :] + w_near * near[c, rows, :] for c in range(COMPS)]
                 )
-                for c in range(COMPS):
-                    main[0, c, g * ny + k, t] = v[c]
-                keep_ends(0, g, k, t, v)
-                p = params(reg[rows, :])
-                for i in range(3):
-                    par[i, g * ny + k, t] = p[i]
+                done.append((g * ny + k, t, v, ends_of(k, v), params(reg[rows, :])))
+        for r, t, v, ends, p in done:
+            keep(0, r, t, v, ends)
+            for i in range(3):
+                par[i, r, t] = p[i]
         return carry
 
     lax.fori_loop(0, ny, fill, 0)
@@ -193,13 +205,13 @@
                     [w_own * cells[c, t] + w_near * cells[COMPS + c, t] for c in range(COMPS)]
                 )
                 for c in range(COMPS):
-                    strip[0, c, side, g, t] = v[c]
+                    strip[0][c, side, g, t] = v[c]
                 p = params(cells[2 * COMPS, t].astype(jnp.int32))
                 for i in range(3):
                     spar[i, side, g, t] = p[i]
                 ends.append(v)
             for c in range(COMPS):
-                seam[0, c, g, t] = jnp.where(tail_lane, ends[0][c], ends[1][c])
+                seam[0][c, g, t] = jnp.where(tail_lane, ends[0][c], ends[1][c])
         return carry
 
     lax.fori_loop(0, tiles, fill_strips, 0)
@@ -221,39 +233,40 @@
         after = (r + 1) & (window - 1)
         before = (r - 1) & (window - 1)
         shift = (LANES - DEPTH * (k + 1)) & (LANES - 1)
-        center = [[main[state, c, r, t] for t in range(tiles)] for c in range(COMPS)]
+        center = [[main[state][c, r, t] for t in range(tiles)] for c in range(COMPS)]
+        done = []
         for t in range(tiles):
             h = []
             for c in range(COMPS):
                 cells = center[c][t]
-                ends = pltpu.roll(seam[state, c, g, t], shift, 1)
+                ends = pltpu.roll(seam[state][c, g, t], shift, 1)
                 s = pltpu.roll(jnp.where(last_lane, ends, cells), 1, 1)
                 s = s + pltpu.roll(jnp.where(first_lane, ends, cells), LANES - 1, 1)
-                s = s + (main[state, c, after, t] + main[state, c, before, t])
+                s = s + (main[state][c, after, t] + main[state][c, before, t])
                 h.append(s + around_z(center[c], t))
             m = [center[c][t] for c in range(COMPS)]
             rate = turn(m, h, par[0, r, t], par[1, r, t], par[2, r, t])
             if state == 0:
                 new = [m[c] + rate[c] for c in range(COMPS)]
             else:
-                new = normal([main[0, c, r, t] + (m[c] + rate[c]) for c in range(COMPS)])
-            for c in range(COMPS):
-                main[1 - state, c, r, t] = new[c]
-            keep_ends(1 - state, g, k, t, new)
+                new = normal([main[0][c, r, t] + (m[c] + rate[c]) for c in range(COMPS)])
+            done.append((r, t, new, ends_of(k, new)))
+        return done
 
     def strip_rows(state):
         def group(g, carry):
             ends = [[None] * tiles, [None] * tiles]
+            done = []
             for side in range(2):
                 start = block == side
                 stop = block == (side + ny - 1) % ny
-                center = [[strip[state, c, side, g, t] for t in range(tiles)] for c in range(COMPS)]
+                center = [[strip[state][c, side, g, t] for t in range(tiles)] for c in range(COMPS)]
                 for t in range(tiles):
                     h = []
                     for c in range(COMPS):
                         cells = center[c][t]
-                        inner = edge[state, c, g, t]
-                        other = strip[state, c, side, 1 - g, t]
+                        inner = edge[state][c, g, t]
+                        other = strip[state][c, side, 1 - g, t]
                         if side == 0:
                             s = pltpu.roll(cells, 1, 1)
                             s = s + pltpu.roll(jnp.where(head_lane, inner, cells), LANES - 1, 1)
@@ -271,29 +284,34 @@
                         new = [m[c] + rate[c] for c in range(COMPS)]
                     else:
                         new = normal(
-                            [strip[0, c, side, g, t] + (m[c] + rate[c]) for c in range(COMPS)]
+                            [strip[0][c, side, g, t] + (m[c] + rate[c]) for c in range(COMPS)]
                         )
-                    for c in range(COMPS):
-                        strip[1 - state, c, side, g, t] = new[c]
+                    done.append((side, t, new))
                     ends[side][t] = new
+            for side, t, new in done:
+                for c in range(COMPS):
+                    strip[1 - state][c, side, g, t] = new[c]
             for t in range(tiles):
                 for c in range(COMPS):
-                    seam[1 - state, c, g, t] = jnp.where(tail_lane, ends[0][t][c], ends[1][t][c])
+                    seam[1 - state][c, g, t] = jnp.where(tail_lane, ends[0][t][c], ends[1][t][c])
             return carry
 
         lax.fori_loop(0, 2, group, 0)
 
     def main_rows(state, first, count):
         def rows(i, carry):
+            done = []
             for u in range(ROWS):
-                main_row(state, (first + ROWS * i + u) & (window - 1))
+                done += main_row(state, (first + ROWS * i + u) & (window - 1))
+            for r, t, new, ends in done:
+                keep(1 - state, r, t, new, ends)
             return carry
 
         lax.fori_loop(0, count // ROWS, rows, 0)
 
     def step(i, carry):
         for state in range(2):
-            margin = DEPTH - 1 - state - 2 * i
+            margin = DEPTH - 2 * state - 2 * i
             main_rows(state, -margin, ny + 2 * margin)
             strip_rows(state)
         return carry
@@ -303,7 +321,7 @@
     def hand_out(k, carry):
         for t in range(tiles):
             for c in range(COMPS):
-                out_ref[c, rows_at(ny, tiles, k, t), :] = main[0, c, k, t]
+                out_ref[c, rows_at(ny, tiles, k, t), :] = main[0][c, k, t]
         return carry
 
     lax.fori_loop(0, ny, hand_out, 0)
@@ -352,6 +370,8 @@
     down = shifted(own, "img", -1, False)
     own_p = around(own, 2)
     reg_p = around(regions, 1)
+
+    up, down, own_p, reg_p = lax.optimization_barrier((up, down, own_p, reg_p))
 
     smem = pl.BlockSpec(memory_space=pltpu.SMEM)
     vmem = pl.BlockSpec(memory_space=pltpu.VMEM)
@@ -386,10 +406,14 @@
         in_specs=[smem] * 3 + [vmem] * 12,
         out_specs=vmem,
         scratch_shapes=[
-            pltpu.VMEM((2, comps, window, tiles) + vreg, f32),
-            pltpu.VMEM((2, comps, 2, 2, tiles) + vreg, f32),
-            pltpu.VMEM((2, comps, 2, tiles) + vreg, f32),
-            pltpu.VMEM((2, comps, 2, tiles) + vreg, f32),
+            pltpu.VMEM((comps, window, tiles) + vreg, f32),
+            pltpu.VMEM((comps, window, tiles) + vreg, f32),
+            pltpu.VMEM((comps, 2, 2, tiles) + vreg, f32),
+            pltpu.VMEM((comps, 2, 2, tiles) + vreg, f32),
+            pltpu.VMEM((comps, 2, tiles) + vreg, f32),
+            pltpu.VMEM((comps, 2, tiles) + vreg, f32),
+            pltpu.VMEM((comps, 2, tiles) + vreg, f32),
+            pltpu.VMEM((comps, 2, tiles) + vreg, f32),
             pltpu.VMEM((3, window, tiles) + vreg, f32),
             pltpu.VMEM((3, 2, 2, tiles) + vreg, f32),
         ],

time: 93.2 us -> 60.8 us (0.65)
  Pallas kernels: 46.3 us -> 22.8 us
  waiting for transfers between devices: 15.3 us -> 7.94 us
  starting transfers between devices: 16.2 us -> 12.7 us
  blocking collectives: 11.8 us -> 13.8 us
    pallas_call x1, Pallas kernels: 43.7 us -> 20.2 us  [body(): pl.pallas_call(functools.partial(evolve_kernel, ny, tiles, images, anisot...]
    ppermute x7, waiting for transfers between devices: 15.3 us -> 7.93 us  [shifted(): return lax.ppermute(cells, axis, pairs)]
    ppermute x7, starting transfers between devices: 16.2 us -> 12.6 us  [shifted(): return lax.ppermute(cells, axis, pairs)]
    all_to_all x1, blocking collectives: 11.8 us -> 13.8 us  [body(): squares = lax.all_to_all(part, ('img', 'gx', 'gy'), 0, 0, tiled=True)]
  transfers between devices with their start and end apart: 9 -> 9, of which waited for: 3 -> 3; matrix products, arithmetic and copies ran while one was open for 0% -> 0% of each run, Pallas kernels for 3% -> 0%
where the time goes in v3:
time: 60.8 us; the launch traced here: 60.5 us
  Pallas kernels  22.8 us (38%)
  blocking collectives  13.8 us (23%)
  starting transfers between devices  12.7 us (21%)
  waiting for transfers between devices  7.94 us (13%)
  local copies, waits for them, and re-layouts  3.21 us (5%)
    pallas_call x1, Pallas kernels, body(): pl.pallas_call(functools.partial(evolve_kernel, ny, tiles, images, anisot...  20.2 us
    all_to_all x1, blocking collectives, body(): squares = lax.all_to_all(part, ('img', 'gx', 'gy'), 0, 0, tiled=True)  13.8 us
    ppermute x7, starting transfers between devices, shifted(): return lax.ppermute(cells, axis, pairs)  12.6 us
    ppermute x7, waiting for transfers between devices, shifted(): return lax.ppermute(cells, axis, pairs)  7.93 us
    unnamed x14, local copies, waits for them, and re-layouts  3.21 us
    pallas_call x1, Pallas kernels, body(): pl.pallas_call(functools.partial(gather_kernel, ny, tiles), out_shape=(ja...  2.54 us
  transfers between devices with their start and end apart: 9, of which 3 were waited for; matrix products, arithmetic and copies ran while one was open for 0% of the time, Pallas kernels for 0%

profile of v3, /device:TPU:0, one launch (start us, length us, event | category | flops | bytes accessed | tf_op | source)
XLA Modules:
  0.0 60.5 jit_solution(13934731952787049080)
XLA Ops:
  0.0 2.9 %collective-permute-start.2 = (f32[3,16,16,128]{3,2,1,0:T(8,128)}, f32[3,16,16,128]{3,2,1,0:T(8,128)S(1)}, u32[]{:S(2)}, u32[]{:S(2)}) collective-permute-start(f32[3,16,16,128]{3,2,1,0:T(8,128)} %bitcast.15), channel_id=1, source_target_pairs={{0,1},{1,0},{2,3},{3,2},{4,5},{5,4},{6,7},{7,6},{8,9},{9,8},{10,11... | collective-permute-start | bytes 1179656 | tf_op jit(solution)/shard_map/ppermute | solution.py:333
  2.9 1.3 %collective-permute-start.1 = (f32[3,16,16,128]{3,2,1,0:T(8,128)}, f32[3,16,16,128]{3,2,1,0:T(8,128)S(1)}, u32[]{:S(2)}, u32[]{:S(2)}) collective-permute-start(f32[3,16,16,128]{3,2,1,0:T(8,128)} %bitcast.16), channel_id=1, source_target_pairs={{8,0},{16,8},{24,16},{9,1},{17,9},{25,17},{10,2},{18,10},{26,18},{... | collective-permute-start | bytes 1179656 | tf_op jit(solution)/shard_map/ppermute | solution.py:333
  4.2 4.6 %collective-permute-start = (f32[3,16,16,128]{3,2,1,0:T(8,128)}, f32[3,16,16,128]{3,2,1,0:T(8,128)S(1)}, u32[]{:S(2)}, u32[]{:S(2)}) collective-permute-start(f32[3,16,16,128]{3,2,1,0:T(8,128)} %bitcast.17), channel_id=1, source_target_pairs={{0,8},{8,16},{16,24},{1,9},{9,17},{17,25},{2,10},{10,18},{18,26},{... | collective-permute-start | bytes 1179656 | tf_op jit(solution)/shard_map/ppermute | solution.py:333
  8.8 0.2 collective-permute-start.3
  9.0 6.1 %collective-permute-done.3 = s32[16,16,128]{2,1,0:T(8,128)S(1)} collective-permute-done((s32[16,16,128]{2,1,0:T(8,128)}, s32[16,16,128]{2,1,0:T(8,128)S(1)}, u32[]{:S(2)}, u32[]{:S(2)}) %collective-permute-start.3) | collective-permute-done | bytes 131104 | tf_op jit(solution)/shard_map/ppermute | solution.py:333
  15.1 0.0 collective-permute-done.2
  15.1 0.5 collective-permute-done.1
  15.6 1.3 %collective-permute-done = f32[3,16,16,128]{3,2,1,0:T(8,128)S(1)} collective-permute-done((f32[3,16,16,128]{3,2,1,0:T(8,128)}, f32[3,16,16,128]{3,2,1,0:T(8,128)S(1)}, u32[]{:S(2)}, u32[]{:S(2)}) %collective-permute-start) | collective-permute-done | bytes 393248 | tf_op jit(solution)/shard_map/ppermute | solution.py:333
  16.9 0.0 copy-start.3
  16.9 0.7 %copy-done.3 = s32[4]{0:T(128)S(1)} copy-done((s32[4]{0:T(128)S(1)}, s32[4]{0:T(128)}, u32[]{:S(2)}) %copy-start.3) | copy-done | bytes 40
  17.5 0.0 copy-start
  17.6 1.0 %copy-done = f32[1,3,16,16,128]{4,3,2,1,0:T(8,128)S(1)} copy-done((f32[1,3,16,16,128]{4,3,2,1,0:T(8,128)S(1)}, f32[1,3,16,16,128]{4,3,2,1,0:T(8,128)}, u32[]{:S(2)}) %copy-start) | copy-done | bytes 393240
  18.5 0.0 copy-start.1
  18.5 0.9 %copy-done.1 = s32[16,16,128]{2,1,0:T(8,128)S(1)} copy-done((s32[16,16,128]{2,1,0:T(8,128)S(1)}, s32[16,16,128]{2,1,0:T(8,128)}, u32[]{:S(2)}) %copy-start.1) | copy-done | bytes 131096
  19.4 0.0 copy-start.2
  19.5 2.5 %gather_images.1 = (f32[32,128]{1,0:T(8,128)S(1)}, f32[3,256,128]{2,1,0:T(8,128)S(1)}, f32[7,2,8,128]{3,2,1,0:T(8,128)S(1)}, f32[7,2,8,128]{3,2,1,0:T(8,128)S(1)}) custom-call(s32[4]{0:T(128)S(1)} %copy-done.3, f32[3,256,128]{2,1,0:T(8,128)S(1)} %bitcast.18, f32[3,256,128]{2,1,0:T(8,128)S(1)} %bitcast.23, f32[3,256,128]{2,1,0:T(8,128)S(1)} %bitcast.22, ...), custom_call_target="tpu_custom_call" | custom-call | tf_op jit(solution)/shard_map/gather_images/pallas_call | solution.py:381
  22.0 0.4 collective-permute-start.4
  22.4 0.0 collective-permute-start.7
  22.4 2.7 %collective-permute-start.5 = (f32[7,2,8,128]{3,2,1,0:T(8,128)S(1)}, f32[7,2,8,128]{3,2,1,0:T(8,128)S(1)}, u32[]{:S(2)}, u32[]{:S(2)}) collective-permute-start(f32[7,2,8,128]{3,2,1,0:T(8,128)S(1)} %get-tuple-element.19), channel_id=1, source_target_pairs={{0,2},{2,4},{4,6},{6,0},{1,3},{3,5},{5,7},{7,1},{8,10},{10,12},{12... | collective-permute-start | bytes 172040 | tf_op jit(solution)/shard_map/ppermute | solution.py:333
  25.2 0.1 collective-permute-start.8
  25.3 0.5 collective-permute-start.6
  25.8 13.8 %all_to_all.11 = f32[32,1,128]{2,1,0:T(1,128)S(1)} all-to-all(f32[32,1,128]{2,1,0:T(1,128)S(1)} %bitcast.29), channel_id=1, replica_groups=mesh['img'=4,'gx'=4,'gy'=2] {'img','gx','gy'}, dimensions={0} | all-to-all | bytes 32768 | tf_op jit(solution)/shard_map/all_to_all | solution.py:399
  39.6 0.0 collective-permute-done.7.leftp_ref
  39.6 0.0 collective-permute-done.5.left_ref
  39.6 0.0 collective-permute-done.8.rightp_ref
  39.6 0.0 collective-permute-done.6.right_ref
  39.6 0.0 collective-permute-done.4
  39.6 0.0 copy-start.4
  39.6 0.0 copy-start.5
  39.6 0.0 copy-start.6
  39.7 0.0 copy-done.2
  39.7 0.6 %copy-done.4 = f32[8]{0:T(128)S(1)} copy-done((f32[8]{0:T(128)S(1)}, f32[8]{0:T(128)}, u32[]{:S(2)}) %copy-start.4) | copy-done | bytes 56
  40.3 0.0 copy-done.5
  40.3 0.0 copy-done.6
  40.3 20.2 %evolve.1 = f32[3,256,128]{2,1,0:T(8,128)} custom-call(s32[4]{0:T(128)S(1)} %copy-done.3, f32[8]{0:T(128)S(1)} %copy-done.4, f32[8]{0:T(128)S(1)} %copy-done.5, f32[32,128]{1,0:T(8,128)S(1)} %bitcast.28, f32[1,3]{1,0:T(1,128)S(1)} %bitcast.30, f32[3,256,128]{2,1,0:T(8,128)S(1)} %bitcast.19, f32[3,256,128]{2,1,0:T(8,128)S(1)} %bitcast.24, ...), custom_call_target="tpu_custom_call" | custom-call | tf_op jit(solution)/shard_map/evolve/pallas_call | solution.py:403
Async XLA Ops:
  0.0 15.1 %collective-permute-start.2 = (f32[3,16,16,128]{3,2,1,0:T(8,128)}, f32[3,16,16,128]{3,2,1,0:T(8,128)S(1)}, u32[]{:S(2)}, u32[]{:S(2)}) collective-permute-start(f32[3,16,16,128]{3,2,1,0:T(8,128)} %bitcast.15), channel_id=1, source_target_pairs={{0,1},{1,0},{2,3},{3,2},{4,5},{5,4},{6,7},{7,6},{8,9},{9,8},{10,11... | collective-permute-start | bytes 1179656 | tf_op jit(solution)/shard_map/ppermute | solution.py:333
  2.9 12.7 %collective-permute-start.1 = (f32[3,16,16,128]{3,2,1,0:T(8,128)}, f32[3,16,16,128]{3,2,1,0:T(8,128)S(1)}, u32[]{:S(2)}, u32[]{:S(2)}) collective-permute-start(f32[3,16,16,128]{3,2,1,0:T(8,128)} %bitcast.16), channel_id=1, source_target_pairs={{8,0},{16,8},{24,16},{9,1},{17,9},{25,17},{10,2},{18,10},{26,18},{... | collective-permute-start | bytes 1179656 | tf_op jit(solution)/shard_map/ppermute | solution.py:333
  4.2 12.7 %collective-permute-start = (f32[3,16,16,128]{3,2,1,0:T(8,128)}, f32[3,16,16,128]{3,2,1,0:T(8,128)S(1)}, u32[]{:S(2)}, u32[]{:S(2)}) collective-permute-start(f32[3,16,16,128]{3,2,1,0:T(8,128)} %bitcast.17), channel_id=1, source_target_pairs={{0,8},{8,16},{16,24},{1,9},{9,17},{17,25},{2,10},{10,18},{18,26},{... | collective-permute-start | bytes 1179656 | tf_op jit(solution)/shard_map/ppermute | solution.py:333
  8.8 6.3 %collective-permute-start.3 = (s32[16,16,128]{2,1,0:T(8,128)}, s32[16,16,128]{2,1,0:T(8,128)S(1)}, u32[]{:S(2)}, u32[]{:S(2)}) collective-permute-start(s32[16,16,128]{2,1,0:T(8,128)} %param.9), channel_id=1, source_target_pairs={{0,1},{1,0},{2,3},{3,2},{4,5},{5,4},{6,7},{7,6},{8,9},{9,8},{10,11... | collective-permute-start | bytes 393224 | tf_op jit(solution)/shard_map/ppermute | solution.py:333
  16.9 0.7 %copy-start.3 = (s32[4]{0:T(128)S(1)}, s32[4]{0:T(128)}, u32[]{:S(2)}) copy-start(s32[4]{0:T(128)} %lower_ref.3) | copy-start | bytes 52
  17.5 1.0 %copy-start = (f32[1,3,16,16,128]{4,3,2,1,0:T(8,128)S(1)}, f32[1,3,16,16,128]{4,3,2,1,0:T(8,128)}, u32[]{:S(2)}) copy-start(f32[1,3,16,16,128]{4,3,2,1,0:T(8,128)} %param.6) | copy-start | bytes 1179652
  18.5 0.9 %copy-start.1 = (s32[16,16,128]{2,1,0:T(8,128)S(1)}, s32[16,16,128]{2,1,0:T(8,128)}, u32[]{:S(2)}) copy-start(s32[16,16,128]{2,1,0:T(8,128)} %param.9) | copy-start | bytes 393220
  19.4 20.2 %copy-start.2 = (s32[16,16,128]{2,1,0:T(8,128)S(1)}, s32[16,16,128]{2,1,0:T(8,128)}, u32[]{:S(2)}) copy-start(s32[16,16,128]{2,1,0:T(8,128)} %param.9) | copy-start | bytes 393220
  22.0 17.6 %collective-permute-start.4 = (f32[3,16,16,128]{3,2,1,0:T(8,128)S(1)}, f32[3,16,16,128]{3,2,1,0:T(8,128)S(1)}, u32[]{:S(2)}, u32[]{:S(2)}) collective-permute-start(f32[3,16,16,128]{3,2,1,0:T(8,128)S(1)} %bitcast.25), channel_id=1, source_target_pairs={{0,1},{1,0},{2,3},{3,2},{4,5},{5,4},{6,7},{7,6},{8,9},{9,8},{10,11... | collective-permute-start | bytes 1179656 | tf_op jit(solution)/shard_map/ppermute | solution.py:333
  22.4 17.2 %collective-permute-start.7 = (f32[7,2,8,128]{3,2,1,0:T(8,128)S(1)}, f32[7,2,8,128]{3,2,1,0:T(8,128)S(1)}, u32[]{:S(2)}, u32[]{:S(2)}) collective-permute-start(f32[7,2,8,128]{3,2,1,0:T(8,128)S(1)} %get-tuple-element.19), channel_id=1, source_target_pairs={{0,3},{1,2},{2,5},{3,4},{4,7},{5,6},{6,1},{7,0},{8,11},{9,10},{10,... | collective-permute-start | bytes 172040 | tf_op jit(solution)/shard_map/ppermute | solution.py:350
  22.4 17.2 %collective-permute-start.5 = (f32[7,2,8,128]{3,2,1,0:T(8,128)S(1)}, f32[7,2,8,128]{3,2,1,0:T(8,128)S(1)}, u32[]{:S(2)}, u32[]{:S(2)}) collective-permute-start(f32[7,2,8,128]{3,2,1,0:T(8,128)S(1)} %get-tuple-element.19), channel_id=1, source_target_pairs={{0,2},{2,4},{4,6},{6,0},{1,3},{3,5},{5,7},{7,1},{8,10},{10,12},{12... | collective-permute-start | bytes 172040 | tf_op jit(solution)/shard_map/ppermute | solution.py:333
  25.2 14.4 %collective-permute-start.8 = (f32[7,2,8,128]{3,2,1,0:T(8,128)S(1)}, f32[7,2,8,128]{3,2,1,0:T(8,128)S(1)}, u32[]{:S(2)}, u32[]{:S(2)}) collective-permute-start(f32[7,2,8,128]{3,2,1,0:T(8,128)S(1)} %get-tuple-element.20), channel_id=1, source_target_pairs={{0,7},{1,6},{2,1},{3,0},{4,3},{5,2},{6,5},{7,4},{8,15},{9,14},{10,... | collective-permute-start | bytes 172040 | tf_op jit(solution)/shard_map/ppermute | solution.py:350
  25.3 14.3 %collective-permute-start.6 = (f32[7,2,8,128]{3,2,1,0:T(8,128)S(1)}, f32[7,2,8,128]{3,2,1,0:T(8,128)S(1)}, u32[]{:S(2)}, u32[]{:S(2)}) collective-permute-start(f32[7,2,8,128]{3,2,1,0:T(8,128)S(1)} %get-tuple-element.20), channel_id=1, source_target_pairs={{0,6},{2,0},{4,2},{6,4},{1,7},{3,1},{5,3},{7,5},{8,14},{10,8},{12,... | collective-permute-start | bytes 172040 | tf_op jit(solution)/shard_map/ppermute | solution.py:333
  39.6 0.7 %copy-start.4 = (f32[8]{0:T(128)S(1)}, f32[8]{0:T(128)}, u32[]{:S(2)}) copy-start(f32[8]{0:T(128)} %aniso_ref.1) | copy-start | bytes 100
  39.6 0.7 %copy-start.5 = (f32[8]{0:T(128)S(1)}, f32[8]{0:T(128)}, u32[]{:S(2)}) copy-start(f32[8]{0:T(128)} %damp_ref.1) | copy-start | bytes 100
  39.6 0.7 %copy-start.6 = (f32[3]{0:T(128)S(1)}, f32[3]{0:T(128)}, u32[]{:S(2)}) copy-start(f32[3]{0:T(128)} %param.8) | copy-start | bytes 40

commit v4 on v3

--- a/solution.py
+++ b/solution.py
@@ -120,14 +120,13 @@
     main1,
     strip0,
     strip1,
-    edge0,
-    edge1,
+    edge,
     seam0,
     seam1,
     par,
     spar,
 ):
-    main, strip, edge, seam = (main0, main1), (strip0, strip1), (edge0, edge1), (seam0, seam1)
+    main, strip, seam = (main0, main1), (strip0, strip1), (seam0, seam1)
     window = ny + 2 * DEPTH
     here = lax.axis_index("img")
     lane = lane_iota()
@@ -172,13 +171,6 @@
         shift = (DEPTH * (k + 1)) & (LANES - 1)
         return [pltpu.roll(new[c], shift, 1) for c in range(COMPS)]
 
-    def keep(state, r, t, new, ends):
-        k = r & (ny - 1)
-        mask = ((lane - (DEPTH * k + DEPTH - 1)) & (LANES - 1)) < 2
-        for c in range(COMPS):
-            main[state][c, r, t] = new[c]
-            pltpu.store(edge[state].at[c, r // ny, t], ends[c], mask=mask)
-
     def fill(k, carry):
         done = []
         for g, (own, near, reg) in enumerate(((m_ref, n_ref, reg_ref), (mp_ref, np_ref, regp_ref))):
@@ -187,14 +179,18 @@
                 v = normal(
                     [w_own * own[c, rows, :] + w_near * near[c, rows, :] for c in range(COMPS)]
                 )
-                done.append((g * ny + k, t, v, ends_of(k, v), params(reg[rows, :])))
-        for r, t, v, ends, p in done:
-            keep(0, r, t, v, ends)
+                done.append((g * ny + k, t, v, params(reg[rows, :])))
+        for r, t, v, p in done:
+            for c in range(COMPS):
+                main0[c, r, t] = v[c]
             for i in range(3):
                 par[i, r, t] = p[i]
         return carry
 
     lax.fori_loop(0, ny, fill, 0)
+
+    def seam_of(left, right):
+        return jnp.where(head_lane, pltpu.roll(left, 1, 1), pltpu.roll(right, LANES - 1, 1))
 
     def fill_strips(t, carry):
         for g, pair in enumerate(((left_ref, right_ref), (leftp_ref, rightp_ref))):
@@ -211,7 +207,7 @@
                     spar[i, side, g, t] = p[i]
                 ends.append(v)
             for c in range(COMPS):
-                seam[0][c, g, t] = jnp.where(tail_lane, ends[0][c], ends[1][c])
+                seam[0][c, g, t] = seam_of(ends[0][c], ends[1][c])
         return carry
 
     lax.fori_loop(0, tiles, fill_strips, 0)
@@ -240,8 +236,8 @@
             for c in range(COMPS):
                 cells = center[c][t]
                 ends = pltpu.roll(seam[state][c, g, t], shift, 1)
-                s = pltpu.roll(jnp.where(last_lane, ends, cells), 1, 1)
-                s = s + pltpu.roll(jnp.where(first_lane, ends, cells), LANES - 1, 1)
+                s = jnp.where(first_lane, ends, pltpu.roll(cells, 1, 1))
+                s = s + jnp.where(last_lane, ends, pltpu.roll(cells, LANES - 1, 1))
                 s = s + (main[state][c, after, t] + main[state][c, before, t])
                 h.append(s + around_z(center[c], t))
             m = [center[c][t] for c in range(COMPS)]
@@ -250,13 +246,12 @@
                 new = [m[c] + rate[c] for c in range(COMPS)]
             else:
                 new = normal([main[0][c, r, t] + (m[c] + rate[c]) for c in range(COMPS)])
-            done.append((r, t, new, ends_of(k, new)))
+            done.append((r, t, new, ends_of(k, m)))
         return done
 
     def strip_rows(state):
-        def group(g, carry):
-            ends = [[None] * tiles, [None] * tiles]
-            done = []
+        done = []
+        for g in range(2):
             for side in range(2):
                 start = block == side
                 stop = block == (side + ny - 1) % ny
@@ -265,7 +260,7 @@
                     h = []
                     for c in range(COMPS):
                         cells = center[c][t]
-                        inner = edge[state][c, g, t]
+                        inner = edge[c, g, t]
                         other = strip[state][c, side, 1 - g, t]
                         if side == 0:
                             s = pltpu.roll(cells, 1, 1)
@@ -286,17 +281,15 @@
                         new = normal(
                             [strip[0][c, side, g, t] + (m[c] + rate[c]) for c in range(COMPS)]
                         )
-                    done.append((side, t, new))
-                    ends[side][t] = new
-            for side, t, new in done:
+                    done.append((side, g, t, new))
+        for side, g, t, new in done:
+            for c in range(COMPS):
+                strip[1 - state][c, side, g, t] = new[c]
+        for g in range(2):
+            for t in range(tiles):
+                left, right = (new for _, h, u, new in done if (h, u) == (g, t))
                 for c in range(COMPS):
-                    strip[1 - state][c, side, g, t] = new[c]
-            for t in range(tiles):
-                for c in range(COMPS):
-                    seam[1 - state][c, g, t] = jnp.where(tail_lane, ends[0][t][c], ends[1][t][c])
-            return carry
-
-        lax.fori_loop(0, 2, group, 0)
+                    seam[1 - state][c, g, t] = seam_of(left[c], right[c])
 
     def main_rows(state, first, count):
         def rows(i, carry):
@@ -304,7 +297,11 @@
             for u in range(ROWS):
                 done += main_row(state, (first + ROWS * i + u) & (window - 1))
             for r, t, new, ends in done:
-                keep(1 - state, r, t, new, ends)
+                k = r & (ny - 1)
+                mask = ((lane - (DEPTH * k + DEPTH - 1)) & (LANES - 1)) < 2
+                for c in range(COMPS):
+                    main[1 - state][c, r, t] = new[c]
+                    pltpu.store(edge.at[c, r // ny, t], ends[c], mask=mask)
             return carry
 
         lax.fori_loop(0, count // ROWS, rows, 0)
@@ -410,7 +407,6 @@
             pltpu.VMEM((comps, window, tiles) + vreg, f32),
             pltpu.VMEM((comps, 2, 2, tiles) + vreg, f32),
             pltpu.VMEM((comps, 2, 2, tiles) + vreg, f32),
-            pltpu.VMEM((comps, 2, tiles) + vreg, f32),
             pltpu.VMEM((comps, 2, tiles) + vreg, f32),
             pltpu.VMEM((comps, 2, tiles) + vreg, f32),
             pltpu.VMEM((comps, 2, tiles) + vreg, f32),

time: 60.8 us -> 54.7 us (0.90)
  Pallas kernels: 22.8 us -> 16.7 us
    pallas_call x1, Pallas kernels: 20.2 us -> 14.1 us  [body(): pl.pallas_call(functools.partial(evolve_kernel, ny, tiles, images, anisot...]
where the time goes in v4:
time: 54.7 us; the launch traced here: 54.5 us
  Pallas kernels  16.7 us (31%)
  blocking collectives  13.8 us (25%)
  starting transfers between devices  12.7 us (23%)
  waiting for transfers between devices  7.94 us (15%)
  local copies, waits for them, and re-layouts  3.21 us (6%)
    pallas_call x1, Pallas kernels, body(): pl.pallas_call(functools.partial(evolve_kernel, ny, tiles, images, anisot...  14.1 us
    all_to_all x1, blocking collectives, body(): squares = lax.all_to_all(part, ('img', 'gx', 'gy'), 0, 0, tiled=True)  13.8 us
    ppermute x7, starting transfers between devices, shifted(): return lax.ppermute(cells, axis, pairs)  12.6 us
    ppermute x7, waiting for transfers between devices, shifted(): return lax.ppermute(cells, axis, pairs)  7.93 us
    unnamed x14, local copies, waits for them, and re-layouts  3.21 us
    pallas_call x1, Pallas kernels, body(): pl.pallas_call(functools.partial(gather_kernel, ny, tiles), out_shape=(ja...  2.54 us
  transfers between devices with their start and end apart: 9, of which 3 were waited for; matrix products, arithmetic and copies ran while one was open for 0% of the time, Pallas kernels for 0%

profile of v4, /device:TPU:0, one launch (start us, length us, event | category | flops | bytes accessed | tf_op | source)
XLA Modules:
  0.0 54.5 jit_solution(5537676737085278671)
XLA Ops:
  0.0 2.9 %collective-permute-start.2 = (f32[3,16,16,128]{3,2,1,0:T(8,128)}, f32[3,16,16,128]{3,2,1,0:T(8,128)S(1)}, u32[]{:S(2)}, u32[]{:S(2)}) collective-permute-start(f32[3,16,16,128]{3,2,1,0:T(8,128)} %bitcast.15), channel_id=1, source_target_pairs={{0,1},{1,0},{2,3},{3,2},{4,5},{5,4},{6,7},{7,6},{8,9},{9,8},{10,11... | collective-permute-start | bytes 1179656 | tf_op jit(solution)/shard_map/ppermute | solution.py:330
  2.9 1.3 %collective-permute-start.1 = (f32[3,16,16,128]{3,2,1,0:T(8,128)}, f32[3,16,16,128]{3,2,1,0:T(8,128)S(1)}, u32[]{:S(2)}, u32[]{:S(2)}) collective-permute-start(f32[3,16,16,128]{3,2,1,0:T(8,128)} %bitcast.16), channel_id=1, source_target_pairs={{8,0},{16,8},{24,16},{9,1},{17,9},{25,17},{10,2},{18,10},{26,18},{... | collective-permute-start | bytes 1179656 | tf_op jit(solution)/shard_map/ppermute | solution.py:330
  4.2 4.6 %collective-permute-start = (f32[3,16,16,128]{3,2,1,0:T(8,128)}, f32[3,16,16,128]{3,2,1,0:T(8,128)S(1)}, u32[]{:S(2)}, u32[]{:S(2)}) collective-permute-start(f32[3,16,16,128]{3,2,1,0:T(8,128)} %bitcast.17), channel_id=1, source_target_pairs={{0,8},{8,16},{16,24},{1,9},{9,17},{17,25},{2,10},{10,18},{18,26},{... | collective-permute-start | bytes 1179656 | tf_op jit(solution)/shard_map/ppermute | solution.py:330
  8.8 0.2 collective-permute-start.3
  9.0 6.1 %collective-permute-done.3 = s32[16,16,128]{2,1,0:T(8,128)S(1)} collective-permute-done((s32[16,16,128]{2,1,0:T(8,128)}, s32[16,16,128]{2,1,0:T(8,128)S(1)}, u32[]{:S(2)}, u32[]{:S(2)}) %collective-permute-start.3) | collective-permute-done | bytes 131104 | tf_op jit(solution)/shard_map/ppermute | solution.py:330
  15.1 0.0 collective-permute-done.2
  15.1 0.5 collective-permute-done.1
  15.6 1.3 %collective-permute-done = f32[3,16,16,128]{3,2,1,0:T(8,128)S(1)} collective-permute-done((f32[3,16,16,128]{3,2,1,0:T(8,128)}, f32[3,16,16,128]{3,2,1,0:T(8,128)S(1)}, u32[]{:S(2)}, u32[]{:S(2)}) %collective-permute-start) | collective-permute-done | bytes 393248 | tf_op jit(solution)/shard_map/ppermute | solution.py:330
  16.9 0.0 copy-start.3
  16.9 0.7 %copy-done.3 = s32[4]{0:T(128)S(1)} copy-done((s32[4]{0:T(128)S(1)}, s32[4]{0:T(128)}, u32[]{:S(2)}) %copy-start.3) | copy-done | bytes 40
  17.5 0.0 copy-start
  17.6 1.0 %copy-done = f32[1,3,16,16,128]{4,3,2,1,0:T(8,128)S(1)} copy-done((f32[1,3,16,16,128]{4,3,2,1,0:T(8,128)S(1)}, f32[1,3,16,16,128]{4,3,2,1,0:T(8,128)}, u32[]{:S(2)}) %copy-start) | copy-done | bytes 393240
  18.5 0.0 copy-start.1
  18.5 0.9 %copy-done.1 = s32[16,16,128]{2,1,0:T(8,128)S(1)} copy-done((s32[16,16,128]{2,1,0:T(8,128)S(1)}, s32[16,16,128]{2,1,0:T(8,128)}, u32[]{:S(2)}) %copy-start.1) | copy-done | bytes 131096
  19.4 0.0 copy-start.2
  19.5 2.5 %gather_images.1 = (f32[32,128]{1,0:T(8,128)S(1)}, f32[3,256,128]{2,1,0:T(8,128)S(1)}, f32[7,2,8,128]{3,2,1,0:T(8,128)S(1)}, f32[7,2,8,128]{3,2,1,0:T(8,128)S(1)}) custom-call(s32[4]{0:T(128)S(1)} %copy-done.3, f32[3,256,128]{2,1,0:T(8,128)S(1)} %bitcast.18, f32[3,256,128]{2,1,0:T(8,128)S(1)} %bitcast.23, f32[3,256,128]{2,1,0:T(8,128)S(1)} %bitcast.22, ...), custom_call_target="tpu_custom_call" | custom-call | tf_op jit(solution)/shard_map/gather_images/pallas_call | solution.py:378
  22.0 0.4 collective-permute-start.4
  22.4 0.0 collective-permute-start.7
  22.4 2.7 %collective-permute-start.5 = (f32[7,2,8,128]{3,2,1,0:T(8,128)S(1)}, f32[7,2,8,128]{3,2,1,0:T(8,128)S(1)}, u32[]{:S(2)}, u32[]{:S(2)}) collective-permute-start(f32[7,2,8,128]{3,2,1,0:T(8,128)S(1)} %get-tuple-element.19), channel_id=1, source_target_pairs={{0,2},{2,4},{4,6},{6,0},{1,3},{3,5},{5,7},{7,1},{8,10},{10,12},{12... | collective-permute-start | bytes 172040 | tf_op jit(solution)/shard_map/ppermute | solution.py:330
  25.2 0.1 collective-permute-start.8
  25.3 0.5 collective-permute-start.6
  25.8 13.8 %all_to_all.11 = f32[32,1,128]{2,1,0:T(1,128)S(1)} all-to-all(f32[32,1,128]{2,1,0:T(1,128)S(1)} %bitcast.29), channel_id=1, replica_groups=mesh['img'=4,'gx'=4,'gy'=2] {'img','gx','gy'}, dimensions={0} | all-to-all | bytes 32768 | tf_op jit(solution)/shard_map/all_to_all | solution.py:396
  39.6 0.0 collective-permute-done.7.leftp_ref
  39.6 0.0 collective-permute-done.5.left_ref
  39.6 0.0 collective-permute-done.8.rightp_ref
  39.6 0.0 collective-permute-done.6.right_ref
  39.6 0.0 collective-permute-done.4
  39.6 0.0 copy-start.4
  39.6 0.0 copy-start.5
  39.6 0.0 copy-start.6
  39.7 0.0 copy-done.2
  39.7 0.6 %copy-done.4 = f32[8]{0:T(128)S(1)} copy-done((f32[8]{0:T(128)S(1)}, f32[8]{0:T(128)}, u32[]{:S(2)}) %copy-start.4) | copy-done | bytes 56
  40.3 0.0 copy-done.5
  40.3 0.0 copy-done.6
  40.3 14.1 %evolve.1 = f32[3,256,128]{2,1,0:T(8,128)} custom-call(s32[4]{0:T(128)S(1)} %copy-done.3, f32[8]{0:T(128)S(1)} %copy-done.4, f32[8]{0:T(128)S(1)} %copy-done.5, f32[32,128]{1,0:T(8,128)S(1)} %bitcast.28, f32[1,3]{1,0:T(1,128)S(1)} %bitcast.30, f32[3,256,128]{2,1,0:T(8,128)S(1)} %bitcast.19, f32[3,256,128]{2,1,0:T(8,128)S(1)} %bitcast.24, ...), custom_call_target="tpu_custom_call" | custom-call | tf_op jit(solution)/shard_map/evolve/pallas_call | solution.py:400
Async XLA Ops:
  0.0 15.1 %collective-permute-start.2 = (f32[3,16,16,128]{3,2,1,0:T(8,128)}, f32[3,16,16,128]{3,2,1,0:T(8,128)S(1)}, u32[]{:S(2)}, u32[]{:S(2)}) collective-permute-start(f32[3,16,16,128]{3,2,1,0:T(8,128)} %bitcast.15), channel_id=1, source_target_pairs={{0,1},{1,0},{2,3},{3,2},{4,5},{5,4},{6,7},{7,6},{8,9},{9,8},{10,11... | collective-permute-start | bytes 1179656 | tf_op jit(solution)/shard_map/ppermute | solution.py:330
  2.9 12.7 %collective-permute-start.1 = (f32[3,16,16,128]{3,2,1,0:T(8,128)}, f32[3,16,16,128]{3,2,1,0:T(8,128)S(1)}, u32[]{:S(2)}, u32[]{:S(2)}) collective-permute-start(f32[3,16,16,128]{3,2,1,0:T(8,128)} %bitcast.16), channel_id=1, source_target_pairs={{8,0},{16,8},{24,16},{9,1},{17,9},{25,17},{10,2},{18,10},{26,18},{... | collective-permute-start | bytes 1179656 | tf_op jit(solution)/shard_map/ppermute | solution.py:330
  4.2 12.7 %collective-permute-start = (f32[3,16,16,128]{3,2,1,0:T(8,128)}, f32[3,16,16,128]{3,2,1,0:T(8,128)S(1)}, u32[]{:S(2)}, u32[]{:S(2)}) collective-permute-start(f32[3,16,16,128]{3,2,1,0:T(8,128)} %bitcast.17), channel_id=1, source_target_pairs={{0,8},{8,16},{16,24},{1,9},{9,17},{17,25},{2,10},{10,18},{18,26},{... | collective-permute-start | bytes 1179656 | tf_op jit(solution)/shard_map/ppermute | solution.py:330
  8.8 6.3 %collective-permute-start.3 = (s32[16,16,128]{2,1,0:T(8,128)}, s32[16,16,128]{2,1,0:T(8,128)S(1)}, u32[]{:S(2)}, u32[]{:S(2)}) collective-permute-start(s32[16,16,128]{2,1,0:T(8,128)} %param.9), channel_id=1, source_target_pairs={{0,1},{1,0},{2,3},{3,2},{4,5},{5,4},{6,7},{7,6},{8,9},{9,8},{10,11... | collective-permute-start | bytes 393224 | tf_op jit(solution)/shard_map/ppermute | solution.py:330
  16.9 0.7 %copy-start.3 = (s32[4]{0:T(128)S(1)}, s32[4]{0:T(128)}, u32[]{:S(2)}) copy-start(s32[4]{0:T(128)} %lower_ref.3) | copy-start | bytes 52
  17.5 1.0 %copy-start = (f32[1,3,16,16,128]{4,3,2,1,0:T(8,128)S(1)}, f32[1,3,16,16,128]{4,3,2,1,0:T(8,128)}, u32[]{:S(2)}) copy-start(f32[1,3,16,16,128]{4,3,2,1,0:T(8,128)} %param.6) | copy-start | bytes 1179652
  18.5 0.9 %copy-start.1 = (s32[16,16,128]{2,1,0:T(8,128)S(1)}, s32[16,16,128]{2,1,0:T(8,128)}, u32[]{:S(2)}) copy-start(s32[16,16,128]{2,1,0:T(8,128)} %param.9) | copy-start | bytes 393220
  19.4 20.2 %copy-start.2 = (s32[16,16,128]{2,1,0:T(8,128)S(1)}, s32[16,16,128]{2,1,0:T(8,128)}, u32[]{:S(2)}) copy-start(s32[16,16,128]{2,1,0:T(8,128)} %param.9) | copy-start | bytes 393220
  22.0 17.6 %collective-permute-start.4 = (f32[3,16,16,128]{3,2,1,0:T(8,128)S(1)}, f32[3,16,16,128]{3,2,1,0:T(8,128)S(1)}, u32[]{:S(2)}, u32[]{:S(2)}) collective-permute-start(f32[3,16,16,128]{3,2,1,0:T(8,128)S(1)} %bitcast.25), channel_id=1, source_target_pairs={{0,1},{1,0},{2,3},{3,2},{4,5},{5,4},{6,7},{7,6},{8,9},{9,8},{10,11... | collective-permute-start | bytes 1179656 | tf_op jit(solution)/shard_map/ppermute | solution.py:330
  22.4 17.2 %collective-permute-start.7 = (f32[7,2,8,128]{3,2,1,0:T(8,128)S(1)}, f32[7,2,8,128]{3,2,1,0:T(8,128)S(1)}, u32[]{:S(2)}, u32[]{:S(2)}) collective-permute-start(f32[7,2,8,128]{3,2,1,0:T(8,128)S(1)} %get-tuple-element.19), channel_id=1, source_target_pairs={{0,3},{1,2},{2,5},{3,4},{4,7},{5,6},{6,1},{7,0},{8,11},{9,10},{10,... | collective-permute-start | bytes 172040 | tf_op jit(solution)/shard_map/ppermute | solution.py:347
  22.4 17.2 %collective-permute-start.5 = (f32[7,2,8,128]{3,2,1,0:T(8,128)S(1)}, f32[7,2,8,128]{3,2,1,0:T(8,128)S(1)}, u32[]{:S(2)}, u32[]{:S(2)}) collective-permute-start(f32[7,2,8,128]{3,2,1,0:T(8,128)S(1)} %get-tuple-element.19), channel_id=1, source_target_pairs={{0,2},{2,4},{4,6},{6,0},{1,3},{3,5},{5,7},{7,1},{8,10},{10,12},{12... | collective-permute-start | bytes 172040 | tf_op jit(solution)/shard_map/ppermute | solution.py:330
  25.2 14.4 %collective-permute-start.8 = (f32[7,2,8,128]{3,2,1,0:T(8,128)S(1)}, f32[7,2,8,128]{3,2,1,0:T(8,128)S(1)}, u32[]{:S(2)}, u32[]{:S(2)}) collective-permute-start(f32[7,2,8,128]{3,2,1,0:T(8,128)S(1)} %get-tuple-element.20), channel_id=1, source_target_pairs={{0,7},{1,6},{2,1},{3,0},{4,3},{5,2},{6,5},{7,4},{8,15},{9,14},{10,... | collective-permute-start | bytes 172040 | tf_op jit(solution)/shard_map/ppermute | solution.py:347
  25.3 14.3 %collective-permute-start.6 = (f32[7,2,8,128]{3,2,1,0:T(8,128)S(1)}, f32[7,2,8,128]{3,2,1,0:T(8,128)S(1)}, u32[]{:S(2)}, u32[]{:S(2)}) collective-permute-start(f32[7,2,8,128]{3,2,1,0:T(8,128)S(1)} %get-tuple-element.20), channel_id=1, source_target_pairs={{0,6},{2,0},{4,2},{6,4},{1,7},{3,1},{5,3},{7,5},{8,14},{10,8},{12,... | collective-permute-start | bytes 172040 | tf_op jit(solution)/shard_map/ppermute | solution.py:330
  39.6 0.7 %copy-start.4 = (f32[8]{0:T(128)S(1)}, f32[8]{0:T(128)}, u32[]{:S(2)}) copy-start(f32[8]{0:T(128)} %aniso_ref.1) | copy-start | bytes 100
  39.6 0.7 %copy-start.5 = (f32[8]{0:T(128)S(1)}, f32[8]{0:T(128)}, u32[]{:S(2)}) copy-start(f32[8]{0:T(128)} %damp_ref.1) | copy-start | bytes 100
  39.6 0.7 %copy-start.6 = (f32[3]{0:T(128)S(1)}, f32[3]{0:T(128)}, u32[]{:S(2)}) copy-start(f32[3]{0:T(128)} %param.8) | copy-start | bytes 40

commit v5 on v4

--- a/solution.py
+++ b/solution.py
@@ -31,49 +31,93 @@
     return pl.ds(y + ny * t, SUB, stride=ny * tiles)
 
 
-def gather_kernel(ny, tiles, lower_ref, m_ref, up_ref, down_ref, reg_ref, part_ref, near_ref, left_ref, right_ref):
+def pack_kernel(
+    ny, tiles, regions, lower_ref, aniso_ref, damp_ref, share_ref, m_ref, reg_ref, both_ref, info_ref
+):
     here = lax.axis_index("img")
-    take_up = lower_ref[here] < here
-    block = lane_iota() // DEPTH
+    lane = lane_iota()
+    block = lane // DEPTH
+
+    def pack(i, carry):
+        done = []
+        for u in range(2):
+            y = 2 * i + u
+            shift = (DEPTH * (y + 1)) & (LANES - 1)
+            left = block == ((y + 1) & (ny - 1))
+            right = block == y
+            for t in range(tiles):
+                rows = rows_at(ny, tiles, y, t)
+                for c in range(COMPS + 1):
+                    cells = m_ref[c, rows, :] if c < COMPS else reg_ref[rows, :].astype(jnp.float32)
+                    done.append((c, t, left, right, pltpu.roll(cells, shift, 1)))
+        for c, t, left, right, cells in done:
+            pltpu.store(both_ref.at[0, c, t], cells, mask=left)
+            pltpu.store(both_ref.at[1, c, t], cells, mask=right)
+        return carry
+
+    lax.fori_loop(0, ny // 2, pack, 0)
+
+    table_a = jnp.zeros((SUB, LANES), jnp.float32)
+    table_d = jnp.zeros((SUB, LANES), jnp.float32)
+    for i in range(regions):
+        table_a = jnp.where(lane == i, 2.0 * aniso_ref[i], table_a)
+        table_d = jnp.where(lane == i, damp_ref[i], table_d)
+    info_ref[0] = table_a
+    info_ref[1] = table_d
+    info_ref[2] = -time_step / (1.0 + table_d * table_d)
+    share = share_ref[...]
+    spot = lax.broadcasted_iota(jnp.int32, share.shape, 1)
+    target = jnp.sum(jnp.where(spot < here, share, 0.0), axis=1, keepdims=True) / jnp.sum(
+        share, axis=1, keepdims=True
+    )
+    info_ref[3] = jnp.broadcast_to(target, (SUB, LANES))
+    info_ref[4] = jnp.full((SUB, LANES), lower_ref[here].astype(jnp.float32))
+
+
+def sort_kernel(both_ref, both_p_ref, left_ref, right_ref):
+    for g, ref in enumerate((both_ref, both_p_ref)):
+        left_ref[g] = ref[0]
+        right_ref[g] = ref[1]
+
+
+def merge_kernel(info_ref, left_ref, right_ref, out_ref, info_out_ref):
+    info_out_ref[...] = info_ref[...]
+    for g in range(2):
+        out_ref[0, g] = left_ref[g, :COMPS]
+        out_ref[1, g] = right_ref[g, :COMPS]
+
+
+def take_first(info_ref, here):
+    odd = (here & 1) == 1
+    below = info_ref[4] < here.astype(jnp.float32)
+    return jnp.where(below, jnp.where(odd, 1, 0), jnp.where(odd, 0, 1)) == 1, odd
+
+
+def gather_kernel(info_ref, m_ref, first_ref, second_ref, part_ref, near_ref):
+    here = lax.axis_index("img")
+    pick, odd = take_first(info_ref, here)
+    chunks = 4
 
     def squares(i, sums):
         sums = list(sums)
-        for u in range(2):
-            rows = pl.ds(pl.multiple_of((2 * i + u) * SUB, SUB), SUB)
-            for c in range(COMPS):
-                up = up_ref[c, rows, :]
-                near_ref[c, rows, :] = jnp.where(take_up, up, down_ref[c, rows, :])
-                diff = m_ref[c, rows, :] - up
+        done = []
+        for u in range(chunks):
+            rows = pl.ds(pl.multiple_of((chunks * i + u) * SUB, SUB), SUB)
+            for c in range(COMPS):
+                one = first_ref[c, rows, :]
+                two = second_ref[c, rows, :]
+                done.append((c, rows, jnp.where(pick, one, two)))
+                diff = m_ref[c, rows, :] - jnp.where(odd, one, two)
                 sums[c + COMPS * u] = sums[c + COMPS * u] + diff * diff
+        for c, rows, cells in done:
+            near_ref[c, rows, :] = cells
         return tuple(sums)
 
     zero = jnp.zeros((SUB, LANES), jnp.float32)
-    sums = lax.fori_loop(0, m_ref.shape[1] // (2 * SUB), squares, (zero,) * (2 * COMPS))
+    sums = lax.fori_loop(0, m_ref.shape[1] // (chunks * SUB), squares, (zero,) * (chunks * COMPS))
     total = jnp.sum(functools.reduce(jnp.add, sums), axis=(0, 1), keepdims=True)
     slot = lax.broadcasted_iota(jnp.int32, part_ref.shape, 1)
     part_ref[...] = jnp.where((slot == here) & (here > 0), total, 0.0)
-
-    def pack(y, carry):
-        shift = (DEPTH * (y + 1)) & (LANES - 1)
-        left = block == ((y + 1) & (ny - 1))
-        right = block == y
-        done = []
-        for t in range(tiles):
-            rows = rows_at(ny, tiles, y, t)
-            for c in range(2 * COMPS + 1):
-                if c < COMPS:
-                    cells = m_ref[c, rows, :]
-                elif c < 2 * COMPS:
-                    cells = near_ref[c - COMPS, rows, :]
-                else:
-                    cells = reg_ref[rows, :].astype(jnp.float32)
-                done.append((c, t, pltpu.roll(cells, shift, 1)))
-        for c, t, cells in done:
-            pltpu.store(left_ref.at[c, t], cells, mask=left)
-            pltpu.store(right_ref.at[c, t], cells, mask=right)
-        return carry
-
-    lax.fori_loop(0, ny, pack, 0)
 
 
 def turn(m, h, a2, b, sc):
@@ -99,12 +143,8 @@
     ny,
     tiles,
     images,
-    regions,
-    lower_ref,
-    aniso_ref,
-    damp_ref,
+    info_ref,
     sq_ref,
-    share_ref,
     m_ref,
     mp_ref,
     n_ref,
@@ -113,8 +153,8 @@
     regp_ref,
     left_ref,
     right_ref,
-    leftp_ref,
-    rightp_ref,
+    first_ref,
+    second_ref,
     out_ref,
     main0,
     main1,
@@ -139,30 +179,20 @@
     top = sub == SUB - 1
     bottom = sub == 0
 
-    lo = lower_ref[here]
-    slot = lax.broadcasted_iota(jnp.int32, (1, LANES), 1)
-    squares = jnp.sum(sq_ref[...], axis=0, keepdims=True)
-    lengths = jnp.where((slot >= 1) & (slot < images), jnp.sqrt(squares + eps), 0.0)
+    pick, _ = take_first(info_ref, here)
+    lo = info_ref[4]
+    slot = lane.astype(jnp.float32)
+    squares = jnp.broadcast_to(jnp.sum(sq_ref[...], axis=0, keepdims=True), (SUB, LANES))
+    lengths = jnp.where((lane >= 1) & (lane < images), jnp.sqrt(squares + eps), 0.0)
     total = jnp.sum(lengths, axis=1, keepdims=True)
     arc = jnp.sum(jnp.where(slot <= lo, lengths, 0.0), axis=1, keepdims=True)
-    gap = jnp.sum(jnp.where(slot == lo + 1, lengths, 0.0), axis=1, keepdims=True)
-    share = share_ref[...]
-    spot = lax.broadcasted_iota(jnp.int32, share.shape, 1)
-    target = jnp.sum(jnp.where(spot < here, share, 0.0), axis=1, keepdims=True) / jnp.sum(
-        share, axis=1, keepdims=True
-    )
-    weight = jnp.clip((target * total - arc) / gap, -0.5, 1.5)
-    weight = jnp.broadcast_to(weight, (SUB, LANES))
-    below = lo < here
+    gap = jnp.sum(jnp.where(slot == lo + 1.0, lengths, 0.0), axis=1, keepdims=True)
+    weight = jnp.clip((info_ref[3] * total - arc) / gap, -0.5, 1.5)
+    below = lo < here.astype(jnp.float32)
     w_own = jnp.where(below, weight, 1.0 - weight)
     w_near = jnp.where(below, 1.0 - weight, weight)
 
-    table_a = jnp.zeros((SUB, LANES), jnp.float32)
-    table_d = jnp.zeros((SUB, LANES), jnp.float32)
-    for i in range(regions):
-        table_a = jnp.where(lane == i, 2.0 * aniso_ref[i], table_a)
-        table_d = jnp.where(lane == i, damp_ref[i], table_d)
-    tables = (table_a, table_d, -time_step / (1.0 + table_d * table_d))
+    tables = (info_ref[0], info_ref[1], info_ref[2])
 
     def params(region):
         return [jnp.take_along_axis(table, region, axis=1) for table in tables]
@@ -193,21 +223,24 @@
         return jnp.where(head_lane, pltpu.roll(left, 1, 1), pltpu.roll(right, LANES - 1, 1))
 
     def fill_strips(t, carry):
-        for g, pair in enumerate(((left_ref, right_ref), (leftp_ref, rightp_ref))):
-            ends = []
-            for side in range(2):
-                cells = pair[side]
-                v = normal(
-                    [w_own * cells[c, t] + w_near * cells[COMPS + c, t] for c in range(COMPS)]
-                )
-                for c in range(COMPS):
-                    strip[0][c, side, g, t] = v[c]
-                p = params(cells[2 * COMPS, t].astype(jnp.int32))
-                for i in range(3):
-                    spar[i, side, g, t] = p[i]
-                ends.append(v)
-            for c in range(COMPS):
-                seam[0][c, g, t] = seam_of(ends[0][c], ends[1][c])
+        done = []
+        for g in range(2):
+            for side, cells in enumerate((left_ref, right_ref)):
+                near = [
+                    jnp.where(pick, first_ref[side, g, c, t], second_ref[side, g, c, t])
+                    for c in range(COMPS)
+                ]
+                v = normal([w_own * cells[g, c, t] + w_near * near[c] for c in range(COMPS)])
+                done.append((side, g, v, params(cells[g, COMPS, t].astype(jnp.int32))))
+        for side, g, v, p in done:
+            for c in range(COMPS):
+                strip0[c, side, g, t] = v[c]
+            for i in range(3):
+                spar[i, side, g, t] = p[i]
+        for g in range(2):
+            left, right = (v for _, h, v, _ in done if h == g)
+            for c in range(COMPS):
+                seam0[c, g, t] = seam_of(left[c], right[c])
         return carry
 
     lax.fori_loop(0, tiles, fill_strips, 0)
@@ -330,6 +363,12 @@
     return lax.ppermute(cells, axis, pairs)
 
 
+def swapped(cells, axis, first):
+    count = lax.axis_size(axis)
+    pairs = [(i, i + 1) for i in range(first, count - 1, 2)]
+    return lax.ppermute(cells, axis, pairs + [(j, i) for i, j in pairs])
+
+
 def around(cells, dim):
     ny = cells.shape[dim]
     if lax.axis_size("gy") == 2:
@@ -339,19 +378,13 @@
     return jnp.concatenate([shifted(head, "gy", -1, True), shifted(tail, "gy", 1, True)], axis=dim)
 
 
-def diagonal(cells, step_x, step_y):
-    nx, ny = lax.axis_size("gx"), lax.axis_size("gy")
-    pairs = [
-        (x * ny + y, (x + step_x) % nx * ny + (y + step_y) % ny) for x in range(nx) for y in range(ny)
-    ]
-    return lax.ppermute(cells, ("gx", "gy"), pairs)
-
-
-def around_strip(cells, step_x, side):
+def around_strips(both):
     if lax.axis_size("gy") == 2:
-        return diagonal(cells, step_x, 1)
-    block = (lax.broadcasted_iota(jnp.int32, cells.shape, cells.ndim - 1) // DEPTH - side) % (LANES // DEPTH)
-    return jnp.where(block < DEPTH, diagonal(cells, step_x, -1), diagonal(cells, step_x, 1))
+        return shifted(both, "gy", 1, True)
+    block = lax.broadcasted_iota(jnp.int32, both.shape, both.ndim - 1) // DEPTH
+    side = lax.broadcasted_iota(jnp.int32, both.shape, 0)
+    head = (block + side - 1) % (LANES // DEPTH) < DEPTH
+    return jnp.where(head, shifted(both, "gy", -1, True), shifted(both, "gy", 1, True))
 
 
 def body(magnetization, lower_image, image_weights, regions, anisotropy, damping):
@@ -363,44 +396,74 @@
     assert ny == 2 * DEPTH and ny * DEPTH == LANES and tiles >= 2
     flat = (comps, nz * ny, nx)
     own = magnetization[0]
-    up = shifted(own, "img", 1, False)
-    down = shifted(own, "img", -1, False)
+    first = swapped(own, "img", 0)
+    second = swapped(own, "img", 1)
     own_p = around(own, 2)
-    reg_p = around(regions, 1)
-
-    up, down, own_p, reg_p = lax.optimization_barrier((up, down, own_p, reg_p))
 
     smem = pl.BlockSpec(memory_space=pltpu.SMEM)
     vmem = pl.BlockSpec(memory_space=pltpu.VMEM)
     f32 = jnp.float32
     limit = pltpu.CompilerParams(vmem_limit_bytes=32 * 1024 * 1024)
-    packed = jax.ShapeDtypeStruct((2 * comps + 1, tiles, SUB, LANES), f32)
-    part, near, left, right = pl.pallas_call(
-        functools.partial(gather_kernel, ny, tiles),
+    vreg = (SUB, LANES)
+    both, info = pl.pallas_call(
+        functools.partial(pack_kernel, ny, tiles, anisotropy.shape[0]),
         out_shape=(
-            jax.ShapeDtypeStruct((devices, LANES), f32),
-            jax.ShapeDtypeStruct(flat, f32),
-            packed,
-            packed,
+            jax.ShapeDtypeStruct((2, comps + 1, tiles) + vreg, f32),
+            jax.ShapeDtypeStruct((5,) + vreg, f32),
         ),
-        in_specs=[smem] + [vmem] * 4,
-        out_specs=(vmem,) * 4,
+        in_specs=[smem] * 3 + [vmem] * 3,
+        out_specs=(vmem,) * 2,
+        compiler_params=limit,
+        name="pack_strips",
+    )(
+        lower_image,
+        anisotropy,
+        damping,
+        image_weights.reshape(1, -1),
+        own.reshape(flat),
+        regions.reshape(flat[1:]),
+    )
+    left, right = pl.pallas_call(
+        sort_kernel,
+        out_shape=(jax.ShapeDtypeStruct((2, comps + 1, tiles) + vreg, f32),) * 2,
+        in_specs=[vmem] * 2,
+        out_specs=(vmem,) * 2,
+        compiler_params=limit,
+        name="sort_strips",
+    )(both, around_strips(both))
+    strips = (shifted(right, "gx", 1, True), shifted(left, "gx", -1, True))
+    strips_all, info = pl.pallas_call(
+        merge_kernel,
+        out_shape=(
+            jax.ShapeDtypeStruct((2, 2, comps, tiles) + vreg, f32),
+            jax.ShapeDtypeStruct(info.shape, f32),
+        ),
+        in_specs=[vmem] * 3,
+        out_specs=(vmem,) * 2,
+        compiler_params=limit,
+        name="merge_strips",
+    )(info, *strips)
+    strips_first = swapped(strips_all, "img", 0)
+    strips_second = swapped(strips_all, "img", 1)
+    reg_p = around(regions, 1)
+
+    info, own_p = lax.optimization_barrier((info, own_p))
+    part, near = pl.pallas_call(
+        gather_kernel,
+        out_shape=(jax.ShapeDtypeStruct((devices, LANES), f32), jax.ShapeDtypeStruct(flat, f32)),
+        in_specs=[vmem] * 4,
+        out_specs=(vmem,) * 2,
         compiler_params=limit,
         name="gather_images",
-    )(lower_image, own.reshape(flat), up.reshape(flat), down.reshape(flat), regions.reshape(flat[1:]))
+    )(info, own.reshape(flat), first.reshape(flat), second.reshape(flat))
     near_p = around(near.reshape(own.shape), 2)
-    strip_r = shifted(left, "gx", -1, True)
-    strip_l = shifted(right, "gx", 1, True)
-    strip_lp = around_strip(right, 1, 0)
-    strip_rp = around_strip(left, -1, 1)
     squares = lax.all_to_all(part, ("img", "gx", "gy"), 0, 0, tiled=True)
 
     window = ny + 2 * DEPTH
-    vreg = (SUB, LANES)
     out = pl.pallas_call(
-        functools.partial(evolve_kernel, ny, tiles, images, anisotropy.shape[0]),
+        functools.partial(evolve_kernel, ny, tiles, images),
         out_shape=jax.ShapeDtypeStruct(flat, f32),
-        in_specs=[smem] * 3 + [vmem] * 12,
+        in_specs=[vmem] * 12,
         out_specs=vmem,
         scratch_shapes=[
             pltpu.VMEM((comps, window, tiles) + vreg, f32),
@@ -416,21 +479,17 @@
         compiler_params=limit,
         name="evolve",
     )(
-        lower_image,
-        anisotropy,
-        damping,
+        info,
         squares,
-        image_weights.reshape(1, -1),
         own.reshape(flat),
         own_p.reshape(flat),
         near,
         near_p.reshape(flat),
         regions.reshape(flat[1:]),
         reg_p.reshape(flat[1:]),
-        strip_l,
-        strip_r,
-        strip_lp,
-        strip_rp,
+        *strips,
+        strips_first,
+        strips_second,
     )
     return out.reshape(magnetization.shape)
 

time: 54.7 us -> 50.5 us (0.923)
  blocking collectives: 13.8 us -> 0 us
  starting transfers between devices: 12.7 us -> 18.7 us
  waiting for transfers between devices: 7.94 us -> 12.9 us
  Pallas kernels: 16.7 us -> 15.9 us
  local copies, waits for them, and re-layouts: 3.21 us -> 2.58 us
    all_to_all x1 -> x0, blocking collectives: 13.8 us -> none  [body(): squares = lax.all_to_all(part, ('img', 'gx', 'gy'), 0, 0, tiled=True)]
    ppermute x2 -> x4, starting transfers between devices: 0.12 us -> 7.2 us  [swapped(): return lax.ppermute(cells, axis, pairs + [(j, i) for i, j in pairs])]
    ppermute x7 -> x6, starting transfers between devices: 12.6 us -> 7.35 us  [shifted(): return lax.ppermute(cells, axis, pairs)]
    all_to_all x0 -> x1, waiting for transfers between devices: none -> 4.41 us  [body(): squares = lax.all_to_all(part, ('img', 'gx', 'gy'), 0, 0, tiled=True)]
    all_to_all x0 -> x1, starting transfers between devices: none -> 4.18 us  [body(): squares = lax.all_to_all(part, ('img', 'gx', 'gy'), 0, 0, tiled=True)]
    pallas_call x2 -> x5, Pallas kernels: 16.7 us -> 15.9 us  [the longest x1 13.6 us: body(): pl.pallas_call(functools.partial(evolve_kernel, ny, tiles, images), out_s...]
    unnamed x14 -> x16, local copies, waits for them, and re-layouts: 3.21 us -> 2.58 us
    ppermute x7 -> x6, waiting for transfers between devices: 7.93 us -> 8.47 us  [shifted(): return lax.ppermute(cells, axis, pairs)]
  transfers between devices with their start and end apart: 9 -> 11, of which waited for: 3 -> 4; matrix products, arithmetic and copies ran while one was open for 0% -> 0% of each run, Pallas kernels for 0% -> 3%
where the time goes in v5:
time: 50.5 us; the launch traced here: 50.3 us
  starting transfers between devices  18.7 us (37%)
  Pallas kernels  15.9 us (31%)
  waiting for transfers between devices  12.9 us (26%)
  local copies, waits for them, and re-layouts  2.58 us (5%)
    pallas_call x1, Pallas kernels, body(): pl.pallas_call(functools.partial(evolve_kernel, ny, tiles, images), out_s...  13.6 us
    ppermute x6, waiting for transfers between devices, shifted(): return lax.ppermute(cells, axis, pairs)  8.47 us
    ppermute x6, starting transfers between devices, shifted(): return lax.ppermute(cells, axis, pairs)  7.35 us
    ppermute x4, starting transfers between devices, swapped(): return lax.ppermute(cells, axis, pairs + [(j, i) for i, j in pairs])  7.2 us
    all_to_all x1, waiting for transfers between devices, body(): squares = lax.all_to_all(part, ('img', 'gx', 'gy'), 0, 0, tiled=True)  4.41 us
    all_to_all x1, starting transfers between devices, body(): squares = lax.all_to_all(part, ('img', 'gx', 'gy'), 0, 0, tiled=True)  4.18 us
    unnamed x16, local copies, waits for them, and re-layouts  2.58 us
    pallas_call x1, Pallas kernels, body(): pl.pallas_call(functools.partial(pack_kernel, ny, tiles, anisotropy.shape...  1.46 us
  transfers between devices with their start and end apart: 11, of which 4 were waited for; matrix products, arithmetic and copies ran while one was open for 0% of the time, Pallas kernels for 3%

profile of v5, /device:TPU:0, one launch (start us, length us, event | category | flops | bytes accessed | tf_op | source)
XLA Modules:
  0.0 50.3 jit_solution(14391443537688831488)
XLA Ops:
  0.0 2.9 %collective-permute-start.3 = (f32[3,16,16,128]{3,2,1,0:T(8,128)}, f32[3,16,16,128]{3,2,1,0:T(8,128)S(1)}, u32[]{:S(2)}, u32[]{:S(2)}) collective-permute-start(f32[3,16,16,128]{3,2,1,0:T(8,128)} %bitcast.15), channel_id=1, source_target_pairs={{0,1},{1,0},{2,3},{3,2},{4,5},{5,4},{6,7},{7,6},{8,9},{9,8},{10,11... | collective-permute-start | bytes 1179656 | tf_op jit(solution)/shard_map/ppermute | solution.py:363
  2.9 1.6 %collective-permute-start.4 = (f32[3,16,16,128]{3,2,1,0:T(8,128)}, f32[3,16,16,128]{3,2,1,0:T(8,128)S(1)}, u32[]{:S(2)}, u32[]{:S(2)}) collective-permute-start(f32[3,16,16,128]{3,2,1,0:T(8,128)} %bitcast.16), channel_id=1, source_target_pairs={{0,8},{16,24},{8,0},{24,16},{1,9},{17,25},{9,1},{25,17},{2,10},{18... | collective-permute-start | bytes 1179656 | tf_op jit(solution)/shard_map/ppermute | solution.py:369
  4.5 0.7 %collective-permute-start.5 = (f32[3,16,16,128]{3,2,1,0:T(8,128)}, f32[3,16,16,128]{3,2,1,0:T(8,128)S(1)}, u32[]{:S(2)}, u32[]{:S(2)}) collective-permute-start(f32[3,16,16,128]{3,2,1,0:T(8,128)} %bitcast.17), channel_id=1, source_target_pairs={{8,16},{16,8},{9,17},{17,9},{10,18},{18,10},{11,19},{19,11},{12,20... | collective-permute-start | bytes 1179656 | tf_op jit(solution)/shard_map/ppermute | solution.py:369
  5.2 0.0 copy-start.7
  5.2 0.0 copy-start.4
  5.2 0.0 copy-start.5
  5.2 0.0 copy-start.6
  5.2 0.6 %copy-done.7 = f32[3]{0:T(128)S(1)} copy-done((f32[3]{0:T(128)S(1)}, f32[3]{0:T(128)}, u32[]{:S(2)}) %copy-start.7) | copy-done | bytes 36
  5.9 0.0 copy-done.4
  5.9 0.0 copy-done.5
  5.9 0.0 copy-done.6
  5.9 0.0 copy-start
  5.9 1.0 %copy-done = f32[1,3,16,16,128]{4,3,2,1,0:T(8,128)S(1)} copy-done((f32[1,3,16,16,128]{4,3,2,1,0:T(8,128)S(1)}, f32[1,3,16,16,128]{4,3,2,1,0:T(8,128)}, u32[]{:S(2)}) %copy-start) | copy-done | bytes 393240
  6.9 0.0 copy-start.2
  6.9 0.9 %copy-done.2 = s32[16,16,128]{2,1,0:T(8,128)S(1)} copy-done((s32[16,16,128]{2,1,0:T(8,128)S(1)}, s32[16,16,128]{2,1,0:T(8,128)}, u32[]{:S(2)}) %copy-start.2) | copy-done | bytes 131096
  7.8 0.0 copy-start.1
  7.8 1.5 %pack_strips.1 = (f32[2,4,2,8,128]{4,3,2,1,0:T(8,128)S(1)}, f32[5,8,128]{2,1,0:T(8,128)S(1)}) custom-call(s32[4]{0:T(128)S(1)} %copy-done.4, f32[8]{0:T(128)S(1)} %copy-done.5, f32[8]{0:T(128)S(1)} %copy-done.6, f32[1,3]{1,0:T(1,128)S(1)} %bitcast.30, f32[3,256,128]{2,1,0:T(8,128)S(1)} %bitcast.18, s32[256,128]{1,0:T(8,128)S(1)} %bitcast.21), custom_call_target="tpu_custom_call" | custom-call | tf_op jit(solution)/shard_map/pack_strips/pallas_call | solution.py:408
  9.3 0.6 %collective-permute-start = (f32[2,4,2,8,128]{4,3,2,1,0:T(8,128)S(1)}, f32[2,4,2,8,128]{4,3,2,1,0:T(8,128)S(1)}, u32[]{:S(2)}, u32[]{:S(2)}) collective-permute-start(f32[2,4,2,8,128]{4,3,2,1,0:T(8,128)S(1)} %get-tuple-element.16.both_ref), channel_id=1, source_target_pairs={{0,1},{1,0},{2,3},{3,2},{4,5},{5,4},{6,7},{7,6},{8,9},{9,8},{10,11... | collective-permute-start | bytes 196616 | tf_op jit(solution)/shard_map/ppermute | solution.py:363
  9.9 3.8 %collective-permute-done.both_p_ref = f32[2,4,2,8,128]{4,3,2,1,0:T(8,128)S(1)} collective-permute-done((f32[2,4,2,8,128]{4,3,2,1,0:T(8,128)S(1)}, f32[2,4,2,8,128]{4,3,2,1,0:T(8,128)S(1)}, u32[]{:S(2)}, u32[]{:S(2)}) %collective-permute-start) | collective-permute-done | bytes 65568 | tf_op jit(solution)/shard_map/ppermute | solution.py:363
  13.7 0.1 collective-permute-start.1
  13.7 1.7 %collective-permute-start.2 = (f32[2,4,2,8,128]{4,3,2,1,0:T(8,128)S(1)}, f32[2,4,2,8,128]{4,3,2,1,0:T(8,128)S(1)}, u32[]{:S(2)}, u32[]{:S(2)}) collective-permute-start(f32[2,4,2,8,128]{4,3,2,1,0:T(8,128)S(1)} %get-tuple-element.18), channel_id=1, source_target_pairs={{0,6},{2,0},{4,2},{6,4},{1,7},{3,1},{5,3},{7,5},{8,14},{10,8},{12,... | collective-permute-start | bytes 196616 | tf_op jit(solution)/shard_map/ppermute | solution.py:363
  15.5 1.9 %collective-permute-done.1.left_ref = f32[2,4,2,8,128]{4,3,2,1,0:T(8,128)S(1)} collective-permute-done((f32[2,4,2,8,128]{4,3,2,1,0:T(8,128)S(1)}, f32[2,4,2,8,128]{4,3,2,1,0:T(8,128)S(1)}, u32[]{:S(2)}, u32[]{:S(2)}) %collective-permute-start.1) | collective-permute-done | bytes 65568 | tf_op jit(solution)/shard_map/ppermute | solution.py:363
  17.4 0.0 collective-permute-done.2.right_ref
  17.4 0.0 collective-permute-done.3
  17.5 0.0 collective-permute-done.4
  17.5 0.0 collective-permute-done.5
  17.5 0.0 copy-done.1
  17.5 0.0 copy-start.3
  17.5 0.9 %gather_images.1 = (f32[32,128]{1,0:T(8,128)}, f32[3,256,128]{2,1,0:T(8,128)S(1)}) custom-call(f32[5,8,128]{2,1,0:T(8,128)S(1)} %get-tuple-element.20.info_ref, f32[3,256,128]{2,1,0:T(8,128)S(1)} %bitcast.19, f32[3,256,128]{2,1,0:T(8,128)S(1)} %bitcast.26, f32[3,256,128]{2,1,0:T(8,128)S(1)} %bitcast.27), custom_call_target="tpu_custom_call" | custom-call | tf_op jit(solution)/shard_map/gather_images/pallas_call | solution.py:451
  18.4 1.7 %collective-permute-start.6 = (f32[3,16,16,128]{3,2,1,0:T(8,128)S(1)}, f32[3,16,16,128]{3,2,1,0:T(8,128)S(1)}, u32[]{:S(2)}, u32[]{:S(2)}) collective-permute-start(f32[3,16,16,128]{3,2,1,0:T(8,128)S(1)} %bitcast.24), channel_id=1, source_target_pairs={{0,1},{1,0},{2,3},{3,2},{4,5},{5,4},{6,7},{7,6},{8,9},{9,8},{10,11... | collective-permute-start | bytes 1179656 | tf_op jit(solution)/shard_map/ppermute | solution.py:363
  20.1 0.0 copy-done.3
  20.1 0.3 collective-permute-start.7
  20.4 4.3 %collective-permute-start.8 = (f32[2,2,3,2,8,128]{5,4,3,2,1,0:T(8,128)S(1)}, f32[2,2,3,2,8,128]{5,4,3,2,1,0:T(8,128)S(1)}, u32[]{:S(2)}, u32[]{:S(2)}) collective-permute-start(f32[2,2,3,2,8,128]{5,4,3,2,1,0:T(8,128)S(1)} %get-tuple-element.24), channel_id=1, source_target_pairs={{0,8},{16,24},{8,0},{24,16},{1,9},{17,25},{9,1},{25,17},{2,10},{18... | collective-permute-start | bytes 294920 | tf_op jit(solution)/shard_map/ppermute | solution.py:369
  24.7 0.7 %collective-permute-start.9 = (f32[2,2,3,2,8,128]{5,4,3,2,1,0:T(8,128)S(1)}, f32[2,2,3,2,8,128]{5,4,3,2,1,0:T(8,128)S(1)}, u32[]{:S(2)}, u32[]{:S(2)}) collective-permute-start(f32[2,2,3,2,8,128]{5,4,3,2,1,0:T(8,128)S(1)} %get-tuple-element.24), channel_id=1, source_target_pairs={{8,16},{16,8},{9,17},{17,9},{10,18},{18,10},{11,19},{19,11},{12,20... | collective-permute-start | bytes 294920 | tf_op jit(solution)/shard_map/ppermute | solution.py:369
  25.3 4.2 %all-to-all-start = ((f32[32,1,128]{2,1,0:T(1,128)}), f32[32,1,128]{2,1,0:T(1,128)S(1)}, u32[]{:S(2)}, u32[]{:S(2)}) async-start(f32[32,1,128]{2,1,0:T(1,128)} %bitcast.7), calls=%async_computation | async-start | bytes 32768 | tf_op jit(solution)/shard_map/all_to_all | solution.py:460
  29.5 2.7 %collective-permute-done.7 = s32[16,16,128]{2,1,0:T(8,128)S(1)} collective-permute-done((s32[16,16,128]{2,1,0:T(8,128)S(1)}, s32[16,16,128]{2,1,0:T(8,128)S(1)}, u32[]{:S(2)}, u32[]{:S(2)}) %collective-permute-start.7) | collective-permute-done | bytes 131104 | tf_op jit(solution)/shard_map/ppermute | solution.py:363
  32.2 0.0 collective-permute-done.8.first_ref
  32.3 0.0 collective-permute-done.9.second_ref
  32.3 4.4 %all-to-all-done = f32[32,1,128]{2,1,0:T(1,128)S(1)} async-done(((f32[32,1,128]{2,1,0:T(1,128)}), f32[32,1,128]{2,1,0:T(1,128)S(1)}, u32[]{:S(2)}, u32[]{:S(2)}) %all-to-all-start) | async-done | bytes 16416 | tf_op jit(solution)/shard_map/all_to_all | solution.py:460
  36.7 0.0 collective-permute-done.6
  36.7 13.6 %evolve.1 = f32[3,256,128]{2,1,0:T(8,128)} custom-call(f32[5,8,128]{2,1,0:T(8,128)S(1)} %get-tuple-element.20.info_ref, f32[32,128]{1,0:T(8,128)S(1)} %bitcast.29, f32[3,256,128]{2,1,0:T(8,128)S(1)} %bitcast.20, f32[3,256,128]{2,1,0:T(8,128)S(1)} %bitcast.23, f32[3,256,128]{2,1,0:T(8,128)S(1)} %get-tuple-element.23.n_ref, f32[3,256,128]{2,1,0:T(8,128)S(1)} %bitcast.25, ...), custom_call_target="tpu_custom_call" | custom-call | tf_op jit(solution)/shard_map/evolve/pallas_call | solution.py:463
  (2 shorter events, 0.0 us)
Async XLA Ops:
  0.0 17.4 %collective-permute-start.3 = (f32[3,16,16,128]{3,2,1,0:T(8,128)}, f32[3,16,16,128]{3,2,1,0:T(8,128)S(1)}, u32[]{:S(2)}, u32[]{:S(2)}) collective-permute-start(f32[3,16,16,128]{3,2,1,0:T(8,128)} %bitcast.15), channel_id=1, source_target_pairs={{0,1},{1,0},{2,3},{3,2},{4,5},{5,4},{6,7},{7,6},{8,9},{9,8},{10,11... | collective-permute-start | bytes 1179656 | tf_op jit(solution)/shard_map/ppermute | solution.py:363
  2.9 14.5 %collective-permute-start.4 = (f32[3,16,16,128]{3,2,1,0:T(8,128)}, f32[3,16,16,128]{3,2,1,0:T(8,128)S(1)}, u32[]{:S(2)}, u32[]{:S(2)}) collective-permute-start(f32[3,16,16,128]{3,2,1,0:T(8,128)} %bitcast.16), channel_id=1, source_target_pairs={{0,8},{16,24},{8,0},{24,16},{1,9},{17,25},{9,1},{25,17},{2,10},{18... | collective-permute-start | bytes 1179656 | tf_op jit(solution)/shard_map/ppermute | solution.py:369
  4.5 12.9 %collective-permute-start.5 = (f32[3,16,16,128]{3,2,1,0:T(8,128)}, f32[3,16,16,128]{3,2,1,0:T(8,128)S(1)}, u32[]{:S(2)}, u32[]{:S(2)}) collective-permute-start(f32[3,16,16,128]{3,2,1,0:T(8,128)} %bitcast.17), channel_id=1, source_target_pairs={{8,16},{16,8},{9,17},{17,9},{10,18},{18,10},{11,19},{19,11},{12,20... | collective-permute-start | bytes 1179656 | tf_op jit(solution)/shard_map/ppermute | solution.py:369
  5.2 0.7 %copy-start.7 = (f32[3]{0:T(128)S(1)}, f32[3]{0:T(128)}, u32[]{:S(2)}) copy-start(f32[3]{0:T(128)} %param.8) | copy-start | bytes 40
  5.2 0.7 %copy-start.4 = (s32[4]{0:T(128)S(1)}, s32[4]{0:T(128)}, u32[]{:S(2)}) copy-start(s32[4]{0:T(128)} %lower_ref.1) | copy-start | bytes 52
  5.2 0.7 %copy-start.5 = (f32[8]{0:T(128)S(1)}, f32[8]{0:T(128)}, u32[]{:S(2)}) copy-start(f32[8]{0:T(128)} %aniso_ref.1) | copy-start | bytes 100
  5.2 0.7 %copy-start.6 = (f32[8]{0:T(128)S(1)}, f32[8]{0:T(128)}, u32[]{:S(2)}) copy-start(f32[8]{0:T(128)} %damp_ref.1) | copy-start | bytes 100
  5.9 1.0 %copy-start = (f32[1,3,16,16,128]{4,3,2,1,0:T(8,128)S(1)}, f32[1,3,16,16,128]{4,3,2,1,0:T(8,128)}, u32[]{:S(2)}) copy-start(f32[1,3,16,16,128]{4,3,2,1,0:T(8,128)} %param.6) | copy-start | bytes 1179652
  6.9 0.9 %copy-start.2 = (s32[16,16,128]{2,1,0:T(8,128)S(1)}, s32[16,16,128]{2,1,0:T(8,128)}, u32[]{:S(2)}) copy-start(s32[16,16,128]{2,1,0:T(8,128)} %param.9) | copy-start | bytes 393220
  7.8 9.7 %copy-start.1 = (f32[1,3,16,16,128]{4,3,2,1,0:T(8,128)S(1)}, f32[1,3,16,16,128]{4,3,2,1,0:T(8,128)}, u32[]{:S(2)}) copy-start(f32[1,3,16,16,128]{4,3,2,1,0:T(8,128)} %param.6) | copy-start | bytes 1179652
  9.3 4.4 %collective-permute-start = (f32[2,4,2,8,128]{4,3,2,1,0:T(8,128)S(1)}, f32[2,4,2,8,128]{4,3,2,1,0:T(8,128)S(1)}, u32[]{:S(2)}, u32[]{:S(2)}) collective-permute-start(f32[2,4,2,8,128]{4,3,2,1,0:T(8,128)S(1)} %get-tuple-element.16.both_ref), channel_id=1, source_target_pairs={{0,1},{1,0},{2,3},{3,2},{4,5},{5,4},{6,7},{7,6},{8,9},{9,8},{10,11... | collective-permute-start | bytes 196616 | tf_op jit(solution)/shard_map/ppermute | solution.py:363
  13.7 3.7 %collective-permute-start.1 = (f32[2,4,2,8,128]{4,3,2,1,0:T(8,128)S(1)}, f32[2,4,2,8,128]{4,3,2,1,0:T(8,128)S(1)}, u32[]{:S(2)}, u32[]{:S(2)}) collective-permute-start(f32[2,4,2,8,128]{4,3,2,1,0:T(8,128)S(1)} %get-tuple-element.17), channel_id=1, source_target_pairs={{0,2},{2,4},{4,6},{6,0},{1,3},{3,5},{5,7},{7,1},{8,10},{10,12},{12... | collective-permute-start | bytes 196616 | tf_op jit(solution)/shard_map/ppermute | solution.py:363
  13.7 3.7 %collective-permute-start.2 = (f32[2,4,2,8,128]{4,3,2,1,0:T(8,128)S(1)}, f32[2,4,2,8,128]{4,3,2,1,0:T(8,128)S(1)}, u32[]{:S(2)}, u32[]{:S(2)}) collective-permute-start(f32[2,4,2,8,128]{4,3,2,1,0:T(8,128)S(1)} %get-tuple-element.18), channel_id=1, source_target_pairs={{0,6},{2,0},{4,2},{6,4},{1,7},{3,1},{5,3},{7,5},{8,14},{10,8},{12,... | collective-permute-start | bytes 196616 | tf_op jit(solution)/shard_map/ppermute | solution.py:363
  17.5 2.6 %copy-start.3 = (s32[16,16,128]{2,1,0:T(8,128)S(1)}, s32[16,16,128]{2,1,0:T(8,128)}, u32[]{:S(2)}) copy-start(s32[16,16,128]{2,1,0:T(8,128)} %param.9) | copy-start | bytes 393220
  18.4 18.3 %collective-permute-start.6 = (f32[3,16,16,128]{3,2,1,0:T(8,128)S(1)}, f32[3,16,16,128]{3,2,1,0:T(8,128)S(1)}, u32[]{:S(2)}, u32[]{:S(2)}) collective-permute-start(f32[3,16,16,128]{3,2,1,0:T(8,128)S(1)} %bitcast.24), channel_id=1, source_target_pairs={{0,1},{1,0},{2,3},{3,2},{4,5},{5,4},{6,7},{7,6},{8,9},{9,8},{10,11... | collective-permute-start | bytes 1179656 | tf_op jit(solution)/shard_map/ppermute | solution.py:363
  20.1 12.1 %collective-permute-start.7 = (s32[16,16,128]{2,1,0:T(8,128)S(1)}, s32[16,16,128]{2,1,0:T(8,128)S(1)}, u32[]{:S(2)}, u32[]{:S(2)}) collective-permute-start(s32[16,16,128]{2,1,0:T(8,128)S(1)} %copy-done.3), channel_id=1, source_target_pairs={{0,1},{1,0},{2,3},{3,2},{4,5},{5,4},{6,7},{7,6},{8,9},{9,8},{10,11... | collective-permute-start | bytes 393224 | tf_op jit(solution)/shard_map/ppermute | solution.py:363
  20.4 11.9 %collective-permute-start.8 = (f32[2,2,3,2,8,128]{5,4,3,2,1,0:T(8,128)S(1)}, f32[2,2,3,2,8,128]{5,4,3,2,1,0:T(8,128)S(1)}, u32[]{:S(2)}, u32[]{:S(2)}) collective-permute-start(f32[2,2,3,2,8,128]{5,4,3,2,1,0:T(8,128)S(1)} %get-tuple-element.24), channel_id=1, source_target_pairs={{0,8},{16,24},{8,0},{24,16},{1,9},{17,25},{9,1},{25,17},{2,10},{18... | collective-permute-start | bytes 294920 | tf_op jit(solution)/shard_map/ppermute | solution.py:369
  24.7 7.6 %collective-permute-start.9 = (f32[2,2,3,2,8,128]{5,4,3,2,1,0:T(8,128)S(1)}, f32[2,2,3,2,8,128]{5,4,3,2,1,0:T(8,128)S(1)}, u32[]{:S(2)}, u32[]{:S(2)}) collective-permute-start(f32[2,2,3,2,8,128]{5,4,3,2,1,0:T(8,128)S(1)} %get-tuple-element.24), channel_id=1, source_target_pairs={{8,16},{16,8},{9,17},{17,9},{10,18},{18,10},{11,19},{19,11},{12,20... | collective-permute-start | bytes 294920 | tf_op jit(solution)/shard_map/ppermute | solution.py:369
  25.3 11.3 %all-to-all-start = ((f32[32,1,128]{2,1,0:T(1,128)}), f32[32,1,128]{2,1,0:T(1,128)S(1)}, u32[]{:S(2)}, u32[]{:S(2)}) async-start(f32[32,1,128]{2,1,0:T(1,128)} %bitcast.7), calls=%async_computation | async-start | bytes 32768 | tf_op jit(solution)/shard_map/all_to_all | solution.py:460

commit v6 on v5

--- a/solution.py
+++ b/solution.py
@@ -80,8 +80,7 @@
         right_ref[g] = ref[1]
 
 
-def merge_kernel(info_ref, left_ref, right_ref, out_ref, info_out_ref):
-    info_out_ref[...] = info_ref[...]
+def merge_kernel(left_ref, right_ref, out_ref):
     for g in range(2):
         out_ref[0, g] = left_ref[g, :COMPS]
         out_ref[1, g] = right_ref[g, :COMPS]
@@ -403,6 +402,7 @@
     smem = pl.BlockSpec(memory_space=pltpu.SMEM)
     vmem = pl.BlockSpec(memory_space=pltpu.VMEM)
     f32 = jnp.float32
+    small = pl.CostEstimate(flops=1000, bytes_accessed=1000, transcendentals=0)
     limit = pltpu.CompilerParams(vmem_limit_bytes=32 * 1024 * 1024)
     vreg = (SUB, LANES)
     both, info = pl.pallas_call(
@@ -414,6 +414,7 @@
         in_specs=[smem] * 3 + [vmem] * 3,
         out_specs=(vmem,) * 2,
         compiler_params=limit,
+        cost_estimate=small,
         name="pack_strips",
     )(
         lower_image,
@@ -423,37 +424,37 @@
         own.reshape(flat),
         regions.reshape(flat[1:]),
     )
+    both_p = around_strips(both)
+    reg_p = around(regions, 1)
     left, right = pl.pallas_call(
         sort_kernel,
         out_shape=(jax.ShapeDtypeStruct((2, comps + 1, tiles) + vreg, f32),) * 2,
         in_specs=[vmem] * 2,
         out_specs=(vmem,) * 2,
         compiler_params=limit,
+        cost_estimate=small,
         name="sort_strips",
-    )(both, around_strips(both))
+    )(both, both_p)
     strips = (shifted(right, "gx", 1, True), shifted(left, "gx", -1, True))
-    strips_all, info = pl.pallas_call(
+    strips_all = pl.pallas_call(
         merge_kernel,
-        out_shape=(
-            jax.ShapeDtypeStruct((2, 2, comps, tiles) + vreg, f32),
-            jax.ShapeDtypeStruct(info.shape, f32),
-        ),
-        in_specs=[vmem] * 3,
-        out_specs=(vmem,) * 2,
+        out_shape=jax.ShapeDtypeStruct((2, 2, comps, tiles) + vreg, f32),
+        in_specs=[vmem] * 2,
+        out_specs=vmem,
         compiler_params=limit,
+        cost_estimate=small,
         name="merge_strips",
-    )(info, *strips)
+    )(*strips)
     strips_first = swapped(strips_all, "img", 0)
     strips_second = swapped(strips_all, "img", 1)
-    reg_p = around(regions, 1)
-
-    info, own_p = lax.optimization_barrier((info, own_p))
+    info, own_p, _ = lax.optimization_barrier((info, own_p, left))
     part, near = pl.pallas_call(
         gather_kernel,
         out_shape=(jax.ShapeDtypeStruct((devices, LANES), f32), jax.ShapeDtypeStruct(flat, f32)),
         in_specs=[vmem] * 4,
         out_specs=(vmem,) * 2,
         compiler_params=limit,
+        cost_estimate=small,
         name="gather_images",
     )(info, own.reshape(flat), first.reshape(flat), second.reshape(flat))
     near_p = around(near.reshape(own.shape), 2)

time: 50.5 us -> 50.4 us (level)
  starting transfers between devices: 18.7 us -> 17 us
  waiting for transfers between devices: 12.9 us -> 14.5 us
    all_to_all x1, waiting for transfers between devices: 4.41 us -> 7.09 us  [body(): squares = lax.all_to_all(part, ('img', 'gx', 'gy'), 0, 0, tiled=True)]
    ppermute x6, starting transfers between devices: 7.35 us -> 6.07 us  [shifted(): return lax.ppermute(cells, axis, pairs)]
    ppermute x6, waiting for transfers between devices: 8.47 us -> 7.34 us  [shifted(): return lax.ppermute(cells, axis, pairs)]
    ppermute x4, starting transfers between devices: 7.2 us -> 6.35 us  [swapped(): return lax.ppermute(cells, axis, pairs + [(j, i) for i, j in pairs])]
where the time goes in v6:
time: 50.4 us; the launch traced here: 50.1 us
  starting transfers between devices  17 us (34%)
  Pallas kernels  15.9 us (32%)
  waiting for transfers between devices  14.5 us (29%)
  local copies, waits for them, and re-layouts  2.58 us (5%)
    pallas_call x1, Pallas kernels, body(): pl.pallas_call(functools.partial(evolve_kernel, ny, tiles, images), out_s...  13.6 us
    ppermute x6, waiting for transfers between devices, shifted(): return lax.ppermute(cells, axis, pairs)  7.34 us
    all_to_all x1, waiting for transfers between devices, body(): squares = lax.all_to_all(part, ('img', 'gx', 'gy'), 0, 0, tiled=True)  7.09 us
    ppermute x4, starting transfers between devices, swapped(): return lax.ppermute(cells, axis, pairs + [(j, i) for i, j in pairs])  6.35 us
    ppermute x6, starting transfers between devices, shifted(): return lax.ppermute(cells, axis, pairs)  6.07 us
    all_to_all x1, starting transfers between devices, body(): squares = lax.all_to_all(part, ('img', 'gx', 'gy'), 0, 0, tiled=True)  4.62 us
    unnamed x16, local copies, waits for them, and re-layouts  2.58 us
    pallas_call x1, Pallas kernels, body(): pl.pallas_call(functools.partial(pack_kernel, ny, tiles, anisotropy.shape...  1.46 us
  transfers between devices with their start and end apart: 11, of which 4 were waited for; matrix products, arithmetic and copies ran while one was open for 0% of the time, Pallas kernels for 3%

profile of v6, /device:TPU:0, one launch (start us, length us, event | category | flops | bytes accessed | tf_op | source)
XLA Modules:
  0.0 50.1 jit_solution(3957708332183748678)
XLA Ops:
  0.0 2.9 %collective-permute-start = (f32[3,16,16,128]{3,2,1,0:T(8,128)}, f32[3,16,16,128]{3,2,1,0:T(8,128)S(1)}, u32[]{:S(2)}, u32[]{:S(2)}) collective-permute-start(f32[3,16,16,128]{3,2,1,0:T(8,128)} %bitcast.15), channel_id=1, source_target_pairs={{0,1},{1,0},{2,3},{3,2},{4,5},{5,4},{6,7},{7,6},{8,9},{9,8},{10,11... | collective-permute-start | bytes 1179656 | tf_op jit(solution)/shard_map/ppermute | solution.py:362
  2.9 1.6 %collective-permute-start.2 = (f32[3,16,16,128]{3,2,1,0:T(8,128)}, f32[3,16,16,128]{3,2,1,0:T(8,128)S(1)}, u32[]{:S(2)}, u32[]{:S(2)}) collective-permute-start(f32[3,16,16,128]{3,2,1,0:T(8,128)} %bitcast.16), channel_id=1, source_target_pairs={{0,8},{16,24},{8,0},{24,16},{1,9},{17,25},{9,1},{25,17},{2,10},{18... | collective-permute-start | bytes 1179656 | tf_op jit(solution)/shard_map/ppermute | solution.py:368
  4.5 0.7 %collective-permute-start.3 = (f32[3,16,16,128]{3,2,1,0:T(8,128)}, f32[3,16,16,128]{3,2,1,0:T(8,128)S(1)}, u32[]{:S(2)}, u32[]{:S(2)}) collective-permute-start(f32[3,16,16,128]{3,2,1,0:T(8,128)} %bitcast.17), channel_id=1, source_target_pairs={{8,16},{16,8},{9,17},{17,9},{10,18},{18,10},{11,19},{19,11},{12,20... | collective-permute-start | bytes 1179656 | tf_op jit(solution)/shard_map/ppermute | solution.py:368
  5.2 0.0 copy-start.7
  5.2 0.0 copy-start.4
  5.2 0.0 copy-start.5
  5.2 0.0 copy-start.6
  5.2 0.6 %copy-done.7 = f32[3]{0:T(128)S(1)} copy-done((f32[3]{0:T(128)S(1)}, f32[3]{0:T(128)}, u32[]{:S(2)}) %copy-start.7) | copy-done | bytes 36
  5.9 0.0 copy-done.4
  5.9 0.0 copy-done.5
  5.9 0.0 copy-done.6
  5.9 0.0 copy-start
  5.9 1.0 %copy-done = f32[1,3,16,16,128]{4,3,2,1,0:T(8,128)S(1)} copy-done((f32[1,3,16,16,128]{4,3,2,1,0:T(8,128)S(1)}, f32[1,3,16,16,128]{4,3,2,1,0:T(8,128)}, u32[]{:S(2)}) %copy-start) | copy-done | bytes 393240
  6.9 0.0 copy-start.2
  6.9 0.9 %copy-done.2 = s32[16,16,128]{2,1,0:T(8,128)S(1)} copy-done((s32[16,16,128]{2,1,0:T(8,128)S(1)}, s32[16,16,128]{2,1,0:T(8,128)}, u32[]{:S(2)}) %copy-start.2) | copy-done | bytes 131096
  7.8 0.0 copy-start.1
  7.8 1.5 %pack_strips.1 = (f32[2,4,2,8,128]{4,3,2,1,0:T(8,128)S(1)}, f32[5,8,128]{2,1,0:T(8,128)S(1)}) custom-call(s32[4]{0:T(128)S(1)} %copy-done.4, f32[8]{0:T(128)S(1)} %copy-done.5, f32[8]{0:T(128)S(1)} %copy-done.6, f32[1,3]{1,0:T(1,128)S(1)} %bitcast.30, f32[3,256,128]{2,1,0:T(8,128)S(1)} %bitcast.18, s32[256,128]{1,0:T(8,128)S(1)} %bitcast.21), custom_call_target="tpu_custom_call" | custom-call | flops 1000 | bytes 1000 | tf_op jit(solution)/shard_map/pack_strips/pallas_call | solution.py:408
  9.3 0.6 %collective-permute-start.1 = (f32[2,4,2,8,128]{4,3,2,1,0:T(8,128)S(1)}, f32[2,4,2,8,128]{4,3,2,1,0:T(8,128)S(1)}, u32[]{:S(2)}, u32[]{:S(2)}) collective-permute-start(f32[2,4,2,8,128]{4,3,2,1,0:T(8,128)S(1)} %get-tuple-element.14.both_ref), channel_id=1, source_target_pairs={{0,1},{1,0},{2,3},{3,2},{4,5},{5,4},{6,7},{7,6},{8,9},{9,8},{10,11... | collective-permute-start | bytes 196616 | tf_op jit(solution)/shard_map/ppermute | solution.py:362
  9.9 3.8 %collective-permute-done.1.both_p_ref = f32[2,4,2,8,128]{4,3,2,1,0:T(8,128)S(1)} collective-permute-done((f32[2,4,2,8,128]{4,3,2,1,0:T(8,128)S(1)}, f32[2,4,2,8,128]{4,3,2,1,0:T(8,128)S(1)}, u32[]{:S(2)}, u32[]{:S(2)}) %collective-permute-start.1) | collective-permute-done | bytes 65568 | tf_op jit(solution)/shard_map/ppermute | solution.py:362
  13.7 0.0 collective-permute-done
  13.7 0.0 collective-permute-done.2
  13.7 0.0 collective-permute-done.3
  13.7 0.0 copy-done.1
  13.7 0.0 copy-start.3
  13.7 0.9 %gather_images.1 = (f32[32,128]{1,0:T(8,128)}, f32[3,256,128]{2,1,0:T(8,128)S(1)}) custom-call(f32[5,8,128]{2,1,0:T(8,128)S(1)} %get-tuple-element.16.info_ref, f32[3,256,128]{2,1,0:T(8,128)S(1)} %bitcast.19, f32[3,256,128]{2,1,0:T(8,128)S(1)} %bitcast.26, f32[3,256,128]{2,1,0:T(8,128)S(1)} %bitcast.27), custom_call_target="tpu_custom_call" | custom-call | flops 1000 | bytes 1000 | tf_op jit(solution)/shard_map/gather_images/pallas_call | solution.py:451
  14.6 1.7 %collective-permute-start.4 = (f32[3,16,16,128]{3,2,1,0:T(8,128)S(1)}, f32[3,16,16,128]{3,2,1,0:T(8,128)S(1)}, u32[]{:S(2)}, u32[]{:S(2)}) collective-permute-start(f32[3,16,16,128]{3,2,1,0:T(8,128)S(1)} %bitcast.24), channel_id=1, source_target_pairs={{0,1},{1,0},{2,3},{3,2},{4,5},{5,4},{6,7},{7,6},{8,9},{9,8},{10,11... | collective-permute-start | bytes 1179656 | tf_op jit(solution)/shard_map/ppermute | solution.py:362
  16.3 0.0 collective-permute-start.7
  16.3 0.5 %collective-permute-start.6 = (f32[2,4,2,8,128]{4,3,2,1,0:T(8,128)S(1)}, f32[2,4,2,8,128]{4,3,2,1,0:T(8,128)S(1)}, u32[]{:S(2)}, u32[]{:S(2)}) collective-permute-start(f32[2,4,2,8,128]{4,3,2,1,0:T(8,128)S(1)} %get-tuple-element.20), channel_id=1, source_target_pairs={{0,2},{2,4},{4,6},{6,0},{1,3},{3,5},{5,7},{7,1},{8,10},{10,12},{12... | collective-permute-start | bytes 196616 | tf_op jit(solution)/shard_map/ppermute | solution.py:362
  16.9 0.0 copy-done.3
  16.9 0.3 collective-permute-start.5
  17.1 1.1 %collective-permute-done.7.right_ref = f32[2,4,2,8,128]{4,3,2,1,0:T(8,128)S(1)} collective-permute-done((f32[2,4,2,8,128]{4,3,2,1,0:T(8,128)S(1)}, f32[2,4,2,8,128]{4,3,2,1,0:T(8,128)S(1)}, u32[]{:S(2)}, u32[]{:S(2)}) %collective-permute-start.7) | collective-permute-done | bytes 65568 | tf_op jit(solution)/shard_map/ppermute | solution.py:362
  18.3 2.4 %collective-permute-done.6.left_ref = f32[2,4,2,8,128]{4,3,2,1,0:T(8,128)S(1)} collective-permute-done((f32[2,4,2,8,128]{4,3,2,1,0:T(8,128)S(1)}, f32[2,4,2,8,128]{4,3,2,1,0:T(8,128)S(1)}, u32[]{:S(2)}, u32[]{:S(2)}) %collective-permute-start.6) | collective-permute-done | bytes 65568 | tf_op jit(solution)/shard_map/ppermute | solution.py:362
  20.7 3.4 %collective-permute-start.8 = (f32[2,2,3,2,8,128]{5,4,3,2,1,0:T(8,128)S(1)}, f32[2,2,3,2,8,128]{5,4,3,2,1,0:T(8,128)S(1)}, u32[]{:S(2)}, u32[]{:S(2)}) collective-permute-start(f32[2,2,3,2,8,128]{5,4,3,2,1,0:T(8,128)S(1)} %merge_strips.1), channel_id=1, source_target_pairs={{0,8},{16,24},{8,0},{24,16},{1,9},{17,25},{9,1},{25,17},{2,10},{18... | collective-permute-start | bytes 294920 | tf_op jit(solution)/shard_map/ppermute | solution.py:368
  24.1 0.7 %collective-permute-start.9 = (f32[2,2,3,2,8,128]{5,4,3,2,1,0:T(8,128)S(1)}, f32[2,2,3,2,8,128]{5,4,3,2,1,0:T(8,128)S(1)}, u32[]{:S(2)}, u32[]{:S(2)}) collective-permute-start(f32[2,2,3,2,8,128]{5,4,3,2,1,0:T(8,128)S(1)} %merge_strips.1), channel_id=1, source_target_pairs={{8,16},{16,8},{9,17},{17,9},{10,18},{18,10},{11,19},{19,11},{12,20... | collective-permute-start | bytes 294920 | tf_op jit(solution)/shard_map/ppermute | solution.py:368
  24.8 4.6 %all-to-all-start = ((f32[32,1,128]{2,1,0:T(1,128)}), f32[32,1,128]{2,1,0:T(1,128)S(1)}, u32[]{:S(2)}, u32[]{:S(2)}) async-start(f32[32,1,128]{2,1,0:T(1,128)} %bitcast.7), calls=%async_computation | async-start | bytes 32768 | tf_op jit(solution)/shard_map/all_to_all | solution.py:461
  29.4 0.0 collective-permute-done.5
  29.4 0.0 collective-permute-done.8.first_ref
  29.4 0.0 collective-permute-done.9.second_ref
  29.4 7.1 %all-to-all-done = f32[32,1,128]{2,1,0:T(1,128)S(1)} async-done(((f32[32,1,128]{2,1,0:T(1,128)}), f32[32,1,128]{2,1,0:T(1,128)S(1)}, u32[]{:S(2)}, u32[]{:S(2)}) %all-to-all-start) | async-done | bytes 16416 | tf_op jit(solution)/shard_map/all_to_all | solution.py:461
  36.5 0.0 collective-permute-done.4
  36.5 13.6 %evolve.1 = f32[3,256,128]{2,1,0:T(8,128)} custom-call(f32[5,8,128]{2,1,0:T(8,128)S(1)} %get-tuple-element.16.info_ref, f32[32,128]{1,0:T(8,128)S(1)} %bitcast.29, f32[3,256,128]{2,1,0:T(8,128)S(1)} %bitcast.20, f32[3,256,128]{2,1,0:T(8,128)S(1)} %bitcast.23, f32[3,256,128]{2,1,0:T(8,128)S(1)} %get-tuple-element.19.n_ref, f32[3,256,128]{2,1,0:T(8,128)S(1)} %bitcast.25, ...), custom_call_target="tpu_custom_call" | custom-call | tf_op jit(solution)/shard_map/evolve/pallas_call | solution.py:464
  (2 shorter events, 0.0 us)
Async XLA Ops:
  0.0 13.7 %collective-permute-start = (f32[3,16,16,128]{3,2,1,0:T(8,128)}, f32[3,16,16,128]{3,2,1,0:T(8,128)S(1)}, u32[]{:S(2)}, u32[]{:S(2)}) collective-permute-start(f32[3,16,16,128]{3,2,1,0:T(8,128)} %bitcast.15), channel_id=1, source_target_pairs={{0,1},{1,0},{2,3},{3,2},{4,5},{5,4},{6,7},{7,6},{8,9},{9,8},{10,11... | collective-permute-start | bytes 1179656 | tf_op jit(solution)/shard_map/ppermute | solution.py:362
  2.9 10.8 %collective-permute-start.2 = (f32[3,16,16,128]{3,2,1,0:T(8,128)}, f32[3,16,16,128]{3,2,1,0:T(8,128)S(1)}, u32[]{:S(2)}, u32[]{:S(2)}) collective-permute-start(f32[3,16,16,128]{3,2,1,0:T(8,128)} %bitcast.16), channel_id=1, source_target_pairs={{0,8},{16,24},{8,0},{24,16},{1,9},{17,25},{9,1},{25,17},{2,10},{18... | collective-permute-start | bytes 1179656 | tf_op jit(solution)/shard_map/ppermute | solution.py:368
  4.5 9.2 %collective-permute-start.3 = (f32[3,16,16,128]{3,2,1,0:T(8,128)}, f32[3,16,16,128]{3,2,1,0:T(8,128)S(1)}, u32[]{:S(2)}, u32[]{:S(2)}) collective-permute-start(f32[3,16,16,128]{3,2,1,0:T(8,128)} %bitcast.17), channel_id=1, source_target_pairs={{8,16},{16,8},{9,17},{17,9},{10,18},{18,10},{11,19},{19,11},{12,20... | collective-permute-start | bytes 1179656 | tf_op jit(solution)/shard_map/ppermute | solution.py:368
  5.2 0.7 %copy-start.7 = (f32[3]{0:T(128)S(1)}, f32[3]{0:T(128)}, u32[]{:S(2)}) copy-start(f32[3]{0:T(128)} %param.8) | copy-start | bytes 40
  5.2 0.7 %copy-start.4 = (s32[4]{0:T(128)S(1)}, s32[4]{0:T(128)}, u32[]{:S(2)}) copy-start(s32[4]{0:T(128)} %lower_ref.1) | copy-start | bytes 52
  5.2 0.7 %copy-start.5 = (f32[8]{0:T(128)S(1)}, f32[8]{0:T(128)}, u32[]{:S(2)}) copy-start(f32[8]{0:T(128)} %aniso_ref.1) | copy-start | bytes 100
  5.2 0.7 %copy-start.6 = (f32[8]{0:T(128)S(1)}, f32[8]{0:T(128)}, u32[]{:S(2)}) copy-start(f32[8]{0:T(128)} %damp_ref.1) | copy-start | bytes 100
  5.9 1.0 %copy-start = (f32[1,3,16,16,128]{4,3,2,1,0:T(8,128)S(1)}, f32[1,3,16,16,128]{4,3,2,1,0:T(8,128)}, u32[]{:S(2)}) copy-start(f32[1,3,16,16,128]{4,3,2,1,0:T(8,128)} %param.6) | copy-start | bytes 1179652
  6.9 0.9 %copy-start.2 = (s32[16,16,128]{2,1,0:T(8,128)S(1)}, s32[16,16,128]{2,1,0:T(8,128)}, u32[]{:S(2)}) copy-start(s32[16,16,128]{2,1,0:T(8,128)} %param.9) | copy-start | bytes 393220
  7.8 5.9 %copy-start.1 = (f32[1,3,16,16,128]{4,3,2,1,0:T(8,128)S(1)}, f32[1,3,16,16,128]{4,3,2,1,0:T(8,128)}, u32[]{:S(2)}) copy-start(f32[1,3,16,16,128]{4,3,2,1,0:T(8,128)} %param.6) | copy-start | bytes 1179652
  9.3 4.4 %collective-permute-start.1 = (f32[2,4,2,8,128]{4,3,2,1,0:T(8,128)S(1)}, f32[2,4,2,8,128]{4,3,2,1,0:T(8,128)S(1)}, u32[]{:S(2)}, u32[]{:S(2)}) collective-permute-start(f32[2,4,2,8,128]{4,3,2,1,0:T(8,128)S(1)} %get-tuple-element.14.both_ref), channel_id=1, source_target_pairs={{0,1},{1,0},{2,3},{3,2},{4,5},{5,4},{6,7},{7,6},{8,9},{9,8},{10,11... | collective-permute-start | bytes 196616 | tf_op jit(solution)/shard_map/ppermute | solution.py:362
  13.7 3.1 %copy-start.3 = (s32[16,16,128]{2,1,0:T(8,128)S(1)}, s32[16,16,128]{2,1,0:T(8,128)}, u32[]{:S(2)}) copy-start(s32[16,16,128]{2,1,0:T(8,128)} %param.9) | copy-start | bytes 393220
  14.6 21.9 %collective-permute-start.4 = (f32[3,16,16,128]{3,2,1,0:T(8,128)S(1)}, f32[3,16,16,128]{3,2,1,0:T(8,128)S(1)}, u32[]{:S(2)}, u32[]{:S(2)}) collective-permute-start(f32[3,16,16,128]{3,2,1,0:T(8,128)S(1)} %bitcast.24), channel_id=1, source_target_pairs={{0,1},{1,0},{2,3},{3,2},{4,5},{5,4},{6,7},{7,6},{8,9},{9,8},{10,11... | collective-permute-start | bytes 1179656 | tf_op jit(solution)/shard_map/ppermute | solution.py:362
  16.3 1.9 %collective-permute-start.7 = (f32[2,4,2,8,128]{4,3,2,1,0:T(8,128)S(1)}, f32[2,4,2,8,128]{4,3,2,1,0:T(8,128)S(1)}, u32[]{:S(2)}, u32[]{:S(2)}) collective-permute-start(f32[2,4,2,8,128]{4,3,2,1,0:T(8,128)S(1)} %get-tuple-element.15), channel_id=1, source_target_pairs={{0,6},{2,0},{4,2},{6,4},{1,7},{3,1},{5,3},{7,5},{8,14},{10,8},{12,... | collective-permute-start | bytes 196616 | tf_op jit(solution)/shard_map/ppermute | solution.py:362
  16.3 4.3 %collective-permute-start.6 = (f32[2,4,2,8,128]{4,3,2,1,0:T(8,128)S(1)}, f32[2,4,2,8,128]{4,3,2,1,0:T(8,128)S(1)}, u32[]{:S(2)}, u32[]{:S(2)}) collective-permute-start(f32[2,4,2,8,128]{4,3,2,1,0:T(8,128)S(1)} %get-tuple-element.20), channel_id=1, source_target_pairs={{0,2},{2,4},{4,6},{6,0},{1,3},{3,5},{5,7},{7,1},{8,10},{10,12},{12... | collective-permute-start | bytes 196616 | tf_op jit(solution)/shard_map/ppermute | solution.py:362
  16.9 12.6 %collective-permute-start.5 = (s32[16,16,128]{2,1,0:T(8,128)S(1)}, s32[16,16,128]{2,1,0:T(8,128)S(1)}, u32[]{:S(2)}, u32[]{:S(2)}) collective-permute-start(s32[16,16,128]{2,1,0:T(8,128)S(1)} %copy-done.3), channel_id=1, source_target_pairs={{0,1},{1,0},{2,3},{3,2},{4,5},{5,4},{6,7},{7,6},{8,9},{9,8},{10,11... | collective-permute-start | bytes 393224 | tf_op jit(solution)/shard_map/ppermute | solution.py:362
  20.7 8.7 %collective-permute-start.8 = (f32[2,2,3,2,8,128]{5,4,3,2,1,0:T(8,128)S(1)}, f32[2,2,3,2,8,128]{5,4,3,2,1,0:T(8,128)S(1)}, u32[]{:S(2)}, u32[]{:S(2)}) collective-permute-start(f32[2,2,3,2,8,128]{5,4,3,2,1,0:T(8,128)S(1)} %merge_strips.1), channel_id=1, source_target_pairs={{0,8},{16,24},{8,0},{24,16},{1,9},{17,25},{9,1},{25,17},{2,10},{18... | collective-permute-start | bytes 294920 | tf_op jit(solution)/shard_map/ppermute | solution.py:368
  24.1 5.3 %collective-permute-start.9 = (f32[2,2,3,2,8,128]{5,4,3,2,1,0:T(8,128)S(1)}, f32[2,2,3,2,8,128]{5,4,3,2,1,0:T(8,128)S(1)}, u32[]{:S(2)}, u32[]{:S(2)}) collective-permute-start(f32[2,2,3,2,8,128]{5,4,3,2,1,0:T(8,128)S(1)} %merge_strips.1), channel_id=1, source_target_pairs={{8,16},{16,8},{9,17},{17,9},{10,18},{18,10},{11,19},{19,11},{12,20... | collective-permute-start | bytes 294920 | tf_op jit(solution)/shard_map/ppermute | solution.py:368
  24.8 11.8 %all-to-all-start = ((f32[32,1,128]{2,1,0:T(1,128)}), f32[32,1,128]{2,1,0:T(1,128)S(1)}, u32[]{:S(2)}, u32[]{:S(2)}) async-start(f32[32,1,128]{2,1,0:T(1,128)} %bitcast.7), calls=%async_computation | async-start | bytes 32768 | tf_op jit(solution)/shard_map/all_to_all | solution.py:461

commit v7 on v5

--- a/solution.py
+++ b/solution.py
@@ -37,7 +37,6 @@
     here = lax.axis_index("img")
     lane = lane_iota()
     block = lane // DEPTH
-
     def pack(i, carry):
         done = []
         for u in range(2):
@@ -55,8 +54,6 @@
             pltpu.store(both_ref.at[1, c, t], cells, mask=right)
         return carry
 
-    lax.fori_loop(0, ny // 2, pack, 0)
-
     table_a = jnp.zeros((SUB, LANES), jnp.float32)
     table_d = jnp.zeros((SUB, LANES), jnp.float32)
     for i in range(regions):
@@ -72,6 +69,8 @@
     )
     info_ref[3] = jnp.broadcast_to(target, (SUB, LANES))
     info_ref[4] = jnp.full((SUB, LANES), lower_ref[here].astype(jnp.float32))
+
+    lax.fori_loop(0, ny // 2, pack, 0)
 
 
 def sort_kernel(both_ref, both_p_ref, left_ref, right_ref):
@@ -398,7 +397,7 @@
     own = magnetization[0]
     first = swapped(own, "img", 0)
     second = swapped(own, "img", 1)
-    own_p = around(own, 2)
+    reg_p = around(regions, 1)
 
     smem = pl.BlockSpec(memory_space=pltpu.SMEM)
     vmem = pl.BlockSpec(memory_space=pltpu.VMEM)
@@ -423,6 +422,9 @@
         own.reshape(flat),
         regions.reshape(flat[1:]),
     )
+    both_p = around_strips(both)
+    own_p = around(lax.optimization_barrier((own, both))[0], 2)
+    both_p, reg_p = lax.optimization_barrier((both_p, reg_p))
     left, right = pl.pallas_call(
         sort_kernel,
         out_shape=(jax.ShapeDtypeStruct((2, comps + 1, tiles) + vreg, f32),) * 2,
@@ -430,7 +432,7 @@
         out_specs=(vmem,) * 2,
         compiler_params=limit,
         name="sort_strips",
-    )(both, around_strips(both))
+    )(both, both_p)
     strips = (shifted(right, "gx", 1, True), shifted(left, "gx", -1, True))
     strips_all, info = pl.pallas_call(
         merge_kernel,
@@ -445,9 +447,6 @@
     )(info, *strips)
     strips_first = swapped(strips_all, "img", 0)
     strips_second = swapped(strips_all, "img", 1)
-    reg_p = around(regions, 1)
-
-    info, own_p = lax.optimization_barrier((info, own_p))
     part, near = pl.pallas_call(
         gather_kernel,
         out_shape=(jax.ShapeDtypeStruct((devices, LANES), f32), jax.ShapeDtypeStruct(flat, f32)),

time: 50.5 us -> 50.4 us (level)
  waiting for transfers between devices: 12.9 us -> 12.2 us
    ppermute x6, waiting for transfers between devices: 8.47 us -> 5.15 us  [shifted(): return lax.ppermute(cells, axis, pairs)]
    all_to_all x1, waiting for transfers between devices: 4.41 us -> 7.09 us  [body(): squares = lax.all_to_all(part, ('img', 'gx', 'gy'), 0, 0, tiled=True)]
    ppermute x6, starting transfers between devices: 7.35 us -> 5.02 us  [shifted(): return lax.ppermute(cells, axis, pairs)]
    ppermute x4, starting transfers between devices: 7.2 us -> 8.73 us  [swapped(): return lax.ppermute(cells, axis, pairs + [(j, i) for i, j in pairs])]
    all_to_all x1, starting transfers between devices: 4.18 us -> 4.98 us  [body(): squares = lax.all_to_all(part, ('img', 'gx', 'gy'), 0, 0, tiled=True)]
  transfers between devices with their start and end apart: 11 -> 11, of which waited for: 4 -> 3; matrix products, arithmetic and copies ran while one was open for 0% -> 0% of each run, Pallas kernels for 3% -> 5%
where the time goes in v7:
time: 50.4 us; the launch traced here: 49.7 us
  starting transfers between devices  18.7 us (37%)
  Pallas kernels  16 us (32%)
  waiting for transfers between devices  12.2 us (24%)
  local copies, waits for them, and re-layouts  2.61 us (5%)
    pallas_call x1, Pallas kernels, body(): pl.pallas_call(functools.partial(evolve_kernel, ny, tiles, images), out_s...  13.6 us
    ppermute x4, starting transfers between devices, swapped(): return lax.ppermute(cells, axis, pairs + [(j, i) for i, j in pairs])  8.73 us
    all_to_all x1, waiting for transfers between devices, body(): squares = lax.all_to_all(part, ('img', 'gx', 'gy'), 0, 0, tiled=True)  7.09 us
    ppermute x6, waiting for transfers between devices, shifted(): return lax.ppermute(cells, axis, pairs)  5.15 us
    ppermute x6, starting transfers between devices, shifted(): return lax.ppermute(cells, axis, pairs)  5.02 us
    all_to_all x1, starting transfers between devices, body(): squares = lax.all_to_all(part, ('img', 'gx', 'gy'), 0, 0, tiled=True)  4.98 us
    unnamed x16, local copies, waits for them, and re-layouts  2.61 us
    pallas_call x1, Pallas kernels, body(): pl.pallas_call(functools.partial(pack_kernel, ny, tiles, anisotropy.shape...  1.51 us
  transfers between devices with their start and end apart: 11, of which 3 were waited for; matrix products, arithmetic and copies ran while one was open for 0% of the time, Pallas kernels for 5%

profile of v7, /device:TPU:0, one launch (start us, length us, event | category | flops | bytes accessed | tf_op | source)
XLA Modules:
  0.0 49.7 jit_solution(1922411653356664480)
XLA Ops:
  0.0 3.0 %collective-permute-start.4 = (f32[3,16,16,128]{3,2,1,0:T(8,128)}, f32[3,16,16,128]{3,2,1,0:T(8,128)S(1)}, u32[]{:S(2)}, u32[]{:S(2)}) collective-permute-start(f32[3,16,16,128]{3,2,1,0:T(8,128)} %bitcast.15), channel_id=1, source_target_pairs={{0,8},{16,24},{8,0},{24,16},{1,9},{17,25},{9,1},{25,17},{2,10},{18... | collective-permute-start | bytes 1179656 | tf_op jit(solution)/shard_map/ppermute | solution.py:368
  3.0 0.7 %collective-permute-start.5 = (f32[3,16,16,128]{3,2,1,0:T(8,128)}, f32[3,16,16,128]{3,2,1,0:T(8,128)S(1)}, u32[]{:S(2)}, u32[]{:S(2)}) collective-permute-start(f32[3,16,16,128]{3,2,1,0:T(8,128)} %bitcast.16), channel_id=1, source_target_pairs={{8,16},{16,8},{9,17},{17,9},{10,18},{18,10},{11,19},{19,11},{12,20... | collective-permute-start | bytes 1179656 | tf_op jit(solution)/shard_map/ppermute | solution.py:368
  3.7 1.6 %collective-permute-start.1 = (s32[16,16,128]{2,1,0:T(8,128)}, s32[16,16,128]{2,1,0:T(8,128)S(1)}, u32[]{:S(2)}, u32[]{:S(2)}) collective-permute-start(s32[16,16,128]{2,1,0:T(8,128)} %param.9), channel_id=1, source_target_pairs={{0,1},{1,0},{2,3},{3,2},{4,5},{5,4},{6,7},{7,6},{8,9},{9,8},{10,11... | collective-permute-start | bytes 393224 | tf_op jit(solution)/shard_map/ppermute | solution.py:362
  5.3 0.0 copy-start.7
  5.3 0.0 copy-start.4
  5.3 0.0 copy-start.5
  5.3 0.0 copy-start.6
  5.3 0.6 %copy-done.7 = f32[3]{0:T(128)S(1)} copy-done((f32[3]{0:T(128)S(1)}, f32[3]{0:T(128)}, u32[]{:S(2)}) %copy-start.7) | copy-done | bytes 36
  5.9 0.0 copy-done.4
  5.9 0.0 copy-done.5
  6.0 0.0 copy-done.6
  6.0 0.0 copy-start
  6.0 1.0 %copy-done = f32[1,3,16,16,128]{4,3,2,1,0:T(8,128)S(1)} copy-done((f32[1,3,16,16,128]{4,3,2,1,0:T(8,128)S(1)}, f32[1,3,16,16,128]{4,3,2,1,0:T(8,128)}, u32[]{:S(2)}) %copy-start) | copy-done | bytes 393240
  7.0 0.0 copy-start.2
  7.0 0.9 %copy-done.2 = s32[16,16,128]{2,1,0:T(8,128)S(1)} copy-done((s32[16,16,128]{2,1,0:T(8,128)S(1)}, s32[16,16,128]{2,1,0:T(8,128)}, u32[]{:S(2)}) %copy-start.2) | copy-done | bytes 131096
  7.9 0.0 copy-start.1
  7.9 1.5 %pack_strips.1 = (f32[2,4,2,8,128]{4,3,2,1,0:T(8,128)S(1)}, f32[5,8,128]{2,1,0:T(8,128)S(1)}) custom-call(s32[4]{0:T(128)S(1)} %copy-done.4, f32[8]{0:T(128)S(1)} %copy-done.5, f32[8]{0:T(128)S(1)} %copy-done.6, f32[1,3]{1,0:T(1,128)S(1)} %bitcast.30, f32[3,256,128]{2,1,0:T(8,128)S(1)} %bitcast.17, s32[256,128]{1,0:T(8,128)S(1)} %bitcast.21), custom_call_target="tpu_custom_call" | custom-call | tf_op jit(solution)/shard_map/pack_strips/pallas_call | solution.py:407
  9.4 0.6 %collective-permute-start = (f32[2,4,2,8,128]{4,3,2,1,0:T(8,128)S(1)}, f32[2,4,2,8,128]{4,3,2,1,0:T(8,128)S(1)}, u32[]{:S(2)}, u32[]{:S(2)}) collective-permute-start(f32[2,4,2,8,128]{4,3,2,1,0:T(8,128)S(1)} %get-tuple-element.17.both_ref), channel_id=1, source_target_pairs={{0,1},{1,0},{2,3},{3,2},{4,5},{5,4},{6,7},{7,6},{8,9},{9,8},{10,11... | collective-permute-start | bytes 196616 | tf_op jit(solution)/shard_map/ppermute | solution.py:362
  10.0 3.7 %collective-permute-done.both_p_ref = f32[2,4,2,8,128]{4,3,2,1,0:T(8,128)S(1)} collective-permute-done((f32[2,4,2,8,128]{4,3,2,1,0:T(8,128)S(1)}, f32[2,4,2,8,128]{4,3,2,1,0:T(8,128)S(1)}, u32[]{:S(2)}, u32[]{:S(2)}) %collective-permute-start) | collective-permute-done | bytes 65568 | tf_op jit(solution)/shard_map/ppermute | solution.py:362
  13.7 0.0 collective-permute-done.1
  13.7 0.1 collective-permute-start.2
  13.8 1.7 %collective-permute-start.3 = (f32[2,4,2,8,128]{4,3,2,1,0:T(8,128)S(1)}, f32[2,4,2,8,128]{4,3,2,1,0:T(8,128)S(1)}, u32[]{:S(2)}, u32[]{:S(2)}) collective-permute-start(f32[2,4,2,8,128]{4,3,2,1,0:T(8,128)S(1)} %get-tuple-element.20), channel_id=1, source_target_pairs={{0,6},{2,0},{4,2},{6,4},{1,7},{3,1},{5,3},{7,5},{8,14},{10,8},{12,... | collective-permute-start | bytes 196616 | tf_op jit(solution)/shard_map/ppermute | solution.py:362
  15.5 0.0 copy-done.1
  15.5 0.5 %collective-permute-start.6 = (f32[3,16,16,128]{3,2,1,0:T(8,128)S(1)}, f32[3,16,16,128]{3,2,1,0:T(8,128)S(1)}, u32[]{:S(2)}, u32[]{:S(2)}) collective-permute-start(f32[3,16,16,128]{3,2,1,0:T(8,128)S(1)} %bitcast.18), channel_id=1, source_target_pairs={{0,1},{1,0},{2,3},{3,2},{4,5},{5,4},{6,7},{7,6},{8,9},{9,8},{10,11... | collective-permute-start | bytes 1179656 | tf_op jit(solution)/shard_map/ppermute | solution.py:362
  16.1 1.4 %collective-permute-done.2.left_ref = f32[2,4,2,8,128]{4,3,2,1,0:T(8,128)S(1)} collective-permute-done((f32[2,4,2,8,128]{4,3,2,1,0:T(8,128)S(1)}, f32[2,4,2,8,128]{4,3,2,1,0:T(8,128)S(1)}, u32[]{:S(2)}, u32[]{:S(2)}) %collective-permute-start.2) | collective-permute-done | bytes 65568 | tf_op jit(solution)/shard_map/ppermute | solution.py:362
  17.5 0.0 collective-permute-done.3.right_ref
  17.5 0.0 collective-permute-done.4
  17.5 0.0 collective-permute-done.5
  17.5 0.0 copy-start.3
  17.5 0.9 %gather_images.1 = (f32[32,128]{1,0:T(8,128)}, f32[3,256,128]{2,1,0:T(8,128)S(1)}) custom-call(f32[5,8,128]{2,1,0:T(8,128)S(1)} %get-tuple-element.21.info_ref, f32[3,256,128]{2,1,0:T(8,128)S(1)} %bitcast.19, f32[3,256,128]{2,1,0:T(8,128)S(1)} %bitcast.26, f32[3,256,128]{2,1,0:T(8,128)S(1)} %bitcast.27), custom_call_target="tpu_custom_call" | custom-call | tf_op jit(solution)/shard_map/gather_images/pallas_call | solution.py:450
  18.4 0.5 %collective-permute-start.7 = (f32[3,16,16,128]{3,2,1,0:T(8,128)S(1)}, f32[3,16,16,128]{3,2,1,0:T(8,128)S(1)}, u32[]{:S(2)}, u32[]{:S(2)}) collective-permute-start(f32[3,16,16,128]{3,2,1,0:T(8,128)S(1)} %bitcast.24), channel_id=1, source_target_pairs={{0,1},{1,0},{2,3},{3,2},{4,5},{5,4},{6,7},{7,6},{8,9},{9,8},{10,11... | collective-permute-start | bytes 1179656 | tf_op jit(solution)/shard_map/ppermute | solution.py:362
  18.9 4.4 %collective-permute-start.8 = (f32[2,2,3,2,8,128]{5,4,3,2,1,0:T(8,128)S(1)}, f32[2,2,3,2,8,128]{5,4,3,2,1,0:T(8,128)S(1)}, u32[]{:S(2)}, u32[]{:S(2)}) collective-permute-start(f32[2,2,3,2,8,128]{5,4,3,2,1,0:T(8,128)S(1)} %get-tuple-element.26), channel_id=1, source_target_pairs={{0,8},{16,24},{8,0},{24,16},{1,9},{17,25},{9,1},{25,17},{2,10},{18... | collective-permute-start | bytes 294920 | tf_op jit(solution)/shard_map/ppermute | solution.py:368
  23.3 0.7 %collective-permute-start.9 = (f32[2,2,3,2,8,128]{5,4,3,2,1,0:T(8,128)S(1)}, f32[2,2,3,2,8,128]{5,4,3,2,1,0:T(8,128)S(1)}, u32[]{:S(2)}, u32[]{:S(2)}) collective-permute-start(f32[2,2,3,2,8,128]{5,4,3,2,1,0:T(8,128)S(1)} %get-tuple-element.26), channel_id=1, source_target_pairs={{8,16},{16,8},{9,17},{17,9},{10,18},{18,10},{11,19},{19,11},{12,20... | collective-permute-start | bytes 294920 | tf_op jit(solution)/shard_map/ppermute | solution.py:368
  24.0 5.0 %all-to-all-start = ((f32[32,1,128]{2,1,0:T(1,128)}), f32[32,1,128]{2,1,0:T(1,128)S(1)}, u32[]{:S(2)}, u32[]{:S(2)}) async-start(f32[32,1,128]{2,1,0:T(1,128)} %bitcast.7), calls=%async_computation | async-start | bytes 32768 | tf_op jit(solution)/shard_map/all_to_all | solution.py:459
  29.0 0.0 collective-permute-done.8.first_ref
  29.0 0.0 collective-permute-done.9.second_ref
  29.0 0.0 collective-permute-done.6
  29.0 7.1 %all-to-all-done = f32[32,1,128]{2,1,0:T(1,128)S(1)} async-done(((f32[32,1,128]{2,1,0:T(1,128)}), f32[32,1,128]{2,1,0:T(1,128)S(1)}, u32[]{:S(2)}, u32[]{:S(2)}) %all-to-all-start) | async-done | bytes 16416 | tf_op jit(solution)/shard_map/all_to_all | solution.py:459
  36.1 0.0 collective-permute-done.7
  36.1 0.0 copy-done.3
  36.1 13.6 %evolve.1 = f32[3,256,128]{2,1,0:T(8,128)} custom-call(f32[5,8,128]{2,1,0:T(8,128)S(1)} %get-tuple-element.21.info_ref, f32[32,128]{1,0:T(8,128)S(1)} %bitcast.29, f32[3,256,128]{2,1,0:T(8,128)S(1)} %bitcast.20, f32[3,256,128]{2,1,0:T(8,128)S(1)} %bitcast.23, f32[3,256,128]{2,1,0:T(8,128)S(1)} %get-tuple-element.24.n_ref, f32[3,256,128]{2,1,0:T(8,128)S(1)} %bitcast.25, ...), custom_call_target="tpu_custom_call" | custom-call | tf_op jit(solution)/shard_map/evolve/pallas_call | solution.py:462
  (2 shorter events, 0.0 us)
Async XLA Ops:
  0.0 17.5 %collective-permute-start.4 = (f32[3,16,16,128]{3,2,1,0:T(8,128)}, f32[3,16,16,128]{3,2,1,0:T(8,128)S(1)}, u32[]{:S(2)}, u32[]{:S(2)}) collective-permute-start(f32[3,16,16,128]{3,2,1,0:T(8,128)} %bitcast.15), channel_id=1, source_target_pairs={{0,8},{16,24},{8,0},{24,16},{1,9},{17,25},{9,1},{25,17},{2,10},{18... | collective-permute-start | bytes 1179656 | tf_op jit(solution)/shard_map/ppermute | solution.py:368
  3.0 14.5 %collective-permute-start.5 = (f32[3,16,16,128]{3,2,1,0:T(8,128)}, f32[3,16,16,128]{3,2,1,0:T(8,128)S(1)}, u32[]{:S(2)}, u32[]{:S(2)}) collective-permute-start(f32[3,16,16,128]{3,2,1,0:T(8,128)} %bitcast.16), channel_id=1, source_target_pairs={{8,16},{16,8},{9,17},{17,9},{10,18},{18,10},{11,19},{19,11},{12,20... | collective-permute-start | bytes 1179656 | tf_op jit(solution)/shard_map/ppermute | solution.py:368
  3.7 10.0 %collective-permute-start.1 = (s32[16,16,128]{2,1,0:T(8,128)}, s32[16,16,128]{2,1,0:T(8,128)S(1)}, u32[]{:S(2)}, u32[]{:S(2)}) collective-permute-start(s32[16,16,128]{2,1,0:T(8,128)} %param.9), channel_id=1, source_target_pairs={{0,1},{1,0},{2,3},{3,2},{4,5},{5,4},{6,7},{7,6},{8,9},{9,8},{10,11... | collective-permute-start | bytes 393224 | tf_op jit(solution)/shard_map/ppermute | solution.py:362
  5.3 0.7 %copy-start.7 = (f32[3]{0:T(128)S(1)}, f32[3]{0:T(128)}, u32[]{:S(2)}) copy-start(f32[3]{0:T(128)} %param.8) | copy-start | bytes 40
  5.3 0.7 %copy-start.4 = (s32[4]{0:T(128)S(1)}, s32[4]{0:T(128)}, u32[]{:S(2)}) copy-start(s32[4]{0:T(128)} %lower_ref.1) | copy-start | bytes 52
  5.3 0.7 %copy-start.5 = (f32[8]{0:T(128)S(1)}, f32[8]{0:T(128)}, u32[]{:S(2)}) copy-start(f32[8]{0:T(128)} %aniso_ref.1) | copy-start | bytes 100
  5.3 0.7 %copy-start.6 = (f32[8]{0:T(128)S(1)}, f32[8]{0:T(128)}, u32[]{:S(2)}) copy-start(f32[8]{0:T(128)} %damp_ref.1) | copy-start | bytes 100
  6.0 1.0 %copy-start = (f32[1,3,16,16,128]{4,3,2,1,0:T(8,128)S(1)}, f32[1,3,16,16,128]{4,3,2,1,0:T(8,128)}, u32[]{:S(2)}) copy-start(f32[1,3,16,16,128]{4,3,2,1,0:T(8,128)} %param.6) | copy-start | bytes 1179652
  7.0 0.9 %copy-start.2 = (s32[16,16,128]{2,1,0:T(8,128)S(1)}, s32[16,16,128]{2,1,0:T(8,128)}, u32[]{:S(2)}) copy-start(s32[16,16,128]{2,1,0:T(8,128)} %param.9) | copy-start | bytes 393220
  7.9 7.7 %copy-start.1 = (f32[1,3,16,16,128]{4,3,2,1,0:T(8,128)S(1)}, f32[1,3,16,16,128]{4,3,2,1,0:T(8,128)}, u32[]{:S(2)}) copy-start(f32[1,3,16,16,128]{4,3,2,1,0:T(8,128)} %param.6) | copy-start | bytes 1179652
  9.4 4.3 %collective-permute-start = (f32[2,4,2,8,128]{4,3,2,1,0:T(8,128)S(1)}, f32[2,4,2,8,128]{4,3,2,1,0:T(8,128)S(1)}, u32[]{:S(2)}, u32[]{:S(2)}) collective-permute-start(f32[2,4,2,8,128]{4,3,2,1,0:T(8,128)S(1)} %get-tuple-element.17.both_ref), channel_id=1, source_target_pairs={{0,1},{1,0},{2,3},{3,2},{4,5},{5,4},{6,7},{7,6},{8,9},{9,8},{10,11... | collective-permute-start | bytes 196616 | tf_op jit(solution)/shard_map/ppermute | solution.py:362
  13.7 3.7 %collective-permute-start.2 = (f32[2,4,2,8,128]{4,3,2,1,0:T(8,128)S(1)}, f32[2,4,2,8,128]{4,3,2,1,0:T(8,128)S(1)}, u32[]{:S(2)}, u32[]{:S(2)}) collective-permute-start(f32[2,4,2,8,128]{4,3,2,1,0:T(8,128)S(1)} %get-tuple-element.19), channel_id=1, source_target_pairs={{0,2},{2,4},{4,6},{6,0},{1,3},{3,5},{5,7},{7,1},{8,10},{10,12},{12... | collective-permute-start | bytes 196616 | tf_op jit(solution)/shard_map/ppermute | solution.py:362
  13.8 3.7 %collective-permute-start.3 = (f32[2,4,2,8,128]{4,3,2,1,0:T(8,128)S(1)}, f32[2,4,2,8,128]{4,3,2,1,0:T(8,128)S(1)}, u32[]{:S(2)}, u32[]{:S(2)}) collective-permute-start(f32[2,4,2,8,128]{4,3,2,1,0:T(8,128)S(1)} %get-tuple-element.20), channel_id=1, source_target_pairs={{0,6},{2,0},{4,2},{6,4},{1,7},{3,1},{5,3},{7,5},{8,14},{10,8},{12,... | collective-permute-start | bytes 196616 | tf_op jit(solution)/shard_map/ppermute | solution.py:362
  15.5 13.4 %collective-permute-start.6 = (f32[3,16,16,128]{3,2,1,0:T(8,128)S(1)}, f32[3,16,16,128]{3,2,1,0:T(8,128)S(1)}, u32[]{:S(2)}, u32[]{:S(2)}) collective-permute-start(f32[3,16,16,128]{3,2,1,0:T(8,128)S(1)} %bitcast.18), channel_id=1, source_target_pairs={{0,1},{1,0},{2,3},{3,2},{4,5},{5,4},{6,7},{7,6},{8,9},{9,8},{10,11... | collective-permute-start | bytes 1179656 | tf_op jit(solution)/shard_map/ppermute | solution.py:362
  17.5 18.6 %copy-start.3 = (s32[16,16,128]{2,1,0:T(8,128)S(1)}, s32[16,16,128]{2,1,0:T(8,128)}, u32[]{:S(2)}) copy-start(s32[16,16,128]{2,1,0:T(8,128)} %param.9) | copy-start | bytes 393220
  18.4 17.7 %collective-permute-start.7 = (f32[3,16,16,128]{3,2,1,0:T(8,128)S(1)}, f32[3,16,16,128]{3,2,1,0:T(8,128)S(1)}, u32[]{:S(2)}, u32[]{:S(2)}) collective-permute-start(f32[3,16,16,128]{3,2,1,0:T(8,128)S(1)} %bitcast.24), channel_id=1, source_target_pairs={{0,1},{1,0},{2,3},{3,2},{4,5},{5,4},{6,7},{7,6},{8,9},{9,8},{10,11... | collective-permute-start | bytes 1179656 | tf_op jit(solution)/shard_map/ppermute | solution.py:362
  18.9 10.0 %collective-permute-start.8 = (f32[2,2,3,2,8,128]{5,4,3,2,1,0:T(8,128)S(1)}, f32[2,2,3,2,8,128]{5,4,3,2,1,0:T(8,128)S(1)}, u32[]{:S(2)}, u32[]{:S(2)}) collective-permute-start(f32[2,2,3,2,8,128]{5,4,3,2,1,0:T(8,128)S(1)} %get-tuple-element.26), channel_id=1, source_target_pairs={{0,8},{16,24},{8,0},{24,16},{1,9},{17,25},{9,1},{25,17},{2,10},{18... | collective-permute-start | bytes 294920 | tf_op jit(solution)/shard_map/ppermute | solution.py:368
  23.3 5.7 %collective-permute-start.9 = (f32[2,2,3,2,8,128]{5,4,3,2,1,0:T(8,128)S(1)}, f32[2,2,3,2,8,128]{5,4,3,2,1,0:T(8,128)S(1)}, u32[]{:S(2)}, u32[]{:S(2)}) collective-permute-start(f32[2,2,3,2,8,128]{5,4,3,2,1,0:T(8,128)S(1)} %get-tuple-element.26), channel_id=1, source_target_pairs={{8,16},{16,8},{9,17},{17,9},{10,18},{18,10},{11,19},{19,11},{12,20... | collective-permute-start | bytes 294920 | tf_op jit(solution)/shard_map/ppermute | solution.py:368
  24.0 12.1 %all-to-all-start = ((f32[32,1,128]{2,1,0:T(1,128)}), f32[32,1,128]{2,1,0:T(1,128)S(1)}, u32[]{:S(2)}, u32[]{:S(2)}) async-start(f32[32,1,128]{2,1,0:T(1,128)} %bitcast.7), calls=%async_computation | async-start | bytes 32768 | tf_op jit(solution)/shard_map/all_to_all | solution.py:459

commit v8 on v7

--- a/solution.py
+++ b/solution.py
@@ -27,12 +27,12 @@
     return lax.broadcasted_iota(jnp.int32, (SUB, LANES), 0)
 
 
-def rows_at(ny, tiles, y, t):
-    return pl.ds(y + ny * t, SUB, stride=ny * tiles)
+def rows_at(ny, tiles, y, t, first=0):
+    return pl.ds(first + y + ny * t, SUB, stride=ny * tiles)
 
 
 def pack_kernel(
-    ny, tiles, regions, lower_ref, aniso_ref, damp_ref, share_ref, m_ref, reg_ref, both_ref, info_ref
+    ny, tiles, regions, lower_ref, aniso_ref, damp_ref, share_ref, m_ref, reg_ref, left_ref, right_ref, info_ref
 ):
     here = lax.axis_index("img")
     lane = lane_iota()
@@ -50,8 +50,8 @@
                     cells = m_ref[c, rows, :] if c < COMPS else reg_ref[rows, :].astype(jnp.float32)
                     done.append((c, t, left, right, pltpu.roll(cells, shift, 1)))
         for c, t, left, right, cells in done:
-            pltpu.store(both_ref.at[0, c, t], cells, mask=left)
-            pltpu.store(both_ref.at[1, c, t], cells, mask=right)
+            pltpu.store(left_ref.at[c, t], cells, mask=left)
+            pltpu.store(right_ref.at[c, t], cells, mask=right)
         return carry
 
     table_a = jnp.zeros((SUB, LANES), jnp.float32)
@@ -73,17 +73,10 @@
     lax.fori_loop(0, ny // 2, pack, 0)
 
 
-def sort_kernel(both_ref, both_p_ref, left_ref, right_ref):
-    for g, ref in enumerate((both_ref, both_p_ref)):
-        left_ref[g] = ref[0]
-        right_ref[g] = ref[1]
-
-
 def merge_kernel(info_ref, left_ref, right_ref, out_ref, info_out_ref):
     info_out_ref[...] = info_ref[...]
-    for g in range(2):
-        out_ref[0, g] = left_ref[g, :COMPS]
-        out_ref[1, g] = right_ref[g, :COMPS]
+    out_ref[0] = left_ref[...]
+    out_ref[1] = right_ref[...]
 
 
 def take_first(info_ref, here):
@@ -92,31 +85,46 @@
     return jnp.where(below, jnp.where(odd, 1, 0), jnp.where(odd, 0, 1)) == 1, odd
 
 
-def gather_kernel(info_ref, m_ref, first_ref, second_ref, part_ref, near_ref):
+def strip_rows_at(cells, tiles, part, c, t):
+    row = cells + ((part * (COMPS + 1) + c) * tiles + t) * SUB
+    return pl.ds(row if isinstance(t, int) else pl.multiple_of(row, SUB), SUB)
+
+
+def gather_kernel(
+    tiles, info_ref, m_ref, first_ref, second_ref, strips_ref, strips1_ref, strips2_ref, part_ref, near_ref
+):
     here = lax.axis_index("img")
     pick, odd = take_first(info_ref, here)
     chunks = 4
+    depth = m_ref.shape[1]
 
     def squares(i, sums):
         sums = list(sums)
         done = []
         for u in range(chunks):
-            rows = pl.ds(pl.multiple_of((chunks * i + u) * SUB, SUB), SUB)
-            for c in range(COMPS):
-                one = first_ref[c, rows, :]
-                two = second_ref[c, rows, :]
-                done.append((c, rows, jnp.where(pick, one, two)))
-                diff = m_ref[c, rows, :] - jnp.where(odd, one, two)
+            start = pl.multiple_of((chunks * i + u) * SUB, SUB)
+            for c in range(COMPS):
+                one = first_ref[c, pl.ds(start, SUB), :]
+                two = second_ref[c, pl.ds(start, SUB), :]
+                done.append((c * depth + start, jnp.where(pick, one, two)))
+                diff = m_ref[c, pl.ds(start, SUB), :] - jnp.where(odd, one, two)
                 sums[c + COMPS * u] = sums[c + COMPS * u] + diff * diff
-        for c, rows, cells in done:
-            near_ref[c, rows, :] = cells
+        for start, cells in done:
+            near_ref[pl.ds(pl.multiple_of(start, SUB), SUB), :] = cells
         return tuple(sums)
 
     zero = jnp.zeros((SUB, LANES), jnp.float32)
-    sums = lax.fori_loop(0, m_ref.shape[1] // (chunks * SUB), squares, (zero,) * (chunks * COMPS))
+    sums = lax.fori_loop(0, depth // (chunks * SUB), squares, (zero,) * (chunks * COMPS))
     total = jnp.sum(functools.reduce(jnp.add, sums), axis=(0, 1), keepdims=True)
     slot = lax.broadcasted_iota(jnp.int32, part_ref.shape, 1)
     part_ref[...] = jnp.where((slot == here) & (here > 0), total, 0.0)
+    for side in range(2):
+        for c in range(COMPS + 1):
+            for t in range(tiles):
+                near_ref[strip_rows_at(COMPS * depth, tiles, side, c, t), :] = jnp.where(
+                    pick, strips1_ref[side, c, t], strips2_ref[side, c, t]
+                )
+                near_ref[strip_rows_at(COMPS * depth, tiles, 2 + side, c, t), :] = strips_ref[side, c, t]
 
 
 def turn(m, h, a2, b, sc):
@@ -150,10 +158,6 @@
     np_ref,
     reg_ref,
     regp_ref,
-    left_ref,
-    right_ref,
-    first_ref,
-    second_ref,
     out_ref,
     main0,
     main1,
@@ -178,7 +182,6 @@
     top = sub == SUB - 1
     bottom = sub == 0
 
-    pick, _ = take_first(info_ref, here)
     lo = info_ref[4]
     slot = lane.astype(jnp.float32)
     squares = jnp.broadcast_to(jnp.sum(sq_ref[...], axis=0, keepdims=True), (SUB, LANES))
@@ -200,13 +203,18 @@
         shift = (DEPTH * (k + 1)) & (LANES - 1)
         return [pltpu.roll(new[c], shift, 1) for c in range(COMPS)]
 
+    depth = m_ref.shape[1]
+
     def fill(k, carry):
         done = []
         for g, (own, near, reg) in enumerate(((m_ref, n_ref, reg_ref), (mp_ref, np_ref, regp_ref))):
             for t in range(tiles):
                 rows = rows_at(ny, tiles, k, t)
                 v = normal(
-                    [w_own * own[c, rows, :] + w_near * near[c, rows, :] for c in range(COMPS)]
+                    [
+                        w_own * own[c, rows, :] + w_near * near[rows_at(ny, tiles, k, t, c * depth), :]
+                        for c in range(COMPS)
+                    ]
                 )
                 done.append((g * ny + k, t, v, params(reg[rows, :])))
         for r, t, v, p in done:
@@ -223,14 +231,17 @@
 
     def fill_strips(t, carry):
         done = []
-        for g in range(2):
-            for side, cells in enumerate((left_ref, right_ref)):
-                near = [
-                    jnp.where(pick, first_ref[side, g, c, t], second_ref[side, g, c, t])
-                    for c in range(COMPS)
-                ]
-                v = normal([w_own * cells[g, c, t] + w_near * near[c] for c in range(COMPS)])
-                done.append((side, g, v, params(cells[g, COMPS, t].astype(jnp.int32))))
+        for g, cells in enumerate((n_ref, np_ref)):
+            for side in range(2):
+                near, own = (
+                    [
+                        cells[strip_rows_at(COMPS * depth, tiles, part, c, t), :]
+                        for c in range(COMPS + 1)
+                    ]
+                    for part in (side, 2 + side)
+                )
+                v = normal([w_own * own[c] + w_near * near[c] for c in range(COMPS)])
+                done.append((side, g, v, params(own[COMPS].astype(jnp.int32))))
         for side, g, v, p in done:
             for c in range(COMPS):
                 strip0[c, side, g, t] = v[c]
@@ -381,7 +392,7 @@
     if lax.axis_size("gy") == 2:
         return shifted(both, "gy", 1, True)
     block = lax.broadcasted_iota(jnp.int32, both.shape, both.ndim - 1) // DEPTH
-    side = lax.broadcasted_iota(jnp.int32, both.shape, 0)
+    side = lax.broadcasted_iota(jnp.int32, both.shape, 1)
     head = (block + side - 1) % (LANES // DEPTH) < DEPTH
     return jnp.where(head, shifted(both, "gy", -1, True), shifted(both, "gy", 1, True))
 
@@ -395,23 +406,21 @@
     assert ny == 2 * DEPTH and ny * DEPTH == LANES and tiles >= 2
     flat = (comps, nz * ny, nx)
     own = magnetization[0]
+    own_p = around(own, 2)
     first = swapped(own, "img", 0)
     second = swapped(own, "img", 1)
-    reg_p = around(regions, 1)
 
     smem = pl.BlockSpec(memory_space=pltpu.SMEM)
     vmem = pl.BlockSpec(memory_space=pltpu.VMEM)
     f32 = jnp.float32
     limit = pltpu.CompilerParams(vmem_limit_bytes=32 * 1024 * 1024)
     vreg = (SUB, LANES)
-    both, info = pl.pallas_call(
+    packed = jax.ShapeDtypeStruct((comps + 1, tiles) + vreg, f32)
+    left, right, info = pl.pallas_call(
         functools.partial(pack_kernel, ny, tiles, anisotropy.shape[0]),
-        out_shape=(
-            jax.ShapeDtypeStruct((2, comps + 1, tiles) + vreg, f32),
-            jax.ShapeDtypeStruct((5,) + vreg, f32),
-        ),
+        out_shape=(packed, packed, jax.ShapeDtypeStruct((5,) + vreg, f32)),
         in_specs=[smem] * 3 + [vmem] * 3,
-        out_specs=(vmem,) * 2,
+        out_specs=(vmem,) * 3,
         compiler_params=limit,
         name="pack_strips",
     )(
@@ -422,47 +431,51 @@
         own.reshape(flat),
         regions.reshape(flat[1:]),
     )
-    both_p = around_strips(both)
-    own_p = around(lax.optimization_barrier((own, both))[0], 2)
-    both_p, reg_p = lax.optimization_barrier((both_p, reg_p))
-    left, right = pl.pallas_call(
-        sort_kernel,
-        out_shape=(jax.ShapeDtypeStruct((2, comps + 1, tiles) + vreg, f32),) * 2,
-        in_specs=[vmem] * 2,
-        out_specs=(vmem,) * 2,
-        compiler_params=limit,
-        name="sort_strips",
-    )(both, both_p)
-    strips = (shifted(right, "gx", 1, True), shifted(left, "gx", -1, True))
-    strips_all, info = pl.pallas_call(
+    strip_l = shifted(right, "gx", 1, True)
+    strip_r = shifted(left, "gx", -1, True)
+    strips, info = pl.pallas_call(
         merge_kernel,
         out_shape=(
-            jax.ShapeDtypeStruct((2, 2, comps, tiles) + vreg, f32),
+            jax.ShapeDtypeStruct((2,) + packed.shape, f32),
             jax.ShapeDtypeStruct(info.shape, f32),
         ),
         in_specs=[vmem] * 3,
         out_specs=(vmem,) * 2,
         compiler_params=limit,
         name="merge_strips",
-    )(info, *strips)
-    strips_first = swapped(strips_all, "img", 0)
-    strips_second = swapped(strips_all, "img", 1)
+    )(info, strip_l, strip_r)
+    strips_first = swapped(strips, "img", 0)
+    strips_second = swapped(strips, "img", 1)
+
+    late_regions, own_p, info = lax.optimization_barrier((regions, own_p, info))
+    reg_p = around(late_regions, 1)
+    info, reg_p = lax.optimization_barrier((info, reg_p))
+    cells = comps * nz * ny
+    rows = cells + 4 * (comps + 1) * tiles * SUB
     part, near = pl.pallas_call(
-        gather_kernel,
-        out_shape=(jax.ShapeDtypeStruct((devices, LANES), f32), jax.ShapeDtypeStruct(flat, f32)),
-        in_specs=[vmem] * 4,
+        functools.partial(gather_kernel, tiles),
+        out_shape=(
+            jax.ShapeDtypeStruct((devices, LANES), f32),
+            jax.ShapeDtypeStruct((rows, LANES), f32),
+        ),
+        in_specs=[vmem] * 7,
         out_specs=(vmem,) * 2,
         compiler_params=limit,
         name="gather_images",
-    )(info, own.reshape(flat), first.reshape(flat), second.reshape(flat))
-    near_p = around(near.reshape(own.shape), 2)
+    )(info, own.reshape(flat), first.reshape(flat), second.reshape(flat), strips, strips_first, strips_second)
+    if lax.axis_size("gy") == 2:
+        near_p = shifted(near, "gy", 1, True)
+    else:
+        tile_p = around(near[:cells].reshape(own.shape), 2).reshape(cells, LANES)
+        rims_p = around_strips(near[cells:].reshape((2, 2, comps + 1, tiles) + vreg)).reshape(-1, LANES)
+        near_p = jnp.concatenate([tile_p, rims_p])
     squares = lax.all_to_all(part, ("img", "gx", "gy"), 0, 0, tiled=True)
 
     window = ny + 2 * DEPTH
     out = pl.pallas_call(
         functools.partial(evolve_kernel, ny, tiles, images),
         out_shape=jax.ShapeDtypeStruct(flat, f32),
-        in_specs=[vmem] * 12,
+        in_specs=[vmem] * 8,
         out_specs=vmem,
         scratch_shapes=[
             pltpu.VMEM((comps, window, tiles) + vreg, f32),
@@ -483,12 +496,9 @@
         own.reshape(flat),
         own_p.reshape(flat),
         near,
-        near_p.reshape(flat),
+        near_p,
         regions.reshape(flat[1:]),
         reg_p.reshape(flat[1:]),
-        *strips,
-        strips_first,
-        strips_second,
     )
     return out.reshape(magnetization.shape)
 

time: 50.4 us -> 51.1 us (1.014); the launches traced: 49.7 us -> 50.9 us
  blocking collectives: 0 us -> 13.9 us
  waiting for transfers between devices: 12.2 us -> 4.36 us
  starting transfers between devices: 18.7 us -> 14.6 us
  Pallas kernels: 16 us -> 15.4 us
    all_to_all x0 -> x1, blocking collectives: none -> 13.9 us  [body(): squares = lax.all_to_all(part, ('img', 'gx', 'gy'), 0, 0, tiled=True)]
    all_to_all x1 -> x0, waiting for transfers between devices: 7.09 us -> none  [body(): squares = lax.all_to_all(part, ('img', 'gx', 'gy'), 0, 0, tiled=True)]
    all_to_all x1 -> x0, starting transfers between devices: 4.98 us -> none  [body(): squares = lax.all_to_all(part, ('img', 'gx', 'gy'), 0, 0, tiled=True)]
    ppermute x6 -> x5, starting transfers between devices: 5.02 us -> 6.6 us  [shifted(): return lax.ppermute(cells, axis, pairs)]
    ppermute x6 -> x5, waiting for transfers between devices: 5.15 us -> 3.9 us  [shifted(): return lax.ppermute(cells, axis, pairs)]
    ppermute x4, starting transfers between devices: 8.73 us -> 8.04 us  [swapped(): return lax.ppermute(cells, axis, pairs + [(j, i) for i, j in pairs])]
    pallas_call x3 -> x2, Pallas kernels: 0.89 us -> 0.27 us  [the longest x1 0.26 us: body(): pl.pallas_call(functools.partial(gather_kernel, tiles), out_shape=(jax.Sh...]
  transfers between devices with their start and end apart: 11 -> 9, of which waited for: 3 -> 3; matrix products, arithmetic and copies ran while one was open for 0% -> 0% of each run, Pallas kernels for 5% -> 3%
where the time goes in v8:
time: 51.1 us; the launch traced here: 50.9 us
  Pallas kernels  15.4 us (30%)
  starting transfers between devices  14.6 us (29%)
  blocking collectives  13.9 us (27%)
  waiting for transfers between devices  4.36 us (9%)
  local copies, waits for them, and re-layouts  2.61 us (5%)
    all_to_all x1, blocking collectives, body(): squares = lax.all_to_all(part, ('img', 'gx', 'gy'), 0, 0, tiled=True)  13.9 us
    pallas_call x1, Pallas kernels, body(): pl.pallas_call(functools.partial(evolve_kernel, ny, tiles, images), out_s...  13.6 us
    ppermute x4, starting transfers between devices, swapped(): return lax.ppermute(cells, axis, pairs + [(j, i) for i, j in pairs])  8.04 us
    ppermute x5, starting transfers between devices, shifted(): return lax.ppermute(cells, axis, pairs)  6.6 us
    ppermute x5, waiting for transfers between devices, shifted(): return lax.ppermute(cells, axis, pairs)  3.9 us
    unnamed x16, local copies, waits for them, and re-layouts  2.61 us
    pallas_call x1, Pallas kernels, body(): pl.pallas_call(functools.partial(pack_kernel, ny, tiles, anisotropy.shape...  1.51 us
  transfers between devices with their start and end apart: 9, of which 3 were waited for; matrix products, arithmetic and copies ran while one was open for 0% of the time, Pallas kernels for 3%

profile of v8, /device:TPU:0, one launch (start us, length us, event | category | flops | bytes accessed | tf_op | source)
XLA Modules:
  0.0 50.9 jit_solution(2392607417261406837)
XLA Ops:
  0.0 2.9 %collective-permute-start = (f32[3,16,16,128]{3,2,1,0:T(8,128)}, f32[3,16,16,128]{3,2,1,0:T(8,128)S(1)}, u32[]{:S(2)}, u32[]{:S(2)}) collective-permute-start(f32[3,16,16,128]{3,2,1,0:T(8,128)} %bitcast.13), channel_id=1, source_target_pairs={{0,1},{1,0},{2,3},{3,2},{4,5},{5,4},{6,7},{7,6},{8,9},{9,8},{10,11... | collective-permute-start | bytes 1179656 | tf_op jit(solution)/shard_map/ppermute | solution.py:373
  2.9 0.7 %collective-permute-start.5 = (f32[3,16,16,128]{3,2,1,0:T(8,128)}, f32[3,16,16,128]{3,2,1,0:T(8,128)S(1)}, u32[]{:S(2)}, u32[]{:S(2)}) collective-permute-start(f32[3,16,16,128]{3,2,1,0:T(8,128)} %bitcast.14), channel_id=1, source_target_pairs={{8,16},{16,8},{9,17},{17,9},{10,18},{18,10},{11,19},{19,11},{12,20... | collective-permute-start | bytes 1179656 | tf_op jit(solution)/shard_map/ppermute | solution.py:379
  3.6 4.4 %collective-permute-start.4 = (f32[3,16,16,128]{3,2,1,0:T(8,128)}, f32[3,16,16,128]{3,2,1,0:T(8,128)S(1)}, u32[]{:S(2)}, u32[]{:S(2)}) collective-permute-start(f32[3,16,16,128]{3,2,1,0:T(8,128)} %bitcast.15), channel_id=1, source_target_pairs={{0,8},{16,24},{8,0},{24,16},{1,9},{17,25},{9,1},{25,17},{2,10},{18... | collective-permute-start | bytes 1179656 | tf_op jit(solution)/shard_map/ppermute | solution.py:379
  8.1 0.0 copy-start.7
  8.1 0.0 copy-start.4
  8.1 0.0 copy-start.5
  8.1 0.0 copy-start.6
  8.1 0.6 %copy-done.7 = f32[3]{0:T(128)S(1)} copy-done((f32[3]{0:T(128)S(1)}, f32[3]{0:T(128)}, u32[]{:S(2)}) %copy-start.7) | copy-done | bytes 36
  8.7 0.0 copy-done.4
  8.7 0.0 copy-done.5
  8.7 0.0 copy-done.6
  8.8 0.0 copy-start
  8.8 1.0 %copy-done = f32[1,3,16,16,128]{4,3,2,1,0:T(8,128)S(1)} copy-done((f32[1,3,16,16,128]{4,3,2,1,0:T(8,128)S(1)}, f32[1,3,16,16,128]{4,3,2,1,0:T(8,128)}, u32[]{:S(2)}) %copy-start) | copy-done | bytes 393240
  9.8 0.0 copy-start.2
  9.8 0.9 %copy-done.2 = s32[16,16,128]{2,1,0:T(8,128)S(1)} copy-done((s32[16,16,128]{2,1,0:T(8,128)S(1)}, s32[16,16,128]{2,1,0:T(8,128)}, u32[]{:S(2)}) %copy-start.2) | copy-done | bytes 131096
  10.7 0.0 copy-start.1
  10.7 1.5 %pack_strips.1 = (f32[4,2,8,128]{3,2,1,0:T(8,128)S(1)}, f32[4,2,8,128]{3,2,1,0:T(8,128)S(1)}, f32[5,8,128]{2,1,0:T(8,128)S(1)}) custom-call(s32[4]{0:T(128)S(1)} %copy-done.4, f32[8]{0:T(128)S(1)} %copy-done.5, f32[8]{0:T(128)S(1)} %copy-done.6, f32[1,3]{1,0:T(1,128)S(1)} %bitcast.27, f32[3,256,128]{2,1,0:T(8,128)S(1)} %bitcast.16, s32[256,128]{1,0:T(8,128)S(1)} %bitcast.19), custom_call_target="tpu_custom_call" | custom-call | tf_op jit(solution)/shard_map/pack_strips/pallas_call | solution.py:419
  12.2 0.1 collective-permute-start.1
  12.2 1.7 %collective-permute-start.2 = (f32[4,2,8,128]{3,2,1,0:T(8,128)S(1)}, f32[4,2,8,128]{3,2,1,0:T(8,128)S(1)}, u32[]{:S(2)}, u32[]{:S(2)}) collective-permute-start(f32[4,2,8,128]{3,2,1,0:T(8,128)S(1)} %get-tuple-element.19), channel_id=1, source_target_pairs={{0,6},{2,0},{4,2},{6,4},{1,7},{3,1},{5,3},{7,5},{8,14},{10,8},{12,... | collective-permute-start | bytes 98312 | tf_op jit(solution)/shard_map/ppermute | solution.py:373
  14.0 1.6 %collective-permute-done.1.left_ref = f32[4,2,8,128]{3,2,1,0:T(8,128)S(1)} collective-permute-done((f32[4,2,8,128]{3,2,1,0:T(8,128)S(1)}, f32[4,2,8,128]{3,2,1,0:T(8,128)S(1)}, u32[]{:S(2)}, u32[]{:S(2)}) %collective-permute-start.1) | collective-permute-done | bytes 32800 | tf_op jit(solution)/shard_map/ppermute | solution.py:373
  15.6 0.0 collective-permute-done.2.right_ref
  15.6 0.0 collective-permute-done
  15.6 0.6 %collective-permute-start.3 = (s32[16,16,128]{2,1,0:T(8,128)S(1)}, s32[16,16,128]{2,1,0:T(8,128)S(1)}, u32[]{:S(2)}, u32[]{:S(2)}) collective-permute-start(s32[16,16,128]{2,1,0:T(8,128)S(1)} %copy-done.2), channel_id=1, source_target_pairs={{0,1},{1,0},{2,3},{3,2},{4,5},{5,4},{6,7},{7,6},{8,9},{9,8},{10,11... | collective-permute-start | bytes 393224 | tf_op jit(solution)/shard_map/ppermute | solution.py:373
  16.2 0.7 %collective-permute-start.7 = (f32[2,4,2,8,128]{4,3,2,1,0:T(8,128)S(1)}, f32[2,4,2,8,128]{4,3,2,1,0:T(8,128)S(1)}, u32[]{:S(2)}, u32[]{:S(2)}) collective-permute-start(f32[2,4,2,8,128]{4,3,2,1,0:T(8,128)S(1)} %get-tuple-element.24.strips_ref), channel_id=1, source_target_pairs={{8,16},{16,8},{9,17},{17,9},{10,18},{18,10},{11,19},{19,11},{12,20... | collective-permute-start | bytes 196616 | tf_op jit(solution)/shard_map/ppermute | solution.py:379
  16.9 2.3 %collective-permute-start.6 = (f32[2,4,2,8,128]{4,3,2,1,0:T(8,128)S(1)}, f32[2,4,2,8,128]{4,3,2,1,0:T(8,128)S(1)}, u32[]{:S(2)}, u32[]{:S(2)}) collective-permute-start(f32[2,4,2,8,128]{4,3,2,1,0:T(8,128)S(1)} %get-tuple-element.24.strips_ref), channel_id=1, source_target_pairs={{0,8},{16,24},{8,0},{24,16},{1,9},{17,25},{9,1},{25,17},{2,10},{18... | collective-permute-start | bytes 196616 | tf_op jit(solution)/shard_map/ppermute | solution.py:379
  19.1 2.3 %collective-permute-done.3 = s32[16,16,128]{2,1,0:T(8,128)S(1)} collective-permute-done((s32[16,16,128]{2,1,0:T(8,128)S(1)}, s32[16,16,128]{2,1,0:T(8,128)S(1)}, u32[]{:S(2)}, u32[]{:S(2)}) %collective-permute-start.3) | collective-permute-done | bytes 131104 | tf_op jit(solution)/shard_map/ppermute | solution.py:373
  21.4 0.0 collective-permute-done.7.strips2_ref
  21.4 0.5 collective-permute-done.6.strips1_ref
  21.9 0.0 collective-permute-done.5
  21.9 0.0 collective-permute-done.4
  21.9 0.0 copy-done.1
  21.9 0.0 copy-start.3
  21.9 0.3 gather_images.1
  22.2 1.3 %collective-permute-start.8 = (f32[1024,128]{1,0:T(8,128)S(1)}, f32[1024,128]{1,0:T(8,128)S(1)}, u32[]{:S(2)}, u32[]{:S(2)}) collective-permute-start(f32[1024,128]{1,0:T(8,128)S(1)} %get-tuple-element.27.n_ref), channel_id=1, source_target_pairs={{0,1},{1,0},{2,3},{3,2},{4,5},{5,4},{6,7},{7,6},{8,9},{9,8},{10,11... | collective-permute-start | bytes 1572872 | tf_op jit(solution)/shard_map/ppermute | solution.py:373
  23.5 13.9 %all_to_all.11 = f32[32,1,128]{2,1,0:T(1,128)S(1)} all-to-all(f32[32,1,128]{2,1,0:T(1,128)S(1)} %bitcast.26), channel_id=1, replica_groups=mesh['img'=4,'gx'=4,'gy'=2] {'img','gx','gy'}, dimensions={0} | all-to-all | bytes 32768 | tf_op jit(solution)/shard_map/all_to_all | solution.py:472
  37.3 0.0 collective-permute-done.8.np_ref
  37.3 0.0 copy-done.3
  37.3 13.6 %evolve.1 = f32[3,256,128]{2,1,0:T(8,128)} custom-call(f32[5,8,128]{2,1,0:T(8,128)S(1)} %get-tuple-element.23.info_ref, f32[32,128]{1,0:T(8,128)S(1)} %bitcast.25, f32[3,256,128]{2,1,0:T(8,128)S(1)} %bitcast.18, f32[3,256,128]{2,1,0:T(8,128)S(1)} %bitcast.21, f32[1024,128]{1,0:T(8,128)S(1)} %get-tuple-element.27.n_ref, ...), custom_call_target="tpu_custom_call" | custom-call | tf_op jit(solution)/shard_map/evolve/pallas_call | solution.py:475
  (1 shorter events, 0.0 us)
Async XLA Ops:
  0.0 15.6 %collective-permute-start = (f32[3,16,16,128]{3,2,1,0:T(8,128)}, f32[3,16,16,128]{3,2,1,0:T(8,128)S(1)}, u32[]{:S(2)}, u32[]{:S(2)}) collective-permute-start(f32[3,16,16,128]{3,2,1,0:T(8,128)} %bitcast.13), channel_id=1, source_target_pairs={{0,1},{1,0},{2,3},{3,2},{4,5},{5,4},{6,7},{7,6},{8,9},{9,8},{10,11... | collective-permute-start | bytes 1179656 | tf_op jit(solution)/shard_map/ppermute | solution.py:373
  2.9 18.9 %collective-permute-start.5 = (f32[3,16,16,128]{3,2,1,0:T(8,128)}, f32[3,16,16,128]{3,2,1,0:T(8,128)S(1)}, u32[]{:S(2)}, u32[]{:S(2)}) collective-permute-start(f32[3,16,16,128]{3,2,1,0:T(8,128)} %bitcast.14), channel_id=1, source_target_pairs={{8,16},{16,8},{9,17},{17,9},{10,18},{18,10},{11,19},{19,11},{12,20... | collective-permute-start | bytes 1179656 | tf_op jit(solution)/shard_map/ppermute | solution.py:379
  3.6 18.3 %collective-permute-start.4 = (f32[3,16,16,128]{3,2,1,0:T(8,128)}, f32[3,16,16,128]{3,2,1,0:T(8,128)S(1)}, u32[]{:S(2)}, u32[]{:S(2)}) collective-permute-start(f32[3,16,16,128]{3,2,1,0:T(8,128)} %bitcast.15), channel_id=1, source_target_pairs={{0,8},{16,24},{8,0},{24,16},{1,9},{17,25},{9,1},{25,17},{2,10},{18... | collective-permute-start | bytes 1179656 | tf_op jit(solution)/shard_map/ppermute | solution.py:379
  8.1 0.7 %copy-start.7 = (f32[3]{0:T(128)S(1)}, f32[3]{0:T(128)}, u32[]{:S(2)}) copy-start(f32[3]{0:T(128)} %param.8) | copy-start | bytes 40
  8.1 0.7 %copy-start.4 = (s32[4]{0:T(128)S(1)}, s32[4]{0:T(128)}, u32[]{:S(2)}) copy-start(s32[4]{0:T(128)} %lower_ref.1) | copy-start | bytes 52
  8.1 0.7 %copy-start.5 = (f32[8]{0:T(128)S(1)}, f32[8]{0:T(128)}, u32[]{:S(2)}) copy-start(f32[8]{0:T(128)} %aniso_ref.1) | copy-start | bytes 100
  8.1 0.7 %copy-start.6 = (f32[8]{0:T(128)S(1)}, f32[8]{0:T(128)}, u32[]{:S(2)}) copy-start(f32[8]{0:T(128)} %damp_ref.1) | copy-start | bytes 100
  8.8 1.0 %copy-start = (f32[1,3,16,16,128]{4,3,2,1,0:T(8,128)S(1)}, f32[1,3,16,16,128]{4,3,2,1,0:T(8,128)}, u32[]{:S(2)}) copy-start(f32[1,3,16,16,128]{4,3,2,1,0:T(8,128)} %param.6) | copy-start | bytes 1179652
  9.8 0.9 %copy-start.2 = (s32[16,16,128]{2,1,0:T(8,128)S(1)}, s32[16,16,128]{2,1,0:T(8,128)}, u32[]{:S(2)}) copy-start(s32[16,16,128]{2,1,0:T(8,128)} %param.9) | copy-start | bytes 393220
  10.7 11.2 %copy-start.1 = (f32[1,3,16,16,128]{4,3,2,1,0:T(8,128)S(1)}, f32[1,3,16,16,128]{4,3,2,1,0:T(8,128)}, u32[]{:S(2)}) copy-start(f32[1,3,16,16,128]{4,3,2,1,0:T(8,128)} %param.6) | copy-start | bytes 1179652
  12.2 3.4 %collective-permute-start.1 = (f32[4,2,8,128]{3,2,1,0:T(8,128)S(1)}, f32[4,2,8,128]{3,2,1,0:T(8,128)S(1)}, u32[]{:S(2)}, u32[]{:S(2)}) collective-permute-start(f32[4,2,8,128]{3,2,1,0:T(8,128)S(1)} %get-tuple-element.18), channel_id=1, source_target_pairs={{0,2},{2,4},{4,6},{6,0},{1,3},{3,5},{5,7},{7,1},{8,10},{10,12},{12... | collective-permute-start | bytes 98312 | tf_op jit(solution)/shard_map/ppermute | solution.py:373
  12.2 3.3 %collective-permute-start.2 = (f32[4,2,8,128]{3,2,1,0:T(8,128)S(1)}, f32[4,2,8,128]{3,2,1,0:T(8,128)S(1)}, u32[]{:S(2)}, u32[]{:S(2)}) collective-permute-start(f32[4,2,8,128]{3,2,1,0:T(8,128)S(1)} %get-tuple-element.19), channel_id=1, source_target_pairs={{0,6},{2,0},{4,2},{6,4},{1,7},{3,1},{5,3},{7,5},{8,14},{10,8},{12,... | collective-permute-start | bytes 98312 | tf_op jit(solution)/shard_map/ppermute | solution.py:373
  15.6 5.8 %collective-permute-start.3 = (s32[16,16,128]{2,1,0:T(8,128)S(1)}, s32[16,16,128]{2,1,0:T(8,128)S(1)}, u32[]{:S(2)}, u32[]{:S(2)}) collective-permute-start(s32[16,16,128]{2,1,0:T(8,128)S(1)} %copy-done.2), channel_id=1, source_target_pairs={{0,1},{1,0},{2,3},{3,2},{4,5},{5,4},{6,7},{7,6},{8,9},{9,8},{10,11... | collective-permute-start | bytes 393224 | tf_op jit(solution)/shard_map/ppermute | solution.py:373
  16.2 5.2 %collective-permute-start.7 = (f32[2,4,2,8,128]{4,3,2,1,0:T(8,128)S(1)}, f32[2,4,2,8,128]{4,3,2,1,0:T(8,128)S(1)}, u32[]{:S(2)}, u32[]{:S(2)}) collective-permute-start(f32[2,4,2,8,128]{4,3,2,1,0:T(8,128)S(1)} %get-tuple-element.24.strips_ref), channel_id=1, source_target_pairs={{8,16},{16,8},{9,17},{17,9},{10,18},{18,10},{11,19},{19,11},{12,20... | collective-permute-start | bytes 196616 | tf_op jit(solution)/shard_map/ppermute | solution.py:379
  16.9 5.0 %collective-permute-start.6 = (f32[2,4,2,8,128]{4,3,2,1,0:T(8,128)S(1)}, f32[2,4,2,8,128]{4,3,2,1,0:T(8,128)S(1)}, u32[]{:S(2)}, u32[]{:S(2)}) collective-permute-start(f32[2,4,2,8,128]{4,3,2,1,0:T(8,128)S(1)} %get-tuple-element.24.strips_ref), channel_id=1, source_target_pairs={{0,8},{16,24},{8,0},{24,16},{1,9},{17,25},{9,1},{25,17},{2,10},{18... | collective-permute-start | bytes 196616 | tf_op jit(solution)/shard_map/ppermute | solution.py:379
  21.9 15.4 %copy-start.3 = (s32[16,16,128]{2,1,0:T(8,128)S(1)}, s32[16,16,128]{2,1,0:T(8,128)}, u32[]{:S(2)}) copy-start(s32[16,16,128]{2,1,0:T(8,128)} %param.9) | copy-start | bytes 393220
  22.2 15.2 %collective-permute-start.8 = (f32[1024,128]{1,0:T(8,128)S(1)}, f32[1024,128]{1,0:T(8,128)S(1)}, u32[]{:S(2)}, u32[]{:S(2)}) collective-permute-start(f32[1024,128]{1,0:T(8,128)S(1)} %get-tuple-element.27.n_ref), channel_id=1, source_target_pairs={{0,1},{1,0},{2,3},{3,2},{4,5},{5,4},{6,7},{7,6},{8,9},{9,8},{10,11... | collective-permute-start | bytes 1572872 | tf_op jit(solution)/shard_map/ppermute | solution.py:373

commit v9 on v8

--- a/solution.py
+++ b/solution.py
@@ -27,8 +27,8 @@
     return lax.broadcasted_iota(jnp.int32, (SUB, LANES), 0)
 
 
-def rows_at(ny, tiles, y, t, first=0):
-    return pl.ds(first + y + ny * t, SUB, stride=ny * tiles)
+def rows_at(ny, tiles, y, t):
+    return pl.ds(y + ny * t, SUB, stride=ny * tiles)
 
 
 def pack_kernel(
@@ -73,8 +73,7 @@
     lax.fori_loop(0, ny // 2, pack, 0)
 
 
-def merge_kernel(info_ref, left_ref, right_ref, out_ref, info_out_ref):
-    info_out_ref[...] = info_ref[...]
+def merge_kernel(left_ref, right_ref, out_ref):
     out_ref[0] = left_ref[...]
     out_ref[1] = right_ref[...]
 
@@ -85,13 +84,8 @@
     return jnp.where(below, jnp.where(odd, 1, 0), jnp.where(odd, 0, 1)) == 1, odd
 
 
-def strip_rows_at(cells, tiles, part, c, t):
-    row = cells + ((part * (COMPS + 1) + c) * tiles + t) * SUB
-    return pl.ds(row if isinstance(t, int) else pl.multiple_of(row, SUB), SUB)
-
-
 def gather_kernel(
-    tiles, info_ref, m_ref, first_ref, second_ref, strips_ref, strips1_ref, strips2_ref, part_ref, near_ref
+    ny, tiles, info_ref, m_ref, first_ref, second_ref, own_left_ref, own_right_ref, part_ref, near_ref, left_ref, right_ref
 ):
     here = lax.axis_index("img")
     pick, odd = take_first(info_ref, here)
@@ -106,11 +100,11 @@
             for c in range(COMPS):
                 one = first_ref[c, pl.ds(start, SUB), :]
                 two = second_ref[c, pl.ds(start, SUB), :]
-                done.append((c * depth + start, jnp.where(pick, one, two)))
+                done.append((c, start, jnp.where(pick, one, two)))
                 diff = m_ref[c, pl.ds(start, SUB), :] - jnp.where(odd, one, two)
                 sums[c + COMPS * u] = sums[c + COMPS * u] + diff * diff
-        for start, cells in done:
-            near_ref[pl.ds(pl.multiple_of(start, SUB), SUB), :] = cells
+        for c, start, cells in done:
+            near_ref[c, pl.ds(start, SUB), :] = cells
         return tuple(sums)
 
     zero = jnp.zeros((SUB, LANES), jnp.float32)
@@ -118,13 +112,27 @@
     total = jnp.sum(functools.reduce(jnp.add, sums), axis=(0, 1), keepdims=True)
     slot = lax.broadcasted_iota(jnp.int32, part_ref.shape, 1)
     part_ref[...] = jnp.where((slot == here) & (here > 0), total, 0.0)
-    for side in range(2):
-        for c in range(COMPS + 1):
+    left_ref[COMPS:] = own_left_ref[...]
+    right_ref[COMPS:] = own_right_ref[...]
+    block = lane_iota() // DEPTH
+
+    def pack(i, carry):
+        done = []
+        for u in range(2):
+            y = 2 * i + u
+            left = block == ((y + 1) & (ny - 1))
+            right = block == y
+            shift = (DEPTH * (y + 1)) & (LANES - 1)
             for t in range(tiles):
-                near_ref[strip_rows_at(COMPS * depth, tiles, side, c, t), :] = jnp.where(
-                    pick, strips1_ref[side, c, t], strips2_ref[side, c, t]
-                )
-                near_ref[strip_rows_at(COMPS * depth, tiles, 2 + side, c, t), :] = strips_ref[side, c, t]
+                for c in range(COMPS):
+                    cells = pltpu.roll(near_ref[c, rows_at(ny, tiles, y, t), :], shift, 1)
+                    done.append((c, t, left, right, cells))
+        for c, t, left, right, cells in done:
+            pltpu.store(left_ref.at[c, t], cells, mask=left)
+            pltpu.store(right_ref.at[c, t], cells, mask=right)
+        return carry
+
+    lax.fori_loop(0, ny // 2, pack, 0)
 
 
 def turn(m, h, a2, b, sc):
@@ -158,6 +166,8 @@
     np_ref,
     reg_ref,
     regp_ref,
+    strips_ref,
+    stripsp_ref,
     out_ref,
     main0,
     main1,
@@ -203,8 +213,6 @@
         shift = (DEPTH * (k + 1)) & (LANES - 1)
         return [pltpu.roll(new[c], shift, 1) for c in range(COMPS)]
 
-    depth = m_ref.shape[1]
-
     def fill(k, carry):
         done = []
         for g, (own, near, reg) in enumerate(((m_ref, n_ref, reg_ref), (mp_ref, np_ref, regp_ref))):
@@ -212,7 +220,7 @@
                 rows = rows_at(ny, tiles, k, t)
                 v = normal(
                     [
-                        w_own * own[c, rows, :] + w_near * near[rows_at(ny, tiles, k, t, c * depth), :]
+                        w_own * own[c, rows, :] + w_near * near[c, rows, :]
                         for c in range(COMPS)
                     ]
                 )
@@ -231,17 +239,12 @@
 
     def fill_strips(t, carry):
         done = []
-        for g, cells in enumerate((n_ref, np_ref)):
+        for g, cells in enumerate((strips_ref, stripsp_ref)):
             for side in range(2):
-                near, own = (
-                    [
-                        cells[strip_rows_at(COMPS * depth, tiles, part, c, t), :]
-                        for c in range(COMPS + 1)
-                    ]
-                    for part in (side, 2 + side)
+                v = normal(
+                    [w_own * cells[side, COMPS + c, t] + w_near * cells[side, c, t] for c in range(COMPS)]
                 )
-                v = normal([w_own * own[c] + w_near * near[c] for c in range(COMPS)])
-                done.append((side, g, v, params(own[COMPS].astype(jnp.int32))))
+                done.append((side, g, v, params(cells[side, 2 * COMPS, t].astype(jnp.int32))))
         for side, g, v, p in done:
             for c in range(COMPS):
                 strip0[c, side, g, t] = v[c]
@@ -392,7 +395,7 @@
     if lax.axis_size("gy") == 2:
         return shifted(both, "gy", 1, True)
     block = lax.broadcasted_iota(jnp.int32, both.shape, both.ndim - 1) // DEPTH
-    side = lax.broadcasted_iota(jnp.int32, both.shape, 1)
+    side = lax.broadcasted_iota(jnp.int32, both.shape, 0)
     head = (block + side - 1) % (LANES // DEPTH) < DEPTH
     return jnp.where(head, shifted(both, "gy", -1, True), shifted(both, "gy", 1, True))
 
@@ -431,51 +434,42 @@
         own.reshape(flat),
         regions.reshape(flat[1:]),
     )
-    strip_l = shifted(right, "gx", 1, True)
-    strip_r = shifted(left, "gx", -1, True)
-    strips, info = pl.pallas_call(
-        merge_kernel,
-        out_shape=(
-            jax.ShapeDtypeStruct((2,) + packed.shape, f32),
-            jax.ShapeDtypeStruct(info.shape, f32),
-        ),
-        in_specs=[vmem] * 3,
-        out_specs=(vmem,) * 2,
-        compiler_params=limit,
-        name="merge_strips",
-    )(info, strip_l, strip_r)
-    strips_first = swapped(strips, "img", 0)
-    strips_second = swapped(strips, "img", 1)
-
     late_regions, own_p, info = lax.optimization_barrier((regions, own_p, info))
     reg_p = around(late_regions, 1)
     info, reg_p = lax.optimization_barrier((info, reg_p))
-    cells = comps * nz * ny
-    rows = cells + 4 * (comps + 1) * tiles * SUB
-    part, near = pl.pallas_call(
-        functools.partial(gather_kernel, tiles),
+    packed = jax.ShapeDtypeStruct((2 * comps + 1, tiles) + vreg, f32)
+    part, near, left, right = pl.pallas_call(
+        functools.partial(gather_kernel, ny, tiles),
         out_shape=(
             jax.ShapeDtypeStruct((devices, LANES), f32),
-            jax.ShapeDtypeStruct((rows, LANES), f32),
+            jax.ShapeDtypeStruct(flat, f32),
+            packed,
+            packed,
         ),
-        in_specs=[vmem] * 7,
-        out_specs=(vmem,) * 2,
+        in_specs=[vmem] * 6,
+        out_specs=(vmem,) * 4,
         compiler_params=limit,
         name="gather_images",
-    )(info, own.reshape(flat), first.reshape(flat), second.reshape(flat), strips, strips_first, strips_second)
-    if lax.axis_size("gy") == 2:
-        near_p = shifted(near, "gy", 1, True)
-    else:
-        tile_p = around(near[:cells].reshape(own.shape), 2).reshape(cells, LANES)
-        rims_p = around_strips(near[cells:].reshape((2, 2, comps + 1, tiles) + vreg)).reshape(-1, LANES)
-        near_p = jnp.concatenate([tile_p, rims_p])
+    )(info, own.reshape(flat), first.reshape(flat), second.reshape(flat), left, right)
+    near_p = around(near.reshape(own.shape), 2)
+    strip_l = shifted(right, "gx", 1, True)
+    strip_r = shifted(left, "gx", -1, True)
+    strips = pl.pallas_call(
+        merge_kernel,
+        out_shape=jax.ShapeDtypeStruct((2,) + packed.shape, f32),
+        in_specs=[vmem] * 2,
+        out_specs=vmem,
+        compiler_params=limit,
+        name="merge_strips",
+    )(strip_l, strip_r)
+    strips_p = around_strips(strips)
     squares = lax.all_to_all(part, ("img", "gx", "gy"), 0, 0, tiled=True)
 
     window = ny + 2 * DEPTH
     out = pl.pallas_call(
         functools.partial(evolve_kernel, ny, tiles, images),
         out_shape=jax.ShapeDtypeStruct(flat, f32),
-        in_specs=[vmem] * 8,
+        in_specs=[vmem] * 10,
         out_specs=vmem,
         scratch_shapes=[
             pltpu.VMEM((comps, window, tiles) + vreg, f32),
@@ -496,9 +490,11 @@
         own.reshape(flat),
         own_p.reshape(flat),
         near,
-        near_p,
+        near_p.reshape(flat),
         regions.reshape(flat[1:]),
         reg_p.reshape(flat[1:]),
+        strips,
+        strips_p,
     )
     return out.reshape(magnetization.shape)
 

time: 51.1 us -> 51.3 us (level)
  starting transfers between devices: 14.6 us -> 13.7 us
  waiting for transfers between devices: 4.36 us -> 5.17 us
  Pallas kernels: 15.4 us -> 16.2 us
    ppermute x4 -> x2, starting transfers between devices: 8.04 us -> 5.11 us  [swapped(): return lax.ppermute(cells, axis, pairs + [(j, i) for i, j in pairs])]
    ppermute x5 -> x6, starting transfers between devices: 6.6 us -> 8.58 us  [shifted(): return lax.ppermute(cells, axis, pairs)]
    ppermute x5 -> x6, waiting for transfers between devices: 3.9 us -> 5.17 us  [shifted(): return lax.ppermute(cells, axis, pairs)]
    pallas_call x2, Pallas kernels: 0.27 us -> 1.06 us  [the longest x1 1.05 us: body(): pl.pallas_call(functools.partial(gather_kernel, ny, tiles), out_shape=(ja...]
  transfers between devices with their start and end apart: 9 -> 8, of which waited for: 3 -> 3; matrix products, arithmetic and copies ran while one was open for 0% -> 0% of each run, Pallas kernels for 3% -> 3%
where the time goes in v9:
time: 51.3 us; the launch traced here: 51.1 us
  Pallas kernels  16.2 us (32%)
  starting transfers between devices  13.7 us (27%)
  blocking collectives  13.4 us (26%)
  waiting for transfers between devices  5.17 us (10%)
  local copies, waits for them, and re-layouts  2.6 us (5%)
    pallas_call x1, Pallas kernels, body(): pl.pallas_call(functools.partial(evolve_kernel, ny, tiles, images), out_s...  13.6 us
    all_to_all x1, blocking collectives, body(): squares = lax.all_to_all(part, ('img', 'gx', 'gy'), 0, 0, tiled=True)  13.4 us
    ppermute x6, starting transfers between devices, shifted(): return lax.ppermute(cells, axis, pairs)  8.58 us
    ppermute x6, waiting for transfers between devices, shifted(): return lax.ppermute(cells, axis, pairs)  5.17 us
    ppermute x2, starting transfers between devices, swapped(): return lax.ppermute(cells, axis, pairs + [(j, i) for i, j in pairs])  5.11 us
    unnamed x16, local copies, waits for them, and re-layouts  2.6 us
    pallas_call x1, Pallas kernels, body(): pl.pallas_call(functools.partial(pack_kernel, ny, tiles, anisotropy.shape...  1.51 us
    pallas_call x1, Pallas kernels, body(): pl.pallas_call(functools.partial(gather_kernel, ny, tiles), out_shape=(ja...  1.05 us
  transfers between devices with their start and end apart: 8, of which 3 were waited for; matrix products, arithmetic and copies ran while one was open for 0% of the time, Pallas kernels for 3%

profile of v9, /device:TPU:0, one launch (start us, length us, event | category | flops | bytes accessed | tf_op | source)
XLA Modules:
  0.0 51.1 jit_solution(17701092156086944286)
XLA Ops:
  0.0 2.9 %collective-permute-start = (f32[3,16,16,128]{3,2,1,0:T(8,128)}, f32[3,16,16,128]{3,2,1,0:T(8,128)S(1)}, u32[]{:S(2)}, u32[]{:S(2)}) collective-permute-start(f32[3,16,16,128]{3,2,1,0:T(8,128)} %bitcast.15), channel_id=1, source_target_pairs={{0,1},{1,0},{2,3},{3,2},{4,5},{5,4},{6,7},{7,6},{8,9},{9,8},{10,11... | collective-permute-start | bytes 1179656 | tf_op jit(solution)/shard_map/ppermute | solution.py:376
  2.9 0.7 %collective-permute-start.3 = (f32[3,16,16,128]{3,2,1,0:T(8,128)}, f32[3,16,16,128]{3,2,1,0:T(8,128)S(1)}, u32[]{:S(2)}, u32[]{:S(2)}) collective-permute-start(f32[3,16,16,128]{3,2,1,0:T(8,128)} %bitcast.16), channel_id=1, source_target_pairs={{8,16},{16,8},{9,17},{17,9},{10,18},{18,10},{11,19},{19,11},{12,20... | collective-permute-start | bytes 1179656 | tf_op jit(solution)/shard_map/ppermute | solution.py:382
  3.6 4.4 %collective-permute-start.2 = (f32[3,16,16,128]{3,2,1,0:T(8,128)}, f32[3,16,16,128]{3,2,1,0:T(8,128)S(1)}, u32[]{:S(2)}, u32[]{:S(2)}) collective-permute-start(f32[3,16,16,128]{3,2,1,0:T(8,128)} %bitcast.17), channel_id=1, source_target_pairs={{0,8},{16,24},{8,0},{24,16},{1,9},{17,25},{9,1},{25,17},{2,10},{18... | collective-permute-start | bytes 1179656 | tf_op jit(solution)/shard_map/ppermute | solution.py:382
  8.1 0.0 copy-start.7
  8.1 0.0 copy-start.4
  8.1 0.0 copy-start.5
  8.1 0.0 copy-start.6
  8.1 0.6 %copy-done.7 = f32[3]{0:T(128)S(1)} copy-done((f32[3]{0:T(128)S(1)}, f32[3]{0:T(128)}, u32[]{:S(2)}) %copy-start.7) | copy-done | bytes 36
  8.7 0.0 copy-done.4
  8.7 0.0 copy-done.5
  8.7 0.0 copy-done.6
  8.8 0.0 copy-start
  8.8 1.0 %copy-done = f32[1,3,16,16,128]{4,3,2,1,0:T(8,128)S(1)} copy-done((f32[1,3,16,16,128]{4,3,2,1,0:T(8,128)S(1)}, f32[1,3,16,16,128]{4,3,2,1,0:T(8,128)}, u32[]{:S(2)}) %copy-start) | copy-done | bytes 393240
  9.8 0.0 copy-start.2
  9.8 0.9 %copy-done.2 = s32[16,16,128]{2,1,0:T(8,128)S(1)} copy-done((s32[16,16,128]{2,1,0:T(8,128)S(1)}, s32[16,16,128]{2,1,0:T(8,128)}, u32[]{:S(2)}) %copy-start.2) | copy-done | bytes 131096
  10.7 0.0 copy-start.1
  10.7 1.5 %pack_strips.1 = (f32[4,2,8,128]{3,2,1,0:T(8,128)S(1)}, f32[4,2,8,128]{3,2,1,0:T(8,128)S(1)}, f32[5,8,128]{2,1,0:T(8,128)S(1)}) custom-call(s32[4]{0:T(128)S(1)} %copy-done.4, f32[8]{0:T(128)S(1)} %copy-done.5, f32[8]{0:T(128)S(1)} %copy-done.6, f32[1,3]{1,0:T(1,128)S(1)} %bitcast.31, f32[3,256,128]{2,1,0:T(8,128)S(1)} %bitcast.18, s32[256,128]{1,0:T(8,128)S(1)} %bitcast.21), custom_call_target="tpu_custom_call" | custom-call | tf_op jit(solution)/shard_map/pack_strips/pallas_call | solution.py:422
  12.2 0.1 collective-permute-done
  12.3 1.7 %collective-permute-start.1 = (s32[16,16,128]{2,1,0:T(8,128)S(1)}, s32[16,16,128]{2,1,0:T(8,128)S(1)}, u32[]{:S(2)}, u32[]{:S(2)}) collective-permute-start(s32[16,16,128]{2,1,0:T(8,128)S(1)} %copy-done.2), channel_id=1, source_target_pairs={{0,1},{1,0},{2,3},{3,2},{4,5},{5,4},{6,7},{7,6},{8,9},{9,8},{10,11... | collective-permute-start | bytes 393224 | tf_op jit(solution)/shard_map/ppermute | solution.py:376
  14.0 3.2 %collective-permute-done.1 = s32[16,16,128]{2,1,0:T(8,128)S(1)} collective-permute-done((s32[16,16,128]{2,1,0:T(8,128)S(1)}, s32[16,16,128]{2,1,0:T(8,128)S(1)}, u32[]{:S(2)}, u32[]{:S(2)}) %collective-permute-start.1) | collective-permute-done | bytes 131104 | tf_op jit(solution)/shard_map/ppermute | solution.py:376
  17.2 0.0 collective-permute-done.3
  17.2 0.0 collective-permute-done.2
  17.2 0.0 copy-done.1
  17.2 1.1 %gather_images.1 = (f32[32,128]{1,0:T(8,128)S(1)}, f32[3,256,128]{2,1,0:T(8,128)S(1)}, f32[7,2,8,128]{3,2,1,0:T(8,128)S(1)}, f32[7,2,8,128]{3,2,1,0:T(8,128)S(1)}) custom-call(f32[5,8,128]{2,1,0:T(8,128)S(1)} %get-tuple-element.20.info_ref, f32[3,256,128]{2,1,0:T(8,128)S(1)} %bitcast.19, f32[3,256,128]{2,1,0:T(8,128)S(1)} %bitcast.27, ...), custom_call_target="tpu_custom_call" | custom-call | tf_op jit(solution)/shard_map/gather_images/pallas_call | solution.py:441
  18.3 1.8 %collective-permute-start.4 = (f32[3,16,16,128]{3,2,1,0:T(8,128)S(1)}, f32[3,16,16,128]{3,2,1,0:T(8,128)S(1)}, u32[]{:S(2)}, u32[]{:S(2)}) collective-permute-start(f32[3,16,16,128]{3,2,1,0:T(8,128)S(1)} %bitcast.24), channel_id=1, source_target_pairs={{0,1},{1,0},{2,3},{3,2},{4,5},{5,4},{6,7},{7,6},{8,9},{9,8},{10,11... | collective-permute-start | bytes 1179656 | tf_op jit(solution)/shard_map/ppermute | solution.py:376
  20.1 0.0 collective-permute-start.5
  20.1 0.0 copy-start.3
  20.1 1.7 %collective-permute-start.6 = (f32[7,2,8,128]{3,2,1,0:T(8,128)S(1)}, f32[7,2,8,128]{3,2,1,0:T(8,128)S(1)}, u32[]{:S(2)}, u32[]{:S(2)}) collective-permute-start(f32[7,2,8,128]{3,2,1,0:T(8,128)S(1)} %get-tuple-element.28), channel_id=1, source_target_pairs={{0,6},{2,0},{4,2},{6,4},{1,7},{3,1},{5,3},{7,5},{8,14},{10,8},{12,... | collective-permute-start | bytes 172040 | tf_op jit(solution)/shard_map/ppermute | solution.py:376
  21.9 1.9 %collective-permute-done.5.left_ref = f32[7,2,8,128]{3,2,1,0:T(8,128)S(1)} collective-permute-done((f32[7,2,8,128]{3,2,1,0:T(8,128)S(1)}, f32[7,2,8,128]{3,2,1,0:T(8,128)S(1)}, u32[]{:S(2)}, u32[]{:S(2)}) %collective-permute-start.5) | collective-permute-done | bytes 57376 | tf_op jit(solution)/shard_map/ppermute | solution.py:376
  23.7 0.0 collective-permute-done.6.right_ref
  23.7 0.3 collective-permute-start.7
  24.1 13.4 %all_to_all.11 = f32[32,1,128]{2,1,0:T(1,128)S(1)} all-to-all(f32[32,1,128]{2,1,0:T(1,128)S(1)} %bitcast.30), channel_id=1, replica_groups=mesh['img'=4,'gx'=4,'gy'=2] {'img','gx','gy'}, dimensions={0} | all-to-all | bytes 32768 | tf_op jit(solution)/shard_map/all_to_all | solution.py:466
  37.5 0.0 collective-permute-done.7.stripsp_ref
  37.5 0.0 collective-permute-done.4
  37.5 0.0 copy-done.3
  37.5 13.6 %evolve.1 = f32[3,256,128]{2,1,0:T(8,128)} custom-call(f32[5,8,128]{2,1,0:T(8,128)S(1)} %get-tuple-element.20.info_ref, f32[32,128]{1,0:T(8,128)S(1)} %bitcast.29, f32[3,256,128]{2,1,0:T(8,128)S(1)} %bitcast.20, f32[3,256,128]{2,1,0:T(8,128)S(1)} %bitcast.23, f32[3,256,128]{2,1,0:T(8,128)S(1)} %get-tuple-element.25.n_ref, f32[3,256,128]{2,1,0:T(8,128)S(1)} %bitcast.25, ...), custom_call_target="tpu_custom_call" | custom-call | tf_op jit(solution)/shard_map/evolve/pallas_call | solution.py:469
  (1 shorter events, 0.0 us)
Async XLA Ops:
  0.0 12.3 %collective-permute-start = (f32[3,16,16,128]{3,2,1,0:T(8,128)}, f32[3,16,16,128]{3,2,1,0:T(8,128)S(1)}, u32[]{:S(2)}, u32[]{:S(2)}) collective-permute-start(f32[3,16,16,128]{3,2,1,0:T(8,128)} %bitcast.15), channel_id=1, source_target_pairs={{0,1},{1,0},{2,3},{3,2},{4,5},{5,4},{6,7},{7,6},{8,9},{9,8},{10,11... | collective-permute-start | bytes 1179656 | tf_op jit(solution)/shard_map/ppermute | solution.py:376
  2.9 14.3 %collective-permute-start.3 = (f32[3,16,16,128]{3,2,1,0:T(8,128)}, f32[3,16,16,128]{3,2,1,0:T(8,128)S(1)}, u32[]{:S(2)}, u32[]{:S(2)}) collective-permute-start(f32[3,16,16,128]{3,2,1,0:T(8,128)} %bitcast.16), channel_id=1, source_target_pairs={{8,16},{16,8},{9,17},{17,9},{10,18},{18,10},{11,19},{19,11},{12,20... | collective-permute-start | bytes 1179656 | tf_op jit(solution)/shard_map/ppermute | solution.py:382
  3.6 13.6 %collective-permute-start.2 = (f32[3,16,16,128]{3,2,1,0:T(8,128)}, f32[3,16,16,128]{3,2,1,0:T(8,128)S(1)}, u32[]{:S(2)}, u32[]{:S(2)}) collective-permute-start(f32[3,16,16,128]{3,2,1,0:T(8,128)} %bitcast.17), channel_id=1, source_target_pairs={{0,8},{16,24},{8,0},{24,16},{1,9},{17,25},{9,1},{25,17},{2,10},{18... | collective-permute-start | bytes 1179656 | tf_op jit(solution)/shard_map/ppermute | solution.py:382
  8.1 0.7 %copy-start.7 = (f32[3]{0:T(128)S(1)}, f32[3]{0:T(128)}, u32[]{:S(2)}) copy-start(f32[3]{0:T(128)} %param.8) | copy-start | bytes 40
  8.1 0.7 %copy-start.4 = (s32[4]{0:T(128)S(1)}, s32[4]{0:T(128)}, u32[]{:S(2)}) copy-start(s32[4]{0:T(128)} %lower_ref.1) | copy-start | bytes 52
  8.1 0.7 %copy-start.5 = (f32[8]{0:T(128)S(1)}, f32[8]{0:T(128)}, u32[]{:S(2)}) copy-start(f32[8]{0:T(128)} %aniso_ref.1) | copy-start | bytes 100
  8.1 0.7 %copy-start.6 = (f32[8]{0:T(128)S(1)}, f32[8]{0:T(128)}, u32[]{:S(2)}) copy-start(f32[8]{0:T(128)} %damp_ref.1) | copy-start | bytes 100
  8.8 1.0 %copy-start = (f32[1,3,16,16,128]{4,3,2,1,0:T(8,128)S(1)}, f32[1,3,16,16,128]{4,3,2,1,0:T(8,128)}, u32[]{:S(2)}) copy-start(f32[1,3,16,16,128]{4,3,2,1,0:T(8,128)} %param.6) | copy-start | bytes 1179652
  9.8 0.9 %copy-start.2 = (s32[16,16,128]{2,1,0:T(8,128)S(1)}, s32[16,16,128]{2,1,0:T(8,128)}, u32[]{:S(2)}) copy-start(s32[16,16,128]{2,1,0:T(8,128)} %param.9) | copy-start | bytes 393220
  10.7 6.6 %copy-start.1 = (f32[1,3,16,16,128]{4,3,2,1,0:T(8,128)S(1)}, f32[1,3,16,16,128]{4,3,2,1,0:T(8,128)}, u32[]{:S(2)}) copy-start(f32[1,3,16,16,128]{4,3,2,1,0:T(8,128)} %param.6) | copy-start | bytes 1179652
  12.3 5.0 %collective-permute-start.1 = (s32[16,16,128]{2,1,0:T(8,128)S(1)}, s32[16,16,128]{2,1,0:T(8,128)S(1)}, u32[]{:S(2)}, u32[]{:S(2)}) collective-permute-start(s32[16,16,128]{2,1,0:T(8,128)S(1)} %copy-done.2), channel_id=1, source_target_pairs={{0,1},{1,0},{2,3},{3,2},{4,5},{5,4},{6,7},{7,6},{8,9},{9,8},{10,11... | collective-permute-start | bytes 393224 | tf_op jit(solution)/shard_map/ppermute | solution.py:376
  18.3 19.2 %collective-permute-start.4 = (f32[3,16,16,128]{3,2,1,0:T(8,128)S(1)}, f32[3,16,16,128]{3,2,1,0:T(8,128)S(1)}, u32[]{:S(2)}, u32[]{:S(2)}) collective-permute-start(f32[3,16,16,128]{3,2,1,0:T(8,128)S(1)} %bitcast.24), channel_id=1, source_target_pairs={{0,1},{1,0},{2,3},{3,2},{4,5},{5,4},{6,7},{7,6},{8,9},{9,8},{10,11... | collective-permute-start | bytes 1179656 | tf_op jit(solution)/shard_map/ppermute | solution.py:376
  20.1 3.6 %collective-permute-start.5 = (f32[7,2,8,128]{3,2,1,0:T(8,128)S(1)}, f32[7,2,8,128]{3,2,1,0:T(8,128)S(1)}, u32[]{:S(2)}, u32[]{:S(2)}) collective-permute-start(f32[7,2,8,128]{3,2,1,0:T(8,128)S(1)} %get-tuple-element.27), channel_id=1, source_target_pairs={{0,2},{2,4},{4,6},{6,0},{1,3},{3,5},{5,7},{7,1},{8,10},{10,12},{12... | collective-permute-start | bytes 172040 | tf_op jit(solution)/shard_map/ppermute | solution.py:376
  20.1 17.4 %copy-start.3 = (s32[16,16,128]{2,1,0:T(8,128)S(1)}, s32[16,16,128]{2,1,0:T(8,128)}, u32[]{:S(2)}) copy-start(s32[16,16,128]{2,1,0:T(8,128)} %param.9) | copy-start | bytes 393220
  20.1 3.6 %collective-permute-start.6 = (f32[7,2,8,128]{3,2,1,0:T(8,128)S(1)}, f32[7,2,8,128]{3,2,1,0:T(8,128)S(1)}, u32[]{:S(2)}, u32[]{:S(2)}) collective-permute-start(f32[7,2,8,128]{3,2,1,0:T(8,128)S(1)} %get-tuple-element.28), channel_id=1, source_target_pairs={{0,6},{2,0},{4,2},{6,4},{1,7},{3,1},{5,3},{7,5},{8,14},{10,8},{12,... | collective-permute-start | bytes 172040 | tf_op jit(solution)/shard_map/ppermute | solution.py:376
  23.7 13.7 %collective-permute-start.7 = (f32[2,7,2,8,128]{4,3,2,1,0:T(8,128)S(1)}, f32[2,7,2,8,128]{4,3,2,1,0:T(8,128)S(1)}, u32[]{:S(2)}, u32[]{:S(2)}) collective-permute-start(f32[2,7,2,8,128]{4,3,2,1,0:T(8,128)S(1)} %merge_strips.1.strips_ref), channel_id=1, source_target_pairs={{0,1},{1,0},{2,3},{3,2},{4,5},{5,4},{6,7},{7,6},{8,9},{9,8},{10,11... | collective-permute-start | bytes 344072 | tf_op jit(solution)/shard_map/ppermute | solution.py:376

commit v10 on v9

--- a/solution.py
+++ b/solution.py
@@ -73,9 +73,11 @@
     lax.fori_loop(0, ny // 2, pack, 0)
 
 
-def merge_kernel(left_ref, right_ref, out_ref):
-    out_ref[0] = left_ref[...]
-    out_ref[1] = right_ref[...]
+def merge_kernel(one_ref, two_ref, out_ref):
+    turned = (lax.axis_index("gx") & 1) == 1
+    one, two = one_ref[...], two_ref[...]
+    out_ref[0] = jnp.where(turned, one, two)
+    out_ref[1] = jnp.where(turned, two, one)
 
 
 def take_first(info_ref, here):
@@ -85,7 +87,7 @@
 
 
 def gather_kernel(
-    ny, tiles, info_ref, m_ref, first_ref, second_ref, own_left_ref, own_right_ref, part_ref, near_ref, left_ref, right_ref
+    ny, tiles, info_ref, m_ref, first_ref, second_ref, own_left_ref, own_right_ref, part_ref, near_ref, one_ref, two_ref
 ):
     here = lax.axis_index("img")
     pick, odd = take_first(info_ref, here)
@@ -112,24 +114,26 @@
     total = jnp.sum(functools.reduce(jnp.add, sums), axis=(0, 1), keepdims=True)
     slot = lax.broadcasted_iota(jnp.int32, part_ref.shape, 1)
     part_ref[...] = jnp.where((slot == here) & (here > 0), total, 0.0)
-    left_ref[COMPS:] = own_left_ref[...]
-    right_ref[COMPS:] = own_right_ref[...]
+    turned = (lax.axis_index("gx") & 1) == 1
+    one_ref[COMPS:] = jnp.where(turned, own_left_ref[...], own_right_ref[...])
+    two_ref[COMPS:] = jnp.where(turned, own_right_ref[...], own_left_ref[...])
     block = lane_iota() // DEPTH
 
     def pack(i, carry):
         done = []
         for u in range(2):
             y = 2 * i + u
-            left = block == ((y + 1) & (ny - 1))
-            right = block == y
+            after = (y + 1) & (ny - 1)
+            one = block == jnp.where(turned, after, y)
+            two = block == jnp.where(turned, y, after)
             shift = (DEPTH * (y + 1)) & (LANES - 1)
             for t in range(tiles):
                 for c in range(COMPS):
                     cells = pltpu.roll(near_ref[c, rows_at(ny, tiles, y, t), :], shift, 1)
-                    done.append((c, t, left, right, cells))
-        for c, t, left, right, cells in done:
-            pltpu.store(left_ref.at[c, t], cells, mask=left)
-            pltpu.store(right_ref.at[c, t], cells, mask=right)
+                    done.append((c, t, one, two, cells))
+        for c, t, one, two, cells in done:
+            pltpu.store(one_ref.at[c, t], cells, mask=one)
+            pltpu.store(two_ref.at[c, t], cells, mask=two)
         return carry
 
     lax.fori_loop(0, ny // 2, pack, 0)
@@ -376,9 +380,9 @@
     return lax.ppermute(cells, axis, pairs)
 
 
-def swapped(cells, axis, first):
+def swapped(cells, axis, first, closed):
     count = lax.axis_size(axis)
-    pairs = [(i, i + 1) for i in range(first, count - 1, 2)]
+    pairs = [(i, (i + 1) % count) for i in range(first, count if closed else count - 1, 2)]
     return lax.ppermute(cells, axis, pairs + [(j, i) for i, j in pairs])
 
 
@@ -405,13 +409,14 @@
     images = local * lax.axis_size("img")
     tiles = nz // SUB
     devices = lax.axis_size(("img", "gx", "gy"))
+    assert lax.axis_size("gx") % 2 == 0
     assert local == 1 and comps == COMPS and nx == LANES
     assert ny == 2 * DEPTH and ny * DEPTH == LANES and tiles >= 2
     flat = (comps, nz * ny, nx)
     own = magnetization[0]
     own_p = around(own, 2)
-    first = swapped(own, "img", 0)
-    second = swapped(own, "img", 1)
+    first = swapped(own, "img", 0, False)
+    second = swapped(own, "img", 1, False)
 
     smem = pl.BlockSpec(memory_space=pltpu.SMEM)
     vmem = pl.BlockSpec(memory_space=pltpu.VMEM)
@@ -434,11 +439,11 @@
         own.reshape(flat),
         regions.reshape(flat[1:]),
     )
-    late_regions, own_p, info = lax.optimization_barrier((regions, own_p, info))
+    late_regions, info = lax.optimization_barrier((regions, info))
     reg_p = around(late_regions, 1)
-    info, reg_p = lax.optimization_barrier((info, reg_p))
+    info, own_p, reg_p = lax.optimization_barrier((info, own_p, reg_p))
     packed = jax.ShapeDtypeStruct((2 * comps + 1, tiles) + vreg, f32)
-    part, near, left, right = pl.pallas_call(
+    part, near, one, two = pl.pallas_call(
         functools.partial(gather_kernel, ny, tiles),
         out_shape=(
             jax.ShapeDtypeStruct((devices, LANES), f32),
@@ -452,8 +457,8 @@
         name="gather_images",
     )(info, own.reshape(flat), first.reshape(flat), second.reshape(flat), left, right)
     near_p = around(near.reshape(own.shape), 2)
-    strip_l = shifted(right, "gx", 1, True)
-    strip_r = shifted(left, "gx", -1, True)
+    one = swapped(one, "gx", 0, True)
+    two = swapped(two, "gx", 1, True)
     strips = pl.pallas_call(
         merge_kernel,
         out_shape=jax.ShapeDtypeStruct((2,) + packed.shape, f32),
@@ -461,7 +466,7 @@
         out_specs=vmem,
         compiler_params=limit,
         name="merge_strips",
-    )(strip_l, strip_r)
+    )(one, two)
     strips_p = around_strips(strips)
     squares = lax.all_to_all(part, ("img", "gx", "gy"), 0, 0, tiled=True)
 

time: 51.3 us -> 49 us (0.955)
  blocking collectives: 13.4 us -> 11.1 us
  starting transfers between devices: 13.7 us -> 12.4 us
  waiting for transfers between devices: 5.17 us -> 6.42 us
    ppermute x6 -> x4, starting transfers between devices: 8.58 us -> 5.69 us  [shifted(): return lax.ppermute(cells, axis, pairs)]
    all_to_all x1, blocking collectives: 13.4 us -> 11.1 us  [body(): squares = lax.all_to_all(part, ('img', 'gx', 'gy'), 0, 0, tiled=True)]
    ppermute x2 -> x4, waiting for transfers between devices: 0.01 us -> 1.98 us  [swapped(): return lax.ppermute(cells, axis, pairs + [(j, i) for i, j in pairs])]
    ppermute x2 -> x4, starting transfers between devices: 5.11 us -> 6.75 us  [swapped(): return lax.ppermute(cells, axis, pairs + [(j, i) for i, j in pairs])]
    ppermute x6 -> x4, waiting for transfers between devices: 5.17 us -> 4.44 us  [shifted(): return lax.ppermute(cells, axis, pairs)]
  transfers between devices with their start and end apart: 8 -> 8, of which waited for: 3 -> 2; matrix products, arithmetic and copies ran while one was open for 0% -> 0% of each run, Pallas kernels for 3% -> 3%
where the time goes in v10:
time: 49 us; the launch traced here: 48.8 us
  Pallas kernels  16.2 us (33%)
  starting transfers between devices  12.4 us (25%)
  blocking collectives  11.1 us (23%)
  waiting for transfers between devices  6.42 us (13%)
  local copies, waits for them, and re-layouts  2.6 us (5%)
    pallas_call x1, Pallas kernels, body(): pl.pallas_call(functools.partial(evolve_kernel, ny, tiles, images), out_s...  13.6 us
    all_to_all x1, blocking collectives, body(): squares = lax.all_to_all(part, ('img', 'gx', 'gy'), 0, 0, tiled=True)  11.1 us
    ppermute x4, starting transfers between devices, swapped(): return lax.ppermute(cells, axis, pairs + [(j, i) for i, j in pairs])  6.75 us
    ppermute x4, starting transfers between devices, shifted(): return lax.ppermute(cells, axis, pairs)  5.69 us
    ppermute x4, waiting for transfers between devices, shifted(): return lax.ppermute(cells, axis, pairs)  4.44 us
    unnamed x16, local copies, waits for them, and re-layouts  2.6 us
    ppermute x4, waiting for transfers between devices, swapped(): return lax.ppermute(cells, axis, pairs + [(j, i) for i, j in pairs])  1.98 us
    pallas_call x1, Pallas kernels, body(): pl.pallas_call(functools.partial(pack_kernel, ny, tiles, anisotropy.shape...  1.51 us
  transfers between devices with their start and end apart: 8, of which 2 were waited for; matrix products, arithmetic and copies ran while one was open for 0% of the time, Pallas kernels for 3%

profile of v10, /device:TPU:0, one launch (start us, length us, event | category | flops | bytes accessed | tf_op | source)
XLA Modules:
  0.0 48.8 jit_solution(14713403511791511966)
XLA Ops:
  0.0 2.9 %collective-permute-start = (f32[3,16,16,128]{3,2,1,0:T(8,128)}, f32[3,16,16,128]{3,2,1,0:T(8,128)S(1)}, u32[]{:S(2)}, u32[]{:S(2)}) collective-permute-start(f32[3,16,16,128]{3,2,1,0:T(8,128)} %bitcast.15), channel_id=1, source_target_pairs={{0,1},{1,0},{2,3},{3,2},{4,5},{5,4},{6,7},{7,6},{8,9},{9,8},{10,11... | collective-permute-start | bytes 1179656 | tf_op jit(solution)/shard_map/ppermute | solution.py:380
  2.9 0.7 %collective-permute-start.3 = (f32[3,16,16,128]{3,2,1,0:T(8,128)}, f32[3,16,16,128]{3,2,1,0:T(8,128)S(1)}, u32[]{:S(2)}, u32[]{:S(2)}) collective-permute-start(f32[3,16,16,128]{3,2,1,0:T(8,128)} %bitcast.16), channel_id=1, source_target_pairs={{8,16},{16,8},{9,17},{17,9},{10,18},{18,10},{11,19},{19,11},{12,20... | collective-permute-start | bytes 1179656 | tf_op jit(solution)/shard_map/ppermute | solution.py:386
  3.6 4.4 %collective-permute-start.2 = (f32[3,16,16,128]{3,2,1,0:T(8,128)}, f32[3,16,16,128]{3,2,1,0:T(8,128)S(1)}, u32[]{:S(2)}, u32[]{:S(2)}) collective-permute-start(f32[3,16,16,128]{3,2,1,0:T(8,128)} %bitcast.17), channel_id=1, source_target_pairs={{0,8},{16,24},{8,0},{24,16},{1,9},{17,25},{9,1},{25,17},{2,10},{18... | collective-permute-start | bytes 1179656 | tf_op jit(solution)/shard_map/ppermute | solution.py:386
  8.1 0.0 copy-start.7
  8.1 0.0 copy-start.4
  8.1 0.0 copy-start.5
  8.1 0.0 copy-start.6
  8.1 0.6 %copy-done.7 = f32[3]{0:T(128)S(1)} copy-done((f32[3]{0:T(128)S(1)}, f32[3]{0:T(128)}, u32[]{:S(2)}) %copy-start.7) | copy-done | bytes 36
  8.7 0.0 copy-done.4
  8.7 0.0 copy-done.5
  8.7 0.0 copy-done.6
  8.8 0.0 copy-start
  8.8 1.0 %copy-done = f32[1,3,16,16,128]{4,3,2,1,0:T(8,128)S(1)} copy-done((f32[1,3,16,16,128]{4,3,2,1,0:T(8,128)S(1)}, f32[1,3,16,16,128]{4,3,2,1,0:T(8,128)}, u32[]{:S(2)}) %copy-start) | copy-done | bytes 393240
  9.8 0.0 copy-start.2
  9.8 0.9 %copy-done.2 = s32[16,16,128]{2,1,0:T(8,128)S(1)} copy-done((s32[16,16,128]{2,1,0:T(8,128)S(1)}, s32[16,16,128]{2,1,0:T(8,128)}, u32[]{:S(2)}) %copy-start.2) | copy-done | bytes 131096
  10.7 0.0 copy-start.1
  10.7 1.5 %pack_strips.1 = (f32[4,2,8,128]{3,2,1,0:T(8,128)S(1)}, f32[4,2,8,128]{3,2,1,0:T(8,128)S(1)}, f32[5,8,128]{2,1,0:T(8,128)S(1)}) custom-call(s32[4]{0:T(128)S(1)} %copy-done.4, f32[8]{0:T(128)S(1)} %copy-done.5, f32[8]{0:T(128)S(1)} %copy-done.6, f32[1,3]{1,0:T(1,128)S(1)} %bitcast.31, f32[3,256,128]{2,1,0:T(8,128)S(1)} %bitcast.18, s32[256,128]{1,0:T(8,128)S(1)} %bitcast.21), custom_call_target="tpu_custom_call" | custom-call | tf_op jit(solution)/shard_map/pack_strips/pallas_call | solution.py:427
  12.2 0.6 %collective-permute-start.1 = (s32[16,16,128]{2,1,0:T(8,128)S(1)}, s32[16,16,128]{2,1,0:T(8,128)S(1)}, u32[]{:S(2)}, u32[]{:S(2)}) collective-permute-start(s32[16,16,128]{2,1,0:T(8,128)S(1)} %copy-done.2), channel_id=1, source_target_pairs={{0,1},{1,0},{2,3},{3,2},{4,5},{5,4},{6,7},{7,6},{8,9},{9,8},{10,11... | collective-permute-start | bytes 393224 | tf_op jit(solution)/shard_map/ppermute | solution.py:380
  12.8 4.4 %collective-permute-done.1 = s32[16,16,128]{2,1,0:T(8,128)S(1)} collective-permute-done((s32[16,16,128]{2,1,0:T(8,128)S(1)}, s32[16,16,128]{2,1,0:T(8,128)S(1)}, u32[]{:S(2)}, u32[]{:S(2)}) %collective-permute-start.1) | collective-permute-done | bytes 131104 | tf_op jit(solution)/shard_map/ppermute | solution.py:380
  17.2 0.0 collective-permute-done
  17.2 0.0 collective-permute-done.3
  17.2 0.0 collective-permute-done.2
  17.2 0.0 copy-done.1
  17.2 1.1 %gather_images.1 = (f32[32,128]{1,0:T(8,128)S(1)}, f32[3,256,128]{2,1,0:T(8,128)S(1)}, f32[7,2,8,128]{3,2,1,0:T(8,128)S(1)}, f32[7,2,8,128]{3,2,1,0:T(8,128)S(1)}) custom-call(f32[5,8,128]{2,1,0:T(8,128)S(1)} %get-tuple-element.20.info_ref, f32[3,256,128]{2,1,0:T(8,128)S(1)} %bitcast.19, f32[3,256,128]{2,1,0:T(8,128)S(1)} %bitcast.27, ...), custom_call_target="tpu_custom_call" | custom-call | tf_op jit(solution)/shard_map/gather_images/pallas_call | solution.py:446
  18.3 0.6 %collective-permute-start.4 = (f32[3,16,16,128]{3,2,1,0:T(8,128)S(1)}, f32[3,16,16,128]{3,2,1,0:T(8,128)S(1)}, u32[]{:S(2)}, u32[]{:S(2)}) collective-permute-start(f32[3,16,16,128]{3,2,1,0:T(8,128)S(1)} %bitcast.24), channel_id=1, source_target_pairs={{0,1},{1,0},{2,3},{3,2},{4,5},{5,4},{6,7},{7,6},{8,9},{9,8},{10,11... | collective-permute-start | bytes 1179656 | tf_op jit(solution)/shard_map/ppermute | solution.py:380
  18.9 0.0 collective-permute-start.5
  18.9 0.0 copy-start.3
  18.9 1.6 %collective-permute-start.6 = (f32[7,2,8,128]{3,2,1,0:T(8,128)S(1)}, f32[7,2,8,128]{3,2,1,0:T(8,128)S(1)}, u32[]{:S(2)}, u32[]{:S(2)}) collective-permute-start(f32[7,2,8,128]{3,2,1,0:T(8,128)S(1)} %get-tuple-element.28), channel_id=1, source_target_pairs={{2,4},{6,0},{4,2},{0,6},{3,5},{7,1},{5,3},{1,7},{10,12},{14,8},{12... | collective-permute-start | bytes 172040 | tf_op jit(solution)/shard_map/ppermute | solution.py:386
  20.5 0.0 collective-permute-done.5.one_ref
  20.5 2.0 %collective-permute-done.6.two_ref = f32[7,2,8,128]{3,2,1,0:T(8,128)S(1)} collective-permute-done((f32[7,2,8,128]{3,2,1,0:T(8,128)S(1)}, f32[7,2,8,128]{3,2,1,0:T(8,128)S(1)}, u32[]{:S(2)}, u32[]{:S(2)}) %collective-permute-start.6) | collective-permute-done | bytes 57376 | tf_op jit(solution)/shard_map/ppermute | solution.py:386
  22.5 1.6 %collective-permute-start.7 = (f32[2,7,2,8,128]{4,3,2,1,0:T(8,128)S(1)}, f32[2,7,2,8,128]{4,3,2,1,0:T(8,128)S(1)}, u32[]{:S(2)}, u32[]{:S(2)}) collective-permute-start(f32[2,7,2,8,128]{4,3,2,1,0:T(8,128)S(1)} %merge_strips.1.strips_ref), channel_id=1, source_target_pairs={{0,1},{1,0},{2,3},{3,2},{4,5},{5,4},{6,7},{7,6},{8,9},{9,8},{10,11... | collective-permute-start | bytes 344072 | tf_op jit(solution)/shard_map/ppermute | solution.py:380
  24.1 11.1 %all_to_all.11 = f32[32,1,128]{2,1,0:T(1,128)S(1)} all-to-all(f32[32,1,128]{2,1,0:T(1,128)S(1)} %bitcast.30), channel_id=1, replica_groups=mesh['img'=4,'gx'=4,'gy'=2] {'img','gx','gy'}, dimensions={0} | all-to-all | bytes 32768 | tf_op jit(solution)/shard_map/all_to_all | solution.py:471
  35.2 0.0 collective-permute-done.7.stripsp_ref
  35.2 0.0 collective-permute-done.4
  35.2 0.0 copy-done.3
  35.2 13.6 %evolve.1 = f32[3,256,128]{2,1,0:T(8,128)} custom-call(f32[5,8,128]{2,1,0:T(8,128)S(1)} %get-tuple-element.20.info_ref, f32[32,128]{1,0:T(8,128)S(1)} %bitcast.29, f32[3,256,128]{2,1,0:T(8,128)S(1)} %bitcast.20, f32[3,256,128]{2,1,0:T(8,128)S(1)} %bitcast.23, f32[3,256,128]{2,1,0:T(8,128)S(1)} %get-tuple-element.25.n_ref, f32[3,256,128]{2,1,0:T(8,128)S(1)} %bitcast.25, ...), custom_call_target="tpu_custom_call" | custom-call | tf_op jit(solution)/shard_map/evolve/pallas_call | solution.py:474
  (1 shorter events, 0.0 us)
Async XLA Ops:
  0.0 17.2 %collective-permute-start = (f32[3,16,16,128]{3,2,1,0:T(8,128)}, f32[3,16,16,128]{3,2,1,0:T(8,128)S(1)}, u32[]{:S(2)}, u32[]{:S(2)}) collective-permute-start(f32[3,16,16,128]{3,2,1,0:T(8,128)} %bitcast.15), channel_id=1, source_target_pairs={{0,1},{1,0},{2,3},{3,2},{4,5},{5,4},{6,7},{7,6},{8,9},{9,8},{10,11... | collective-permute-start | bytes 1179656 | tf_op jit(solution)/shard_map/ppermute | solution.py:380
  2.9 14.3 %collective-permute-start.3 = (f32[3,16,16,128]{3,2,1,0:T(8,128)}, f32[3,16,16,128]{3,2,1,0:T(8,128)S(1)}, u32[]{:S(2)}, u32[]{:S(2)}) collective-permute-start(f32[3,16,16,128]{3,2,1,0:T(8,128)} %bitcast.16), channel_id=1, source_target_pairs={{8,16},{16,8},{9,17},{17,9},{10,18},{18,10},{11,19},{19,11},{12,20... | collective-permute-start | bytes 1179656 | tf_op jit(solution)/shard_map/ppermute | solution.py:386
  3.6 13.6 %collective-permute-start.2 = (f32[3,16,16,128]{3,2,1,0:T(8,128)}, f32[3,16,16,128]{3,2,1,0:T(8,128)S(1)}, u32[]{:S(2)}, u32[]{:S(2)}) collective-permute-start(f32[3,16,16,128]{3,2,1,0:T(8,128)} %bitcast.17), channel_id=1, source_target_pairs={{0,8},{16,24},{8,0},{24,16},{1,9},{17,25},{9,1},{25,17},{2,10},{18... | collective-permute-start | bytes 1179656 | tf_op jit(solution)/shard_map/ppermute | solution.py:386
  8.1 0.7 %copy-start.7 = (f32[3]{0:T(128)S(1)}, f32[3]{0:T(128)}, u32[]{:S(2)}) copy-start(f32[3]{0:T(128)} %param.8) | copy-start | bytes 40
  8.1 0.7 %copy-start.4 = (s32[4]{0:T(128)S(1)}, s32[4]{0:T(128)}, u32[]{:S(2)}) copy-start(s32[4]{0:T(128)} %lower_ref.1) | copy-start | bytes 52
  8.1 0.7 %copy-start.5 = (f32[8]{0:T(128)S(1)}, f32[8]{0:T(128)}, u32[]{:S(2)}) copy-start(f32[8]{0:T(128)} %aniso_ref.1) | copy-start | bytes 100
  8.1 0.7 %copy-start.6 = (f32[8]{0:T(128)S(1)}, f32[8]{0:T(128)}, u32[]{:S(2)}) copy-start(f32[8]{0:T(128)} %damp_ref.1) | copy-start | bytes 100
  8.8 1.0 %copy-start = (f32[1,3,16,16,128]{4,3,2,1,0:T(8,128)S(1)}, f32[1,3,16,16,128]{4,3,2,1,0:T(8,128)}, u32[]{:S(2)}) copy-start(f32[1,3,16,16,128]{4,3,2,1,0:T(8,128)} %param.6) | copy-start | bytes 1179652
  9.8 0.9 %copy-start.2 = (s32[16,16,128]{2,1,0:T(8,128)S(1)}, s32[16,16,128]{2,1,0:T(8,128)}, u32[]{:S(2)}) copy-start(s32[16,16,128]{2,1,0:T(8,128)} %param.9) | copy-start | bytes 393220
  10.7 6.6 %copy-start.1 = (f32[1,3,16,16,128]{4,3,2,1,0:T(8,128)S(1)}, f32[1,3,16,16,128]{4,3,2,1,0:T(8,128)}, u32[]{:S(2)}) copy-start(f32[1,3,16,16,128]{4,3,2,1,0:T(8,128)} %param.6) | copy-start | bytes 1179652
  12.2 5.0 %collective-permute-start.1 = (s32[16,16,128]{2,1,0:T(8,128)S(1)}, s32[16,16,128]{2,1,0:T(8,128)S(1)}, u32[]{:S(2)}, u32[]{:S(2)}) collective-permute-start(s32[16,16,128]{2,1,0:T(8,128)S(1)} %copy-done.2), channel_id=1, source_target_pairs={{0,1},{1,0},{2,3},{3,2},{4,5},{5,4},{6,7},{7,6},{8,9},{9,8},{10,11... | collective-permute-start | bytes 393224 | tf_op jit(solution)/shard_map/ppermute | solution.py:380
  18.3 16.9 %collective-permute-start.4 = (f32[3,16,16,128]{3,2,1,0:T(8,128)S(1)}, f32[3,16,16,128]{3,2,1,0:T(8,128)S(1)}, u32[]{:S(2)}, u32[]{:S(2)}) collective-permute-start(f32[3,16,16,128]{3,2,1,0:T(8,128)S(1)} %bitcast.24), channel_id=1, source_target_pairs={{0,1},{1,0},{2,3},{3,2},{4,5},{5,4},{6,7},{7,6},{8,9},{9,8},{10,11... | collective-permute-start | bytes 1179656 | tf_op jit(solution)/shard_map/ppermute | solution.py:380
  18.9 1.6 %collective-permute-start.5 = (f32[7,2,8,128]{3,2,1,0:T(8,128)S(1)}, f32[7,2,8,128]{3,2,1,0:T(8,128)S(1)}, u32[]{:S(2)}, u32[]{:S(2)}) collective-permute-start(f32[7,2,8,128]{3,2,1,0:T(8,128)S(1)} %get-tuple-element.27), channel_id=1, source_target_pairs={{0,2},{4,6},{2,0},{6,4},{1,3},{5,7},{3,1},{7,5},{8,10},{12,14},{10... | collective-permute-start | bytes 172040 | tf_op jit(solution)/shard_map/ppermute | solution.py:386
  18.9 16.3 %copy-start.3 = (s32[16,16,128]{2,1,0:T(8,128)S(1)}, s32[16,16,128]{2,1,0:T(8,128)}, u32[]{:S(2)}) copy-start(s32[16,16,128]{2,1,0:T(8,128)} %param.9) | copy-start | bytes 393220
  18.9 3.6 %collective-permute-start.6 = (f32[7,2,8,128]{3,2,1,0:T(8,128)S(1)}, f32[7,2,8,128]{3,2,1,0:T(8,128)S(1)}, u32[]{:S(2)}, u32[]{:S(2)}) collective-permute-start(f32[7,2,8,128]{3,2,1,0:T(8,128)S(1)} %get-tuple-element.28), channel_id=1, source_target_pairs={{2,4},{6,0},{4,2},{0,6},{3,5},{7,1},{5,3},{1,7},{10,12},{14,8},{12... | collective-permute-start | bytes 172040 | tf_op jit(solution)/shard_map/ppermute | solution.py:386
  22.5 12.6 %collective-permute-start.7 = (f32[2,7,2,8,128]{4,3,2,1,0:T(8,128)S(1)}, f32[2,7,2,8,128]{4,3,2,1,0:T(8,128)S(1)}, u32[]{:S(2)}, u32[]{:S(2)}) collective-permute-start(f32[2,7,2,8,128]{4,3,2,1,0:T(8,128)S(1)} %merge_strips.1.strips_ref), channel_id=1, source_target_pairs={{0,1},{1,0},{2,3},{3,2},{4,5},{5,4},{6,7},{7,6},{8,9},{9,8},{10,11... | collective-permute-start | bytes 344072 | tf_op jit(solution)/shard_map/ppermute | solution.py:380

commit v11 on v10

--- a/solution.py
+++ b/solution.py
@@ -217,18 +217,16 @@
         shift = (DEPTH * (k + 1)) & (LANES - 1)
         return [pltpu.roll(new[c], shift, 1) for c in range(COMPS)]
 
-    def fill(k, carry):
-        done = []
-        for g, (own, near, reg) in enumerate(((m_ref, n_ref, reg_ref), (mp_ref, np_ref, regp_ref))):
-            for t in range(tiles):
-                rows = rows_at(ny, tiles, k, t)
-                v = normal(
-                    [
-                        w_own * own[c, rows, :] + w_near * near[c, rows, :]
-                        for c in range(COMPS)
-                    ]
-                )
-                done.append((g * ny + k, t, v, params(reg[rows, :])))
+    def fill(i, carry):
+        done = []
+        for k in (2 * i, 2 * i + 1):
+            for g, (own, near, reg) in enumerate(((m_ref, n_ref, reg_ref), (mp_ref, np_ref, regp_ref))):
+                for t in range(tiles):
+                    rows = rows_at(ny, tiles, k, t)
+                    v = normal(
+                        [w_own * own[c, rows, :] + w_near * near[c, rows, :] for c in range(COMPS)]
+                    )
+                    done.append((g * ny + k, t, v, params(reg[rows, :])))
         for r, t, v, p in done:
             for c in range(COMPS):
                 main0[c, r, t] = v[c]
@@ -236,7 +234,7 @@
                 par[i, r, t] = p[i]
         return carry
 
-    lax.fori_loop(0, ny, fill, 0)
+    lax.fori_loop(0, ny // 2, fill, 0)
 
     def seam_of(left, right):
         return jnp.where(head_lane, pltpu.roll(left, 1, 1), pltpu.roll(right, LANES - 1, 1))
@@ -273,30 +271,36 @@
             under = jnp.where(bottom, 0.0, pltpu.roll(cells[tiles - 1], 1, 0))
         return above + under
 
-    def main_row(state, r):
+    def main_sums(state, r):
         g = r // ny
         k = r & (ny - 1)
         after = (r + 1) & (window - 1)
         before = (r - 1) & (window - 1)
         shift = (LANES - DEPTH * (k + 1)) & (LANES - 1)
         center = [[main[state][c, r, t] for t in range(tiles)] for c in range(COMPS)]
-        done = []
+        sums, ends = [], []
         for t in range(tiles):
-            h = []
             for c in range(COMPS):
                 cells = center[c][t]
-                ends = pltpu.roll(seam[state][c, g, t], shift, 1)
-                s = jnp.where(first_lane, ends, pltpu.roll(cells, 1, 1))
-                s = s + jnp.where(last_lane, ends, pltpu.roll(cells, LANES - 1, 1))
+                rim = pltpu.roll(seam[state][c, g, t], shift, 1)
+                s = jnp.where(first_lane, rim, pltpu.roll(cells, 1, 1))
+                s = s + jnp.where(last_lane, rim, pltpu.roll(cells, LANES - 1, 1))
                 s = s + (main[state][c, after, t] + main[state][c, before, t])
-                h.append(s + around_z(center[c], t))
-            m = [center[c][t] for c in range(COMPS)]
+                sums.append(s + around_z(center[c], t))
+            ends.append((r, t, ends_of(k, [center[c][t] for c in range(COMPS)])))
+        return sums, ends
+
+    def main_turn(state, r, sums):
+        done = []
+        for t in range(tiles):
+            m = [main[state][c, r, t] for c in range(COMPS)]
+            h = sums[COMPS * t : COMPS * (t + 1)]
             rate = turn(m, h, par[0, r, t], par[1, r, t], par[2, r, t])
             if state == 0:
                 new = [m[c] + rate[c] for c in range(COMPS)]
             else:
                 new = normal([main[0][c, r, t] + (m[c] + rate[c]) for c in range(COMPS)])
-            done.append((r, t, new, ends_of(k, m)))
+            done.append((r, t, new))
         return done
 
     def strip_rows(state):
@@ -342,19 +346,28 @@
                     seam[1 - state][c, g, t] = seam_of(left[c], right[c])
 
     def main_rows(state, first, count):
-        def rows(i, carry):
-            done = []
+        def rows(i, sums):
+            done, ends, later = [], [], []
+            each = COMPS * tiles
             for u in range(ROWS):
-                done += main_row(state, (first + ROWS * i + u) & (window - 1))
-            for r, t, new, ends in done:
+                r = (first + ROWS * (i - 1) + u) & (window - 1)
+                done += main_turn(state, r, sums[each * u : each * (u + 1)])
+            for u in range(ROWS):
+                found, row_ends = main_sums(state, (first + ROWS * i + u) & (window - 1))
+                later += found
+                ends += row_ends
+            for r, t, new in done:
+                for c in range(COMPS):
+                    main[1 - state][c, r, t] = new[c]
+            for r, t, row_ends in ends:
                 k = r & (ny - 1)
                 mask = ((lane - (DEPTH * k + DEPTH - 1)) & (LANES - 1)) < 2
                 for c in range(COMPS):
-                    main[1 - state][c, r, t] = new[c]
-                    pltpu.store(edge.at[c, r // ny, t], ends[c], mask=mask)
-            return carry
-
-        lax.fori_loop(0, count // ROWS, rows, 0)
+                    pltpu.store(edge.at[c, r // ny, t], row_ends[c], mask=mask)
+            return tuple(later)
+
+        zero = jnp.zeros((SUB, LANES), jnp.float32)
+        lax.fori_loop(0, count // ROWS + 1, rows, (zero,) * (COMPS * tiles * ROWS))
 
     def step(i, carry):
         for state in range(2):
@@ -365,13 +378,14 @@
 
     lax.fori_loop(0, STEPS, step, 0)
 
-    def hand_out(k, carry):
-        for t in range(tiles):
-            for c in range(COMPS):
-                out_ref[c, rows_at(ny, tiles, k, t), :] = main[0][c, k, t]
+    def hand_out(i, carry):
+        for k in (2 * i, 2 * i + 1):
+            for t in range(tiles):
+                for c in range(COMPS):
+                    out_ref[c, rows_at(ny, tiles, k, t), :] = main0[c, k, t]
         return carry
 
-    lax.fori_loop(0, ny, hand_out, 0)
+    lax.fori_loop(0, ny // 2, hand_out, 0)
 
 
 def shifted(cells, axis, step, closed):

time: 49 us -> 50 us (1.020)
  Pallas kernels: 16.2 us -> 17.2 us
    pallas_call x1, Pallas kernels: 13.6 us -> 14.7 us  [body(): pl.pallas_call(functools.partial(evolve_kernel, ny, tiles, images), out_s...]
where the time goes in v11:
time: 50 us; the launch traced here: 49.8 us
  Pallas kernels  17.2 us (34%)
  starting transfers between devices  12.4 us (25%)
  blocking collectives  11.1 us (22%)
  waiting for transfers between devices  6.42 us (13%)
  local copies, waits for them, and re-layouts  2.6 us (5%)
    pallas_call x1, Pallas kernels, body(): pl.pallas_call(functools.partial(evolve_kernel, ny, tiles, images), out_s...  14.7 us
    all_to_all x1, blocking collectives, body(): squares = lax.all_to_all(part, ('img', 'gx', 'gy'), 0, 0, tiled=True)  11.1 us
    ppermute x4, starting transfers between devices, swapped(): return lax.ppermute(cells, axis, pairs + [(j, i) for i, j in pairs])  6.75 us
    ppermute x4, starting transfers between devices, shifted(): return lax.ppermute(cells, axis, pairs)  5.69 us
    ppermute x4, waiting for transfers between devices, shifted(): return lax.ppermute(cells, axis, pairs)  4.44 us
    unnamed x16, local copies, waits for them, and re-layouts  2.6 us
    ppermute x4, waiting for transfers between devices, swapped(): return lax.ppermute(cells, axis, pairs + [(j, i) for i, j in pairs])  1.98 us
    pallas_call x1, Pallas kernels, body(): pl.pallas_call(functools.partial(pack_kernel, ny, tiles, anisotropy.shape...  1.51 us
  transfers between devices with their start and end apart: 8, of which 2 were waited for; matrix products, arithmetic and copies ran while one was open for 0% of the time, Pallas kernels for 3%

profile of v11, /device:TPU:0, one launch (start us, length us, event | category | flops | bytes accessed | tf_op | source)
XLA Modules:
  0.0 49.8 jit_solution(12610948752562333259)
XLA Ops:
  0.0 2.9 %collective-permute-start = (f32[3,16,16,128]{3,2,1,0:T(8,128)}, f32[3,16,16,128]{3,2,1,0:T(8,128)S(1)}, u32[]{:S(2)}, u32[]{:S(2)}) collective-permute-start(f32[3,16,16,128]{3,2,1,0:T(8,128)} %bitcast.15), channel_id=1, source_target_pairs={{0,1},{1,0},{2,3},{3,2},{4,5},{5,4},{6,7},{7,6},{8,9},{9,8},{10,11... | collective-permute-start | bytes 1179656 | tf_op jit(solution)/shard_map/ppermute | solution.py:394
  2.9 0.7 %collective-permute-start.3 = (f32[3,16,16,128]{3,2,1,0:T(8,128)}, f32[3,16,16,128]{3,2,1,0:T(8,128)S(1)}, u32[]{:S(2)}, u32[]{:S(2)}) collective-permute-start(f32[3,16,16,128]{3,2,1,0:T(8,128)} %bitcast.16), channel_id=1, source_target_pairs={{8,16},{16,8},{9,17},{17,9},{10,18},{18,10},{11,19},{19,11},{12,20... | collective-permute-start | bytes 1179656 | tf_op jit(solution)/shard_map/ppermute | solution.py:400
  3.6 4.4 %collective-permute-start.2 = (f32[3,16,16,128]{3,2,1,0:T(8,128)}, f32[3,16,16,128]{3,2,1,0:T(8,128)S(1)}, u32[]{:S(2)}, u32[]{:S(2)}) collective-permute-start(f32[3,16,16,128]{3,2,1,0:T(8,128)} %bitcast.17), channel_id=1, source_target_pairs={{0,8},{16,24},{8,0},{24,16},{1,9},{17,25},{9,1},{25,17},{2,10},{18... | collective-permute-start | bytes 1179656 | tf_op jit(solution)/shard_map/ppermute | solution.py:400
  8.1 0.0 copy-start.7
  8.1 0.0 copy-start.4
  8.1 0.0 copy-start.5
  8.1 0.0 copy-start.6
  8.1 0.6 %copy-done.7 = f32[3]{0:T(128)S(1)} copy-done((f32[3]{0:T(128)S(1)}, f32[3]{0:T(128)}, u32[]{:S(2)}) %copy-start.7) | copy-done | bytes 36
  8.7 0.0 copy-done.4
  8.7 0.0 copy-done.5
  8.7 0.0 copy-done.6
  8.8 0.0 copy-start
  8.8 1.0 %copy-done = f32[1,3,16,16,128]{4,3,2,1,0:T(8,128)S(1)} copy-done((f32[1,3,16,16,128]{4,3,2,1,0:T(8,128)S(1)}, f32[1,3,16,16,128]{4,3,2,1,0:T(8,128)}, u32[]{:S(2)}) %copy-start) | copy-done | bytes 393240
  9.8 0.0 copy-start.2
  9.8 0.9 %copy-done.2 = s32[16,16,128]{2,1,0:T(8,128)S(1)} copy-done((s32[16,16,128]{2,1,0:T(8,128)S(1)}, s32[16,16,128]{2,1,0:T(8,128)}, u32[]{:S(2)}) %copy-start.2) | copy-done | bytes 131096
  10.7 0.0 copy-start.1
  10.7 1.5 %pack_strips.1 = (f32[4,2,8,128]{3,2,1,0:T(8,128)S(1)}, f32[4,2,8,128]{3,2,1,0:T(8,128)S(1)}, f32[5,8,128]{2,1,0:T(8,128)S(1)}) custom-call(s32[4]{0:T(128)S(1)} %copy-done.4, f32[8]{0:T(128)S(1)} %copy-done.5, f32[8]{0:T(128)S(1)} %copy-done.6, f32[1,3]{1,0:T(1,128)S(1)} %bitcast.31, f32[3,256,128]{2,1,0:T(8,128)S(1)} %bitcast.18, s32[256,128]{1,0:T(8,128)S(1)} %bitcast.21), custom_call_target="tpu_custom_call" | custom-call | tf_op jit(solution)/shard_map/pack_strips/pallas_call | solution.py:441
  12.2 0.6 %collective-permute-start.1 = (s32[16,16,128]{2,1,0:T(8,128)S(1)}, s32[16,16,128]{2,1,0:T(8,128)S(1)}, u32[]{:S(2)}, u32[]{:S(2)}) collective-permute-start(s32[16,16,128]{2,1,0:T(8,128)S(1)} %copy-done.2), channel_id=1, source_target_pairs={{0,1},{1,0},{2,3},{3,2},{4,5},{5,4},{6,7},{7,6},{8,9},{9,8},{10,11... | collective-permute-start | bytes 393224 | tf_op jit(solution)/shard_map/ppermute | solution.py:394
  12.8 4.4 %collective-permute-done.1 = s32[16,16,128]{2,1,0:T(8,128)S(1)} collective-permute-done((s32[16,16,128]{2,1,0:T(8,128)S(1)}, s32[16,16,128]{2,1,0:T(8,128)S(1)}, u32[]{:S(2)}, u32[]{:S(2)}) %collective-permute-start.1) | collective-permute-done | bytes 131104 | tf_op jit(solution)/shard_map/ppermute | solution.py:394
  17.2 0.0 collective-permute-done
  17.2 0.0 collective-permute-done.3
  17.2 0.0 collective-permute-done.2
  17.2 0.0 copy-done.1
  17.2 1.1 %gather_images.1 = (f32[32,128]{1,0:T(8,128)S(1)}, f32[3,256,128]{2,1,0:T(8,128)S(1)}, f32[7,2,8,128]{3,2,1,0:T(8,128)S(1)}, f32[7,2,8,128]{3,2,1,0:T(8,128)S(1)}) custom-call(f32[5,8,128]{2,1,0:T(8,128)S(1)} %get-tuple-element.20.info_ref, f32[3,256,128]{2,1,0:T(8,128)S(1)} %bitcast.19, f32[3,256,128]{2,1,0:T(8,128)S(1)} %bitcast.27, ...), custom_call_target="tpu_custom_call" | custom-call | tf_op jit(solution)/shard_map/gather_images/pallas_call | solution.py:460
  18.3 0.6 %collective-permute-start.4 = (f32[3,16,16,128]{3,2,1,0:T(8,128)S(1)}, f32[3,16,16,128]{3,2,1,0:T(8,128)S(1)}, u32[]{:S(2)}, u32[]{:S(2)}) collective-permute-start(f32[3,16,16,128]{3,2,1,0:T(8,128)S(1)} %bitcast.24), channel_id=1, source_target_pairs={{0,1},{1,0},{2,3},{3,2},{4,5},{5,4},{6,7},{7,6},{8,9},{9,8},{10,11... | collective-permute-start | bytes 1179656 | tf_op jit(solution)/shard_map/ppermute | solution.py:394
  18.9 0.0 collective-permute-start.5
  18.9 0.0 copy-start.3
  18.9 1.6 %collective-permute-start.6 = (f32[7,2,8,128]{3,2,1,0:T(8,128)S(1)}, f32[7,2,8,128]{3,2,1,0:T(8,128)S(1)}, u32[]{:S(2)}, u32[]{:S(2)}) collective-permute-start(f32[7,2,8,128]{3,2,1,0:T(8,128)S(1)} %get-tuple-element.28), channel_id=1, source_target_pairs={{2,4},{6,0},{4,2},{0,6},{3,5},{7,1},{5,3},{1,7},{10,12},{14,8},{12... | collective-permute-start | bytes 172040 | tf_op jit(solution)/shard_map/ppermute | solution.py:400
  20.5 0.0 collective-permute-done.5.one_ref
  20.5 2.0 %collective-permute-done.6.two_ref = f32[7,2,8,128]{3,2,1,0:T(8,128)S(1)} collective-permute-done((f32[7,2,8,128]{3,2,1,0:T(8,128)S(1)}, f32[7,2,8,128]{3,2,1,0:T(8,128)S(1)}, u32[]{:S(2)}, u32[]{:S(2)}) %collective-permute-start.6) | collective-permute-done | bytes 57376 | tf_op jit(solution)/shard_map/ppermute | solution.py:400
  22.5 1.6 %collective-permute-start.7 = (f32[2,7,2,8,128]{4,3,2,1,0:T(8,128)S(1)}, f32[2,7,2,8,128]{4,3,2,1,0:T(8,128)S(1)}, u32[]{:S(2)}, u32[]{:S(2)}) collective-permute-start(f32[2,7,2,8,128]{4,3,2,1,0:T(8,128)S(1)} %merge_strips.1.strips_ref), channel_id=1, source_target_pairs={{0,1},{1,0},{2,3},{3,2},{4,5},{5,4},{6,7},{7,6},{8,9},{9,8},{10,11... | collective-permute-start | bytes 344072 | tf_op jit(solution)/shard_map/ppermute | solution.py:394
  24.1 11.1 %all_to_all.11 = f32[32,1,128]{2,1,0:T(1,128)S(1)} all-to-all(f32[32,1,128]{2,1,0:T(1,128)S(1)} %bitcast.30), channel_id=1, replica_groups=mesh['img'=4,'gx'=4,'gy'=2] {'img','gx','gy'}, dimensions={0} | all-to-all | bytes 32768 | tf_op jit(solution)/shard_map/all_to_all | solution.py:485
  35.2 0.0 collective-permute-done.7.stripsp_ref
  35.2 0.0 collective-permute-done.4
  35.2 0.0 copy-done.3
  35.2 14.7 %evolve.1 = f32[3,256,128]{2,1,0:T(8,128)} custom-call(f32[5,8,128]{2,1,0:T(8,128)S(1)} %get-tuple-element.20.info_ref, f32[32,128]{1,0:T(8,128)S(1)} %bitcast.29, f32[3,256,128]{2,1,0:T(8,128)S(1)} %bitcast.20, f32[3,256,128]{2,1,0:T(8,128)S(1)} %bitcast.23, f32[3,256,128]{2,1,0:T(8,128)S(1)} %get-tuple-element.25.n_ref, f32[3,256,128]{2,1,0:T(8,128)S(1)} %bitcast.25, ...), custom_call_target="tpu_custom_call" | custom-call | tf_op jit(solution)/shard_map/evolve/pallas_call | solution.py:488
  (1 shorter events, 0.0 us)
Async XLA Ops:
  0.0 17.2 %collective-permute-start = (f32[3,16,16,128]{3,2,1,0:T(8,128)}, f32[3,16,16,128]{3,2,1,0:T(8,128)S(1)}, u32[]{:S(2)}, u32[]{:S(2)}) collective-permute-start(f32[3,16,16,128]{3,2,1,0:T(8,128)} %bitcast.15), channel_id=1, source_target_pairs={{0,1},{1,0},{2,3},{3,2},{4,5},{5,4},{6,7},{7,6},{8,9},{9,8},{10,11... | collective-permute-start | bytes 1179656 | tf_op jit(solution)/shard_map/ppermute | solution.py:394
  2.9 14.3 %collective-permute-start.3 = (f32[3,16,16,128]{3,2,1,0:T(8,128)}, f32[3,16,16,128]{3,2,1,0:T(8,128)S(1)}, u32[]{:S(2)}, u32[]{:S(2)}) collective-permute-start(f32[3,16,16,128]{3,2,1,0:T(8,128)} %bitcast.16), channel_id=1, source_target_pairs={{8,16},{16,8},{9,17},{17,9},{10,18},{18,10},{11,19},{19,11},{12,20... | collective-permute-start | bytes 1179656 | tf_op jit(solution)/shard_map/ppermute | solution.py:400
  3.6 13.6 %collective-permute-start.2 = (f32[3,16,16,128]{3,2,1,0:T(8,128)}, f32[3,16,16,128]{3,2,1,0:T(8,128)S(1)}, u32[]{:S(2)}, u32[]{:S(2)}) collective-permute-start(f32[3,16,16,128]{3,2,1,0:T(8,128)} %bitcast.17), channel_id=1, source_target_pairs={{0,8},{16,24},{8,0},{24,16},{1,9},{17,25},{9,1},{25,17},{2,10},{18... | collective-permute-start | bytes 1179656 | tf_op jit(solution)/shard_map/ppermute | solution.py:400
  8.1 0.7 %copy-start.7 = (f32[3]{0:T(128)S(1)}, f32[3]{0:T(128)}, u32[]{:S(2)}) copy-start(f32[3]{0:T(128)} %param.8) | copy-start | bytes 40
  8.1 0.7 %copy-start.4 = (s32[4]{0:T(128)S(1)}, s32[4]{0:T(128)}, u32[]{:S(2)}) copy-start(s32[4]{0:T(128)} %lower_ref.1) | copy-start | bytes 52
  8.1 0.7 %copy-start.5 = (f32[8]{0:T(128)S(1)}, f32[8]{0:T(128)}, u32[]{:S(2)}) copy-start(f32[8]{0:T(128)} %aniso_ref.1) | copy-start | bytes 100
  8.1 0.7 %copy-start.6 = (f32[8]{0:T(128)S(1)}, f32[8]{0:T(128)}, u32[]{:S(2)}) copy-start(f32[8]{0:T(128)} %damp_ref.1) | copy-start | bytes 100
  8.8 1.0 %copy-start = (f32[1,3,16,16,128]{4,3,2,1,0:T(8,128)S(1)}, f32[1,3,16,16,128]{4,3,2,1,0:T(8,128)}, u32[]{:S(2)}) copy-start(f32[1,3,16,16,128]{4,3,2,1,0:T(8,128)} %param.6) | copy-start | bytes 1179652
  9.8 0.9 %copy-start.2 = (s32[16,16,128]{2,1,0:T(8,128)S(1)}, s32[16,16,128]{2,1,0:T(8,128)}, u32[]{:S(2)}) copy-start(s32[16,16,128]{2,1,0:T(8,128)} %param.9) | copy-start | bytes 393220
  10.7 6.6 %copy-start.1 = (f32[1,3,16,16,128]{4,3,2,1,0:T(8,128)S(1)}, f32[1,3,16,16,128]{4,3,2,1,0:T(8,128)}, u32[]{:S(2)}) copy-start(f32[1,3,16,16,128]{4,3,2,1,0:T(8,128)} %param.6) | copy-start | bytes 1179652
  12.2 5.0 %collective-permute-start.1 = (s32[16,16,128]{2,1,0:T(8,128)S(1)}, s32[16,16,128]{2,1,0:T(8,128)S(1)}, u32[]{:S(2)}, u32[]{:S(2)}) collective-permute-start(s32[16,16,128]{2,1,0:T(8,128)S(1)} %copy-done.2), channel_id=1, source_target_pairs={{0,1},{1,0},{2,3},{3,2},{4,5},{5,4},{6,7},{7,6},{8,9},{9,8},{10,11... | collective-permute-start | bytes 393224 | tf_op jit(solution)/shard_map/ppermute | solution.py:394
  18.3 16.9 %collective-permute-start.4 = (f32[3,16,16,128]{3,2,1,0:T(8,128)S(1)}, f32[3,16,16,128]{3,2,1,0:T(8,128)S(1)}, u32[]{:S(2)}, u32[]{:S(2)}) collective-permute-start(f32[3,16,16,128]{3,2,1,0:T(8,128)S(1)} %bitcast.24), channel_id=1, source_target_pairs={{0,1},{1,0},{2,3},{3,2},{4,5},{5,4},{6,7},{7,6},{8,9},{9,8},{10,11... | collective-permute-start | bytes 1179656 | tf_op jit(solution)/shard_map/ppermute | solution.py:394
  18.9 1.6 %collective-permute-start.5 = (f32[7,2,8,128]{3,2,1,0:T(8,128)S(1)}, f32[7,2,8,128]{3,2,1,0:T(8,128)S(1)}, u32[]{:S(2)}, u32[]{:S(2)}) collective-permute-start(f32[7,2,8,128]{3,2,1,0:T(8,128)S(1)} %get-tuple-element.27), channel_id=1, source_target_pairs={{0,2},{4,6},{2,0},{6,4},{1,3},{5,7},{3,1},{7,5},{8,10},{12,14},{10... | collective-permute-start | bytes 172040 | tf_op jit(solution)/shard_map/ppermute | solution.py:400
  18.9 16.3 %copy-start.3 = (s32[16,16,128]{2,1,0:T(8,128)S(1)}, s32[16,16,128]{2,1,0:T(8,128)}, u32[]{:S(2)}) copy-start(s32[16,16,128]{2,1,0:T(8,128)} %param.9) | copy-start | bytes 393220
  18.9 3.6 %collective-permute-start.6 = (f32[7,2,8,128]{3,2,1,0:T(8,128)S(1)}, f32[7,2,8,128]{3,2,1,0:T(8,128)S(1)}, u32[]{:S(2)}, u32[]{:S(2)}) collective-permute-start(f32[7,2,8,128]{3,2,1,0:T(8,128)S(1)} %get-tuple-element.28), channel_id=1, source_target_pairs={{2,4},{6,0},{4,2},{0,6},{3,5},{7,1},{5,3},{1,7},{10,12},{14,8},{12... | collective-permute-start | bytes 172040 | tf_op jit(solution)/shard_map/ppermute | solution.py:400
  22.5 12.6 %collective-permute-start.7 = (f32[2,7,2,8,128]{4,3,2,1,0:T(8,128)S(1)}, f32[2,7,2,8,128]{4,3,2,1,0:T(8,128)S(1)}, u32[]{:S(2)}, u32[]{:S(2)}) collective-permute-start(f32[2,7,2,8,128]{4,3,2,1,0:T(8,128)S(1)} %merge_strips.1.strips_ref), channel_id=1, source_target_pairs={{0,1},{1,0},{2,3},{3,2},{4,5},{5,4},{6,7},{7,6},{8,9},{9,8},{10,11... | collective-permute-start | bytes 344072 | tf_op jit(solution)/shard_map/ppermute | solution.py:394

commit v12 on v10

--- a/solution.py
+++ b/solution.py
@@ -217,26 +217,33 @@
         shift = (DEPTH * (k + 1)) & (LANES - 1)
         return [pltpu.roll(new[c], shift, 1) for c in range(COMPS)]
 
-    def fill(k, carry):
-        done = []
-        for g, (own, near, reg) in enumerate(((m_ref, n_ref, reg_ref), (mp_ref, np_ref, regp_ref))):
-            for t in range(tiles):
-                rows = rows_at(ny, tiles, k, t)
-                v = normal(
-                    [
-                        w_own * own[c, rows, :] + w_near * near[c, rows, :]
-                        for c in range(COMPS)
-                    ]
-                )
-                done.append((g * ny + k, t, v, params(reg[rows, :])))
+    def place(r, t, offset=0):
+        row = (tiles + 1) * SUB * r + SUB * (0 if t == 0 else 2 if t == tiles - 1 else t + 2)
+        return pl.ds(row + offset if offset else pl.multiple_of(row, SUB), SUB)
+
+    zero = jnp.zeros((SUB, LANES), jnp.float32)
+
+    def fill(i, carry):
+        done = []
+        for k in (2 * i, 2 * i + 1):
+            for g, (own, near, reg) in enumerate(((m_ref, n_ref, reg_ref), (mp_ref, np_ref, regp_ref))):
+                for t in range(tiles):
+                    rows = rows_at(ny, tiles, k, t)
+                    v = normal(
+                        [w_own * own[c, rows, :] + w_near * near[c, rows, :] for c in range(COMPS)]
+                    )
+                    done.append((g * ny + k, t, v, params(reg[rows, :])))
         for r, t, v, p in done:
             for c in range(COMPS):
-                main0[c, r, t] = v[c]
+                main0[c, place(r, t), :] = v[c]
+                if t == 0:
+                    main0[c, place(r, t, SUB), :] = zero
+                    main1[c, place(r, t, SUB), :] = zero
             for i in range(3):
                 par[i, r, t] = p[i]
         return carry
 
-    lax.fori_loop(0, ny, fill, 0)
+    lax.fori_loop(0, ny // 2, fill, 0)
 
     def seam_of(left, right):
         return jnp.where(head_lane, pltpu.roll(left, 1, 1), pltpu.roll(right, LANES - 1, 1))
@@ -279,23 +286,30 @@
         after = (r + 1) & (window - 1)
         before = (r - 1) & (window - 1)
         shift = (LANES - DEPTH * (k + 1)) & (LANES - 1)
-        center = [[main[state][c, r, t] for t in range(tiles)] for c in range(COMPS)]
         done = []
         for t in range(tiles):
-            h = []
+            m, h = [], []
             for c in range(COMPS):
-                cells = center[c][t]
+                cells = main[state][c, place(r, t), :]
                 ends = pltpu.roll(seam[state][c, g, t], shift, 1)
                 s = jnp.where(first_lane, ends, pltpu.roll(cells, 1, 1))
                 s = s + jnp.where(last_lane, ends, pltpu.roll(cells, LANES - 1, 1))
-                s = s + (main[state][c, after, t] + main[state][c, before, t])
-                h.append(s + around_z(center[c], t))
-            m = [center[c][t] for c in range(COMPS)]
+                s = s + (main[state][c, place(after, t), :] + main[state][c, place(before, t), :])
+                if t + 1 < tiles:
+                    above = main[state][c, place(r, t + 1), :]
+                else:
+                    above = main[state][c, place(r, 0, 1), :]
+                if t > 0:
+                    under = main[state][c, place(r, t - 1), :]
+                else:
+                    under = main[state][c, place(r, tiles - 1, -1), :]
+                h.append(s + (above + under))
+                m.append(cells)
             rate = turn(m, h, par[0, r, t], par[1, r, t], par[2, r, t])
             if state == 0:
                 new = [m[c] + rate[c] for c in range(COMPS)]
             else:
-                new = normal([main[0][c, r, t] + (m[c] + rate[c]) for c in range(COMPS)])
+                new = normal([main[0][c, place(r, t), :] + (m[c] + rate[c]) for c in range(COMPS)])
             done.append((r, t, new, ends_of(k, m)))
         return done
 
@@ -350,7 +364,7 @@
                 k = r & (ny - 1)
                 mask = ((lane - (DEPTH * k + DEPTH - 1)) & (LANES - 1)) < 2
                 for c in range(COMPS):
-                    main[1 - state][c, r, t] = new[c]
+                    main[1 - state][c, place(r, t), :] = new[c]
                     pltpu.store(edge.at[c, r // ny, t], ends[c], mask=mask)
             return carry
 
@@ -365,13 +379,14 @@
 
     lax.fori_loop(0, STEPS, step, 0)
 
-    def hand_out(k, carry):
-        for t in range(tiles):
-            for c in range(COMPS):
-                out_ref[c, rows_at(ny, tiles, k, t), :] = main[0][c, k, t]
+    def hand_out(i, carry):
+        for k in (2 * i, 2 * i + 1):
+            for t in range(tiles):
+                for c in range(COMPS):
+                    out_ref[c, rows_at(ny, tiles, k, t), :] = main0[c, place(k, t), :]
         return carry
 
-    lax.fori_loop(0, ny, hand_out, 0)
+    lax.fori_loop(0, ny // 2, hand_out, 0)
 
 
 def shifted(cells, axis, step, closed):
@@ -477,8 +492,8 @@
         in_specs=[vmem] * 10,
         out_specs=vmem,
         scratch_shapes=[
-            pltpu.VMEM((comps, window, tiles) + vreg, f32),
-            pltpu.VMEM((comps, window, tiles) + vreg, f32),
+            pltpu.VMEM((comps, window * (tiles + 1) * SUB, LANES), f32),
+            pltpu.VMEM((comps, window * (tiles + 1) * SUB, LANES), f32),
             pltpu.VMEM((comps, 2, 2, tiles) + vreg, f32),
             pltpu.VMEM((comps, 2, 2, tiles) + vreg, f32),
             pltpu.VMEM((comps, 2, tiles) + vreg, f32),

time: 49 us -> 49.6 us (1.012)
  Pallas kernels: 16.2 us -> 16.8 us
    pallas_call x1, Pallas kernels: 13.6 us -> 14.2 us  [body(): pl.pallas_call(functools.partial(evolve_kernel, ny, tiles, images), out_s...]
where the time goes in v12:
time: 49.6 us; the launch traced here: 49.4 us
  Pallas kernels  16.8 us (34%)
  starting transfers between devices  12.4 us (25%)
  blocking collectives  11.1 us (22%)
  waiting for transfers between devices  6.42 us (13%)
  local copies, waits for them, and re-layouts  2.6 us (5%)
    pallas_call x1, Pallas kernels, body(): pl.pallas_call(functools.partial(evolve_kernel, ny, tiles, images), out_s...  14.2 us
    all_to_all x1, blocking collectives, body(): squares = lax.all_to_all(part, ('img', 'gx', 'gy'), 0, 0, tiled=True)  11.1 us
    ppermute x4, starting transfers between devices, swapped(): return lax.ppermute(cells, axis, pairs + [(j, i) for i, j in pairs])  6.75 us
    ppermute x4, starting transfers between devices, shifted(): return lax.ppermute(cells, axis, pairs)  5.69 us
    ppermute x4, waiting for transfers between devices, shifted(): return lax.ppermute(cells, axis, pairs)  4.44 us
    unnamed x16, local copies, waits for them, and re-layouts  2.6 us
    ppermute x4, waiting for transfers between devices, swapped(): return lax.ppermute(cells, axis, pairs + [(j, i) for i, j in pairs])  1.98 us
    pallas_call x1, Pallas kernels, body(): pl.pallas_call(functools.partial(pack_kernel, ny, tiles, anisotropy.shape...  1.51 us
  transfers between devices with their start and end apart: 8, of which 2 were waited for; matrix products, arithmetic and copies ran while one was open for 0% of the time, Pallas kernels for 3%

profile of v12, /device:TPU:0, one launch (start us, length us, event | category | flops | bytes accessed | tf_op | source)
XLA Modules:
  0.0 49.4 jit_solution(11553135357317937560)
XLA Ops:
  0.0 2.9 %collective-permute-start = (f32[3,16,16,128]{3,2,1,0:T(8,128)}, f32[3,16,16,128]{3,2,1,0:T(8,128)S(1)}, u32[]{:S(2)}, u32[]{:S(2)}) collective-permute-start(f32[3,16,16,128]{3,2,1,0:T(8,128)} %bitcast.15), channel_id=1, source_target_pairs={{0,1},{1,0},{2,3},{3,2},{4,5},{5,4},{6,7},{7,6},{8,9},{9,8},{10,11... | collective-permute-start | bytes 1179656 | tf_op jit(solution)/shard_map/ppermute | solution.py:395
  2.9 0.7 %collective-permute-start.3 = (f32[3,16,16,128]{3,2,1,0:T(8,128)}, f32[3,16,16,128]{3,2,1,0:T(8,128)S(1)}, u32[]{:S(2)}, u32[]{:S(2)}) collective-permute-start(f32[3,16,16,128]{3,2,1,0:T(8,128)} %bitcast.16), channel_id=1, source_target_pairs={{8,16},{16,8},{9,17},{17,9},{10,18},{18,10},{11,19},{19,11},{12,20... | collective-permute-start | bytes 1179656 | tf_op jit(solution)/shard_map/ppermute | solution.py:401
  3.6 4.4 %collective-permute-start.2 = (f32[3,16,16,128]{3,2,1,0:T(8,128)}, f32[3,16,16,128]{3,2,1,0:T(8,128)S(1)}, u32[]{:S(2)}, u32[]{:S(2)}) collective-permute-start(f32[3,16,16,128]{3,2,1,0:T(8,128)} %bitcast.17), channel_id=1, source_target_pairs={{0,8},{16,24},{8,0},{24,16},{1,9},{17,25},{9,1},{25,17},{2,10},{18... | collective-permute-start | bytes 1179656 | tf_op jit(solution)/shard_map/ppermute | solution.py:401
  8.1 0.0 copy-start.7
  8.1 0.0 copy-start.4
  8.1 0.0 copy-start.5
  8.1 0.0 copy-start.6
  8.1 0.6 %copy-done.7 = f32[3]{0:T(128)S(1)} copy-done((f32[3]{0:T(128)S(1)}, f32[3]{0:T(128)}, u32[]{:S(2)}) %copy-start.7) | copy-done | bytes 36
  8.7 0.0 copy-done.4
  8.7 0.0 copy-done.5
  8.7 0.0 copy-done.6
  8.8 0.0 copy-start
  8.8 1.0 %copy-done = f32[1,3,16,16,128]{4,3,2,1,0:T(8,128)S(1)} copy-done((f32[1,3,16,16,128]{4,3,2,1,0:T(8,128)S(1)}, f32[1,3,16,16,128]{4,3,2,1,0:T(8,128)}, u32[]{:S(2)}) %copy-start) | copy-done | bytes 393240
  9.8 0.0 copy-start.2
  9.8 0.9 %copy-done.2 = s32[16,16,128]{2,1,0:T(8,128)S(1)} copy-done((s32[16,16,128]{2,1,0:T(8,128)S(1)}, s32[16,16,128]{2,1,0:T(8,128)}, u32[]{:S(2)}) %copy-start.2) | copy-done | bytes 131096
  10.7 0.0 copy-start.1
  10.7 1.5 %pack_strips.1 = (f32[4,2,8,128]{3,2,1,0:T(8,128)S(1)}, f32[4,2,8,128]{3,2,1,0:T(8,128)S(1)}, f32[5,8,128]{2,1,0:T(8,128)S(1)}) custom-call(s32[4]{0:T(128)S(1)} %copy-done.4, f32[8]{0:T(128)S(1)} %copy-done.5, f32[8]{0:T(128)S(1)} %copy-done.6, f32[1,3]{1,0:T(1,128)S(1)} %bitcast.31, f32[3,256,128]{2,1,0:T(8,128)S(1)} %bitcast.18, s32[256,128]{1,0:T(8,128)S(1)} %bitcast.21), custom_call_target="tpu_custom_call" | custom-call | tf_op jit(solution)/shard_map/pack_strips/pallas_call | solution.py:442
  12.2 0.6 %collective-permute-start.1 = (s32[16,16,128]{2,1,0:T(8,128)S(1)}, s32[16,16,128]{2,1,0:T(8,128)S(1)}, u32[]{:S(2)}, u32[]{:S(2)}) collective-permute-start(s32[16,16,128]{2,1,0:T(8,128)S(1)} %copy-done.2), channel_id=1, source_target_pairs={{0,1},{1,0},{2,3},{3,2},{4,5},{5,4},{6,7},{7,6},{8,9},{9,8},{10,11... | collective-permute-start | bytes 393224 | tf_op jit(solution)/shard_map/ppermute | solution.py:395
  12.8 4.4 %collective-permute-done.1 = s32[16,16,128]{2,1,0:T(8,128)S(1)} collective-permute-done((s32[16,16,128]{2,1,0:T(8,128)S(1)}, s32[16,16,128]{2,1,0:T(8,128)S(1)}, u32[]{:S(2)}, u32[]{:S(2)}) %collective-permute-start.1) | collective-permute-done | bytes 131104 | tf_op jit(solution)/shard_map/ppermute | solution.py:395
  17.2 0.0 collective-permute-done
  17.2 0.0 collective-permute-done.3
  17.2 0.0 collective-permute-done.2
  17.2 0.0 copy-done.1
  17.2 1.1 %gather_images.1 = (f32[32,128]{1,0:T(8,128)S(1)}, f32[3,256,128]{2,1,0:T(8,128)S(1)}, f32[7,2,8,128]{3,2,1,0:T(8,128)S(1)}, f32[7,2,8,128]{3,2,1,0:T(8,128)S(1)}) custom-call(f32[5,8,128]{2,1,0:T(8,128)S(1)} %get-tuple-element.20.info_ref, f32[3,256,128]{2,1,0:T(8,128)S(1)} %bitcast.19, f32[3,256,128]{2,1,0:T(8,128)S(1)} %bitcast.27, ...), custom_call_target="tpu_custom_call" | custom-call | tf_op jit(solution)/shard_map/gather_images/pallas_call | solution.py:461
  18.3 0.6 %collective-permute-start.4 = (f32[3,16,16,128]{3,2,1,0:T(8,128)S(1)}, f32[3,16,16,128]{3,2,1,0:T(8,128)S(1)}, u32[]{:S(2)}, u32[]{:S(2)}) collective-permute-start(f32[3,16,16,128]{3,2,1,0:T(8,128)S(1)} %bitcast.24), channel_id=1, source_target_pairs={{0,1},{1,0},{2,3},{3,2},{4,5},{5,4},{6,7},{7,6},{8,9},{9,8},{10,11... | collective-permute-start | bytes 1179656 | tf_op jit(solution)/shard_map/ppermute | solution.py:395
  18.9 0.0 collective-permute-start.5
  18.9 0.0 copy-start.3
  18.9 1.6 %collective-permute-start.6 = (f32[7,2,8,128]{3,2,1,0:T(8,128)S(1)}, f32[7,2,8,128]{3,2,1,0:T(8,128)S(1)}, u32[]{:S(2)}, u32[]{:S(2)}) collective-permute-start(f32[7,2,8,128]{3,2,1,0:T(8,128)S(1)} %get-tuple-element.28), channel_id=1, source_target_pairs={{2,4},{6,0},{4,2},{0,6},{3,5},{7,1},{5,3},{1,7},{10,12},{14,8},{12... | collective-permute-start | bytes 172040 | tf_op jit(solution)/shard_map/ppermute | solution.py:401
  20.5 0.0 collective-permute-done.5.one_ref
  20.5 2.0 %collective-permute-done.6.two_ref = f32[7,2,8,128]{3,2,1,0:T(8,128)S(1)} collective-permute-done((f32[7,2,8,128]{3,2,1,0:T(8,128)S(1)}, f32[7,2,8,128]{3,2,1,0:T(8,128)S(1)}, u32[]{:S(2)}, u32[]{:S(2)}) %collective-permute-start.6) | collective-permute-done | bytes 57376 | tf_op jit(solution)/shard_map/ppermute | solution.py:401
  22.5 1.6 %collective-permute-start.7 = (f32[2,7,2,8,128]{4,3,2,1,0:T(8,128)S(1)}, f32[2,7,2,8,128]{4,3,2,1,0:T(8,128)S(1)}, u32[]{:S(2)}, u32[]{:S(2)}) collective-permute-start(f32[2,7,2,8,128]{4,3,2,1,0:T(8,128)S(1)} %merge_strips.1.strips_ref), channel_id=1, source_target_pairs={{0,1},{1,0},{2,3},{3,2},{4,5},{5,4},{6,7},{7,6},{8,9},{9,8},{10,11... | collective-permute-start | bytes 344072 | tf_op jit(solution)/shard_map/ppermute | solution.py:395
  24.1 11.1 %all_to_all.11 = f32[32,1,128]{2,1,0:T(1,128)S(1)} all-to-all(f32[32,1,128]{2,1,0:T(1,128)S(1)} %bitcast.30), channel_id=1, replica_groups=mesh['img'=4,'gx'=4,'gy'=2] {'img','gx','gy'}, dimensions={0} | all-to-all | bytes 32768 | tf_op jit(solution)/shard_map/all_to_all | solution.py:486
  35.2 0.0 collective-permute-done.7.stripsp_ref
  35.2 0.0 collective-permute-done.4
  35.2 0.0 copy-done.3
  35.2 14.2 %evolve.1 = f32[3,256,128]{2,1,0:T(8,128)} custom-call(f32[5,8,128]{2,1,0:T(8,128)S(1)} %get-tuple-element.20.info_ref, f32[32,128]{1,0:T(8,128)S(1)} %bitcast.29, f32[3,256,128]{2,1,0:T(8,128)S(1)} %bitcast.20, f32[3,256,128]{2,1,0:T(8,128)S(1)} %bitcast.23, f32[3,256,128]{2,1,0:T(8,128)S(1)} %get-tuple-element.25.n_ref, f32[3,256,128]{2,1,0:T(8,128)S(1)} %bitcast.25, ...), custom_call_target="tpu_custom_call" | custom-call | tf_op jit(solution)/shard_map/evolve/pallas_call | solution.py:489
  (1 shorter events, 0.0 us)
Async XLA Ops:
  0.0 17.2 %collective-permute-start = (f32[3,16,16,128]{3,2,1,0:T(8,128)}, f32[3,16,16,128]{3,2,1,0:T(8,128)S(1)}, u32[]{:S(2)}, u32[]{:S(2)}) collective-permute-start(f32[3,16,16,128]{3,2,1,0:T(8,128)} %bitcast.15), channel_id=1, source_target_pairs={{0,1},{1,0},{2,3},{3,2},{4,5},{5,4},{6,7},{7,6},{8,9},{9,8},{10,11... | collective-permute-start | bytes 1179656 | tf_op jit(solution)/shard_map/ppermute | solution.py:395
  2.9 14.3 %collective-permute-start.3 = (f32[3,16,16,128]{3,2,1,0:T(8,128)}, f32[3,16,16,128]{3,2,1,0:T(8,128)S(1)}, u32[]{:S(2)}, u32[]{:S(2)}) collective-permute-start(f32[3,16,16,128]{3,2,1,0:T(8,128)} %bitcast.16), channel_id=1, source_target_pairs={{8,16},{16,8},{9,17},{17,9},{10,18},{18,10},{11,19},{19,11},{12,20... | collective-permute-start | bytes 1179656 | tf_op jit(solution)/shard_map/ppermute | solution.py:401
  3.6 13.6 %collective-permute-start.2 = (f32[3,16,16,128]{3,2,1,0:T(8,128)}, f32[3,16,16,128]{3,2,1,0:T(8,128)S(1)}, u32[]{:S(2)}, u32[]{:S(2)}) collective-permute-start(f32[3,16,16,128]{3,2,1,0:T(8,128)} %bitcast.17), channel_id=1, source_target_pairs={{0,8},{16,24},{8,0},{24,16},{1,9},{17,25},{9,1},{25,17},{2,10},{18... | collective-permute-start | bytes 1179656 | tf_op jit(solution)/shard_map/ppermute | solution.py:401
  8.1 0.7 %copy-start.7 = (f32[3]{0:T(128)S(1)}, f32[3]{0:T(128)}, u32[]{:S(2)}) copy-start(f32[3]{0:T(128)} %param.8) | copy-start | bytes 40
  8.1 0.7 %copy-start.4 = (s32[4]{0:T(128)S(1)}, s32[4]{0:T(128)}, u32[]{:S(2)}) copy-start(s32[4]{0:T(128)} %lower_ref.1) | copy-start | bytes 52
  8.1 0.7 %copy-start.5 = (f32[8]{0:T(128)S(1)}, f32[8]{0:T(128)}, u32[]{:S(2)}) copy-start(f32[8]{0:T(128)} %aniso_ref.1) | copy-start | bytes 100
  8.1 0.7 %copy-start.6 = (f32[8]{0:T(128)S(1)}, f32[8]{0:T(128)}, u32[]{:S(2)}) copy-start(f32[8]{0:T(128)} %damp_ref.1) | copy-start | bytes 100
  8.8 1.0 %copy-start = (f32[1,3,16,16,128]{4,3,2,1,0:T(8,128)S(1)}, f32[1,3,16,16,128]{4,3,2,1,0:T(8,128)}, u32[]{:S(2)}) copy-start(f32[1,3,16,16,128]{4,3,2,1,0:T(8,128)} %param.6) | copy-start | bytes 1179652
  9.8 0.9 %copy-start.2 = (s32[16,16,128]{2,1,0:T(8,128)S(1)}, s32[16,16,128]{2,1,0:T(8,128)}, u32[]{:S(2)}) copy-start(s32[16,16,128]{2,1,0:T(8,128)} %param.9) | copy-start | bytes 393220
  10.7 6.6 %copy-start.1 = (f32[1,3,16,16,128]{4,3,2,1,0:T(8,128)S(1)}, f32[1,3,16,16,128]{4,3,2,1,0:T(8,128)}, u32[]{:S(2)}) copy-start(f32[1,3,16,16,128]{4,3,2,1,0:T(8,128)} %param.6) | copy-start | bytes 1179652
  12.2 5.0 %collective-permute-start.1 = (s32[16,16,128]{2,1,0:T(8,128)S(1)}, s32[16,16,128]{2,1,0:T(8,128)S(1)}, u32[]{:S(2)}, u32[]{:S(2)}) collective-permute-start(s32[16,16,128]{2,1,0:T(8,128)S(1)} %copy-done.2), channel_id=1, source_target_pairs={{0,1},{1,0},{2,3},{3,2},{4,5},{5,4},{6,7},{7,6},{8,9},{9,8},{10,11... | collective-permute-start | bytes 393224 | tf_op jit(solution)/shard_map/ppermute | solution.py:395
  18.3 16.9 %collective-permute-start.4 = (f32[3,16,16,128]{3,2,1,0:T(8,128)S(1)}, f32[3,16,16,128]{3,2,1,0:T(8,128)S(1)}, u32[]{:S(2)}, u32[]{:S(2)}) collective-permute-start(f32[3,16,16,128]{3,2,1,0:T(8,128)S(1)} %bitcast.24), channel_id=1, source_target_pairs={{0,1},{1,0},{2,3},{3,2},{4,5},{5,4},{6,7},{7,6},{8,9},{9,8},{10,11... | collective-permute-start | bytes 1179656 | tf_op jit(solution)/shard_map/ppermute | solution.py:395
  18.9 1.6 %collective-permute-start.5 = (f32[7,2,8,128]{3,2,1,0:T(8,128)S(1)}, f32[7,2,8,128]{3,2,1,0:T(8,128)S(1)}, u32[]{:S(2)}, u32[]{:S(2)}) collective-permute-start(f32[7,2,8,128]{3,2,1,0:T(8,128)S(1)} %get-tuple-element.27), channel_id=1, source_target_pairs={{0,2},{4,6},{2,0},{6,4},{1,3},{5,7},{3,1},{7,5},{8,10},{12,14},{10... | collective-permute-start | bytes 172040 | tf_op jit(solution)/shard_map/ppermute | solution.py:401
  18.9 16.3 %copy-start.3 = (s32[16,16,128]{2,1,0:T(8,128)S(1)}, s32[16,16,128]{2,1,0:T(8,128)}, u32[]{:S(2)}) copy-start(s32[16,16,128]{2,1,0:T(8,128)} %param.9) | copy-start | bytes 393220
  18.9 3.6 %collective-permute-start.6 = (f32[7,2,8,128]{3,2,1,0:T(8,128)S(1)}, f32[7,2,8,128]{3,2,1,0:T(8,128)S(1)}, u32[]{:S(2)}, u32[]{:S(2)}) collective-permute-start(f32[7,2,8,128]{3,2,1,0:T(8,128)S(1)} %get-tuple-element.28), channel_id=1, source_target_pairs={{2,4},{6,0},{4,2},{0,6},{3,5},{7,1},{5,3},{1,7},{10,12},{14,8},{12... | collective-permute-start | bytes 172040 | tf_op jit(solution)/shard_map/ppermute | solution.py:401
  22.5 12.6 %collective-permute-start.7 = (f32[2,7,2,8,128]{4,3,2,1,0:T(8,128)S(1)}, f32[2,7,2,8,128]{4,3,2,1,0:T(8,128)S(1)}, u32[]{:S(2)}, u32[]{:S(2)}) collective-permute-start(f32[2,7,2,8,128]{4,3,2,1,0:T(8,128)S(1)} %merge_strips.1.strips_ref), channel_id=1, source_target_pairs={{0,1},{1,0},{2,3},{3,2},{4,5},{5,4},{6,7},{7,6},{8,9},{9,8},{10,11... | collective-permute-start | bytes 344072 | tf_op jit(solution)/shard_map/ppermute | solution.py:395

commit v13 on v10

--- a/solution.py
+++ b/solution.py
@@ -112,7 +112,7 @@
     zero = jnp.zeros((SUB, LANES), jnp.float32)
     sums = lax.fori_loop(0, depth // (chunks * SUB), squares, (zero,) * (chunks * COMPS))
     total = jnp.sum(functools.reduce(jnp.add, sums), axis=(0, 1), keepdims=True)
-    slot = lax.broadcasted_iota(jnp.int32, part_ref.shape, 1)
+    slot = lane_iota()
     part_ref[...] = jnp.where((slot == here) & (here > 0), total, 0.0)
     turned = (lax.axis_index("gx") & 1) == 1
     one_ref[COMPS:] = jnp.where(turned, own_left_ref[...], own_right_ref[...])
@@ -163,7 +163,6 @@
     tiles,
     images,
     info_ref,
-    sq_ref,
     m_ref,
     mp_ref,
     n_ref,
@@ -172,17 +171,10 @@
     regp_ref,
     strips_ref,
     stripsp_ref,
-    out_ref,
-    main0,
-    main1,
-    strip0,
-    strip1,
-    edge,
-    seam0,
-    seam1,
-    par,
-    spar,
+    *refs,
 ):
+    *sq_refs, out_ref = refs[:-9]
+    main0, main1, strip0, strip1, edge, seam0, seam1, par, spar = refs[-9:]
     main, strip, seam = (main0, main1), (strip0, strip1), (seam0, seam1)
     window = ny + 2 * DEPTH
     here = lax.axis_index("img")
@@ -198,7 +190,7 @@
 
     lo = info_ref[4]
     slot = lane.astype(jnp.float32)
-    squares = jnp.broadcast_to(jnp.sum(sq_ref[...], axis=0, keepdims=True), (SUB, LANES))
+    squares = functools.reduce(jnp.add, [ref[...] for ref in sq_refs])
     lengths = jnp.where((lane >= 1) & (lane < images), jnp.sqrt(squares + eps), 0.0)
     total = jnp.sum(lengths, axis=1, keepdims=True)
     arc = jnp.sum(jnp.where(slot <= lo, lengths, 0.0), axis=1, keepdims=True)
@@ -386,6 +378,18 @@
     return lax.ppermute(cells, axis, pairs + [(j, i) for i, j in pairs])
 
 
+def paired(cells, axis, step):
+    return lax.ppermute(cells, axis, [(i, i ^ step) for i in range(lax.axis_size(axis))])
+
+
+def paired_sum(part, axis):
+    step = 1
+    while step < lax.axis_size(axis):
+        part = part + paired(part, axis, step)
+        step *= 2
+    return part
+
+
 def around(cells, dim):
     ny = cells.shape[dim]
     if lax.axis_size("gy") == 2:
@@ -408,7 +412,6 @@
     local, comps, nz, ny, nx = magnetization.shape
     images = local * lax.axis_size("img")
     tiles = nz // SUB
-    devices = lax.axis_size(("img", "gx", "gy"))
     assert lax.axis_size("gx") % 2 == 0
     assert local == 1 and comps == COMPS and nx == LANES
     assert ny == 2 * DEPTH and ny * DEPTH == LANES and tiles >= 2
@@ -446,7 +449,7 @@
     part, near, one, two = pl.pallas_call(
         functools.partial(gather_kernel, ny, tiles),
         out_shape=(
-            jax.ShapeDtypeStruct((devices, LANES), f32),
+            jax.ShapeDtypeStruct(vreg, f32),
             jax.ShapeDtypeStruct(flat, f32),
             packed,
             packed,
@@ -459,6 +462,9 @@
     near_p = around(near.reshape(own.shape), 2)
     one = swapped(one, "gx", 0, True)
     two = swapped(two, "gx", 1, True)
+    pairs = [lax.axis_size(axis) for axis in ("img", "gx", "gy")] == [4, 4, 2]
+    if pairs:
+        part, one, two = lax.optimization_barrier((paired_sum(part, "img"), one, two))
     strips = pl.pallas_call(
         merge_kernel,
         out_shape=jax.ShapeDtypeStruct((2,) + packed.shape, f32),
@@ -468,13 +474,17 @@
         name="merge_strips",
     )(one, two)
     strips_p = around_strips(strips)
-    squares = lax.all_to_all(part, ("img", "gx", "gy"), 0, 0, tiled=True)
+    if pairs:
+        part, near_p = lax.optimization_barrier((paired_sum(part, "gx"), near_p))
+        squares = [part, paired(part, "gy", 1)]
+    else:
+        squares = [lax.psum(part, ("img", "gx", "gy"))]
 
     window = ny + 2 * DEPTH
     out = pl.pallas_call(
         functools.partial(evolve_kernel, ny, tiles, images),
         out_shape=jax.ShapeDtypeStruct(flat, f32),
-        in_specs=[vmem] * 10,
+        in_specs=[vmem] * (9 + len(squares)),
         out_specs=vmem,
         scratch_shapes=[
             pltpu.VMEM((comps, window, tiles) + vreg, f32),
@@ -491,7 +501,6 @@
         name="evolve",
     )(
         info,
-        squares,
         own.reshape(flat),
         own_p.reshape(flat),
         near,
@@ -500,6 +509,7 @@
         reg_p.reshape(flat[1:]),
         strips,
         strips_p,
+        *squares,
     )
     return out.reshape(magnetization.shape)
 

time: 49 us -> 52.6 us (1.073)
  blocking collectives: 11.1 us -> 0 us
  waiting for transfers between devices: 6.42 us -> 16.9 us
  starting transfers between devices: 12.4 us -> 16.5 us
    ppermute x0 -> x5, waiting for transfers between devices: none -> 12.5 us  [paired(): lax.ppermute(cells, axis, [(i, i ^ step) for i in range(lax.axis_size(axi...]
    all_to_all x1 -> x0, blocking collectives: 11.1 us -> none  [body(): squares = lax.all_to_all(part, ('img', 'gx', 'gy'), 0, 0, tiled=True)]
    ppermute x0 -> x5, starting transfers between devices: none -> 4.02 us  [paired(): lax.ppermute(cells, axis, [(i, i ^ step) for i in range(lax.axis_size(axi...]
    ppermute x4, waiting for transfers between devices: 1.98 us -> 0.01 us  [swapped(): return lax.ppermute(cells, axis, pairs + [(j, i) for i, j in pairs])]
  transfers between devices with their start and end apart: 8 -> 13, of which waited for: 2 -> 6; matrix products, arithmetic and copies ran while one was open for 0% -> 0% of each run, Pallas kernels for 3% -> 3%
where the time goes in v13:
time: 52.6 us; the launch traced here: 52.4 us
  waiting for transfers between devices  16.9 us (32%)
  starting transfers between devices  16.5 us (31%)
  Pallas kernels  16.4 us (31%)
  local copies, waits for them, and re-layouts  2.6 us (5%)
    pallas_call x1, Pallas kernels, body(): pl.pallas_call(functools.partial(evolve_kernel, ny, tiles, images), out_s...  13.8 us
    ppermute x5, waiting for transfers between devices, paired(): lax.ppermute(cells, axis, [(i, i ^ step) for i in range(lax.axis_size(axi...  12.5 us
    ppermute x4, starting transfers between devices, swapped(): return lax.ppermute(cells, axis, pairs + [(j, i) for i, j in pairs])  6.75 us
    ppermute x4, starting transfers between devices, shifted(): return lax.ppermute(cells, axis, pairs)  5.69 us
    ppermute x4, waiting for transfers between devices, shifted(): return lax.ppermute(cells, axis, pairs)  4.44 us
    ppermute x5, starting transfers between devices, paired(): lax.ppermute(cells, axis, [(i, i ^ step) for i in range(lax.axis_size(axi...  4.02 us
    unnamed x16, local copies, waits for them, and re-layouts  2.6 us
    pallas_call x1, Pallas kernels, body(): pl.pallas_call(functools.partial(pack_kernel, ny, tiles, anisotropy.shape...  1.51 us
  transfers between devices with their start and end apart: 13, of which 6 were waited for; matrix products, arithmetic and copies ran while one was open for 0% of the time, Pallas kernels for 3%

profile of v13, /device:TPU:0, one launch (start us, length us, event | category | flops | bytes accessed | tf_op | source)
XLA Modules:
  0.0 52.4 jit_solution(11523894742651634984)
XLA Ops:
  0.0 2.9 %collective-permute-start = (f32[3,16,16,128]{3,2,1,0:T(8,128)}, f32[3,16,16,128]{3,2,1,0:T(8,128)S(1)}, u32[]{:S(2)}, u32[]{:S(2)}) collective-permute-start(f32[3,16,16,128]{3,2,1,0:T(8,128)} %bitcast.11), channel_id=1, source_target_pairs={{0,1},{1,0},{2,3},{3,2},{4,5},{5,4},{6,7},{7,6},{8,9},{9,8},{10,11... | collective-permute-start | bytes 1179656 | tf_op jit(solution)/shard_map/ppermute | solution.py:372
  2.9 0.7 %collective-permute-start.3 = (f32[3,16,16,128]{3,2,1,0:T(8,128)}, f32[3,16,16,128]{3,2,1,0:T(8,128)S(1)}, u32[]{:S(2)}, u32[]{:S(2)}) collective-permute-start(f32[3,16,16,128]{3,2,1,0:T(8,128)} %bitcast.12), channel_id=1, source_target_pairs={{8,16},{16,8},{9,17},{17,9},{10,18},{18,10},{11,19},{19,11},{12,20... | collective-permute-start | bytes 1179656 | tf_op jit(solution)/shard_map/ppermute | solution.py:378
  3.6 4.4 %collective-permute-start.2 = (f32[3,16,16,128]{3,2,1,0:T(8,128)}, f32[3,16,16,128]{3,2,1,0:T(8,128)S(1)}, u32[]{:S(2)}, u32[]{:S(2)}) collective-permute-start(f32[3,16,16,128]{3,2,1,0:T(8,128)} %bitcast.13), channel_id=1, source_target_pairs={{0,8},{16,24},{8,0},{24,16},{1,9},{17,25},{9,1},{25,17},{2,10},{18... | collective-permute-start | bytes 1179656 | tf_op jit(solution)/shard_map/ppermute | solution.py:378
  8.1 0.0 copy-start.7
  8.1 0.0 copy-start.4
  8.1 0.0 copy-start.5
  8.1 0.0 copy-start.6
  8.1 0.6 %copy-done.7 = f32[3]{0:T(128)S(1)} copy-done((f32[3]{0:T(128)S(1)}, f32[3]{0:T(128)}, u32[]{:S(2)}) %copy-start.7) | copy-done | bytes 36
  8.7 0.0 copy-done.4
  8.7 0.0 copy-done.5
  8.7 0.0 copy-done.6
  8.8 0.0 copy-start
  8.8 1.0 %copy-done = f32[1,3,16,16,128]{4,3,2,1,0:T(8,128)S(1)} copy-done((f32[1,3,16,16,128]{4,3,2,1,0:T(8,128)S(1)}, f32[1,3,16,16,128]{4,3,2,1,0:T(8,128)}, u32[]{:S(2)}) %copy-start) | copy-done | bytes 393240
  9.8 0.0 copy-start.2
  9.8 0.9 %copy-done.2 = s32[16,16,128]{2,1,0:T(8,128)S(1)} copy-done((s32[16,16,128]{2,1,0:T(8,128)S(1)}, s32[16,16,128]{2,1,0:T(8,128)}, u32[]{:S(2)}) %copy-start.2) | copy-done | bytes 131096
  10.7 0.0 copy-start.1
  10.7 1.5 %pack_strips.1 = (f32[4,2,8,128]{3,2,1,0:T(8,128)S(1)}, f32[4,2,8,128]{3,2,1,0:T(8,128)S(1)}, f32[5,8,128]{2,1,0:T(8,128)S(1)}) custom-call(s32[4]{0:T(128)S(1)} %copy-done.4, f32[8]{0:T(128)S(1)} %copy-done.5, f32[8]{0:T(128)S(1)} %copy-done.6, f32[1,3]{1,0:T(1,128)S(1)} %bitcast.25, f32[3,256,128]{2,1,0:T(8,128)S(1)} %bitcast.14, s32[256,128]{1,0:T(8,128)S(1)} %bitcast.17), custom_call_target="tpu_custom_call" | custom-call | tf_op jit(solution)/shard_map/pack_strips/pallas_call | solution.py:430
  12.2 0.6 %collective-permute-start.1 = (s32[16,16,128]{2,1,0:T(8,128)S(1)}, s32[16,16,128]{2,1,0:T(8,128)S(1)}, u32[]{:S(2)}, u32[]{:S(2)}) collective-permute-start(s32[16,16,128]{2,1,0:T(8,128)S(1)} %copy-done.2), channel_id=1, source_target_pairs={{0,1},{1,0},{2,3},{3,2},{4,5},{5,4},{6,7},{7,6},{8,9},{9,8},{10,11... | collective-permute-start | bytes 393224 | tf_op jit(solution)/shard_map/ppermute | solution.py:372
  12.8 4.4 %collective-permute-done.1 = s32[16,16,128]{2,1,0:T(8,128)S(1)} collective-permute-done((s32[16,16,128]{2,1,0:T(8,128)S(1)}, s32[16,16,128]{2,1,0:T(8,128)S(1)}, u32[]{:S(2)}, u32[]{:S(2)}) %collective-permute-start.1) | collective-permute-done | bytes 131104 | tf_op jit(solution)/shard_map/ppermute | solution.py:372
  17.2 0.0 collective-permute-done
  17.2 0.0 collective-permute-done.3
  17.2 0.0 collective-permute-done.2
  17.2 0.0 copy-done.1
  17.2 1.1 %gather_images.1 = (f32[8,128]{1,0:T(8,128)S(1)}, f32[3,256,128]{2,1,0:T(8,128)S(1)}, f32[7,2,8,128]{3,2,1,0:T(8,128)S(1)}, f32[7,2,8,128]{3,2,1,0:T(8,128)S(1)}) custom-call(f32[5,8,128]{2,1,0:T(8,128)S(1)} %get-tuple-element.25.info_ref, f32[3,256,128]{2,1,0:T(8,128)S(1)} %bitcast.15, f32[3,256,128]{2,1,0:T(8,128)S(1)} %bitcast.23, ...), custom_call_target="tpu_custom_call" | custom-call | tf_op jit(solution)/shard_map/gather_images/pallas_call | solution.py:449
  18.3 0.6 %collective-permute-start.10 = (f32[3,16,16,128]{3,2,1,0:T(8,128)S(1)}, f32[3,16,16,128]{3,2,1,0:T(8,128)S(1)}, u32[]{:S(2)}, u32[]{:S(2)}) collective-permute-start(f32[3,16,16,128]{3,2,1,0:T(8,128)S(1)} %bitcast.20), channel_id=1, source_target_pairs={{0,1},{1,0},{2,3},{3,2},{4,5},{5,4},{6,7},{7,6},{8,9},{9,8},{10,11... | collective-permute-start | bytes 1179656 | tf_op jit(solution)/shard_map/ppermute | solution.py:372
  18.9 0.0 collective-permute-start.6
  18.9 1.6 %collective-permute-start.7 = (f32[7,2,8,128]{3,2,1,0:T(8,128)S(1)}, f32[7,2,8,128]{3,2,1,0:T(8,128)S(1)}, u32[]{:S(2)}, u32[]{:S(2)}) collective-permute-start(f32[7,2,8,128]{3,2,1,0:T(8,128)S(1)} %get-tuple-element.32), channel_id=1, source_target_pairs={{2,4},{6,0},{4,2},{0,6},{3,5},{7,1},{5,3},{1,7},{10,12},{14,8},{12... | collective-permute-start | bytes 172040 | tf_op jit(solution)/shard_map/ppermute | solution.py:378
  20.5 1.3 %collective-permute-start.4 = (f32[8,128]{1,0:T(8,128)S(1)}, f32[8,128]{1,0:T(8,128)S(1)}, u32[]{:S(2)}, u32[]{:S(2)}) collective-permute-start(f32[8,128]{1,0:T(8,128)S(1)} %get-tuple-element.30), channel_id=1, source_target_pairs={{0,8},{8,0},{16,24},{24,16},{1,9},{9,1},{17,25},{25,17},{2,10},{10... | collective-permute-start | bytes 12296 | tf_op jit(solution)/shard_map/ppermute | solution.py:382
  21.9 2.3 %collective-permute-done.4 = f32[8,128]{1,0:T(8,128)S(1)} collective-permute-done((f32[8,128]{1,0:T(8,128)S(1)}, f32[8,128]{1,0:T(8,128)S(1)}, u32[]{:S(2)}, u32[]{:S(2)}) %collective-permute-start.4) | collective-permute-done | bytes 4128 | tf_op jit(solution)/shard_map/ppermute | solution.py:382
  24.2 1.7 %collective-permute-start.5 = (f32[8,128]{1,0:T(8,128)S(1)}, f32[8,128]{1,0:T(8,128)S(1)}, u32[]{:S(2)}, u32[]{:S(2)}) collective-permute-start(f32[8,128]{1,0:T(8,128)S(1)} %add.12), channel_id=1, source_target_pairs={{0,16},{8,24},{16,0},{24,8},{1,17},{9,25},{17,1},{25,9},{2,18},{10... | collective-permute-start | bytes 12296 | tf_op jit(solution)/shard_map/ppermute | solution.py:382
  25.8 2.9 %collective-permute-done.5 = f32[8,128]{1,0:T(8,128)S(1)} collective-permute-done((f32[8,128]{1,0:T(8,128)S(1)}, f32[8,128]{1,0:T(8,128)S(1)}, u32[]{:S(2)}, u32[]{:S(2)}) %collective-permute-start.5) | collective-permute-done | bytes 4128 | tf_op jit(solution)/shard_map/ppermute | solution.py:382
  28.7 0.0 copy-start.3
  28.7 0.0 collective-permute-done.6.one_ref
  28.7 0.0 collective-permute-done.7.two_ref
  28.7 1.6 %collective-permute-start.11 = (f32[2,7,2,8,128]{4,3,2,1,0:T(8,128)S(1)}, f32[2,7,2,8,128]{4,3,2,1,0:T(8,128)S(1)}, u32[]{:S(2)}, u32[]{:S(2)}) collective-permute-start(f32[2,7,2,8,128]{4,3,2,1,0:T(8,128)S(1)} %merge_strips.1.strips_ref), channel_id=1, source_target_pairs={{0,1},{1,0},{2,3},{3,2},{4,5},{5,4},{6,7},{7,6},{8,9},{9,8},{10,11... | collective-permute-start | bytes 344072 | tf_op jit(solution)/shard_map/ppermute | solution.py:372
  30.3 0.0 collective-permute-start.8
  30.3 1.2 %collective-permute-done.8 = f32[8,128]{1,0:T(8,128)S(1)} collective-permute-done((f32[8,128]{1,0:T(8,128)S(1)}, f32[8,128]{1,0:T(8,128)S(1)}, u32[]{:S(2)}, u32[]{:S(2)}) %collective-permute-start.8) | collective-permute-done | bytes 4128 | tf_op jit(solution)/shard_map/ppermute | solution.py:382
  31.4 0.5 collective-permute-start.9
  31.9 3.1 %collective-permute-done.9 = f32[8,128]{1,0:T(8,128)S(1)} collective-permute-done((f32[8,128]{1,0:T(8,128)S(1)}, f32[8,128]{1,0:T(8,128)S(1)}, u32[]{:S(2)}, u32[]{:S(2)}) %collective-permute-start.9) | collective-permute-done | bytes 4128 | tf_op jit(solution)/shard_map/ppermute | solution.py:382
  35.1 0.0 collective-permute-done.10
  35.1 0.5 %collective-permute-start.12 = (f32[8,128]{1,0:T(8,128)S(1)}, f32[8,128]{1,0:T(8,128)S(1)}, u32[]{:S(2)}, u32[]{:S(2)}) collective-permute-start(f32[8,128]{1,0:T(8,128)S(1)} %add.15.refs_0_), channel_id=1, source_target_pairs={{0,1},{1,0},{2,3},{3,2},{4,5},{5,4},{6,7},{7,6},{8,9},{9,8},{10,11... | collective-permute-start | bytes 12296 | tf_op jit(solution)/shard_map/ppermute | solution.py:382
  35.6 0.0 collective-permute-done.11.stripsp_ref
  35.6 3.1 %collective-permute-done.12.refs_1_ = f32[8,128]{1,0:T(8,128)S(1)} collective-permute-done((f32[8,128]{1,0:T(8,128)S(1)}, f32[8,128]{1,0:T(8,128)S(1)}, u32[]{:S(2)}, u32[]{:S(2)}) %collective-permute-start.12) | collective-permute-done | bytes 4128 | tf_op jit(solution)/shard_map/ppermute | solution.py:382
  38.7 0.0 copy-done.3
  38.7 13.8 %evolve.1 = f32[3,256,128]{2,1,0:T(8,128)} custom-call(f32[5,8,128]{2,1,0:T(8,128)S(1)} %get-tuple-element.25.info_ref, f32[3,256,128]{2,1,0:T(8,128)S(1)} %bitcast.16, f32[3,256,128]{2,1,0:T(8,128)S(1)} %bitcast.19, f32[3,256,128]{2,1,0:T(8,128)S(1)} %get-tuple-element.29.n_ref, f32[3,256,128]{2,1,0:T(8,128)S(1)} %bitcast.21, s32[256,128]{1,0:T(8,128)S(1)} %bitcast.18, ...), custom_call_target="tpu_custom_call" | custom-call | tf_op jit(solution)/shard_map/evolve/pallas_call | solution.py:484
  (5 shorter events, 0.0 us)
Async XLA Ops:
  0.0 17.2 %collective-permute-start = (f32[3,16,16,128]{3,2,1,0:T(8,128)}, f32[3,16,16,128]{3,2,1,0:T(8,128)S(1)}, u32[]{:S(2)}, u32[]{:S(2)}) collective-permute-start(f32[3,16,16,128]{3,2,1,0:T(8,128)} %bitcast.11), channel_id=1, source_target_pairs={{0,1},{1,0},{2,3},{3,2},{4,5},{5,4},{6,7},{7,6},{8,9},{9,8},{10,11... | collective-permute-start | bytes 1179656 | tf_op jit(solution)/shard_map/ppermute | solution.py:372
  2.9 14.3 %collective-permute-start.3 = (f32[3,16,16,128]{3,2,1,0:T(8,128)}, f32[3,16,16,128]{3,2,1,0:T(8,128)S(1)}, u32[]{:S(2)}, u32[]{:S(2)}) collective-permute-start(f32[3,16,16,128]{3,2,1,0:T(8,128)} %bitcast.12), channel_id=1, source_target_pairs={{8,16},{16,8},{9,17},{17,9},{10,18},{18,10},{11,19},{19,11},{12,20... | collective-permute-start | bytes 1179656 | tf_op jit(solution)/shard_map/ppermute | solution.py:378
  3.6 13.6 %collective-permute-start.2 = (f32[3,16,16,128]{3,2,1,0:T(8,128)}, f32[3,16,16,128]{3,2,1,0:T(8,128)S(1)}, u32[]{:S(2)}, u32[]{:S(2)}) collective-permute-start(f32[3,16,16,128]{3,2,1,0:T(8,128)} %bitcast.13), channel_id=1, source_target_pairs={{0,8},{16,24},{8,0},{24,16},{1,9},{17,25},{9,1},{25,17},{2,10},{18... | collective-permute-start | bytes 1179656 | tf_op jit(solution)/shard_map/ppermute | solution.py:378
  8.1 0.7 %copy-start.7 = (f32[3]{0:T(128)S(1)}, f32[3]{0:T(128)}, u32[]{:S(2)}) copy-start(f32[3]{0:T(128)} %param.8) | copy-start | bytes 40
  8.1 0.7 %copy-start.4 = (s32[4]{0:T(128)S(1)}, s32[4]{0:T(128)}, u32[]{:S(2)}) copy-start(s32[4]{0:T(128)} %lower_ref.1) | copy-start | bytes 52
  8.1 0.7 %copy-start.5 = (f32[8]{0:T(128)S(1)}, f32[8]{0:T(128)}, u32[]{:S(2)}) copy-start(f32[8]{0:T(128)} %aniso_ref.1) | copy-start | bytes 100
  8.1 0.7 %copy-start.6 = (f32[8]{0:T(128)S(1)}, f32[8]{0:T(128)}, u32[]{:S(2)}) copy-start(f32[8]{0:T(128)} %damp_ref.1) | copy-start | bytes 100
  8.8 1.0 %copy-start = (f32[1,3,16,16,128]{4,3,2,1,0:T(8,128)S(1)}, f32[1,3,16,16,128]{4,3,2,1,0:T(8,128)}, u32[]{:S(2)}) copy-start(f32[1,3,16,16,128]{4,3,2,1,0:T(8,128)} %param.6) | copy-start | bytes 1179652
  9.8 0.9 %copy-start.2 = (s32[16,16,128]{2,1,0:T(8,128)S(1)}, s32[16,16,128]{2,1,0:T(8,128)}, u32[]{:S(2)}) copy-start(s32[16,16,128]{2,1,0:T(8,128)} %param.9) | copy-start | bytes 393220
  10.7 6.6 %copy-start.1 = (f32[1,3,16,16,128]{4,3,2,1,0:T(8,128)S(1)}, f32[1,3,16,16,128]{4,3,2,1,0:T(8,128)}, u32[]{:S(2)}) copy-start(f32[1,3,16,16,128]{4,3,2,1,0:T(8,128)} %param.6) | copy-start | bytes 1179652
  12.2 5.0 %collective-permute-start.1 = (s32[16,16,128]{2,1,0:T(8,128)S(1)}, s32[16,16,128]{2,1,0:T(8,128)S(1)}, u32[]{:S(2)}, u32[]{:S(2)}) collective-permute-start(s32[16,16,128]{2,1,0:T(8,128)S(1)} %copy-done.2), channel_id=1, source_target_pairs={{0,1},{1,0},{2,3},{3,2},{4,5},{5,4},{6,7},{7,6},{8,9},{9,8},{10,11... | collective-permute-start | bytes 393224 | tf_op jit(solution)/shard_map/ppermute | solution.py:372
  18.3 16.7 %collective-permute-start.10 = (f32[3,16,16,128]{3,2,1,0:T(8,128)S(1)}, f32[3,16,16,128]{3,2,1,0:T(8,128)S(1)}, u32[]{:S(2)}, u32[]{:S(2)}) collective-permute-start(f32[3,16,16,128]{3,2,1,0:T(8,128)S(1)} %bitcast.20), channel_id=1, source_target_pairs={{0,1},{1,0},{2,3},{3,2},{4,5},{5,4},{6,7},{7,6},{8,9},{9,8},{10,11... | collective-permute-start | bytes 1179656 | tf_op jit(solution)/shard_map/ppermute | solution.py:372
  18.9 9.8 %collective-permute-start.6 = (f32[7,2,8,128]{3,2,1,0:T(8,128)S(1)}, f32[7,2,8,128]{3,2,1,0:T(8,128)S(1)}, u32[]{:S(2)}, u32[]{:S(2)}) collective-permute-start(f32[7,2,8,128]{3,2,1,0:T(8,128)S(1)} %get-tuple-element.31), channel_id=1, source_target_pairs={{0,2},{4,6},{2,0},{6,4},{1,3},{5,7},{3,1},{7,5},{8,10},{12,14},{10... | collective-permute-start | bytes 172040 | tf_op jit(solution)/shard_map/ppermute | solution.py:378
  18.9 9.8 %collective-permute-start.7 = (f32[7,2,8,128]{3,2,1,0:T(8,128)S(1)}, f32[7,2,8,128]{3,2,1,0:T(8,128)S(1)}, u32[]{:S(2)}, u32[]{:S(2)}) collective-permute-start(f32[7,2,8,128]{3,2,1,0:T(8,128)S(1)} %get-tuple-element.32), channel_id=1, source_target_pairs={{2,4},{6,0},{4,2},{0,6},{3,5},{7,1},{5,3},{1,7},{10,12},{14,8},{12... | collective-permute-start | bytes 172040 | tf_op jit(solution)/shard_map/ppermute | solution.py:378
  20.5 3.6 %collective-permute-start.4 = (f32[8,128]{1,0:T(8,128)S(1)}, f32[8,128]{1,0:T(8,128)S(1)}, u32[]{:S(2)}, u32[]{:S(2)}) collective-permute-start(f32[8,128]{1,0:T(8,128)S(1)} %get-tuple-element.30), channel_id=1, source_target_pairs={{0,8},{8,0},{16,24},{24,16},{1,9},{9,1},{17,25},{25,17},{2,10},{10... | collective-permute-start | bytes 12296 | tf_op jit(solution)/shard_map/ppermute | solution.py:382
  24.2 4.5 %collective-permute-start.5 = (f32[8,128]{1,0:T(8,128)S(1)}, f32[8,128]{1,0:T(8,128)S(1)}, u32[]{:S(2)}, u32[]{:S(2)}) collective-permute-start(f32[8,128]{1,0:T(8,128)S(1)} %add.12), channel_id=1, source_target_pairs={{0,16},{8,24},{16,0},{24,8},{1,17},{9,25},{17,1},{25,9},{2,18},{10... | collective-permute-start | bytes 12296 | tf_op jit(solution)/shard_map/ppermute | solution.py:382
  28.7 10.0 %copy-start.3 = (s32[16,16,128]{2,1,0:T(8,128)S(1)}, s32[16,16,128]{2,1,0:T(8,128)}, u32[]{:S(2)}) copy-start(s32[16,16,128]{2,1,0:T(8,128)} %param.9) | copy-start | bytes 393220
  28.7 6.9 %collective-permute-start.11 = (f32[2,7,2,8,128]{4,3,2,1,0:T(8,128)S(1)}, f32[2,7,2,8,128]{4,3,2,1,0:T(8,128)S(1)}, u32[]{:S(2)}, u32[]{:S(2)}) collective-permute-start(f32[2,7,2,8,128]{4,3,2,1,0:T(8,128)S(1)} %merge_strips.1.strips_ref), channel_id=1, source_target_pairs={{0,1},{1,0},{2,3},{3,2},{4,5},{5,4},{6,7},{7,6},{8,9},{9,8},{10,11... | collective-permute-start | bytes 344072 | tf_op jit(solution)/shard_map/ppermute | solution.py:372
  30.3 1.2 %collective-permute-start.8 = (f32[8,128]{1,0:T(8,128)S(1)}, f32[8,128]{1,0:T(8,128)S(1)}, u32[]{:S(2)}, u32[]{:S(2)}) collective-permute-start(f32[8,128]{1,0:T(8,128)S(1)} %add.13), channel_id=1, source_target_pairs={{0,2},{2,0},{4,6},{6,4},{1,3},{3,1},{5,7},{7,5},{8,10},{10,8},{12,... | collective-permute-start | bytes 12296 | tf_op jit(solution)/shard_map/ppermute | solution.py:382
  31.4 3.6 %collective-permute-start.9 = (f32[8,128]{1,0:T(8,128)S(1)}, f32[8,128]{1,0:T(8,128)S(1)}, u32[]{:S(2)}, u32[]{:S(2)}) collective-permute-start(f32[8,128]{1,0:T(8,128)S(1)} %add.14), channel_id=1, source_target_pairs={{0,4},{2,6},{4,0},{6,2},{1,5},{3,7},{5,1},{7,3},{8,12},{10,14},{12... | collective-permute-start | bytes 12296 | tf_op jit(solution)/shard_map/ppermute | solution.py:382
  35.1 3.6 %collective-permute-start.12 = (f32[8,128]{1,0:T(8,128)S(1)}, f32[8,128]{1,0:T(8,128)S(1)}, u32[]{:S(2)}, u32[]{:S(2)}) collective-permute-start(f32[8,128]{1,0:T(8,128)S(1)} %add.15.refs_0_), channel_id=1, source_target_pairs={{0,1},{1,0},{2,3},{3,2},{4,5},{5,4},{6,7},{7,6},{8,9},{9,8},{10,11... | collective-permute-start | bytes 12296 | tf_op jit(solution)/shard_map/ppermute | solution.py:382

commit v14 on v10

--- a/solution.py
+++ b/solution.py
@@ -167,7 +167,8 @@
     m_ref,
     mp_ref,
     n_ref,
-    np_ref,
+    np1_ref,
+    np2_ref,
     reg_ref,
     regp_ref,
     strips_ref,
@@ -196,6 +197,7 @@
     top = sub == SUB - 1
     bottom = sub == 0
 
+    pick, _ = take_first(info_ref, here)
     lo = info_ref[4]
     slot = lane.astype(jnp.float32)
     squares = jnp.broadcast_to(jnp.sum(sq_ref[...], axis=0, keepdims=True), (SUB, LANES))
@@ -219,15 +221,16 @@
 
     def fill(k, carry):
         done = []
-        for g, (own, near, reg) in enumerate(((m_ref, n_ref, reg_ref), (mp_ref, np_ref, regp_ref))):
+        for g, (own, reg) in enumerate(((m_ref, reg_ref), (mp_ref, regp_ref))):
             for t in range(tiles):
                 rows = rows_at(ny, tiles, k, t)
-                v = normal(
-                    [
-                        w_own * own[c, rows, :] + w_near * near[c, rows, :]
-                        for c in range(COMPS)
+                if g == 0:
+                    near = [n_ref[c, rows, :] for c in range(COMPS)]
+                else:
+                    near = [
+                        jnp.where(pick, np1_ref[c, rows, :], np2_ref[c, rows, :]) for c in range(COMPS)
                     ]
-                )
+                v = normal([w_own * own[c, rows, :] + w_near * near[c] for c in range(COMPS)])
                 done.append((g * ny + k, t, v, params(reg[rows, :])))
         for r, t, v, p in done:
             for c in range(COMPS):
@@ -441,7 +444,9 @@
     )
     late_regions, info = lax.optimization_barrier((regions, info))
     reg_p = around(late_regions, 1)
-    info, own_p, reg_p = lax.optimization_barrier((info, own_p, reg_p))
+    own_p, info = lax.optimization_barrier((own_p, info))
+    first_p = swapped(own_p, "img", 0, False)
+    second_p = swapped(own_p, "img", 1, False)
     packed = jax.ShapeDtypeStruct((2 * comps + 1, tiles) + vreg, f32)
     part, near, one, two = pl.pallas_call(
         functools.partial(gather_kernel, ny, tiles),
@@ -456,9 +461,9 @@
         compiler_params=limit,
         name="gather_images",
     )(info, own.reshape(flat), first.reshape(flat), second.reshape(flat), left, right)
-    near_p = around(near.reshape(own.shape), 2)
     one = swapped(one, "gx", 0, True)
     two = swapped(two, "gx", 1, True)
+    one, reg_p = lax.optimization_barrier((one, reg_p))
     strips = pl.pallas_call(
         merge_kernel,
         out_shape=jax.ShapeDtypeStruct((2,) + packed.shape, f32),
@@ -474,7 +479,7 @@
     out = pl.pallas_call(
         functools.partial(evolve_kernel, ny, tiles, images),
         out_shape=jax.ShapeDtypeStruct(flat, f32),
-        in_specs=[vmem] * 10,
+        in_specs=[vmem] * 11,
         out_specs=vmem,
         scratch_shapes=[
             pltpu.VMEM((comps, window, tiles) + vreg, f32),
@@ -495,7 +500,8 @@
         own.reshape(flat),
         own_p.reshape(flat),
         near,
-        near_p.reshape(flat),
+        first_p.reshape(flat),
+        second_p.reshape(flat),
         regions.reshape(flat[1:]),
         reg_p.reshape(flat[1:]),
         strips,

time: 49 us -> 50.2 us (1.024)
  starting transfers between devices: 12.4 us -> 17.2 us
  waiting for transfers between devices: 6.42 us -> 2.62 us
  Pallas kernels: 16.2 us -> 17.7 us
  local copies, waits for them, and re-layouts: 2.6 us -> 1.7 us
    ppermute x4 -> x6, starting transfers between devices: 6.75 us -> 12.2 us  [swapped(): return lax.ppermute(cells, axis, pairs + [(j, i) for i, j in pairs])]
    ppermute x4 -> x3, waiting for transfers between devices: 4.44 us -> 1.48 us  [shifted(): return lax.ppermute(cells, axis, pairs)]
    pallas_call x1, Pallas kernels: 13.6 us -> 14.7 us  [body(): pl.pallas_call(functools.partial(evolve_kernel, ny, tiles, images), out_s...]
    unnamed x16 -> x12, local copies, waits for them, and re-layouts: 2.6 us -> 1.7 us
    ppermute x4 -> x6, waiting for transfers between devices: 1.98 us -> 1.14 us  [swapped(): return lax.ppermute(cells, axis, pairs + [(j, i) for i, j in pairs])]
    ppermute x4 -> x3, starting transfers between devices: 5.69 us -> 5.03 us  [shifted(): return lax.ppermute(cells, axis, pairs)]
  transfers between devices with their start and end apart: 8 -> 9, of which waited for: 2 -> 3; matrix products, arithmetic and copies ran while one was open for 0% -> 0% of each run, Pallas kernels for 3% -> 6%
where the time goes in v14:
time: 50.2 us; the launch traced here: 49.9 us
  Pallas kernels  17.7 us (35%)
  starting transfers between devices  17.2 us (34%)
  blocking collectives  10.7 us (21%)
  waiting for transfers between devices  2.62 us (5%)
  local copies, waits for them, and re-layouts  1.7 us (3%)
    pallas_call x1, Pallas kernels, body(): pl.pallas_call(functools.partial(evolve_kernel, ny, tiles, images), out_s...  14.7 us
    ppermute x6, starting transfers between devices, swapped(): return lax.ppermute(cells, axis, pairs + [(j, i) for i, j in pairs])  12.2 us
    all_to_all x1, blocking collectives, body(): squares = lax.all_to_all(part, ('img', 'gx', 'gy'), 0, 0, tiled=True)  10.7 us
    ppermute x3, starting transfers between devices, shifted(): return lax.ppermute(cells, axis, pairs)  5.03 us
    pallas_call x1, Pallas kernels, body(): pl.pallas_call(functools.partial(pack_kernel, ny, tiles, anisotropy.shape...  1.93 us
    unnamed x12, local copies, waits for them, and re-layouts  1.7 us
    ppermute x3, waiting for transfers between devices, shifted(): return lax.ppermute(cells, axis, pairs)  1.48 us
    ppermute x6, waiting for transfers between devices, swapped(): return lax.ppermute(cells, axis, pairs + [(j, i) for i, j in pairs])  1.14 us
  transfers between devices with their start and end apart: 9, of which 3 were waited for; matrix products, arithmetic and copies ran while one was open for 0% of the time, Pallas kernels for 6%

profile of v14, /device:TPU:0, one launch (start us, length us, event | category | flops | bytes accessed | tf_op | source)
XLA Modules:
  0.0 49.9 jit_solution(1016099631332589539)
XLA Ops:
  0.0 2.9 %collective-permute-start = (f32[3,16,16,128]{3,2,1,0:T(8,128)}, f32[3,16,16,128]{3,2,1,0:T(8,128)S(1)}, u32[]{:S(2)}, u32[]{:S(2)}) collective-permute-start(f32[3,16,16,128]{3,2,1,0:T(8,128)} %bitcast.15), channel_id=1, source_target_pairs={{0,1},{1,0},{2,3},{3,2},{4,5},{5,4},{6,7},{7,6},{8,9},{9,8},{10,11... | collective-permute-start | bytes 1179656 | tf_op jit(solution)/shard_map/ppermute | solution.py:383
  2.9 0.7 %collective-permute-start.2 = (f32[3,16,16,128]{3,2,1,0:T(8,128)}, f32[3,16,16,128]{3,2,1,0:T(8,128)S(1)}, u32[]{:S(2)}, u32[]{:S(2)}) collective-permute-start(f32[3,16,16,128]{3,2,1,0:T(8,128)} %bitcast.16), channel_id=1, source_target_pairs={{8,16},{16,8},{9,17},{17,9},{10,18},{18,10},{11,19},{19,11},{12,20... | collective-permute-start | bytes 1179656 | tf_op jit(solution)/shard_map/ppermute | solution.py:389
  3.6 4.4 %collective-permute-start.1 = (f32[3,16,16,128]{3,2,1,0:T(8,128)}, f32[3,16,16,128]{3,2,1,0:T(8,128)S(1)}, u32[]{:S(2)}, u32[]{:S(2)}) collective-permute-start(f32[3,16,16,128]{3,2,1,0:T(8,128)} %bitcast.17), channel_id=1, source_target_pairs={{0,8},{16,24},{8,0},{24,16},{1,9},{17,25},{9,1},{25,17},{2,10},{18... | collective-permute-start | bytes 1179656 | tf_op jit(solution)/shard_map/ppermute | solution.py:389
  8.1 0.0 copy-start.5
  8.1 0.0 copy-start.2
  8.1 0.0 copy-start.3
  8.1 0.0 copy-start.4
  8.1 0.6 %copy-done.5 = f32[3]{0:T(128)S(1)} copy-done((f32[3]{0:T(128)S(1)}, f32[3]{0:T(128)}, u32[]{:S(2)}) %copy-start.5) | copy-done | bytes 36
  8.7 0.0 copy-done.2
  8.7 0.0 copy-done.3
  8.7 0.0 copy-done.4
  8.8 0.0 copy-start
  8.8 1.0 %copy-done = f32[1,3,16,16,128]{4,3,2,1,0:T(8,128)S(1)} copy-done((f32[1,3,16,16,128]{4,3,2,1,0:T(8,128)S(1)}, f32[1,3,16,16,128]{4,3,2,1,0:T(8,128)}, u32[]{:S(2)}) %copy-start) | copy-done | bytes 393240
  9.8 0.0 copy-start.1
  9.8 1.9 %pack_strips.1 = (f32[4,2,8,128]{3,2,1,0:T(8,128)S(1)}, f32[4,2,8,128]{3,2,1,0:T(8,128)S(1)}, f32[5,8,128]{2,1,0:T(8,128)S(1)}) custom-call(s32[4]{0:T(128)S(1)} %copy-done.2, f32[8]{0:T(128)S(1)} %copy-done.3, f32[8]{0:T(128)S(1)} %copy-done.4, f32[1,3]{1,0:T(1,128)S(1)} %bitcast.29, f32[3,256,128]{2,1,0:T(8,128)S(1)} %bitcast.18, s32[256,128]{1,0:T(8,128)} %bitcast.3.reg_ref), custom_call_target="tpu_custom_call" | custom-call | tf_op jit(solution)/shard_map/pack_strips/pallas_call | solution.py:430
  11.7 0.6 %collective-permute-done = f32[3,16,16,128]{3,2,1,0:T(8,128)S(1)} collective-permute-done((f32[3,16,16,128]{3,2,1,0:T(8,128)}, f32[3,16,16,128]{3,2,1,0:T(8,128)S(1)}, u32[]{:S(2)}, u32[]{:S(2)}) %collective-permute-start) | collective-permute-done | bytes 393248 | tf_op jit(solution)/shard_map/ppermute | solution.py:383
  12.3 0.7 %collective-permute-start.4 = (f32[3,16,16,128]{3,2,1,0:T(8,128)S(1)}, f32[3,16,16,128]{3,2,1,0:T(8,128)S(1)}, u32[]{:S(2)}, u32[]{:S(2)}) collective-permute-start(f32[3,16,16,128]{3,2,1,0:T(8,128)S(1)} %collective-permute-done), channel_id=1, source_target_pairs={{8,16},{16,8},{9,17},{17,9},{10,18},{18,10},{11,19},{19,11},{12,20... | collective-permute-start | bytes 1179656 | tf_op jit(solution)/shard_map/ppermute | solution.py:389
  12.9 4.7 %collective-permute-start.3 = (f32[3,16,16,128]{3,2,1,0:T(8,128)S(1)}, f32[3,16,16,128]{3,2,1,0:T(8,128)S(1)}, u32[]{:S(2)}, u32[]{:S(2)}) collective-permute-start(f32[3,16,16,128]{3,2,1,0:T(8,128)S(1)} %collective-permute-done), channel_id=1, source_target_pairs={{0,8},{16,24},{8,0},{24,16},{1,9},{17,25},{9,1},{25,17},{2,10},{18... | collective-permute-start | bytes 1179656 | tf_op jit(solution)/shard_map/ppermute | solution.py:389
  17.6 1.5 %collective-permute-start.6 = (s32[16,16,128]{2,1,0:T(8,128)}, s32[16,16,128]{2,1,0:T(8,128)S(1)}, u32[]{:S(2)}, u32[]{:S(2)}) collective-permute-start(s32[16,16,128]{2,1,0:T(8,128)} %param.9), channel_id=1, source_target_pairs={{0,1},{1,0},{2,3},{3,2},{4,5},{5,4},{6,7},{7,6},{8,9},{9,8},{10,11... | collective-permute-start | bytes 393224 | tf_op jit(solution)/shard_map/ppermute | solution.py:383
  19.1 0.0 collective-permute-done.2
  19.1 0.0 collective-permute-done.1
  19.1 0.0 copy-done.1
  19.1 1.1 %gather_images.1 = (f32[32,128]{1,0:T(8,128)S(1)}, f32[3,256,128]{2,1,0:T(8,128)S(1)}, f32[7,2,8,128]{3,2,1,0:T(8,128)S(1)}, f32[7,2,8,128]{3,2,1,0:T(8,128)S(1)}) custom-call(f32[5,8,128]{2,1,0:T(8,128)S(1)} %get-tuple-element.20.info_ref, f32[3,256,128]{2,1,0:T(8,128)S(1)} %bitcast.19, f32[3,256,128]{2,1,0:T(8,128)S(1)} %bitcast.22, ...), custom_call_target="tpu_custom_call" | custom-call | tf_op jit(solution)/shard_map/gather_images/pallas_call | solution.py:451
  20.2 0.1 collective-permute-start.5
  20.3 1.6 %collective-permute-start.7 = (f32[7,2,8,128]{3,2,1,0:T(8,128)S(1)}, f32[7,2,8,128]{3,2,1,0:T(8,128)S(1)}, u32[]{:S(2)}, u32[]{:S(2)}) collective-permute-start(f32[7,2,8,128]{3,2,1,0:T(8,128)S(1)} %get-tuple-element.30), channel_id=1, source_target_pairs={{2,4},{6,0},{4,2},{0,6},{3,5},{7,1},{5,3},{1,7},{10,12},{14,8},{12... | collective-permute-start | bytes 172040 | tf_op jit(solution)/shard_map/ppermute | solution.py:389
  21.9 0.9 %collective-permute-done.6 = s32[16,16,128]{2,1,0:T(8,128)S(1)} collective-permute-done((s32[16,16,128]{2,1,0:T(8,128)}, s32[16,16,128]{2,1,0:T(8,128)S(1)}, u32[]{:S(2)}, u32[]{:S(2)}) %collective-permute-start.6) | collective-permute-done | bytes 131104 | tf_op jit(solution)/shard_map/ppermute | solution.py:383
  22.8 0.0 collective-permute-done.5.one_ref
  22.8 1.1 %collective-permute-done.7.two_ref = f32[7,2,8,128]{3,2,1,0:T(8,128)S(1)} collective-permute-done((f32[7,2,8,128]{3,2,1,0:T(8,128)S(1)}, f32[7,2,8,128]{3,2,1,0:T(8,128)S(1)}, u32[]{:S(2)}, u32[]{:S(2)}) %collective-permute-start.7) | collective-permute-done | bytes 57376 | tf_op jit(solution)/shard_map/ppermute | solution.py:389
  24.0 0.6 %collective-permute-start.8 = (f32[2,7,2,8,128]{4,3,2,1,0:T(8,128)S(1)}, f32[2,7,2,8,128]{4,3,2,1,0:T(8,128)S(1)}, u32[]{:S(2)}, u32[]{:S(2)}) collective-permute-start(f32[2,7,2,8,128]{4,3,2,1,0:T(8,128)S(1)} %merge_strips.1.strips_ref), channel_id=1, source_target_pairs={{0,1},{1,0},{2,3},{3,2},{4,5},{5,4},{6,7},{7,6},{8,9},{9,8},{10,11... | collective-permute-start | bytes 344072 | tf_op jit(solution)/shard_map/ppermute | solution.py:383
  24.6 10.7 %all_to_all.11 = f32[32,1,128]{2,1,0:T(1,128)S(1)} all-to-all(f32[32,1,128]{2,1,0:T(1,128)S(1)} %bitcast.28), channel_id=1, replica_groups=mesh['img'=4,'gx'=4,'gy'=2] {'img','gx','gy'}, dimensions={0} | all-to-all | bytes 32768 | tf_op jit(solution)/shard_map/all_to_all | solution.py:476
  35.2 0.0 collective-permute-done.8.stripsp_ref
  35.2 0.0 collective-permute-done.4
  35.2 0.0 collective-permute-done.3
  35.2 14.7 %evolve.1 = f32[3,256,128]{2,1,0:T(8,128)} custom-call(f32[5,8,128]{2,1,0:T(8,128)S(1)} %get-tuple-element.20.info_ref, f32[32,128]{1,0:T(8,128)S(1)} %bitcast.27, f32[3,256,128]{2,1,0:T(8,128)S(1)} %bitcast.20, f32[3,256,128]{2,1,0:T(8,128)S(1)} %bitcast.23, f32[3,256,128]{2,1,0:T(8,128)S(1)} %get-tuple-element.25.n_ref, f32[3,256,128]{2,1,0:T(8,128)S(1)} %bitcast.25, ...), custom_call_target="tpu_custom_call" | custom-call | tf_op jit(solution)/shard_map/evolve/pallas_call | solution.py:479
  (1 shorter events, 0.0 us)
Async XLA Ops:
  0.0 12.3 %collective-permute-start = (f32[3,16,16,128]{3,2,1,0:T(8,128)}, f32[3,16,16,128]{3,2,1,0:T(8,128)S(1)}, u32[]{:S(2)}, u32[]{:S(2)}) collective-permute-start(f32[3,16,16,128]{3,2,1,0:T(8,128)} %bitcast.15), channel_id=1, source_target_pairs={{0,1},{1,0},{2,3},{3,2},{4,5},{5,4},{6,7},{7,6},{8,9},{9,8},{10,11... | collective-permute-start | bytes 1179656 | tf_op jit(solution)/shard_map/ppermute | solution.py:383
  2.9 16.2 %collective-permute-start.2 = (f32[3,16,16,128]{3,2,1,0:T(8,128)}, f32[3,16,16,128]{3,2,1,0:T(8,128)S(1)}, u32[]{:S(2)}, u32[]{:S(2)}) collective-permute-start(f32[3,16,16,128]{3,2,1,0:T(8,128)} %bitcast.16), channel_id=1, source_target_pairs={{8,16},{16,8},{9,17},{17,9},{10,18},{18,10},{11,19},{19,11},{12,20... | collective-permute-start | bytes 1179656 | tf_op jit(solution)/shard_map/ppermute | solution.py:389
  3.6 15.5 %collective-permute-start.1 = (f32[3,16,16,128]{3,2,1,0:T(8,128)}, f32[3,16,16,128]{3,2,1,0:T(8,128)S(1)}, u32[]{:S(2)}, u32[]{:S(2)}) collective-permute-start(f32[3,16,16,128]{3,2,1,0:T(8,128)} %bitcast.17), channel_id=1, source_target_pairs={{0,8},{16,24},{8,0},{24,16},{1,9},{17,25},{9,1},{25,17},{2,10},{18... | collective-permute-start | bytes 1179656 | tf_op jit(solution)/shard_map/ppermute | solution.py:389
  8.1 0.7 %copy-start.5 = (f32[3]{0:T(128)S(1)}, f32[3]{0:T(128)}, u32[]{:S(2)}) copy-start(f32[3]{0:T(128)} %param.8) | copy-start | bytes 40
  8.1 0.7 %copy-start.2 = (s32[4]{0:T(128)S(1)}, s32[4]{0:T(128)}, u32[]{:S(2)}) copy-start(s32[4]{0:T(128)} %lower_ref.1) | copy-start | bytes 52
  8.1 0.7 %copy-start.3 = (f32[8]{0:T(128)S(1)}, f32[8]{0:T(128)}, u32[]{:S(2)}) copy-start(f32[8]{0:T(128)} %aniso_ref.1) | copy-start | bytes 100
  8.1 0.7 %copy-start.4 = (f32[8]{0:T(128)S(1)}, f32[8]{0:T(128)}, u32[]{:S(2)}) copy-start(f32[8]{0:T(128)} %damp_ref.1) | copy-start | bytes 100
  8.8 1.0 %copy-start = (f32[1,3,16,16,128]{4,3,2,1,0:T(8,128)S(1)}, f32[1,3,16,16,128]{4,3,2,1,0:T(8,128)}, u32[]{:S(2)}) copy-start(f32[1,3,16,16,128]{4,3,2,1,0:T(8,128)} %param.6) | copy-start | bytes 1179652
  9.8 9.4 %copy-start.1 = (f32[1,3,16,16,128]{4,3,2,1,0:T(8,128)S(1)}, f32[1,3,16,16,128]{4,3,2,1,0:T(8,128)}, u32[]{:S(2)}) copy-start(f32[1,3,16,16,128]{4,3,2,1,0:T(8,128)} %param.6) | copy-start | bytes 1179652
  12.3 23.0 %collective-permute-start.4 = (f32[3,16,16,128]{3,2,1,0:T(8,128)S(1)}, f32[3,16,16,128]{3,2,1,0:T(8,128)S(1)}, u32[]{:S(2)}, u32[]{:S(2)}) collective-permute-start(f32[3,16,16,128]{3,2,1,0:T(8,128)S(1)} %collective-permute-done), channel_id=1, source_target_pairs={{8,16},{16,8},{9,17},{17,9},{10,18},{18,10},{11,19},{19,11},{12,20... | collective-permute-start | bytes 1179656 | tf_op jit(solution)/shard_map/ppermute | solution.py:389
  12.9 22.3 %collective-permute-start.3 = (f32[3,16,16,128]{3,2,1,0:T(8,128)S(1)}, f32[3,16,16,128]{3,2,1,0:T(8,128)S(1)}, u32[]{:S(2)}, u32[]{:S(2)}) collective-permute-start(f32[3,16,16,128]{3,2,1,0:T(8,128)S(1)} %collective-permute-done), channel_id=1, source_target_pairs={{0,8},{16,24},{8,0},{24,16},{1,9},{17,25},{9,1},{25,17},{2,10},{18... | collective-permute-start | bytes 1179656 | tf_op jit(solution)/shard_map/ppermute | solution.py:389
  17.6 5.2 %collective-permute-start.6 = (s32[16,16,128]{2,1,0:T(8,128)}, s32[16,16,128]{2,1,0:T(8,128)S(1)}, u32[]{:S(2)}, u32[]{:S(2)}) collective-permute-start(s32[16,16,128]{2,1,0:T(8,128)} %param.9), channel_id=1, source_target_pairs={{0,1},{1,0},{2,3},{3,2},{4,5},{5,4},{6,7},{7,6},{8,9},{9,8},{10,11... | collective-permute-start | bytes 393224 | tf_op jit(solution)/shard_map/ppermute | solution.py:383
  20.2 2.6 %collective-permute-start.5 = (f32[7,2,8,128]{3,2,1,0:T(8,128)S(1)}, f32[7,2,8,128]{3,2,1,0:T(8,128)S(1)}, u32[]{:S(2)}, u32[]{:S(2)}) collective-permute-start(f32[7,2,8,128]{3,2,1,0:T(8,128)S(1)} %get-tuple-element.26), channel_id=1, source_target_pairs={{0,2},{4,6},{2,0},{6,4},{1,3},{5,7},{3,1},{7,5},{8,10},{12,14},{10... | collective-permute-start | bytes 172040 | tf_op jit(solution)/shard_map/ppermute | solution.py:389
  20.3 3.7 %collective-permute-start.7 = (f32[7,2,8,128]{3,2,1,0:T(8,128)S(1)}, f32[7,2,8,128]{3,2,1,0:T(8,128)S(1)}, u32[]{:S(2)}, u32[]{:S(2)}) collective-permute-start(f32[7,2,8,128]{3,2,1,0:T(8,128)S(1)} %get-tuple-element.30), channel_id=1, source_target_pairs={{2,4},{6,0},{4,2},{0,6},{3,5},{7,1},{5,3},{1,7},{10,12},{14,8},{12... | collective-permute-start | bytes 172040 | tf_op jit(solution)/shard_map/ppermute | solution.py:389
  24.0 11.3 %collective-permute-start.8 = (f32[2,7,2,8,128]{4,3,2,1,0:T(8,128)S(1)}, f32[2,7,2,8,128]{4,3,2,1,0:T(8,128)S(1)}, u32[]{:S(2)}, u32[]{:S(2)}) collective-permute-start(f32[2,7,2,8,128]{4,3,2,1,0:T(8,128)S(1)} %merge_strips.1.strips_ref), channel_id=1, source_target_pairs={{0,1},{1,0},{2,3},{3,2},{4,5},{5,4},{6,7},{7,6},{8,9},{9,8},{10,11... | collective-permute-start | bytes 344072 | tf_op jit(solution)/shard_map/ppermute | solution.py:383

commit v15 on v10

--- a/solution.py
+++ b/solution.py
@@ -112,8 +112,8 @@
     zero = jnp.zeros((SUB, LANES), jnp.float32)
     sums = lax.fori_loop(0, depth // (chunks * SUB), squares, (zero,) * (chunks * COMPS))
     total = jnp.sum(functools.reduce(jnp.add, sums), axis=(0, 1), keepdims=True)
-    slot = lax.broadcasted_iota(jnp.int32, part_ref.shape, 1)
-    part_ref[...] = jnp.where((slot == here) & (here > 0), total, 0.0)
+    slot = lane_iota()
+    part_ref[...] = jnp.where((slot == here) & (here > 0) & (sub_iota() == 0), total, 0.0)
     turned = (lax.axis_index("gx") & 1) == 1
     one_ref[COMPS:] = jnp.where(turned, own_left_ref[...], own_right_ref[...])
     two_ref[COMPS:] = jnp.where(turned, own_right_ref[...], own_left_ref[...])
@@ -408,7 +408,6 @@
     local, comps, nz, ny, nx = magnetization.shape
     images = local * lax.axis_size("img")
     tiles = nz // SUB
-    devices = lax.axis_size(("img", "gx", "gy"))
     assert lax.axis_size("gx") % 2 == 0
     assert local == 1 and comps == COMPS and nx == LANES
     assert ny == 2 * DEPTH and ny * DEPTH == LANES and tiles >= 2
@@ -446,7 +445,7 @@
     part, near, one, two = pl.pallas_call(
         functools.partial(gather_kernel, ny, tiles),
         out_shape=(
-            jax.ShapeDtypeStruct((devices, LANES), f32),
+            jax.ShapeDtypeStruct(vreg, f32),
             jax.ShapeDtypeStruct(flat, f32),
             packed,
             packed,
@@ -468,7 +467,7 @@
         name="merge_strips",
     )(one, two)
     strips_p = around_strips(strips)
-    squares = lax.all_to_all(part, ("img", "gx", "gy"), 0, 0, tiled=True)
+    squares = lax.all_gather(part, ("img", "gx", "gy"), axis=0, tiled=True)
 
     window = ny + 2 * DEPTH
     out = pl.pallas_call(

time: 49 us -> 106 us (2.16)
  blocking collectives: 11.1 us -> 67.8 us
    all_gather x0 -> x1, blocking collectives: none -> 67.8 us  [body(): squares = lax.all_gather(part, ('img', 'gx', 'gy'), axis=0, tiled=True)]
    all_to_all x1 -> x0, blocking collectives: 11.1 us -> none  [body(): squares = lax.all_to_all(part, ('img', 'gx', 'gy'), 0, 0, tiled=True)]
  transfers between devices with their start and end apart: 8 -> 8, of which waited for: 2 -> 2; matrix products, arithmetic and copies ran while one was open for 0% -> 0% of each run, Pallas kernels for 3% -> 1%
where the time goes in v15:
time: 106 us
  blocking collectives  67.8 us (64%)
  Pallas kernels  16.2 us (15%)
  starting transfers between devices  12.4 us (12%)
  waiting for transfers between devices  6.42 us (6%)
  local copies, waits for them, and re-layouts  2.6 us (2%)
    all_gather x1, blocking collectives, body(): squares = lax.all_gather(part, ('img', 'gx', 'gy'), axis=0, tiled=True)  67.8 us
    pallas_call x1, Pallas kernels, body(): pl.pallas_call(functools.partial(evolve_kernel, ny, tiles, images), out_s...  13.6 us
    ppermute x4, starting transfers between devices, swapped(): return lax.ppermute(cells, axis, pairs + [(j, i) for i, j in pairs])  6.75 us
    ppermute x4, starting transfers between devices, shifted(): return lax.ppermute(cells, axis, pairs)  5.69 us
    ppermute x4, waiting for transfers between devices, shifted(): return lax.ppermute(cells, axis, pairs)  4.44 us
    unnamed x16, local copies, waits for them, and re-layouts  2.6 us
  transfers between devices with their start and end apart: 8, of which 2 were waited for; matrix products, arithmetic and copies ran while one was open for 0% of the time, Pallas kernels for 1%

profile of v15, /device:TPU:0, one launch (start us, length us, event | category | flops | bytes accessed | tf_op | source)
XLA Modules:
  0.0 105.5 jit_solution(10381545465241199455)
XLA Ops:
  0.0 2.9 %collective-permute-start = (f32[3,16,16,128]{3,2,1,0:T(8,128)}, f32[3,16,16,128]{3,2,1,0:T(8,128)S(1)}, u32[]{:S(2)}, u32[]{:S(2)}) collective-permute-start(f32[3,16,16,128]{3,2,1,0:T(8,128)} %bitcast.11), channel_id=1, source_target_pairs={{0,1},{1,0},{2,3},{3,2},{4,5},{5,4},{6,7},{7,6},{8,9},{9,8},{10,11... | collective-permute-start | bytes 1179656 | tf_op jit(solution)/shard_map/ppermute | solution.py:380
  2.9 0.7 collective-permute-start.3
  3.6 4.4 %collective-permute-start.2 = (f32[3,16,16,128]{3,2,1,0:T(8,128)}, f32[3,16,16,128]{3,2,1,0:T(8,128)S(1)}, u32[]{:S(2)}, u32[]{:S(2)}) collective-permute-start(f32[3,16,16,128]{3,2,1,0:T(8,128)} %bitcast.13), channel_id=1, source_target_pairs={{0,8},{16,24},{8,0},{24,16},{1,9},{17,25},{9,1},{25,17},{2,10},{18... | collective-permute-start | bytes 1179656 | tf_op jit(solution)/shard_map/ppermute | solution.py:386
  8.1 0.0 copy-start.7
  8.1 0.0 copy-start.4
  8.1 0.0 copy-start.5
  8.1 0.0 copy-start.6
  8.1 0.6 copy-done.7
  8.7 0.0 copy-done.4
  8.7 0.0 copy-done.5
  8.7 0.0 copy-done.6
  8.8 0.0 copy-start
  8.8 1.0 copy-done
  9.8 0.0 copy-start.2
  9.8 0.9 copy-done.2
  10.7 0.0 copy-start.1
  10.7 1.5 %pack_strips.1 = (f32[4,2,8,128]{3,2,1,0:T(8,128)S(1)}, f32[4,2,8,128]{3,2,1,0:T(8,128)S(1)}, f32[5,8,128]{2,1,0:T(8,128)S(1)}) custom-call(s32[4]{0:T(128)S(1)} %copy-done.4, f32[8]{0:T(128)S(1)} %copy-done.5, f32[8]{0:T(128)S(1)} %copy-done.6, f32[1,3]{1,0:T(1,128)S(1)} %bitcast.25, f32[3,256,128]{2,1,0:T(8,128)S(1)} %bitcast.14, s32[256,128]{1,0:T(8,128)S(1)} %bitcast.17), custom_call_target="tpu_custom_call" | custom-call | tf_op jit(solution)/shard_map/pack_strips/pallas_call | solution.py:426
  12.2 0.6 collective-permute-start.1
  12.8 4.4 %collective-permute-done.1 = s32[16,16,128]{2,1,0:T(8,128)S(1)} collective-permute-done((s32[16,16,128]{2,1,0:T(8,128)S(1)}, s32[16,16,128]{2,1,0:T(8,128)S(1)}, u32[]{:S(2)}, u32[]{:S(2)}) %collective-permute-start.1) | collective-permute-done | bytes 131104 | tf_op jit(solution)/shard_map/ppermute | solution.py:380
  17.2 0.0 collective-permute-done
  17.2 0.0 collective-permute-done.3
  17.2 0.0 collective-permute-done.2
  17.2 0.0 copy-done.1
  17.2 1.1 %gather_images.1 = (f32[8,128]{1,0:T(8,128)S(1)}, f32[3,256,128]{2,1,0:T(8,128)S(1)}, f32[7,2,8,128]{3,2,1,0:T(8,128)S(1)}, f32[7,2,8,128]{3,2,1,0:T(8,128)S(1)}) custom-call(f32[5,8,128]{2,1,0:T(8,128)S(1)} %get-tuple-element.20.info_ref, f32[3,256,128]{2,1,0:T(8,128)S(1)} %bitcast.15, f32[3,256,128]{2,1,0:T(8,128)S(1)} %bitcast.23, ...), custom_call_target="tpu_custom_call" | custom-call | tf_op jit(solution)/shard_map/gather_images/pallas_call | solution.py:445
  18.3 0.6 collective-permute-start.4
  18.9 0.0 collective-permute-start.5
  18.9 0.0 copy-start.3
  18.9 1.6 %collective-permute-start.6 = (f32[7,2,8,128]{3,2,1,0:T(8,128)S(1)}, f32[7,2,8,128]{3,2,1,0:T(8,128)S(1)}, u32[]{:S(2)}, u32[]{:S(2)}) collective-permute-start(f32[7,2,8,128]{3,2,1,0:T(8,128)S(1)} %get-tuple-element.28), channel_id=1, source_target_pairs={{2,4},{6,0},{4,2},{0,6},{3,5},{7,1},{5,3},{1,7},{10,12},{14,8},{12... | collective-permute-start | bytes 172040 | tf_op jit(solution)/shard_map/ppermute | solution.py:386
  20.5 0.0 collective-permute-done.5.one_ref
  20.5 2.0 %collective-permute-done.6.two_ref = f32[7,2,8,128]{3,2,1,0:T(8,128)S(1)} collective-permute-done((f32[7,2,8,128]{3,2,1,0:T(8,128)S(1)}, f32[7,2,8,128]{3,2,1,0:T(8,128)S(1)}, u32[]{:S(2)}, u32[]{:S(2)}) %collective-permute-start.6) | collective-permute-done | bytes 57376 | tf_op jit(solution)/shard_map/ppermute | solution.py:386
  22.5 1.6 %collective-permute-start.7 = (f32[2,7,2,8,128]{4,3,2,1,0:T(8,128)S(1)}, f32[2,7,2,8,128]{4,3,2,1,0:T(8,128)S(1)}, u32[]{:S(2)}, u32[]{:S(2)}) collective-permute-start(f32[2,7,2,8,128]{4,3,2,1,0:T(8,128)S(1)} %merge_strips.1.strips_ref), channel_id=1, source_target_pairs={{0,1},{1,0},{2,3},{3,2},{4,5},{5,4},{6,7},{7,6},{8,9},{9,8},{10,11... | collective-permute-start | bytes 344072 | tf_op jit(solution)/shard_map/ppermute | solution.py:380
  24.1 67.8 %all_gather.3.sq_ref = f32[256,128]{1,0:T(8,128)S(1)} all-gather(f32[8,128]{1,0:T(8,128)S(1)} %get-tuple-element.23), channel_id=1, replica_groups=mesh['img'=4,'gx'=4,'gy'=2] {'img','gx','gy'}, dimensions={0}, use_global_device_ids=true | all-gather | bytes 135168 | tf_op jit(solution)/shard_map/all_gather | solution.py:470
  91.9 0.0 collective-permute-done.7.stripsp_ref
  91.9 0.0 collective-permute-done.4
  91.9 0.0 copy-done.3
  91.9 13.6 %evolve.1 = f32[3,256,128]{2,1,0:T(8,128)} custom-call(f32[5,8,128]{2,1,0:T(8,128)S(1)} %get-tuple-element.20.info_ref, f32[256,128]{1,0:T(8,128)S(1)} %all_gather.3.sq_ref, f32[3,256,128]{2,1,0:T(8,128)S(1)} %bitcast.16, f32[3,256,128]{2,1,0:T(8,128)S(1)} %bitcast.19, f32[3,256,128]{2,1,0:T(8,128)S(1)} %get-tuple-element.25.n_ref, ...), custom_call_target="tpu_custom_call" | custom-call | tf_op jit(solution)/shard_map/evolve/pallas_call | solution.py:473
  (1 shorter events, 0.0 us)
Async XLA Ops:
  0.0 17.2 %collective-permute-start = (f32[3,16,16,128]{3,2,1,0:T(8,128)}, f32[3,16,16,128]{3,2,1,0:T(8,128)S(1)}, u32[]{:S(2)}, u32[]{:S(2)}) collective-permute-start(f32[3,16,16,128]{3,2,1,0:T(8,128)} %bitcast.11), channel_id=1, source_target_pairs={{0,1},{1,0},{2,3},{3,2},{4,5},{5,4},{6,7},{7,6},{8,9},{9,8},{10,11... | collective-permute-start | bytes 1179656 | tf_op jit(solution)/shard_map/ppermute | solution.py:380
  2.9 14.3 %collective-permute-start.3 = (f32[3,16,16,128]{3,2,1,0:T(8,128)}, f32[3,16,16,128]{3,2,1,0:T(8,128)S(1)}, u32[]{:S(2)}, u32[]{:S(2)}) collective-permute-start(f32[3,16,16,128]{3,2,1,0:T(8,128)} %bitcast.12), channel_id=1, source_target_pairs={{8,16},{16,8},{9,17},{17,9},{10,18},{18,10},{11,19},{19,11},{12,20... | collective-permute-start | bytes 1179656 | tf_op jit(solution)/shard_map/ppermute | solution.py:386
  3.6 13.6 %collective-permute-start.2 = (f32[3,16,16,128]{3,2,1,0:T(8,128)}, f32[3,16,16,128]{3,2,1,0:T(8,128)S(1)}, u32[]{:S(2)}, u32[]{:S(2)}) collective-permute-start(f32[3,16,16,128]{3,2,1,0:T(8,128)} %bitcast.13), channel_id=1, source_target_pairs={{0,8},{16,24},{8,0},{24,16},{1,9},{17,25},{9,1},{25,17},{2,10},{18... | collective-permute-start | bytes 1179656 | tf_op jit(solution)/shard_map/ppermute | solution.py:386
  8.1 0.7 copy-start.7
  8.1 0.7 copy-start.4
  8.1 0.7 copy-start.5
  8.1 0.7 copy-start.6
  8.8 1.0 copy-start
  9.8 0.9 copy-start.2
  10.7 6.6 %copy-start.1 = (f32[1,3,16,16,128]{4,3,2,1,0:T(8,128)S(1)}, f32[1,3,16,16,128]{4,3,2,1,0:T(8,128)}, u32[]{:S(2)}) copy-start(f32[1,3,16,16,128]{4,3,2,1,0:T(8,128)} %param.6) | copy-start | bytes 1179652
  12.2 5.0 %collective-permute-start.1 = (s32[16,16,128]{2,1,0:T(8,128)S(1)}, s32[16,16,128]{2,1,0:T(8,128)S(1)}, u32[]{:S(2)}, u32[]{:S(2)}) collective-permute-start(s32[16,16,128]{2,1,0:T(8,128)S(1)} %copy-done.2), channel_id=1, source_target_pairs={{0,1},{1,0},{2,3},{3,2},{4,5},{5,4},{6,7},{7,6},{8,9},{9,8},{10,11... | collective-permute-start | bytes 393224 | tf_op jit(solution)/shard_map/ppermute | solution.py:380
  18.3 73.6 %collective-permute-start.4 = (f32[3,16,16,128]{3,2,1,0:T(8,128)S(1)}, f32[3,16,16,128]{3,2,1,0:T(8,128)S(1)}, u32[]{:S(2)}, u32[]{:S(2)}) collective-permute-start(f32[3,16,16,128]{3,2,1,0:T(8,128)S(1)} %bitcast.20), channel_id=1, source_target_pairs={{0,1},{1,0},{2,3},{3,2},{4,5},{5,4},{6,7},{7,6},{8,9},{9,8},{10,11... | collective-permute-start | bytes 1179656 | tf_op jit(solution)/shard_map/ppermute | solution.py:380
  18.9 1.6 %collective-permute-start.5 = (f32[7,2,8,128]{3,2,1,0:T(8,128)S(1)}, f32[7,2,8,128]{3,2,1,0:T(8,128)S(1)}, u32[]{:S(2)}, u32[]{:S(2)}) collective-permute-start(f32[7,2,8,128]{3,2,1,0:T(8,128)S(1)} %get-tuple-element.27), channel_id=1, source_target_pairs={{0,2},{4,6},{2,0},{6,4},{1,3},{5,7},{3,1},{7,5},{8,10},{12,14},{10... | collective-permute-start | bytes 172040 | tf_op jit(solution)/shard_map/ppermute | solution.py:386
  18.9 73.0 %copy-start.3 = (s32[16,16,128]{2,1,0:T(8,128)S(1)}, s32[16,16,128]{2,1,0:T(8,128)}, u32[]{:S(2)}) copy-start(s32[16,16,128]{2,1,0:T(8,128)} %param.9) | copy-start | bytes 393220
  18.9 3.6 %collective-permute-start.6 = (f32[7,2,8,128]{3,2,1,0:T(8,128)S(1)}, f32[7,2,8,128]{3,2,1,0:T(8,128)S(1)}, u32[]{:S(2)}, u32[]{:S(2)}) collective-permute-start(f32[7,2,8,128]{3,2,1,0:T(8,128)S(1)} %get-tuple-element.28), channel_id=1, source_target_pairs={{2,4},{6,0},{4,2},{0,6},{3,5},{7,1},{5,3},{1,7},{10,12},{14,8},{12... | collective-permute-start | bytes 172040 | tf_op jit(solution)/shard_map/ppermute | solution.py:386
  22.5 69.3 %collective-permute-start.7 = (f32[2,7,2,8,128]{4,3,2,1,0:T(8,128)S(1)}, f32[2,7,2,8,128]{4,3,2,1,0:T(8,128)S(1)}, u32[]{:S(2)}, u32[]{:S(2)}) collective-permute-start(f32[2,7,2,8,128]{4,3,2,1,0:T(8,128)S(1)} %merge_strips.1.strips_ref), channel_id=1, source_target_pairs={{0,1},{1,0},{2,3},{3,2},{4,5},{5,4},{6,7},{7,6},{8,9},{9,8},{10,11... | collective-permute-start | bytes 344072 | tf_op jit(solution)/shard_map/ppermute | solution.py:380

commit v16 on v14

--- a/solution.py
+++ b/solution.py
@@ -31,29 +31,9 @@
     return pl.ds(y + ny * t, SUB, stride=ny * tiles)
 
 
-def pack_kernel(
-    ny, tiles, regions, lower_ref, aniso_ref, damp_ref, share_ref, m_ref, reg_ref, left_ref, right_ref, info_ref
-):
+def info_kernel(regions, lower_ref, aniso_ref, damp_ref, share_ref, info_ref):
     here = lax.axis_index("img")
     lane = lane_iota()
-    block = lane // DEPTH
-    def pack(i, carry):
-        done = []
-        for u in range(2):
-            y = 2 * i + u
-            shift = (DEPTH * (y + 1)) & (LANES - 1)
-            left = block == ((y + 1) & (ny - 1))
-            right = block == y
-            for t in range(tiles):
-                rows = rows_at(ny, tiles, y, t)
-                for c in range(COMPS + 1):
-                    cells = m_ref[c, rows, :] if c < COMPS else reg_ref[rows, :].astype(jnp.float32)
-                    done.append((c, t, left, right, pltpu.roll(cells, shift, 1)))
-        for c, t, left, right, cells in done:
-            pltpu.store(left_ref.at[c, t], cells, mask=left)
-            pltpu.store(right_ref.at[c, t], cells, mask=right)
-        return carry
-
     table_a = jnp.zeros((SUB, LANES), jnp.float32)
     table_d = jnp.zeros((SUB, LANES), jnp.float32)
     for i in range(regions):
@@ -70,15 +50,6 @@
     info_ref[3] = jnp.broadcast_to(target, (SUB, LANES))
     info_ref[4] = jnp.full((SUB, LANES), lower_ref[here].astype(jnp.float32))
 
-    lax.fori_loop(0, ny // 2, pack, 0)
-
-
-def merge_kernel(one_ref, two_ref, out_ref):
-    turned = (lax.axis_index("gx") & 1) == 1
-    one, two = one_ref[...], two_ref[...]
-    out_ref[0] = jnp.where(turned, one, two)
-    out_ref[1] = jnp.where(turned, two, one)
-
 
 def take_first(info_ref, here):
     odd = (here & 1) == 1
@@ -86,9 +57,7 @@
     return jnp.where(below, jnp.where(odd, 1, 0), jnp.where(odd, 0, 1)) == 1, odd
 
 
-def gather_kernel(
-    ny, tiles, info_ref, m_ref, first_ref, second_ref, own_left_ref, own_right_ref, part_ref, near_ref, one_ref, two_ref
-):
+def gather_kernel(info_ref, m_ref, first_ref, second_ref, part_ref, near_ref):
     here = lax.axis_index("img")
     pick, odd = take_first(info_ref, here)
     chunks = 4
@@ -114,29 +83,10 @@
     total = jnp.sum(functools.reduce(jnp.add, sums), axis=(0, 1), keepdims=True)
     slot = lax.broadcasted_iota(jnp.int32, part_ref.shape, 1)
     part_ref[...] = jnp.where((slot == here) & (here > 0), total, 0.0)
-    turned = (lax.axis_index("gx") & 1) == 1
-    one_ref[COMPS:] = jnp.where(turned, own_left_ref[...], own_right_ref[...])
-    two_ref[COMPS:] = jnp.where(turned, own_right_ref[...], own_left_ref[...])
-    block = lane_iota() // DEPTH
-
-    def pack(i, carry):
-        done = []
-        for u in range(2):
-            y = 2 * i + u
-            after = (y + 1) & (ny - 1)
-            one = block == jnp.where(turned, after, y)
-            two = block == jnp.where(turned, y, after)
-            shift = (DEPTH * (y + 1)) & (LANES - 1)
-            for t in range(tiles):
-                for c in range(COMPS):
-                    cells = pltpu.roll(near_ref[c, rows_at(ny, tiles, y, t), :], shift, 1)
-                    done.append((c, t, one, two, cells))
-        for c, t, one, two, cells in done:
-            pltpu.store(one_ref.at[c, t], cells, mask=one)
-            pltpu.store(two_ref.at[c, t], cells, mask=two)
-        return carry
-
-    lax.fori_loop(0, ny // 2, pack, 0)
+
+
+def is_turned():
+    return (lax.axis_index("gx") & 1) == 1
 
 
 def turn(m, h, a2, b, sc):
@@ -158,45 +108,13 @@
     return tuple(x * scale for x in v)
 
 
-def evolve_kernel(
-    ny,
-    tiles,
-    images,
-    info_ref,
-    sq_ref,
-    m_ref,
-    mp_ref,
-    n_ref,
-    np1_ref,
-    np2_ref,
-    reg_ref,
-    regp_ref,
-    strips_ref,
-    stripsp_ref,
-    out_ref,
-    main0,
-    main1,
-    strip0,
-    strip1,
-    edge,
-    seam0,
-    seam1,
-    par,
-    spar,
+def start_kernel(
+    ny, tiles, images, info_ref, sq_ref, m_ref, mp_ref, n_ref, np1_ref, np2_ref, reg_ref, regp_ref, main_ref, one_ref, two_ref
 ):
-    main, strip, seam = (main0, main1), (strip0, strip1), (seam0, seam1)
-    window = ny + 2 * DEPTH
     here = lax.axis_index("img")
     lane = lane_iota()
-    sub = sub_iota()
     block = lane // DEPTH
-    first_lane = lane == 0
-    last_lane = lane == LANES - 1
-    head_lane = lane % DEPTH == 0
-    tail_lane = lane % DEPTH == DEPTH - 1
-    top = sub == SUB - 1
-    bottom = sub == 0
-
+    turned = is_turned()
     pick, _ = take_first(info_ref, here)
     lo = info_ref[4]
     slot = lane.astype(jnp.float32)
@@ -210,17 +128,12 @@
     w_own = jnp.where(below, weight, 1.0 - weight)
     w_near = jnp.where(below, 1.0 - weight, weight)
 
-    tables = (info_ref[0], info_ref[1], info_ref[2])
-
-    def params(region):
-        return [jnp.take_along_axis(table, region, axis=1) for table in tables]
-
-    def ends_of(k, new):
+    def fill(k, carry):
+        done = []
+        after = (k + 1) & (ny - 1)
+        one = block == jnp.where(turned, after, k)
+        two = block == jnp.where(turned, k, after)
         shift = (DEPTH * (k + 1)) & (LANES - 1)
-        return [pltpu.roll(new[c], shift, 1) for c in range(COMPS)]
-
-    def fill(k, carry):
-        done = []
         for g, (own, reg) in enumerate(((m_ref, reg_ref), (mp_ref, regp_ref))):
             for t in range(tiles):
                 rows = rows_at(ny, tiles, k, t)
@@ -231,27 +144,94 @@
                         jnp.where(pick, np1_ref[c, rows, :], np2_ref[c, rows, :]) for c in range(COMPS)
                     ]
                 v = normal([w_own * own[c, rows, :] + w_near * near[c] for c in range(COMPS)])
-                done.append((g * ny + k, t, v, params(reg[rows, :])))
-        for r, t, v, p in done:
-            for c in range(COMPS):
-                main0[c, r, t] = v[c]
+                v = list(v) + [reg[rows, :].astype(jnp.float32)]
+                done.append((g, t, v, [pltpu.roll(x, shift, 1) for x in v]))
+        for g, t, v, ends in done:
+            for c in range(COMPS):
+                main_ref[c, g * ny + k, t] = v[c]
+            for c in range(COMPS + 1):
+                pltpu.store(one_ref.at[g, c, t], ends[c], mask=one)
+                pltpu.store(two_ref.at[g, c, t], ends[c], mask=two)
+        return carry
+
+    lax.fori_loop(0, ny, fill, 0)
+
+
+def look_up(info_ref, region):
+    return [jnp.take_along_axis(info_ref[i], region, axis=1) for i in range(3)]
+
+
+def look_up_kernel(ny, tiles, info_ref, reg_ref, regp_ref, par_ref):
+    def fill(k, carry):
+        done = []
+        for g, reg in enumerate((reg_ref, regp_ref)):
+            for t in range(tiles):
+                done.append((g * ny + k, t, look_up(info_ref, reg[rows_at(ny, tiles, k, t), :])))
+        for r, t, p in done:
             for i in range(3):
-                par[i, r, t] = p[i]
+                par_ref[i, r, t] = p[i]
         return carry
 
     lax.fori_loop(0, ny, fill, 0)
+
+
+def evolve_kernel(
+    ny,
+    tiles,
+    info_ref,
+    start_ref,
+    par,
+    one_ref,
+    two_ref,
+    out_ref,
+    main0,
+    main1,
+    strip0,
+    strip1,
+    edge,
+    seam0,
+    seam1,
+    spar,
+):
+    main, strip, seam = (main0, main1), (strip0, strip1), (seam0, seam1)
+    window = ny + 2 * DEPTH
+    lane = lane_iota()
+    sub = sub_iota()
+    block = lane // DEPTH
+    first_lane = lane == 0
+    last_lane = lane == LANES - 1
+    head_lane = lane % DEPTH == 0
+    tail_lane = lane % DEPTH == DEPTH - 1
+    top = sub == SUB - 1
+    bottom = sub == 0
+    turned = is_turned()
+
+    def ends_of(k, new):
+        shift = (DEPTH * (k + 1)) & (LANES - 1)
+        return [pltpu.roll(new[c], shift, 1) for c in range(COMPS)]
+
+    def copy(r, carry):
+        for u in range(2):
+            for t in range(tiles):
+                for c in range(COMPS):
+                    main0[c, 2 * r + u, t] = start_ref[c, 2 * r + u, t]
+        return carry
+
+    lax.fori_loop(0, window // 2, copy, 0)
 
     def seam_of(left, right):
         return jnp.where(head_lane, pltpu.roll(left, 1, 1), pltpu.roll(right, LANES - 1, 1))
 
     def fill_strips(t, carry):
         done = []
-        for g, cells in enumerate((strips_ref, stripsp_ref)):
-            for side in range(2):
-                v = normal(
-                    [w_own * cells[side, COMPS + c, t] + w_near * cells[side, c, t] for c in range(COMPS)]
-                )
-                done.append((side, g, v, params(cells[side, 2 * COMPS, t].astype(jnp.int32))))
+        for g in range(2):
+            one = [one_ref[g, c, t] for c in range(COMPS + 1)]
+            two = [two_ref[g, c, t] for c in range(COMPS + 1)]
+            left = [jnp.where(turned, x, y) for x, y in zip(one, two)]
+            right = [jnp.where(turned, y, x) for x, y in zip(one, two)]
+            for side, cells in enumerate((left, right)):
+                p = look_up(info_ref, cells[COMPS].astype(jnp.int32))
+                done.append((side, g, cells[:COMPS], p))
         for side, g, v, p in done:
             for c in range(COMPS):
                 strip0[c, side, g, t] = v[c]
@@ -398,15 +378,6 @@
     return jnp.concatenate([shifted(head, "gy", -1, True), shifted(tail, "gy", 1, True)], axis=dim)
 
 
-def around_strips(both):
-    if lax.axis_size("gy") == 2:
-        return shifted(both, "gy", 1, True)
-    block = lax.broadcasted_iota(jnp.int32, both.shape, both.ndim - 1) // DEPTH
-    side = lax.broadcasted_iota(jnp.int32, both.shape, 0)
-    head = (block + side - 1) % (LANES // DEPTH) < DEPTH
-    return jnp.where(head, shifted(both, "gy", -1, True), shifted(both, "gy", 1, True))
-
-
 def body(magnetization, lower_image, image_weights, regions, anisotropy, damping):
     local, comps, nz, ny, nx = magnetization.shape
     images = local * lax.axis_size("img")
@@ -426,60 +397,63 @@
     f32 = jnp.float32
     limit = pltpu.CompilerParams(vmem_limit_bytes=32 * 1024 * 1024)
     vreg = (SUB, LANES)
-    packed = jax.ShapeDtypeStruct((comps + 1, tiles) + vreg, f32)
-    left, right, info = pl.pallas_call(
-        functools.partial(pack_kernel, ny, tiles, anisotropy.shape[0]),
-        out_shape=(packed, packed, jax.ShapeDtypeStruct((5,) + vreg, f32)),
-        in_specs=[smem] * 3 + [vmem] * 3,
-        out_specs=(vmem,) * 3,
+    info = pl.pallas_call(
+        functools.partial(info_kernel, anisotropy.shape[0]),
+        out_shape=jax.ShapeDtypeStruct((5,) + vreg, f32),
+        in_specs=[smem] * 3 + [vmem],
+        out_specs=vmem,
         compiler_params=limit,
-        name="pack_strips",
-    )(
-        lower_image,
-        anisotropy,
-        damping,
-        image_weights.reshape(1, -1),
-        own.reshape(flat),
-        regions.reshape(flat[1:]),
-    )
-    late_regions, info = lax.optimization_barrier((regions, info))
-    reg_p = around(late_regions, 1)
+        name="small_arguments",
+    )(lower_image, anisotropy, damping, image_weights.reshape(1, -1))
     own_p, info = lax.optimization_barrier((own_p, info))
     first_p = swapped(own_p, "img", 0, False)
     second_p = swapped(own_p, "img", 1, False)
-    packed = jax.ShapeDtypeStruct((2 * comps + 1, tiles) + vreg, f32)
-    part, near, one, two = pl.pallas_call(
-        functools.partial(gather_kernel, ny, tiles),
-        out_shape=(
-            jax.ShapeDtypeStruct((devices, LANES), f32),
-            jax.ShapeDtypeStruct(flat, f32),
-            packed,
-            packed,
-        ),
-        in_specs=[vmem] * 6,
-        out_specs=(vmem,) * 4,
+    late_regions, info = lax.optimization_barrier((regions, info))
+    reg_p = around(late_regions, 1)
+    part, near = pl.pallas_call(
+        gather_kernel,
+        out_shape=(jax.ShapeDtypeStruct((devices, LANES), f32), jax.ShapeDtypeStruct(flat, f32)),
+        in_specs=[vmem] * 4,
+        out_specs=(vmem,) * 2,
         compiler_params=limit,
         name="gather_images",
-    )(info, own.reshape(flat), first.reshape(flat), second.reshape(flat), left, right)
+    )(info, own.reshape(flat), first.reshape(flat), second.reshape(flat))
+    squares = lax.all_to_all(part, ("img", "gx", "gy"), 0, 0, tiled=True)
+
+    window = ny + 2 * DEPTH
+    tile_rows = (regions.reshape(flat[1:]), reg_p.reshape(flat[1:]))
+    packed = jax.ShapeDtypeStruct((2, comps + 1, tiles) + vreg, f32)
+    start, one, two = pl.pallas_call(
+        functools.partial(start_kernel, ny, tiles, images),
+        out_shape=(jax.ShapeDtypeStruct((comps, window, tiles) + vreg, f32), packed, packed),
+        in_specs=[vmem] * 9,
+        out_specs=(vmem,) * 3,
+        compiler_params=limit,
+        name="start",
+    )(
+        info,
+        squares,
+        own.reshape(flat),
+        own_p.reshape(flat),
+        near,
+        first_p.reshape(flat),
+        second_p.reshape(flat),
+        *tile_rows,
+    )
     one = swapped(one, "gx", 0, True)
     two = swapped(two, "gx", 1, True)
-    one, reg_p = lax.optimization_barrier((one, reg_p))
-    strips = pl.pallas_call(
-        merge_kernel,
-        out_shape=jax.ShapeDtypeStruct((2,) + packed.shape, f32),
-        in_specs=[vmem] * 2,
+    par = pl.pallas_call(
+        functools.partial(look_up_kernel, ny, tiles),
+        out_shape=jax.ShapeDtypeStruct((3, window, tiles) + vreg, f32),
+        in_specs=[vmem] * 3,
         out_specs=vmem,
         compiler_params=limit,
-        name="merge_strips",
-    )(one, two)
-    strips_p = around_strips(strips)
-    squares = lax.all_to_all(part, ("img", "gx", "gy"), 0, 0, tiled=True)
-
-    window = ny + 2 * DEPTH
+        name="parameters",
+    )(info, *tile_rows)
     out = pl.pallas_call(
-        functools.partial(evolve_kernel, ny, tiles, images),
+        functools.partial(evolve_kernel, ny, tiles),
         out_shape=jax.ShapeDtypeStruct(flat, f32),
-        in_specs=[vmem] * 11,
+        in_specs=[vmem] * 5,
         out_specs=vmem,
         scratch_shapes=[
             pltpu.VMEM((comps, window, tiles) + vreg, f32),
@@ -489,24 +463,11 @@
             pltpu.VMEM((comps, 2, tiles) + vreg, f32),
             pltpu.VMEM((comps, 2, tiles) + vreg, f32),
             pltpu.VMEM((comps, 2, tiles) + vreg, f32),
-            pltpu.VMEM((3, window, tiles) + vreg, f32),
             pltpu.VMEM((3, 2, 2, tiles) + vreg, f32),
         ],
         compiler_params=limit,
         name="evolve",
-    )(
-        info,
-        squares,
-        own.reshape(flat),
-        own_p.reshape(flat),
-        near,
-        first_p.reshape(flat),
-        second_p.reshape(flat),
-        regions.reshape(flat[1:]),
-        reg_p.reshape(flat[1:]),
-        strips,
-        strips_p,
-    )
+    )(info, start, par, one, two)
     return out.reshape(magnetization.shape)
 
 

time: 50.2 us -> 49.4 us (0.984)
  waiting for transfers between devices: 2.62 us -> 5.25 us
  starting transfers between devices: 17.2 us -> 15.6 us
  blocking collectives: 10.7 us -> 9.68 us
  local copies, waits for them, and re-layouts: 1.7 us -> 1.01 us
    ppermute x3 -> x2, waiting for transfers between devices: 1.48 us -> 3.56 us  [shifted(): return lax.ppermute(cells, axis, pairs)]
    ppermute x6, starting transfers between devices: 12.2 us -> 11.1 us  [swapped(): return lax.ppermute(cells, axis, pairs + [(j, i) for i, j in pairs])]
    all_to_all x1, blocking collectives: 10.7 us -> 9.68 us  [body(): squares = lax.all_to_all(part, ('img', 'gx', 'gy'), 0, 0, tiled=True)]
    unnamed x12, local copies, waits for them, and re-layouts: 1.7 us -> 1.01 us
    ppermute x6, waiting for transfers between devices: 1.14 us -> 1.69 us  [swapped(): return lax.ppermute(cells, axis, pairs + [(j, i) for i, j in pairs])]
    ppermute x3 -> x2, starting transfers between devices: 5.03 us -> 4.51 us  [shifted(): return lax.ppermute(cells, axis, pairs)]
    pallas_call x4 -> x5, Pallas kernels: 17.7 us -> 17.6 us  [the longest x1 12 us: body(): pl.pallas_call(functools.partial(evolve_kernel, ny, tiles), out_shape=jax...]
  transfers between devices with their start and end apart: 9 -> 8, of which waited for: 3 -> 2; matrix products, arithmetic and copies ran while one was open for 0% -> 0% of each run, Pallas kernels for 6% -> 5%
where the time goes in v16:
time: 49.4 us; the launch traced here: 49.2 us
  Pallas kernels  17.6 us (36%)
  starting transfers between devices  15.6 us (32%)
  blocking collectives  9.68 us (20%)
  waiting for transfers between devices  5.25 us (11%)
  local copies, waits for them, and re-layouts  1.01 us (2%)
    pallas_call x1, Pallas kernels, body(): pl.pallas_call(functools.partial(evolve_kernel, ny, tiles), out_shape=jax...  12 us
    ppermute x6, starting transfers between devices, swapped(): return lax.ppermute(cells, axis, pairs + [(j, i) for i, j in pairs])  11.1 us
    all_to_all x1, blocking collectives, body(): squares = lax.all_to_all(part, ('img', 'gx', 'gy'), 0, 0, tiled=True)  9.68 us
    ppermute x2, starting transfers between devices, shifted(): return lax.ppermute(cells, axis, pairs)  4.51 us
    ppermute x2, waiting for transfers between devices, shifted(): return lax.ppermute(cells, axis, pairs)  3.56 us
    pallas_call x1, Pallas kernels, body(): pl.pallas_call(functools.partial(start_kernel, ny, tiles, images), out_sh...  3.07 us
    ppermute x6, waiting for transfers between devices, swapped(): return lax.ppermute(cells, axis, pairs + [(j, i) for i, j in pairs])  1.69 us
    pallas_call x1, Pallas kernels, body(): pl.pallas_call(functools.partial(look_up_kernel, ny, tiles), out_shape=ja...  1.57 us
  transfers between devices with their start and end apart: 8, of which 2 were waited for; matrix products, arithmetic and copies ran while one was open for 0% of the time, Pallas kernels for 5%

profile of v16, /device:TPU:0, one launch (start us, length us, event | category | flops | bytes accessed | tf_op | source)
XLA Modules:
  0.0 49.2 jit_solution(12691865299796205145)
XLA Ops:
  0.0 0.0 copy-start.5
  0.0 0.0 copy-start.2
  0.0 0.0 copy-start.3
  0.0 0.0 copy-start.4
  0.0 3.0 %collective-permute-start = (f32[3,16,16,128]{3,2,1,0:T(8,128)}, f32[3,16,16,128]{3,2,1,0:T(8,128)S(1)}, u32[]{:S(2)}, u32[]{:S(2)}) collective-permute-start(f32[3,16,16,128]{3,2,1,0:T(8,128)} %bitcast.15), channel_id=1, source_target_pairs={{0,1},{1,0},{2,3},{3,2},{4,5},{5,4},{6,7},{7,6},{8,9},{9,8},{10,11... | collective-permute-start | bytes 1179656 | tf_op jit(solution)/shard_map/ppermute | solution.py:363
  3.0 0.7 %collective-permute-start.2 = (f32[3,16,16,128]{3,2,1,0:T(8,128)}, f32[3,16,16,128]{3,2,1,0:T(8,128)S(1)}, u32[]{:S(2)}, u32[]{:S(2)}) collective-permute-start(f32[3,16,16,128]{3,2,1,0:T(8,128)} %bitcast.16), channel_id=1, source_target_pairs={{8,16},{16,8},{9,17},{17,9},{10,18},{18,10},{11,19},{19,11},{12,20... | collective-permute-start | bytes 1179656 | tf_op jit(solution)/shard_map/ppermute | solution.py:369
  3.7 4.4 %collective-permute-start.1 = (f32[3,16,16,128]{3,2,1,0:T(8,128)}, f32[3,16,16,128]{3,2,1,0:T(8,128)S(1)}, u32[]{:S(2)}, u32[]{:S(2)}) collective-permute-start(f32[3,16,16,128]{3,2,1,0:T(8,128)} %bitcast.17), channel_id=1, source_target_pairs={{0,8},{16,24},{8,0},{24,16},{1,9},{17,25},{9,1},{25,17},{2,10},{18... | collective-permute-start | bytes 1179656 | tf_op jit(solution)/shard_map/ppermute | solution.py:369
  8.1 0.0 copy-done.5
  8.2 0.0 copy-done.2
  8.2 0.0 copy-done.3
  8.2 0.0 copy-done.4
  8.2 0.6 %small_arguments.1.info_ref = f32[5,8,128]{2,1,0:T(8,128)S(1)} custom-call(s32[4]{0:T(128)S(1)} %copy-done.2, f32[8]{0:T(128)S(1)} %copy-done.3, f32[8]{0:T(128)S(1)} %copy-done.4, f32[1,3]{1,0:T(1,128)S(1)} %bitcast.31), custom_call_target="tpu_custom_call" | custom-call | tf_op jit(solution)/shard_map/small_arguments/pallas_call | solution.py:400
  8.8 3.6 %collective-permute-done = f32[3,16,16,128]{3,2,1,0:T(8,128)S(1)} collective-permute-done((f32[3,16,16,128]{3,2,1,0:T(8,128)}, f32[3,16,16,128]{3,2,1,0:T(8,128)S(1)}, u32[]{:S(2)}, u32[]{:S(2)}) %collective-permute-start) | collective-permute-done | bytes 393248 | tf_op jit(solution)/shard_map/ppermute | solution.py:363
  12.4 0.7 %collective-permute-start.4 = (f32[3,16,16,128]{3,2,1,0:T(8,128)S(1)}, f32[3,16,16,128]{3,2,1,0:T(8,128)S(1)}, u32[]{:S(2)}, u32[]{:S(2)}) collective-permute-start(f32[3,16,16,128]{3,2,1,0:T(8,128)S(1)} %collective-permute-done), channel_id=1, source_target_pairs={{8,16},{16,8},{9,17},{17,9},{10,18},{18,10},{11,19},{19,11},{12,20... | collective-permute-start | bytes 1179656 | tf_op jit(solution)/shard_map/ppermute | solution.py:369
  13.0 4.7 %collective-permute-start.3 = (f32[3,16,16,128]{3,2,1,0:T(8,128)S(1)}, f32[3,16,16,128]{3,2,1,0:T(8,128)S(1)}, u32[]{:S(2)}, u32[]{:S(2)}) collective-permute-start(f32[3,16,16,128]{3,2,1,0:T(8,128)S(1)} %collective-permute-done), channel_id=1, source_target_pairs={{0,8},{16,24},{8,0},{24,16},{1,9},{17,25},{9,1},{25,17},{2,10},{18... | collective-permute-start | bytes 1179656 | tf_op jit(solution)/shard_map/ppermute | solution.py:369
  17.7 1.5 %collective-permute-start.5 = (s32[16,16,128]{2,1,0:T(8,128)}, s32[16,16,128]{2,1,0:T(8,128)S(1)}, u32[]{:S(2)}, u32[]{:S(2)}) collective-permute-start(s32[16,16,128]{2,1,0:T(8,128)} %param.9), channel_id=1, source_target_pairs={{0,1},{1,0},{2,3},{3,2},{4,5},{5,4},{6,7},{7,6},{8,9},{9,8},{10,11... | collective-permute-start | bytes 393224 | tf_op jit(solution)/shard_map/ppermute | solution.py:363
  19.2 0.0 collective-permute-done.2
  19.2 0.0 collective-permute-done.1
  19.2 0.0 copy-start
  19.2 1.0 %copy-done = f32[1,3,16,16,128]{4,3,2,1,0:T(8,128)S(1)} copy-done((f32[1,3,16,16,128]{4,3,2,1,0:T(8,128)S(1)}, f32[1,3,16,16,128]{4,3,2,1,0:T(8,128)}, u32[]{:S(2)}) %copy-start) | copy-done | bytes 393240
  20.2 0.0 copy-start.1
  20.2 0.2 gather_images.1
  20.5 9.7 %all_to_all.11 = f32[32,1,128]{2,1,0:T(1,128)S(1)} all-to-all(f32[32,1,128]{2,1,0:T(1,128)S(1)} %bitcast.30), channel_id=1, replica_groups=mesh['img'=4,'gx'=4,'gy'=2] {'img','gx','gy'}, dimensions={0} | all-to-all | bytes 32768 | tf_op jit(solution)/shard_map/all_to_all | solution.py:421
  30.2 0.0 collective-permute-done.5
  30.2 0.0 collective-permute-done.4
  30.2 0.0 collective-permute-done.3
  30.2 0.0 copy-done.1
  30.2 3.1 %start.1 = (f32[3,32,2,8,128]{4,3,2,1,0:T(8,128)S(1)}, f32[2,4,2,8,128]{4,3,2,1,0:T(8,128)S(1)}, f32[2,4,2,8,128]{4,3,2,1,0:T(8,128)S(1)}) custom-call(f32[5,8,128]{2,1,0:T(8,128)S(1)} %small_arguments.1.info_ref, f32[32,128]{1,0:T(8,128)S(1)} %bitcast.29, f32[3,256,128]{2,1,0:T(8,128)S(1)} %bitcast.19, f32[3,256,128]{2,1,0:T(8,128)S(1)} %bitcast.26, ...), custom_call_target="tpu_custom_call" | custom-call | tf_op jit(solution)/shard_map/start/pallas_call | solution.py:426
  33.2 0.0 collective-permute-start.6
  33.3 0.6 %collective-permute-start.7 = (f32[2,4,2,8,128]{4,3,2,1,0:T(8,128)S(1)}, f32[2,4,2,8,128]{4,3,2,1,0:T(8,128)S(1)}, u32[]{:S(2)}, u32[]{:S(2)}) collective-permute-start(f32[2,4,2,8,128]{4,3,2,1,0:T(8,128)S(1)} %get-tuple-element.22), channel_id=1, source_target_pairs={{2,4},{6,0},{4,2},{0,6},{3,5},{7,1},{5,3},{1,7},{10,12},{14,8},{12... | collective-permute-start | bytes 196616 | tf_op jit(solution)/shard_map/ppermute | solution.py:369
  33.9 1.6 %parameters.1.par = f32[3,32,2,8,128]{4,3,2,1,0:T(8,128)S(1)} custom-call(f32[5,8,128]{2,1,0:T(8,128)S(1)} %small_arguments.1.info_ref, s32[256,128]{1,0:T(8,128)S(1)} %bitcast.21, s32[256,128]{1,0:T(8,128)S(1)} %bitcast.23), custom_call_target="tpu_custom_call" | custom-call | tf_op jit(solution)/shard_map/parameters/pallas_call | solution.py:445
  35.5 0.0 collective-permute-done.6.one_ref
  35.5 1.7 %collective-permute-done.7.two_ref = f32[2,4,2,8,128]{4,3,2,1,0:T(8,128)S(1)} collective-permute-done((f32[2,4,2,8,128]{4,3,2,1,0:T(8,128)S(1)}, f32[2,4,2,8,128]{4,3,2,1,0:T(8,128)S(1)}, u32[]{:S(2)}, u32[]{:S(2)}) %collective-permute-start.7) | collective-permute-done | bytes 65568 | tf_op jit(solution)/shard_map/ppermute | solution.py:369
  37.2 12.0 %evolve.1 = f32[3,256,128]{2,1,0:T(8,128)} custom-call(f32[5,8,128]{2,1,0:T(8,128)S(1)} %small_arguments.1.info_ref, f32[3,32,2,8,128]{4,3,2,1,0:T(8,128)S(1)} %get-tuple-element.20.start_ref, f32[3,32,2,8,128]{4,3,2,1,0:T(8,128)S(1)} %parameters.1.par, f32[2,4,2,8,128]{4,3,2,1,0:T(8,128)S(1)} %collective-permute-done.6.one_ref, ...), custom_call_target="tpu_custom_call" | custom-call | tf_op jit(solution)/shard_map/evolve/pallas_call | solution.py:453
Async XLA Ops:
  0.0 8.2 %copy-start.5 = (f32[3]{0:T(128)S(1)}, f32[3]{0:T(128)}, u32[]{:S(2)}) copy-start(f32[3]{0:T(128)} %param.8) | copy-start | bytes 40
  0.0 8.2 %copy-start.2 = (s32[4]{0:T(128)S(1)}, s32[4]{0:T(128)}, u32[]{:S(2)}) copy-start(s32[4]{0:T(128)} %lower_ref.1) | copy-start | bytes 52
  0.0 8.2 %copy-start.3 = (f32[8]{0:T(128)S(1)}, f32[8]{0:T(128)}, u32[]{:S(2)}) copy-start(f32[8]{0:T(128)} %aniso_ref.1) | copy-start | bytes 100
  0.0 8.2 %copy-start.4 = (f32[8]{0:T(128)S(1)}, f32[8]{0:T(128)}, u32[]{:S(2)}) copy-start(f32[8]{0:T(128)} %damp_ref.1) | copy-start | bytes 100
  0.0 12.3 %collective-permute-start = (f32[3,16,16,128]{3,2,1,0:T(8,128)}, f32[3,16,16,128]{3,2,1,0:T(8,128)S(1)}, u32[]{:S(2)}, u32[]{:S(2)}) collective-permute-start(f32[3,16,16,128]{3,2,1,0:T(8,128)} %bitcast.15), channel_id=1, source_target_pairs={{0,1},{1,0},{2,3},{3,2},{4,5},{5,4},{6,7},{7,6},{8,9},{9,8},{10,11... | collective-permute-start | bytes 1179656 | tf_op jit(solution)/shard_map/ppermute | solution.py:363
  3.0 16.2 %collective-permute-start.2 = (f32[3,16,16,128]{3,2,1,0:T(8,128)}, f32[3,16,16,128]{3,2,1,0:T(8,128)S(1)}, u32[]{:S(2)}, u32[]{:S(2)}) collective-permute-start(f32[3,16,16,128]{3,2,1,0:T(8,128)} %bitcast.16), channel_id=1, source_target_pairs={{8,16},{16,8},{9,17},{17,9},{10,18},{18,10},{11,19},{19,11},{12,20... | collective-permute-start | bytes 1179656 | tf_op jit(solution)/shard_map/ppermute | solution.py:369
  3.7 15.5 %collective-permute-start.1 = (f32[3,16,16,128]{3,2,1,0:T(8,128)}, f32[3,16,16,128]{3,2,1,0:T(8,128)S(1)}, u32[]{:S(2)}, u32[]{:S(2)}) collective-permute-start(f32[3,16,16,128]{3,2,1,0:T(8,128)} %bitcast.17), channel_id=1, source_target_pairs={{0,8},{16,24},{8,0},{24,16},{1,9},{17,25},{9,1},{25,17},{2,10},{18... | collective-permute-start | bytes 1179656 | tf_op jit(solution)/shard_map/ppermute | solution.py:369
  12.4 17.8 %collective-permute-start.4 = (f32[3,16,16,128]{3,2,1,0:T(8,128)S(1)}, f32[3,16,16,128]{3,2,1,0:T(8,128)S(1)}, u32[]{:S(2)}, u32[]{:S(2)}) collective-permute-start(f32[3,16,16,128]{3,2,1,0:T(8,128)S(1)} %collective-permute-done), channel_id=1, source_target_pairs={{8,16},{16,8},{9,17},{17,9},{10,18},{18,10},{11,19},{19,11},{12,20... | collective-permute-start | bytes 1179656 | tf_op jit(solution)/shard_map/ppermute | solution.py:369
  13.0 17.1 %collective-permute-start.3 = (f32[3,16,16,128]{3,2,1,0:T(8,128)S(1)}, f32[3,16,16,128]{3,2,1,0:T(8,128)S(1)}, u32[]{:S(2)}, u32[]{:S(2)}) collective-permute-start(f32[3,16,16,128]{3,2,1,0:T(8,128)S(1)} %collective-permute-done), channel_id=1, source_target_pairs={{0,8},{16,24},{8,0},{24,16},{1,9},{17,25},{9,1},{25,17},{2,10},{18... | collective-permute-start | bytes 1179656 | tf_op jit(solution)/shard_map/ppermute | solution.py:369
  17.7 12.4 %collective-permute-start.5 = (s32[16,16,128]{2,1,0:T(8,128)}, s32[16,16,128]{2,1,0:T(8,128)S(1)}, u32[]{:S(2)}, u32[]{:S(2)}) collective-permute-start(s32[16,16,128]{2,1,0:T(8,128)} %param.9), channel_id=1, source_target_pairs={{0,1},{1,0},{2,3},{3,2},{4,5},{5,4},{6,7},{7,6},{8,9},{9,8},{10,11... | collective-permute-start | bytes 393224 | tf_op jit(solution)/shard_map/ppermute | solution.py:363
  19.2 1.0 %copy-start = (f32[1,3,16,16,128]{4,3,2,1,0:T(8,128)S(1)}, f32[1,3,16,16,128]{4,3,2,1,0:T(8,128)}, u32[]{:S(2)}) copy-start(f32[1,3,16,16,128]{4,3,2,1,0:T(8,128)} %param.6) | copy-start | bytes 1179652
  20.2 9.9 %copy-start.1 = (s32[16,16,128]{2,1,0:T(8,128)S(1)}, s32[16,16,128]{2,1,0:T(8,128)}, u32[]{:S(2)}) copy-start(s32[16,16,128]{2,1,0:T(8,128)} %param.9) | copy-start | bytes 393220
  33.2 2.2 %collective-permute-start.6 = (f32[2,4,2,8,128]{4,3,2,1,0:T(8,128)S(1)}, f32[2,4,2,8,128]{4,3,2,1,0:T(8,128)S(1)}, u32[]{:S(2)}, u32[]{:S(2)}) collective-permute-start(f32[2,4,2,8,128]{4,3,2,1,0:T(8,128)S(1)} %get-tuple-element.21), channel_id=1, source_target_pairs={{0,2},{4,6},{2,0},{6,4},{1,3},{5,7},{3,1},{7,5},{8,10},{12,14},{10... | collective-permute-start | bytes 196616 | tf_op jit(solution)/shard_map/ppermute | solution.py:369
  33.3 3.9 %collective-permute-start.7 = (f32[2,4,2,8,128]{4,3,2,1,0:T(8,128)S(1)}, f32[2,4,2,8,128]{4,3,2,1,0:T(8,128)S(1)}, u32[]{:S(2)}, u32[]{:S(2)}) collective-permute-start(f32[2,4,2,8,128]{4,3,2,1,0:T(8,128)S(1)} %get-tuple-element.22), channel_id=1, source_target_pairs={{2,4},{6,0},{4,2},{0,6},{3,5},{7,1},{5,3},{1,7},{10,12},{14,8},{12... | collective-permute-start | bytes 196616 | tf_op jit(solution)/shard_map/ppermute | solution.py:369

commit v17 on v16

--- a/solution.py
+++ b/solution.py
@@ -16,6 +16,7 @@
 SUB = 8
 LANES = 128
 COMPS = 3
+ALONG_Z = 2
 ROWS = 4
 
 
@@ -31,7 +32,7 @@
     return pl.ds(y + ny * t, SUB, stride=ny * tiles)
 
 
-def info_kernel(regions, lower_ref, aniso_ref, damp_ref, share_ref, info_ref):
+def info_kernel(regions, lower_ref, aniso_ref, damp_ref, share_ref, m_ref, reg_ref, info_ref):
     here = lax.axis_index("img")
     lane = lane_iota()
     table_a = jnp.zeros((SUB, LANES), jnp.float32)
@@ -57,7 +58,7 @@
     return jnp.where(below, jnp.where(odd, 1, 0), jnp.where(odd, 0, 1)) == 1, odd
 
 
-def gather_kernel(info_ref, m_ref, first_ref, second_ref, part_ref, near_ref):
+def gather_kernel(info_ref, m_ref, first_ref, second_ref, part_ref, near_ref, sent_ref):
     here = lax.axis_index("img")
     pick, odd = take_first(info_ref, here)
     chunks = 4
@@ -76,6 +77,8 @@
                 sums[c + COMPS * u] = sums[c + COMPS * u] + diff * diff
         for c, start, cells in done:
             near_ref[c, pl.ds(start, SUB), :] = cells
+            if c >= ALONG_Z:
+                sent_ref[c - ALONG_Z, pl.ds(start, SUB), :] = cells
         return tuple(sums)
 
     zero = jnp.zeros((SUB, LANES), jnp.float32)
@@ -109,7 +112,7 @@
 
 
 def start_kernel(
-    ny, tiles, images, info_ref, sq_ref, m_ref, mp_ref, n_ref, np1_ref, np2_ref, reg_ref, regp_ref, main_ref, one_ref, two_ref
+    ny, tiles, images, info_ref, sq_ref, m_ref, mp_ref, n_ref, np1_ref, np2_ref, np3_ref, reg_ref, regp_ref, main_ref, one_ref, two_ref
 ):
     here = lax.axis_index("img")
     lane = lane_iota()
@@ -141,7 +144,10 @@
                     near = [n_ref[c, rows, :] for c in range(COMPS)]
                 else:
                     near = [
-                        jnp.where(pick, np1_ref[c, rows, :], np2_ref[c, rows, :]) for c in range(COMPS)
+                        jnp.where(pick, np1_ref[c, rows, :], np2_ref[c, rows, :])
+                        if c < ALONG_Z
+                        else np3_ref[c - ALONG_Z, rows, :]
+                        for c in range(COMPS)
                     ]
                 v = normal([w_own * own[c, rows, :] + w_near * near[c] for c in range(COMPS)])
                 v = list(v) + [reg[rows, :].astype(jnp.float32)]
@@ -209,15 +215,6 @@
     def ends_of(k, new):
         shift = (DEPTH * (k + 1)) & (LANES - 1)
         return [pltpu.roll(new[c], shift, 1) for c in range(COMPS)]
-
-    def copy(r, carry):
-        for u in range(2):
-            for t in range(tiles):
-                for c in range(COMPS):
-                    main0[c, 2 * r + u, t] = start_ref[c, 2 * r + u, t]
-        return carry
-
-    lax.fori_loop(0, window // 2, copy, 0)
 
     def seam_of(left, right):
         return jnp.where(head_lane, pltpu.roll(left, 1, 1), pltpu.roll(right, LANES - 1, 1))
@@ -400,24 +397,37 @@
     info = pl.pallas_call(
         functools.partial(info_kernel, anisotropy.shape[0]),
         out_shape=jax.ShapeDtypeStruct((5,) + vreg, f32),
-        in_specs=[smem] * 3 + [vmem],
+        in_specs=[smem] * 3 + [vmem] * 3,
         out_specs=vmem,
         compiler_params=limit,
         name="small_arguments",
-    )(lower_image, anisotropy, damping, image_weights.reshape(1, -1))
+    )(
+        lower_image,
+        anisotropy,
+        damping,
+        image_weights.reshape(1, -1),
+        own.reshape(flat),
+        regions.reshape(flat[1:]),
+    )
     own_p, info = lax.optimization_barrier((own_p, info))
-    first_p = swapped(own_p, "img", 0, False)
-    second_p = swapped(own_p, "img", 1, False)
+    first_p = swapped(own_p[:ALONG_Z], "img", 0, False)
+    second_p = swapped(own_p[:ALONG_Z], "img", 1, False)
     late_regions, info = lax.optimization_barrier((regions, info))
     reg_p = around(late_regions, 1)
-    part, near = pl.pallas_call(
+    info, reg_p = lax.optimization_barrier((info, reg_p))
+    part, near, sent = pl.pallas_call(
         gather_kernel,
-        out_shape=(jax.ShapeDtypeStruct((devices, LANES), f32), jax.ShapeDtypeStruct(flat, f32)),
+        out_shape=(
+            jax.ShapeDtypeStruct((devices, LANES), f32),
+            jax.ShapeDtypeStruct(flat, f32),
+            jax.ShapeDtypeStruct((comps - ALONG_Z,) + flat[1:], f32),
+        ),
         in_specs=[vmem] * 4,
-        out_specs=(vmem,) * 2,
+        out_specs=(vmem,) * 3,
         compiler_params=limit,
         name="gather_images",
     )(info, own.reshape(flat), first.reshape(flat), second.reshape(flat))
+    sent_p = around(sent.reshape((comps - ALONG_Z,) + own.shape[1:]), 2)
     squares = lax.all_to_all(part, ("img", "gx", "gy"), 0, 0, tiled=True)
 
     window = ny + 2 * DEPTH
@@ -426,7 +436,7 @@
     start, one, two = pl.pallas_call(
         functools.partial(start_kernel, ny, tiles, images),
         out_shape=(jax.ShapeDtypeStruct((comps, window, tiles) + vreg, f32), packed, packed),
-        in_specs=[vmem] * 9,
+        in_specs=[vmem] * 10,
         out_specs=(vmem,) * 3,
         compiler_params=limit,
         name="start",
@@ -436,8 +446,9 @@
         own.reshape(flat),
         own_p.reshape(flat),
         near,
-        first_p.reshape(flat),
-        second_p.reshape(flat),
+        first_p.reshape((ALONG_Z,) + flat[1:]),
+        second_p.reshape((ALONG_Z,) + flat[1:]),
+        sent_p.reshape((comps - ALONG_Z,) + flat[1:]),
         *tile_rows,
     )
     one = swapped(one, "gx", 0, True)
@@ -450,13 +461,13 @@
         compiler_params=limit,
         name="parameters",
     )(info, *tile_rows)
-    out = pl.pallas_call(
+    out, _ = pl.pallas_call(
         functools.partial(evolve_kernel, ny, tiles),
-        out_shape=jax.ShapeDtypeStruct(flat, f32),
+        out_shape=(jax.ShapeDtypeStruct(flat, f32), jax.ShapeDtypeStruct(start.shape, f32)),
         in_specs=[vmem] * 5,
-        out_specs=vmem,
+        out_specs=(vmem,) * 2,
+        input_output_aliases={1: 1},
         scratch_shapes=[
-            pltpu.VMEM((comps, window, tiles) + vreg, f32),
             pltpu.VMEM((comps, window, tiles) + vreg, f32),
             pltpu.VMEM((comps, 2, 2, tiles) + vreg, f32),
             pltpu.VMEM((comps, 2, 2, tiles) + vreg, f32),

time: 49.4 us -> 50.4 us (1.020)
  waiting for transfers between devices: 5.25 us -> 2.66 us
  local copies, waits for them, and re-layouts: 1.01 us -> 2.62 us
  blocking collectives: 9.68 us -> 11.2 us
  starting transfers between devices: 15.6 us -> 16.2 us
    ppermute x2 -> x3, waiting for transfers between devices: 3.56 us -> 0.97 us  [shifted(): return lax.ppermute(cells, axis, pairs)]
    unnamed x12 -> x16, local copies, waits for them, and re-layouts: 1.01 us -> 2.61 us
    all_to_all x1, blocking collectives: 9.68 us -> 11.2 us  [body(): squares = lax.all_to_all(part, ('img', 'gx', 'gy'), 0, 0, tiled=True)]
    ppermute x2 -> x3, starting transfers between devices: 4.51 us -> 5.28 us  [shifted(): return lax.ppermute(cells, axis, pairs)]
  transfers between devices with their start and end apart: 8 -> 9, of which waited for: 2 -> 2; matrix products, arithmetic and copies ran while one was open for 0% -> 0% of each run, Pallas kernels for 5% -> 5%
where the time goes in v17:
time: 50.4 us; the launch traced here: 50.1 us
  Pallas kernels  17.4 us (35%)
  starting transfers between devices  16.2 us (32%)
  blocking collectives  11.2 us (22%)
  waiting for transfers between devices  2.66 us (5%)
  local copies, waits for them, and re-layouts  2.62 us (5%)
    pallas_call x1, Pallas kernels, body(): pl.pallas_call(functools.partial(evolve_kernel, ny, tiles), out_shape=(ja...  12 us
    all_to_all x1, blocking collectives, body(): squares = lax.all_to_all(part, ('img', 'gx', 'gy'), 0, 0, tiled=True)  11.2 us
    ppermute x6, starting transfers between devices, swapped(): return lax.ppermute(cells, axis, pairs + [(j, i) for i, j in pairs])  10.9 us
    ppermute x3, starting transfers between devices, shifted(): return lax.ppermute(cells, axis, pairs)  5.28 us
    pallas_call x1, Pallas kernels, body(): pl.pallas_call(functools.partial(start_kernel, ny, tiles, images), out_sh...  2.91 us
    unnamed x16, local copies, waits for them, and re-layouts  2.61 us
    ppermute x6, waiting for transfers between devices, swapped(): return lax.ppermute(cells, axis, pairs + [(j, i) for i, j in pairs])  1.69 us
    pallas_call x1, Pallas kernels, body(): pl.pallas_call(functools.partial(look_up_kernel, ny, tiles), out_shape=ja...  1.57 us
  transfers between devices with their start and end apart: 9, of which 2 were waited for; matrix products, arithmetic and copies ran while one was open for 0% of the time, Pallas kernels for 5%

profile of v17, /device:TPU:0, one launch (start us, length us, event | category | flops | bytes accessed | tf_op | source)
XLA Modules:
  0.0 50.1 jit_solution(8964616381590823224)
XLA Ops:
  0.0 2.9 %collective-permute-start = (f32[3,16,16,128]{3,2,1,0:T(8,128)}, f32[3,16,16,128]{3,2,1,0:T(8,128)S(1)}, u32[]{:S(2)}, u32[]{:S(2)}) collective-permute-start(f32[3,16,16,128]{3,2,1,0:T(8,128)} %bitcast.17), channel_id=1, source_target_pairs={{0,1},{1,0},{2,3},{3,2},{4,5},{5,4},{6,7},{7,6},{8,9},{9,8},{10,11... | collective-permute-start | bytes 1179656 | tf_op jit(solution)/shard_map/ppermute | solution.py:360
  2.9 0.7 %collective-permute-start.3 = (f32[3,16,16,128]{3,2,1,0:T(8,128)}, f32[3,16,16,128]{3,2,1,0:T(8,128)S(1)}, u32[]{:S(2)}, u32[]{:S(2)}) collective-permute-start(f32[3,16,16,128]{3,2,1,0:T(8,128)} %bitcast.18), channel_id=1, source_target_pairs={{8,16},{16,8},{9,17},{17,9},{10,18},{18,10},{11,19},{19,11},{12,20... | collective-permute-start | bytes 1179656 | tf_op jit(solution)/shard_map/ppermute | solution.py:366
  3.6 4.4 %collective-permute-start.2 = (f32[3,16,16,128]{3,2,1,0:T(8,128)}, f32[3,16,16,128]{3,2,1,0:T(8,128)S(1)}, u32[]{:S(2)}, u32[]{:S(2)}) collective-permute-start(f32[3,16,16,128]{3,2,1,0:T(8,128)} %bitcast.19), channel_id=1, source_target_pairs={{0,8},{16,24},{8,0},{24,16},{1,9},{17,25},{9,1},{25,17},{2,10},{18... | collective-permute-start | bytes 1179656 | tf_op jit(solution)/shard_map/ppermute | solution.py:366
  8.1 0.0 copy-start.7
  8.1 0.0 copy-start.4
  8.1 0.0 copy-start.5
  8.1 0.0 copy-start.6
  8.1 0.6 %copy-done.7 = f32[3]{0:T(128)S(1)} copy-done((f32[3]{0:T(128)S(1)}, f32[3]{0:T(128)}, u32[]{:S(2)}) %copy-start.7) | copy-done | bytes 36
  8.7 0.0 copy-done.4
  8.7 0.0 copy-done.5
  8.8 0.0 copy-done.6
  8.8 0.0 copy-start
  8.8 1.0 %copy-done = f32[1,3,16,16,128]{4,3,2,1,0:T(8,128)S(1)} copy-done((f32[1,3,16,16,128]{4,3,2,1,0:T(8,128)S(1)}, f32[1,3,16,16,128]{4,3,2,1,0:T(8,128)}, u32[]{:S(2)}) %copy-start) | copy-done | bytes 393240
  9.8 0.0 copy-start.2
  9.8 0.9 %copy-done.2 = s32[16,16,128]{2,1,0:T(8,128)S(1)} copy-done((s32[16,16,128]{2,1,0:T(8,128)S(1)}, s32[16,16,128]{2,1,0:T(8,128)}, u32[]{:S(2)}) %copy-start.2) | copy-done | bytes 131096
  10.7 0.6 %small_arguments.1.info_ref = f32[5,8,128]{2,1,0:T(8,128)S(1)} custom-call(s32[4]{0:T(128)S(1)} %copy-done.4, f32[8]{0:T(128)S(1)} %copy-done.5, f32[8]{0:T(128)S(1)} %copy-done.6, f32[1,3]{1,0:T(1,128)S(1)} %bitcast.36, f32[3,256,128]{2,1,0:T(8,128)S(1)} %bitcast.20, s32[256,128]{1,0:T(8,128)S(1)} %bitcast.23), custom_call_target="tpu_custom_call" | custom-call | tf_op jit(solution)/shard_map/small_arguments/pallas_call | solution.py:397
  11.3 0.0 copy-start.1
  11.3 1.0 %collective-permute-done = f32[3,16,16,128]{3,2,1,0:T(8,128)S(1)} collective-permute-done((f32[3,16,16,128]{3,2,1,0:T(8,128)}, f32[3,16,16,128]{3,2,1,0:T(8,128)S(1)}, u32[]{:S(2)}, u32[]{:S(2)}) %collective-permute-start) | collective-permute-done | bytes 393248 | tf_op jit(solution)/shard_map/ppermute | solution.py:360
  12.3 1.7 %collective-permute-start.1 = (s32[16,16,128]{2,1,0:T(8,128)S(1)}, s32[16,16,128]{2,1,0:T(8,128)S(1)}, u32[]{:S(2)}, u32[]{:S(2)}) collective-permute-start(s32[16,16,128]{2,1,0:T(8,128)S(1)} %copy-done.2), channel_id=1, source_target_pairs={{0,1},{1,0},{2,3},{3,2},{4,5},{5,4},{6,7},{7,6},{8,9},{9,8},{10,11... | collective-permute-start | bytes 393224 | tf_op jit(solution)/shard_map/ppermute | solution.py:360
  14.0 0.7 %collective-permute-start.5 = (f32[2,16,16,128]{3,2,1,0:T(8,128)S(1)}, f32[2,16,16,128]{3,2,1,0:T(8,128)S(1)}, u32[]{:S(2)}, u32[]{:S(2)}) collective-permute-start(f32[2,16,16,128]{3,2,1,0:T(8,128)S(1)} %slice.4), channel_id=1, source_target_pairs={{8,16},{16,8},{9,17},{17,9},{10,18},{18,10},{11,19},{19,11},{12,20... | collective-permute-start | bytes 786440 | tf_op jit(solution)/shard_map/ppermute | solution.py:366
  14.7 4.4 %collective-permute-start.4 = (f32[2,16,16,128]{3,2,1,0:T(8,128)S(1)}, f32[2,16,16,128]{3,2,1,0:T(8,128)S(1)}, u32[]{:S(2)}, u32[]{:S(2)}) collective-permute-start(f32[2,16,16,128]{3,2,1,0:T(8,128)S(1)} %slice.4), channel_id=1, source_target_pairs={{0,8},{16,24},{8,0},{24,16},{1,9},{17,25},{9,1},{25,17},{2,10},{18... | collective-permute-start | bytes 786440 | tf_op jit(solution)/shard_map/ppermute | solution.py:366
  19.2 0.0 collective-permute-done.1
  19.2 0.0 collective-permute-done.3
  19.2 0.0 collective-permute-done.2
  19.2 0.0 copy-done.1
  19.2 0.0 copy-start.3
  19.2 0.3 gather_images.1
  19.5 0.6 %collective-permute-start.6 = (f32[1,16,16,128]{3,2,1,0:T(8,128)S(1)}, f32[1,16,16,128]{3,2,1,0:T(8,128)S(1)}, u32[]{:S(2)}, u32[]{:S(2)}) collective-permute-start(f32[1,16,16,128]{3,2,1,0:T(8,128)S(1)} %bitcast.37), channel_id=1, source_target_pairs={{0,1},{1,0},{2,3},{3,2},{4,5},{5,4},{6,7},{7,6},{8,9},{9,8},{10,11... | collective-permute-start | bytes 393224 | tf_op jit(solution)/shard_map/ppermute | solution.py:360
  20.1 11.2 %all_to_all.11 = f32[32,1,128]{2,1,0:T(1,128)S(1)} all-to-all(f32[32,1,128]{2,1,0:T(1,128)S(1)} %bitcast.35), channel_id=1, replica_groups=mesh['img'=4,'gx'=4,'gy'=2] {'img','gx','gy'}, dimensions={0} | all-to-all | bytes 32768 | tf_op jit(solution)/shard_map/all_to_all | solution.py:431
  31.3 0.0 collective-permute-done.6
  31.3 0.0 collective-permute-done.5
  31.3 0.0 collective-permute-done.4
  31.3 0.0 copy-done.3
  31.3 2.9 %start.1 = (f32[3,32,2,8,128]{4,3,2,1,0:T(8,128)S(1)}, f32[2,4,2,8,128]{4,3,2,1,0:T(8,128)S(1)}, f32[2,4,2,8,128]{4,3,2,1,0:T(8,128)S(1)}) custom-call(f32[5,8,128]{2,1,0:T(8,128)S(1)} %small_arguments.1.info_ref, f32[32,128]{1,0:T(8,128)S(1)} %bitcast.34, f32[3,256,128]{2,1,0:T(8,128)S(1)} %bitcast.22, f32[3,256,128]{2,1,0:T(8,128)S(1)} %bitcast.26, ...), custom_call_target="tpu_custom_call" | custom-call | tf_op jit(solution)/shard_map/start/pallas_call | solution.py:436
  34.2 0.0 collective-permute-start.7
  34.2 0.6 %collective-permute-start.8 = (f32[2,4,2,8,128]{4,3,2,1,0:T(8,128)S(1)}, f32[2,4,2,8,128]{4,3,2,1,0:T(8,128)S(1)}, u32[]{:S(2)}, u32[]{:S(2)}) collective-permute-start(f32[2,4,2,8,128]{4,3,2,1,0:T(8,128)S(1)} %get-tuple-element.29), channel_id=1, source_target_pairs={{2,4},{6,0},{4,2},{0,6},{3,5},{7,1},{5,3},{1,7},{10,12},{14,8},{12... | collective-permute-start | bytes 196616 | tf_op jit(solution)/shard_map/ppermute | solution.py:366
  34.9 1.6 %parameters.1.par = f32[3,32,2,8,128]{4,3,2,1,0:T(8,128)S(1)} custom-call(f32[5,8,128]{2,1,0:T(8,128)S(1)} %small_arguments.1.info_ref, s32[256,128]{1,0:T(8,128)S(1)} %bitcast.25, s32[256,128]{1,0:T(8,128)S(1)} %bitcast.28), custom_call_target="tpu_custom_call" | custom-call | tf_op jit(solution)/shard_map/parameters/pallas_call | solution.py:456
  36.4 0.0 collective-permute-done.7.one_ref
  36.4 1.7 %collective-permute-done.8.two_ref = f32[2,4,2,8,128]{4,3,2,1,0:T(8,128)S(1)} collective-permute-done((f32[2,4,2,8,128]{4,3,2,1,0:T(8,128)S(1)}, f32[2,4,2,8,128]{4,3,2,1,0:T(8,128)S(1)}, u32[]{:S(2)}, u32[]{:S(2)}) %collective-permute-start.8) | collective-permute-done | bytes 65568 | tf_op jit(solution)/shard_map/ppermute | solution.py:366
  38.1 12.0 %evolve.1 = (f32[3,256,128]{2,1,0:T(8,128)}, f32[3,32,2,8,128]{4,3,2,1,0:T(8,128)S(1)}) custom-call(f32[5,8,128]{2,1,0:T(8,128)S(1)} %small_arguments.1.info_ref, f32[3,32,2,8,128]{4,3,2,1,0:T(8,128)S(1)} %get-tuple-element.27.start_ref, f32[3,32,2,8,128]{4,3,2,1,0:T(8,128)S(1)} %parameters.1.par, ...), custom_call_target="tpu_custom_call", output_to_operand_aliasing={{1}: (1, {})} | custom-call | tf_op jit(solution)/shard_map/evolve/pallas_call | solution.py:464
  (1 shorter events, 0.0 us)
Async XLA Ops:
  0.0 12.3 %collective-permute-start = (f32[3,16,16,128]{3,2,1,0:T(8,128)}, f32[3,16,16,128]{3,2,1,0:T(8,128)S(1)}, u32[]{:S(2)}, u32[]{:S(2)}) collective-permute-start(f32[3,16,16,128]{3,2,1,0:T(8,128)} %bitcast.17), channel_id=1, source_target_pairs={{0,1},{1,0},{2,3},{3,2},{4,5},{5,4},{6,7},{7,6},{8,9},{9,8},{10,11... | collective-permute-start | bytes 1179656 | tf_op jit(solution)/shard_map/ppermute | solution.py:360
  2.9 16.2 %collective-permute-start.3 = (f32[3,16,16,128]{3,2,1,0:T(8,128)}, f32[3,16,16,128]{3,2,1,0:T(8,128)S(1)}, u32[]{:S(2)}, u32[]{:S(2)}) collective-permute-start(f32[3,16,16,128]{3,2,1,0:T(8,128)} %bitcast.18), channel_id=1, source_target_pairs={{8,16},{16,8},{9,17},{17,9},{10,18},{18,10},{11,19},{19,11},{12,20... | collective-permute-start | bytes 1179656 | tf_op jit(solution)/shard_map/ppermute | solution.py:366
  3.6 15.5 %collective-permute-start.2 = (f32[3,16,16,128]{3,2,1,0:T(8,128)}, f32[3,16,16,128]{3,2,1,0:T(8,128)S(1)}, u32[]{:S(2)}, u32[]{:S(2)}) collective-permute-start(f32[3,16,16,128]{3,2,1,0:T(8,128)} %bitcast.19), channel_id=1, source_target_pairs={{0,8},{16,24},{8,0},{24,16},{1,9},{17,25},{9,1},{25,17},{2,10},{18... | collective-permute-start | bytes 1179656 | tf_op jit(solution)/shard_map/ppermute | solution.py:366
  8.1 0.7 %copy-start.7 = (f32[3]{0:T(128)S(1)}, f32[3]{0:T(128)}, u32[]{:S(2)}) copy-start(f32[3]{0:T(128)} %param.8) | copy-start | bytes 40
  8.1 0.7 %copy-start.4 = (s32[4]{0:T(128)S(1)}, s32[4]{0:T(128)}, u32[]{:S(2)}) copy-start(s32[4]{0:T(128)} %lower_ref.1) | copy-start | bytes 52
  8.1 0.7 %copy-start.5 = (f32[8]{0:T(128)S(1)}, f32[8]{0:T(128)}, u32[]{:S(2)}) copy-start(f32[8]{0:T(128)} %aniso_ref.1) | copy-start | bytes 100
  8.1 0.7 %copy-start.6 = (f32[8]{0:T(128)S(1)}, f32[8]{0:T(128)}, u32[]{:S(2)}) copy-start(f32[8]{0:T(128)} %damp_ref.1) | copy-start | bytes 100
  8.8 1.0 %copy-start = (f32[1,3,16,16,128]{4,3,2,1,0:T(8,128)S(1)}, f32[1,3,16,16,128]{4,3,2,1,0:T(8,128)}, u32[]{:S(2)}) copy-start(f32[1,3,16,16,128]{4,3,2,1,0:T(8,128)} %param.6) | copy-start | bytes 1179652
  9.8 0.9 %copy-start.2 = (s32[16,16,128]{2,1,0:T(8,128)S(1)}, s32[16,16,128]{2,1,0:T(8,128)}, u32[]{:S(2)}) copy-start(s32[16,16,128]{2,1,0:T(8,128)} %param.9) | copy-start | bytes 393220
  11.3 7.9 %copy-start.1 = (f32[1,3,16,16,128]{4,3,2,1,0:T(8,128)S(1)}, f32[1,3,16,16,128]{4,3,2,1,0:T(8,128)}, u32[]{:S(2)}) copy-start(f32[1,3,16,16,128]{4,3,2,1,0:T(8,128)} %param.6) | copy-start | bytes 1179652
  12.3 6.9 %collective-permute-start.1 = (s32[16,16,128]{2,1,0:T(8,128)S(1)}, s32[16,16,128]{2,1,0:T(8,128)S(1)}, u32[]{:S(2)}, u32[]{:S(2)}) collective-permute-start(s32[16,16,128]{2,1,0:T(8,128)S(1)} %copy-done.2), channel_id=1, source_target_pairs={{0,1},{1,0},{2,3},{3,2},{4,5},{5,4},{6,7},{7,6},{8,9},{9,8},{10,11... | collective-permute-start | bytes 393224 | tf_op jit(solution)/shard_map/ppermute | solution.py:360
  14.0 17.2 %collective-permute-start.5 = (f32[2,16,16,128]{3,2,1,0:T(8,128)S(1)}, f32[2,16,16,128]{3,2,1,0:T(8,128)S(1)}, u32[]{:S(2)}, u32[]{:S(2)}) collective-permute-start(f32[2,16,16,128]{3,2,1,0:T(8,128)S(1)} %slice.4), channel_id=1, source_target_pairs={{8,16},{16,8},{9,17},{17,9},{10,18},{18,10},{11,19},{19,11},{12,20... | collective-permute-start | bytes 786440 | tf_op jit(solution)/shard_map/ppermute | solution.py:366
  14.7 16.6 %collective-permute-start.4 = (f32[2,16,16,128]{3,2,1,0:T(8,128)S(1)}, f32[2,16,16,128]{3,2,1,0:T(8,128)S(1)}, u32[]{:S(2)}, u32[]{:S(2)}) collective-permute-start(f32[2,16,16,128]{3,2,1,0:T(8,128)S(1)} %slice.4), channel_id=1, source_target_pairs={{0,8},{16,24},{8,0},{24,16},{1,9},{17,25},{9,1},{25,17},{2,10},{18... | collective-permute-start | bytes 786440 | tf_op jit(solution)/shard_map/ppermute | solution.py:366
  19.2 12.1 %copy-start.3 = (s32[16,16,128]{2,1,0:T(8,128)S(1)}, s32[16,16,128]{2,1,0:T(8,128)}, u32[]{:S(2)}) copy-start(s32[16,16,128]{2,1,0:T(8,128)} %param.9) | copy-start | bytes 393220
  19.5 11.8 %collective-permute-start.6 = (f32[1,16,16,128]{3,2,1,0:T(8,128)S(1)}, f32[1,16,16,128]{3,2,1,0:T(8,128)S(1)}, u32[]{:S(2)}, u32[]{:S(2)}) collective-permute-start(f32[1,16,16,128]{3,2,1,0:T(8,128)S(1)} %bitcast.37), channel_id=1, source_target_pairs={{0,1},{1,0},{2,3},{3,2},{4,5},{5,4},{6,7},{7,6},{8,9},{9,8},{10,11... | collective-permute-start | bytes 393224 | tf_op jit(solution)/shard_map/ppermute | solution.py:360
  34.2 2.2 %collective-permute-start.7 = (f32[2,4,2,8,128]{4,3,2,1,0:T(8,128)S(1)}, f32[2,4,2,8,128]{4,3,2,1,0:T(8,128)S(1)}, u32[]{:S(2)}, u32[]{:S(2)}) collective-permute-start(f32[2,4,2,8,128]{4,3,2,1,0:T(8,128)S(1)} %get-tuple-element.28), channel_id=1, source_target_pairs={{0,2},{4,6},{2,0},{6,4},{1,3},{5,7},{3,1},{7,5},{8,10},{12,14},{10... | collective-permute-start | bytes 196616 | tf_op jit(solution)/shard_map/ppermute | solution.py:366
  34.2 3.9 %collective-permute-start.8 = (f32[2,4,2,8,128]{4,3,2,1,0:T(8,128)S(1)}, f32[2,4,2,8,128]{4,3,2,1,0:T(8,128)S(1)}, u32[]{:S(2)}, u32[]{:S(2)}) collective-permute-start(f32[2,4,2,8,128]{4,3,2,1,0:T(8,128)S(1)} %get-tuple-element.29), channel_id=1, source_target_pairs={{2,4},{6,0},{4,2},{0,6},{3,5},{7,1},{5,3},{1,7},{10,12},{14,8},{12... | collective-permute-start | bytes 196616 | tf_op jit(solution)/shard_map/ppermute | solution.py:366

commit v18 on v17

--- a/solution.py
+++ b/solution.py
@@ -131,28 +131,29 @@
     w_own = jnp.where(below, weight, 1.0 - weight)
     w_near = jnp.where(below, 1.0 - weight, weight)
 
-    def fill(k, carry):
-        done = []
-        after = (k + 1) & (ny - 1)
-        one = block == jnp.where(turned, after, k)
-        two = block == jnp.where(turned, k, after)
-        shift = (DEPTH * (k + 1)) & (LANES - 1)
-        for g, (own, reg) in enumerate(((m_ref, reg_ref), (mp_ref, regp_ref))):
-            for t in range(tiles):
-                rows = rows_at(ny, tiles, k, t)
-                if g == 0:
-                    near = [n_ref[c, rows, :] for c in range(COMPS)]
-                else:
-                    near = [
-                        jnp.where(pick, np1_ref[c, rows, :], np2_ref[c, rows, :])
-                        if c < ALONG_Z
-                        else np3_ref[c - ALONG_Z, rows, :]
-                        for c in range(COMPS)
-                    ]
-                v = normal([w_own * own[c, rows, :] + w_near * near[c] for c in range(COMPS)])
-                v = list(v) + [reg[rows, :].astype(jnp.float32)]
-                done.append((g, t, v, [pltpu.roll(x, shift, 1) for x in v]))
-        for g, t, v, ends in done:
+    def fill(i, carry):
+        done = []
+        for k in (2 * i, 2 * i + 1):
+            after = (k + 1) & (ny - 1)
+            one = block == jnp.where(turned, after, k)
+            two = block == jnp.where(turned, k, after)
+            shift = (DEPTH * (k + 1)) & (LANES - 1)
+            for g, (own, reg) in enumerate(((m_ref, reg_ref), (mp_ref, regp_ref))):
+                for t in range(tiles):
+                    rows = rows_at(ny, tiles, k, t)
+                    if g == 0:
+                        near = [n_ref[c, rows, :] for c in range(COMPS)]
+                    else:
+                        near = [
+                            jnp.where(pick, np1_ref[c, rows, :], np2_ref[c, rows, :])
+                            if c < ALONG_Z
+                            else np3_ref[c - ALONG_Z, rows, :]
+                            for c in range(COMPS)
+                        ]
+                    v = normal([w_own * own[c, rows, :] + w_near * near[c] for c in range(COMPS)])
+                    v = list(v) + [reg[rows, :].astype(jnp.float32)]
+                    done.append((k, g, t, one, two, v, [pltpu.roll(x, shift, 1) for x in v]))
+        for k, g, t, one, two, v, ends in done:
             for c in range(COMPS):
                 main_ref[c, g * ny + k, t] = v[c]
             for c in range(COMPS + 1):
@@ -160,7 +161,7 @@
                 pltpu.store(two_ref.at[g, c, t], ends[c], mask=two)
         return carry
 
-    lax.fori_loop(0, ny, fill, 0)
+    lax.fori_loop(0, ny // 2, fill, 0)
 
 
 def look_up(info_ref, region):
@@ -414,7 +415,6 @@
     second_p = swapped(own_p[:ALONG_Z], "img", 1, False)
     late_regions, info = lax.optimization_barrier((regions, info))
     reg_p = around(late_regions, 1)
-    info, reg_p = lax.optimization_barrier((info, reg_p))
     part, near, sent = pl.pallas_call(
         gather_kernel,
         out_shape=(

time: 50.4 us -> 49 us (0.972)
  Pallas kernels: 17.4 us -> 16.6 us
  blocking collectives: 11.2 us -> 10.6 us
    pallas_call x1, Pallas kernels: 2.91 us -> 2.13 us  [body(): pl.pallas_call(functools.partial(start_kernel, ny, tiles, images), out_sh...]
    all_to_all x1, blocking collectives: 11.2 us -> 10.6 us  [body(): squares = lax.all_to_all(part, ('img', 'gx', 'gy'), 0, 0, tiled=True)]
where the time goes in v18:
time: 49 us; the launch traced here: 48.8 us
  Pallas kernels  16.6 us (34%)
  starting transfers between devices  16.2 us (33%)
  blocking collectives  10.6 us (22%)
  waiting for transfers between devices  2.66 us (5%)
  local copies, waits for them, and re-layouts  2.62 us (5%)
    pallas_call x1, Pallas kernels, body(): pl.pallas_call(functools.partial(evolve_kernel, ny, tiles), out_shape=(ja...  12 us
    ppermute x6, starting transfers between devices, swapped(): return lax.ppermute(cells, axis, pairs + [(j, i) for i, j in pairs])  11.2 us
    all_to_all x1, blocking collectives, body(): squares = lax.all_to_all(part, ('img', 'gx', 'gy'), 0, 0, tiled=True)  10.6 us
    ppermute x3, starting transfers between devices, shifted(): return lax.ppermute(cells, axis, pairs)  5.05 us
    unnamed x16, local copies, waits for them, and re-layouts  2.61 us
    pallas_call x1, Pallas kernels, body(): pl.pallas_call(functools.partial(start_kernel, ny, tiles, images), out_sh...  2.13 us
    ppermute x6, waiting for transfers between devices, swapped(): return lax.ppermute(cells, axis, pairs + [(j, i) for i, j in pairs])  1.69 us
    pallas_call x1, Pallas kernels, body(): pl.pallas_call(functools.partial(look_up_kernel, ny, tiles), out_shape=ja...  1.57 us
  transfers between devices with their start and end apart: 9, of which 2 were waited for; matrix products, arithmetic and copies ran while one was open for 0% of the time, Pallas kernels for 5%

profile of v18, /device:TPU:0, one launch (start us, length us, event | category | flops | bytes accessed | tf_op | source)
XLA Modules:
  0.0 48.8 jit_solution(17418043697747999526)
XLA Ops:
  0.0 2.9 %collective-permute-start = (f32[3,16,16,128]{3,2,1,0:T(8,128)}, f32[3,16,16,128]{3,2,1,0:T(8,128)S(1)}, u32[]{:S(2)}, u32[]{:S(2)}) collective-permute-start(f32[3,16,16,128]{3,2,1,0:T(8,128)} %bitcast.17), channel_id=1, source_target_pairs={{0,1},{1,0},{2,3},{3,2},{4,5},{5,4},{6,7},{7,6},{8,9},{9,8},{10,11... | collective-permute-start | bytes 1179656 | tf_op jit(solution)/shard_map/ppermute | solution.py:361
  2.9 0.7 %collective-permute-start.2 = (f32[3,16,16,128]{3,2,1,0:T(8,128)}, f32[3,16,16,128]{3,2,1,0:T(8,128)S(1)}, u32[]{:S(2)}, u32[]{:S(2)}) collective-permute-start(f32[3,16,16,128]{3,2,1,0:T(8,128)} %bitcast.18), channel_id=1, source_target_pairs={{8,16},{16,8},{9,17},{17,9},{10,18},{18,10},{11,19},{19,11},{12,20... | collective-permute-start | bytes 1179656 | tf_op jit(solution)/shard_map/ppermute | solution.py:367
  3.6 4.4 %collective-permute-start.1 = (f32[3,16,16,128]{3,2,1,0:T(8,128)}, f32[3,16,16,128]{3,2,1,0:T(8,128)S(1)}, u32[]{:S(2)}, u32[]{:S(2)}) collective-permute-start(f32[3,16,16,128]{3,2,1,0:T(8,128)} %bitcast.19), channel_id=1, source_target_pairs={{0,8},{16,24},{8,0},{24,16},{1,9},{17,25},{9,1},{25,17},{2,10},{18... | collective-permute-start | bytes 1179656 | tf_op jit(solution)/shard_map/ppermute | solution.py:367
  8.1 0.0 copy-start.7
  8.1 0.0 copy-start.4
  8.1 0.0 copy-start.5
  8.1 0.0 copy-start.6
  8.1 0.6 %copy-done.7 = f32[3]{0:T(128)S(1)} copy-done((f32[3]{0:T(128)S(1)}, f32[3]{0:T(128)}, u32[]{:S(2)}) %copy-start.7) | copy-done | bytes 36
  8.7 0.0 copy-done.4
  8.7 0.0 copy-done.5
  8.8 0.0 copy-done.6
  8.8 0.0 copy-start
  8.8 1.0 %copy-done = f32[1,3,16,16,128]{4,3,2,1,0:T(8,128)S(1)} copy-done((f32[1,3,16,16,128]{4,3,2,1,0:T(8,128)S(1)}, f32[1,3,16,16,128]{4,3,2,1,0:T(8,128)}, u32[]{:S(2)}) %copy-start) | copy-done | bytes 393240
  9.8 0.0 copy-start.2
  9.8 0.9 %copy-done.2 = s32[16,16,128]{2,1,0:T(8,128)S(1)} copy-done((s32[16,16,128]{2,1,0:T(8,128)S(1)}, s32[16,16,128]{2,1,0:T(8,128)}, u32[]{:S(2)}) %copy-start.2) | copy-done | bytes 131096
  10.7 0.6 %small_arguments.1.info_ref = f32[5,8,128]{2,1,0:T(8,128)S(1)} custom-call(s32[4]{0:T(128)S(1)} %copy-done.4, f32[8]{0:T(128)S(1)} %copy-done.5, f32[8]{0:T(128)S(1)} %copy-done.6, f32[1,3]{1,0:T(1,128)S(1)} %bitcast.36, f32[3,256,128]{2,1,0:T(8,128)S(1)} %bitcast.20, s32[256,128]{1,0:T(8,128)S(1)} %bitcast.23), custom_call_target="tpu_custom_call" | custom-call | tf_op jit(solution)/shard_map/small_arguments/pallas_call | solution.py:398
  11.3 0.0 copy-start.1
  11.3 1.0 %collective-permute-done = f32[3,16,16,128]{3,2,1,0:T(8,128)S(1)} collective-permute-done((f32[3,16,16,128]{3,2,1,0:T(8,128)}, f32[3,16,16,128]{3,2,1,0:T(8,128)S(1)}, u32[]{:S(2)}, u32[]{:S(2)}) %collective-permute-start) | collective-permute-done | bytes 393248 | tf_op jit(solution)/shard_map/ppermute | solution.py:361
  12.3 0.7 %collective-permute-start.4 = (f32[2,16,16,128]{3,2,1,0:T(8,128)S(1)}, f32[2,16,16,128]{3,2,1,0:T(8,128)S(1)}, u32[]{:S(2)}, u32[]{:S(2)}) collective-permute-start(f32[2,16,16,128]{3,2,1,0:T(8,128)S(1)} %slice.4), channel_id=1, source_target_pairs={{8,16},{16,8},{9,17},{17,9},{10,18},{18,10},{11,19},{19,11},{12,20... | collective-permute-start | bytes 786440 | tf_op jit(solution)/shard_map/ppermute | solution.py:367
  13.0 4.7 %collective-permute-start.3 = (f32[2,16,16,128]{3,2,1,0:T(8,128)S(1)}, f32[2,16,16,128]{3,2,1,0:T(8,128)S(1)}, u32[]{:S(2)}, u32[]{:S(2)}) collective-permute-start(f32[2,16,16,128]{3,2,1,0:T(8,128)S(1)} %slice.4), channel_id=1, source_target_pairs={{0,8},{16,24},{8,0},{24,16},{1,9},{17,25},{9,1},{25,17},{2,10},{18... | collective-permute-start | bytes 786440 | tf_op jit(solution)/shard_map/ppermute | solution.py:367
  17.7 0.0 collective-permute-done.2
  17.7 0.0 collective-permute-done.1
  17.7 0.0 copy-done.1
  17.7 0.0 copy-start.3
  17.7 0.3 gather_images.1
  18.0 1.6 %collective-permute-start.5 = (f32[1,16,16,128]{3,2,1,0:T(8,128)S(1)}, f32[1,16,16,128]{3,2,1,0:T(8,128)S(1)}, u32[]{:S(2)}, u32[]{:S(2)}) collective-permute-start(f32[1,16,16,128]{3,2,1,0:T(8,128)S(1)} %bitcast.37), channel_id=1, source_target_pairs={{0,1},{1,0},{2,3},{3,2},{4,5},{5,4},{6,7},{7,6},{8,9},{9,8},{10,11... | collective-permute-start | bytes 393224 | tf_op jit(solution)/shard_map/ppermute | solution.py:361
  19.5 0.0 copy-done.3
  19.5 0.6 %collective-permute-start.6 = (s32[16,16,128]{2,1,0:T(8,128)S(1)}, s32[16,16,128]{2,1,0:T(8,128)S(1)}, u32[]{:S(2)}, u32[]{:S(2)}) collective-permute-start(s32[16,16,128]{2,1,0:T(8,128)S(1)} %copy-done.3), channel_id=1, source_target_pairs={{0,1},{1,0},{2,3},{3,2},{4,5},{5,4},{6,7},{7,6},{8,9},{9,8},{10,11... | collective-permute-start | bytes 393224 | tf_op jit(solution)/shard_map/ppermute | solution.py:361
  20.1 10.6 %all_to_all.11 = f32[32,1,128]{2,1,0:T(1,128)S(1)} all-to-all(f32[32,1,128]{2,1,0:T(1,128)S(1)} %bitcast.35), channel_id=1, replica_groups=mesh['img'=4,'gx'=4,'gy'=2] {'img','gx','gy'}, dimensions={0} | all-to-all | bytes 32768 | tf_op jit(solution)/shard_map/all_to_all | solution.py:431
  30.7 0.0 collective-permute-done.5
  30.7 0.0 collective-permute-done.6
  30.7 0.0 collective-permute-done.4
  30.7 0.0 collective-permute-done.3
  30.7 2.1 %start.1 = (f32[3,32,2,8,128]{4,3,2,1,0:T(8,128)S(1)}, f32[2,4,2,8,128]{4,3,2,1,0:T(8,128)S(1)}, f32[2,4,2,8,128]{4,3,2,1,0:T(8,128)S(1)}) custom-call(f32[5,8,128]{2,1,0:T(8,128)S(1)} %small_arguments.1.info_ref, f32[32,128]{1,0:T(8,128)S(1)} %bitcast.34, f32[3,256,128]{2,1,0:T(8,128)S(1)} %bitcast.22, f32[3,256,128]{2,1,0:T(8,128)S(1)} %bitcast.26, ...), custom_call_target="tpu_custom_call" | custom-call | tf_op jit(solution)/shard_map/start/pallas_call | solution.py:436
  32.8 0.0 collective-permute-start.7
  32.9 0.6 %collective-permute-start.8 = (f32[2,4,2,8,128]{4,3,2,1,0:T(8,128)S(1)}, f32[2,4,2,8,128]{4,3,2,1,0:T(8,128)S(1)}, u32[]{:S(2)}, u32[]{:S(2)}) collective-permute-start(f32[2,4,2,8,128]{4,3,2,1,0:T(8,128)S(1)} %get-tuple-element.25), channel_id=1, source_target_pairs={{2,4},{6,0},{4,2},{0,6},{3,5},{7,1},{5,3},{1,7},{10,12},{14,8},{12... | collective-permute-start | bytes 196616 | tf_op jit(solution)/shard_map/ppermute | solution.py:367
  33.5 1.6 %parameters.1.par = f32[3,32,2,8,128]{4,3,2,1,0:T(8,128)S(1)} custom-call(f32[5,8,128]{2,1,0:T(8,128)S(1)} %small_arguments.1.info_ref, s32[256,128]{1,0:T(8,128)S(1)} %bitcast.25, s32[256,128]{1,0:T(8,128)S(1)} %bitcast.28), custom_call_target="tpu_custom_call" | custom-call | tf_op jit(solution)/shard_map/parameters/pallas_call | solution.py:456
  35.1 0.0 collective-permute-done.7.one_ref
  35.1 1.7 %collective-permute-done.8.two_ref = f32[2,4,2,8,128]{4,3,2,1,0:T(8,128)S(1)} collective-permute-done((f32[2,4,2,8,128]{4,3,2,1,0:T(8,128)S(1)}, f32[2,4,2,8,128]{4,3,2,1,0:T(8,128)S(1)}, u32[]{:S(2)}, u32[]{:S(2)}) %collective-permute-start.8) | collective-permute-done | bytes 65568 | tf_op jit(solution)/shard_map/ppermute | solution.py:367
  36.8 12.0 %evolve.1 = (f32[3,256,128]{2,1,0:T(8,128)}, f32[3,32,2,8,128]{4,3,2,1,0:T(8,128)S(1)}) custom-call(f32[5,8,128]{2,1,0:T(8,128)S(1)} %small_arguments.1.info_ref, f32[3,32,2,8,128]{4,3,2,1,0:T(8,128)S(1)} %get-tuple-element.23.start_ref, f32[3,32,2,8,128]{4,3,2,1,0:T(8,128)S(1)} %parameters.1.par, ...), custom_call_target="tpu_custom_call", output_to_operand_aliasing={{1}: (1, {})} | custom-call | tf_op jit(solution)/shard_map/evolve/pallas_call | solution.py:464
  (1 shorter events, 0.0 us)
Async XLA Ops:
  0.0 12.3 %collective-permute-start = (f32[3,16,16,128]{3,2,1,0:T(8,128)}, f32[3,16,16,128]{3,2,1,0:T(8,128)S(1)}, u32[]{:S(2)}, u32[]{:S(2)}) collective-permute-start(f32[3,16,16,128]{3,2,1,0:T(8,128)} %bitcast.17), channel_id=1, source_target_pairs={{0,1},{1,0},{2,3},{3,2},{4,5},{5,4},{6,7},{7,6},{8,9},{9,8},{10,11... | collective-permute-start | bytes 1179656 | tf_op jit(solution)/shard_map/ppermute | solution.py:361
  2.9 14.7 %collective-permute-start.2 = (f32[3,16,16,128]{3,2,1,0:T(8,128)}, f32[3,16,16,128]{3,2,1,0:T(8,128)S(1)}, u32[]{:S(2)}, u32[]{:S(2)}) collective-permute-start(f32[3,16,16,128]{3,2,1,0:T(8,128)} %bitcast.18), channel_id=1, source_target_pairs={{8,16},{16,8},{9,17},{17,9},{10,18},{18,10},{11,19},{19,11},{12,20... | collective-permute-start | bytes 1179656 | tf_op jit(solution)/shard_map/ppermute | solution.py:367
  3.6 14.1 %collective-permute-start.1 = (f32[3,16,16,128]{3,2,1,0:T(8,128)}, f32[3,16,16,128]{3,2,1,0:T(8,128)S(1)}, u32[]{:S(2)}, u32[]{:S(2)}) collective-permute-start(f32[3,16,16,128]{3,2,1,0:T(8,128)} %bitcast.19), channel_id=1, source_target_pairs={{0,8},{16,24},{8,0},{24,16},{1,9},{17,25},{9,1},{25,17},{2,10},{18... | collective-permute-start | bytes 1179656 | tf_op jit(solution)/shard_map/ppermute | solution.py:367
  8.1 0.7 %copy-start.7 = (f32[3]{0:T(128)S(1)}, f32[3]{0:T(128)}, u32[]{:S(2)}) copy-start(f32[3]{0:T(128)} %param.8) | copy-start | bytes 40
  8.1 0.7 %copy-start.4 = (s32[4]{0:T(128)S(1)}, s32[4]{0:T(128)}, u32[]{:S(2)}) copy-start(s32[4]{0:T(128)} %lower_ref.1) | copy-start | bytes 52
  8.1 0.7 %copy-start.5 = (f32[8]{0:T(128)S(1)}, f32[8]{0:T(128)}, u32[]{:S(2)}) copy-start(f32[8]{0:T(128)} %aniso_ref.1) | copy-start | bytes 100
  8.1 0.7 %copy-start.6 = (f32[8]{0:T(128)S(1)}, f32[8]{0:T(128)}, u32[]{:S(2)}) copy-start(f32[8]{0:T(128)} %damp_ref.1) | copy-start | bytes 100
  8.8 1.0 %copy-start = (f32[1,3,16,16,128]{4,3,2,1,0:T(8,128)S(1)}, f32[1,3,16,16,128]{4,3,2,1,0:T(8,128)}, u32[]{:S(2)}) copy-start(f32[1,3,16,16,128]{4,3,2,1,0:T(8,128)} %param.6) | copy-start | bytes 1179652
  9.8 0.9 %copy-start.2 = (s32[16,16,128]{2,1,0:T(8,128)S(1)}, s32[16,16,128]{2,1,0:T(8,128)}, u32[]{:S(2)}) copy-start(s32[16,16,128]{2,1,0:T(8,128)} %param.9) | copy-start | bytes 393220
  11.3 6.4 %copy-start.1 = (f32[1,3,16,16,128]{4,3,2,1,0:T(8,128)S(1)}, f32[1,3,16,16,128]{4,3,2,1,0:T(8,128)}, u32[]{:S(2)}) copy-start(f32[1,3,16,16,128]{4,3,2,1,0:T(8,128)} %param.6) | copy-start | bytes 1179652
  12.3 18.4 %collective-permute-start.4 = (f32[2,16,16,128]{3,2,1,0:T(8,128)S(1)}, f32[2,16,16,128]{3,2,1,0:T(8,128)S(1)}, u32[]{:S(2)}, u32[]{:S(2)}) collective-permute-start(f32[2,16,16,128]{3,2,1,0:T(8,128)S(1)} %slice.4), channel_id=1, source_target_pairs={{8,16},{16,8},{9,17},{17,9},{10,18},{18,10},{11,19},{19,11},{12,20... | collective-permute-start | bytes 786440 | tf_op jit(solution)/shard_map/ppermute | solution.py:367
  13.0 17.7 %collective-permute-start.3 = (f32[2,16,16,128]{3,2,1,0:T(8,128)S(1)}, f32[2,16,16,128]{3,2,1,0:T(8,128)S(1)}, u32[]{:S(2)}, u32[]{:S(2)}) collective-permute-start(f32[2,16,16,128]{3,2,1,0:T(8,128)S(1)} %slice.4), channel_id=1, source_target_pairs={{0,8},{16,24},{8,0},{24,16},{1,9},{17,25},{9,1},{25,17},{2,10},{18... | collective-permute-start | bytes 786440 | tf_op jit(solution)/shard_map/ppermute | solution.py:367
  17.7 1.8 %copy-start.3 = (s32[16,16,128]{2,1,0:T(8,128)S(1)}, s32[16,16,128]{2,1,0:T(8,128)}, u32[]{:S(2)}) copy-start(s32[16,16,128]{2,1,0:T(8,128)} %param.9) | copy-start | bytes 393220
  18.0 12.7 %collective-permute-start.5 = (f32[1,16,16,128]{3,2,1,0:T(8,128)S(1)}, f32[1,16,16,128]{3,2,1,0:T(8,128)S(1)}, u32[]{:S(2)}, u32[]{:S(2)}) collective-permute-start(f32[1,16,16,128]{3,2,1,0:T(8,128)S(1)} %bitcast.37), channel_id=1, source_target_pairs={{0,1},{1,0},{2,3},{3,2},{4,5},{5,4},{6,7},{7,6},{8,9},{9,8},{10,11... | collective-permute-start | bytes 393224 | tf_op jit(solution)/shard_map/ppermute | solution.py:361
  19.5 11.1 %collective-permute-start.6 = (s32[16,16,128]{2,1,0:T(8,128)S(1)}, s32[16,16,128]{2,1,0:T(8,128)S(1)}, u32[]{:S(2)}, u32[]{:S(2)}) collective-permute-start(s32[16,16,128]{2,1,0:T(8,128)S(1)} %copy-done.3), channel_id=1, source_target_pairs={{0,1},{1,0},{2,3},{3,2},{4,5},{5,4},{6,7},{7,6},{8,9},{9,8},{10,11... | collective-permute-start | bytes 393224 | tf_op jit(solution)/shard_map/ppermute | solution.py:361
  32.8 2.3 %collective-permute-start.7 = (f32[2,4,2,8,128]{4,3,2,1,0:T(8,128)S(1)}, f32[2,4,2,8,128]{4,3,2,1,0:T(8,128)S(1)}, u32[]{:S(2)}, u32[]{:S(2)}) collective-permute-start(f32[2,4,2,8,128]{4,3,2,1,0:T(8,128)S(1)} %get-tuple-element.24), channel_id=1, source_target_pairs={{0,2},{4,6},{2,0},{6,4},{1,3},{5,7},{3,1},{7,5},{8,10},{12,14},{10... | collective-permute-start | bytes 196616 | tf_op jit(solution)/shard_map/ppermute | solution.py:367
  32.9 3.9 %collective-permute-start.8 = (f32[2,4,2,8,128]{4,3,2,1,0:T(8,128)S(1)}, f32[2,4,2,8,128]{4,3,2,1,0:T(8,128)S(1)}, u32[]{:S(2)}, u32[]{:S(2)}) collective-permute-start(f32[2,4,2,8,128]{4,3,2,1,0:T(8,128)S(1)} %get-tuple-element.25), channel_id=1, source_target_pairs={{2,4},{6,0},{4,2},{0,6},{3,5},{7,1},{5,3},{1,7},{10,12},{14,8},{12... | collective-permute-start | bytes 196616 | tf_op jit(solution)/shard_map/ppermute | solution.py:367

commit v19 on v10

--- a/solution.py
+++ b/solution.py
@@ -158,6 +158,25 @@
     return tuple(x * scale for x in v)
 
 
+def look_up(info_ref, region):
+    return [jnp.take_along_axis(info_ref[i], region, axis=1) for i in range(3)]
+
+
+def look_up_kernel(ny, tiles, info_ref, reg_ref, regp_ref, par_ref):
+    def fill(i, carry):
+        done = []
+        for k in (2 * i, 2 * i + 1):
+            for g, reg in enumerate((reg_ref, regp_ref)):
+                for t in range(tiles):
+                    done.append((g * ny + k, t, look_up(info_ref, reg[rows_at(ny, tiles, k, t), :])))
+        for r, t, p in done:
+            for i in range(3):
+                par_ref[i, r, t] = p[i]
+        return carry
+
+    lax.fori_loop(0, ny // 2, fill, 0)
+
+
 def evolve_kernel(
     ny,
     tiles,
@@ -168,8 +187,7 @@
     mp_ref,
     n_ref,
     np_ref,
-    reg_ref,
-    regp_ref,
+    par,
     strips_ref,
     stripsp_ref,
     out_ref,
@@ -180,7 +198,6 @@
     edge,
     seam0,
     seam1,
-    par,
     spar,
 ):
     main, strip, seam = (main0, main1), (strip0, strip1), (seam0, seam1)
@@ -208,35 +225,26 @@
     w_own = jnp.where(below, weight, 1.0 - weight)
     w_near = jnp.where(below, 1.0 - weight, weight)
 
-    tables = (info_ref[0], info_ref[1], info_ref[2])
-
-    def params(region):
-        return [jnp.take_along_axis(table, region, axis=1) for table in tables]
-
     def ends_of(k, new):
         shift = (DEPTH * (k + 1)) & (LANES - 1)
         return [pltpu.roll(new[c], shift, 1) for c in range(COMPS)]
 
-    def fill(k, carry):
-        done = []
-        for g, (own, near, reg) in enumerate(((m_ref, n_ref, reg_ref), (mp_ref, np_ref, regp_ref))):
-            for t in range(tiles):
-                rows = rows_at(ny, tiles, k, t)
-                v = normal(
-                    [
-                        w_own * own[c, rows, :] + w_near * near[c, rows, :]
-                        for c in range(COMPS)
-                    ]
-                )
-                done.append((g * ny + k, t, v, params(reg[rows, :])))
-        for r, t, v, p in done:
+    def fill(i, carry):
+        done = []
+        for k in (2 * i, 2 * i + 1):
+            for g, (own, near) in enumerate(((m_ref, n_ref), (mp_ref, np_ref))):
+                for t in range(tiles):
+                    rows = rows_at(ny, tiles, k, t)
+                    v = normal(
+                        [w_own * own[c, rows, :] + w_near * near[c, rows, :] for c in range(COMPS)]
+                    )
+                    done.append((g * ny + k, t, v))
+        for r, t, v in done:
             for c in range(COMPS):
                 main0[c, r, t] = v[c]
-            for i in range(3):
-                par[i, r, t] = p[i]
-        return carry
-
-    lax.fori_loop(0, ny, fill, 0)
+        return carry
+
+    lax.fori_loop(0, ny // 2, fill, 0)
 
     def seam_of(left, right):
         return jnp.where(head_lane, pltpu.roll(left, 1, 1), pltpu.roll(right, LANES - 1, 1))
@@ -248,7 +256,7 @@
                 v = normal(
                     [w_own * cells[side, COMPS + c, t] + w_near * cells[side, c, t] for c in range(COMPS)]
                 )
-                done.append((side, g, v, params(cells[side, 2 * COMPS, t].astype(jnp.int32))))
+                done.append((side, g, v, look_up(info_ref, cells[side, 2 * COMPS, t].astype(jnp.int32))))
         for side, g, v, p in done:
             for c in range(COMPS):
                 strip0[c, side, g, t] = v[c]
@@ -365,13 +373,14 @@
 
     lax.fori_loop(0, STEPS, step, 0)
 
-    def hand_out(k, carry):
-        for t in range(tiles):
-            for c in range(COMPS):
-                out_ref[c, rows_at(ny, tiles, k, t), :] = main[0][c, k, t]
-        return carry
-
-    lax.fori_loop(0, ny, hand_out, 0)
+    def hand_out(i, carry):
+        for k in (2 * i, 2 * i + 1):
+            for t in range(tiles):
+                for c in range(COMPS):
+                    out_ref[c, rows_at(ny, tiles, k, t), :] = main0[c, k, t]
+        return carry
+
+    lax.fori_loop(0, ny // 2, hand_out, 0)
 
 
 def shifted(cells, axis, step, closed):
@@ -459,6 +468,16 @@
     near_p = around(near.reshape(own.shape), 2)
     one = swapped(one, "gx", 0, True)
     two = swapped(two, "gx", 1, True)
+    window = ny + 2 * DEPTH
+    par = pl.pallas_call(
+        functools.partial(look_up_kernel, ny, tiles),
+        out_shape=jax.ShapeDtypeStruct((3, window, tiles) + vreg, f32),
+        in_specs=[vmem] * 3,
+        out_specs=vmem,
+        compiler_params=limit,
+        name="parameters",
+    )(info, regions.reshape(flat[1:]), reg_p.reshape(flat[1:]))
+    one, par = lax.optimization_barrier((one, par))
     strips = pl.pallas_call(
         merge_kernel,
         out_shape=jax.ShapeDtypeStruct((2,) + packed.shape, f32),
@@ -470,11 +489,10 @@
     strips_p = around_strips(strips)
     squares = lax.all_to_all(part, ("img", "gx", "gy"), 0, 0, tiled=True)
 
-    window = ny + 2 * DEPTH
     out = pl.pallas_call(
         functools.partial(evolve_kernel, ny, tiles, images),
         out_shape=jax.ShapeDtypeStruct(flat, f32),
-        in_specs=[vmem] * 10,
+        in_specs=[vmem] * 9,
         out_specs=vmem,
         scratch_shapes=[
             pltpu.VMEM((comps, window, tiles) + vreg, f32),
@@ -484,7 +502,6 @@
             pltpu.VMEM((comps, 2, tiles) + vreg, f32),
             pltpu.VMEM((comps, 2, tiles) + vreg, f32),
             pltpu.VMEM((comps, 2, tiles) + vreg, f32),
-            pltpu.VMEM((3, window, tiles) + vreg, f32),
             pltpu.VMEM((3, 2, 2, tiles) + vreg, f32),
         ],
         compiler_params=limit,
@@ -496,8 +513,7 @@
         own_p.reshape(flat),
         near,
         near_p.reshape(flat),
-        regions.reshape(flat[1:]),
-        reg_p.reshape(flat[1:]),
+        par,
         strips,
         strips_p,
     )

time: 49 us -> 48.5 us (0.990)
  waiting for transfers between devices: 6.42 us -> 5.42 us
  Pallas kernels: 16.2 us -> 16.7 us
    ppermute x4, waiting for transfers between devices: 1.98 us -> 0.98 us  [swapped(): return lax.ppermute(cells, axis, pairs + [(j, i) for i, j in pairs])]
    pallas_call x0 -> x1, Pallas kernels: none -> 0.98 us  [body(): pl.pallas_call(functools.partial(look_up_kernel, ny, tiles), out_shape=ja...]
  transfers between devices with their start and end apart: 8 -> 8, of which waited for: 2 -> 2; matrix products, arithmetic and copies ran while one was open for 0% -> 0% of each run, Pallas kernels for 3% -> 5%
where the time goes in v19:
time: 48.5 us; the launch traced here: 48.3 us
  Pallas kernels  16.7 us (34%)
  starting transfers between devices  12.4 us (26%)
  blocking collectives  11.1 us (23%)
  waiting for transfers between devices  5.42 us (11%)
  local copies, waits for them, and re-layouts  2.61 us (5%)
    pallas_call x1, Pallas kernels, body(): pl.pallas_call(functools.partial(evolve_kernel, ny, tiles, images), out_s...  13.1 us
    all_to_all x1, blocking collectives, body(): squares = lax.all_to_all(part, ('img', 'gx', 'gy'), 0, 0, tiled=True)  11.1 us
    ppermute x4, starting transfers between devices, swapped(): return lax.ppermute(cells, axis, pairs + [(j, i) for i, j in pairs])  6.75 us
    ppermute x4, starting transfers between devices, shifted(): return lax.ppermute(cells, axis, pairs)  5.69 us
    ppermute x4, waiting for transfers between devices, shifted(): return lax.ppermute(cells, axis, pairs)  4.44 us
    unnamed x16, local copies, waits for them, and re-layouts  2.61 us
    pallas_call x1, Pallas kernels, body(): pl.pallas_call(functools.partial(pack_kernel, ny, tiles, anisotropy.shape...  1.51 us
    pallas_call x1, Pallas kernels, body(): pl.pallas_call(functools.partial(gather_kernel, ny, tiles), out_shape=(ja...  1.05 us
  transfers between devices with their start and end apart: 8, of which 2 were waited for; matrix products, arithmetic and copies ran while one was open for 0% of the time, Pallas kernels for 5%

profile of v19, /device:TPU:0, one launch (start us, length us, event | category | flops | bytes accessed | tf_op | source)
XLA Modules:
  0.0 48.3 jit_solution(15522813731508591458)
XLA Ops:
  0.0 2.9 %collective-permute-start = (f32[3,16,16,128]{3,2,1,0:T(8,128)}, f32[3,16,16,128]{3,2,1,0:T(8,128)S(1)}, u32[]{:S(2)}, u32[]{:S(2)}) collective-permute-start(f32[3,16,16,128]{3,2,1,0:T(8,128)} %bitcast.15), channel_id=1, source_target_pairs={{0,1},{1,0},{2,3},{3,2},{4,5},{5,4},{6,7},{7,6},{8,9},{9,8},{10,11... | collective-permute-start | bytes 1179656 | tf_op jit(solution)/shard_map/ppermute | solution.py:389
  2.9 0.7 %collective-permute-start.3 = (f32[3,16,16,128]{3,2,1,0:T(8,128)}, f32[3,16,16,128]{3,2,1,0:T(8,128)S(1)}, u32[]{:S(2)}, u32[]{:S(2)}) collective-permute-start(f32[3,16,16,128]{3,2,1,0:T(8,128)} %bitcast.16), channel_id=1, source_target_pairs={{8,16},{16,8},{9,17},{17,9},{10,18},{18,10},{11,19},{19,11},{12,20... | collective-permute-start | bytes 1179656 | tf_op jit(solution)/shard_map/ppermute | solution.py:395
  3.6 4.4 %collective-permute-start.2 = (f32[3,16,16,128]{3,2,1,0:T(8,128)}, f32[3,16,16,128]{3,2,1,0:T(8,128)S(1)}, u32[]{:S(2)}, u32[]{:S(2)}) collective-permute-start(f32[3,16,16,128]{3,2,1,0:T(8,128)} %bitcast.17), channel_id=1, source_target_pairs={{0,8},{16,24},{8,0},{24,16},{1,9},{17,25},{9,1},{25,17},{2,10},{18... | collective-permute-start | bytes 1179656 | tf_op jit(solution)/shard_map/ppermute | solution.py:395
  8.1 0.0 copy-start.7
  8.1 0.0 copy-start.4
  8.1 0.0 copy-start.5
  8.1 0.0 copy-start.6
  8.1 0.6 %copy-done.7 = f32[3]{0:T(128)S(1)} copy-done((f32[3]{0:T(128)S(1)}, f32[3]{0:T(128)}, u32[]{:S(2)}) %copy-start.7) | copy-done | bytes 36
  8.7 0.0 copy-done.4
  8.7 0.0 copy-done.5
  8.7 0.0 copy-done.6
  8.8 0.0 copy-start
  8.8 1.0 %copy-done = f32[1,3,16,16,128]{4,3,2,1,0:T(8,128)S(1)} copy-done((f32[1,3,16,16,128]{4,3,2,1,0:T(8,128)S(1)}, f32[1,3,16,16,128]{4,3,2,1,0:T(8,128)}, u32[]{:S(2)}) %copy-start) | copy-done | bytes 393240
  9.8 0.0 copy-start.2
  9.8 0.9 %copy-done.2 = s32[16,16,128]{2,1,0:T(8,128)S(1)} copy-done((s32[16,16,128]{2,1,0:T(8,128)S(1)}, s32[16,16,128]{2,1,0:T(8,128)}, u32[]{:S(2)}) %copy-start.2) | copy-done | bytes 131096
  10.7 0.0 copy-start.1
  10.7 1.5 %pack_strips.1 = (f32[4,2,8,128]{3,2,1,0:T(8,128)S(1)}, f32[4,2,8,128]{3,2,1,0:T(8,128)S(1)}, f32[5,8,128]{2,1,0:T(8,128)S(1)}) custom-call(s32[4]{0:T(128)S(1)} %copy-done.4, f32[8]{0:T(128)S(1)} %copy-done.5, f32[8]{0:T(128)S(1)} %copy-done.6, f32[1,3]{1,0:T(1,128)S(1)} %bitcast.31, f32[3,256,128]{2,1,0:T(8,128)S(1)} %bitcast.18, s32[256,128]{1,0:T(8,128)S(1)} %bitcast.21), custom_call_target="tpu_custom_call" | custom-call | tf_op jit(solution)/shard_map/pack_strips/pallas_call | solution.py:436
  12.2 0.6 %collective-permute-start.1 = (s32[16,16,128]{2,1,0:T(8,128)S(1)}, s32[16,16,128]{2,1,0:T(8,128)S(1)}, u32[]{:S(2)}, u32[]{:S(2)}) collective-permute-start(s32[16,16,128]{2,1,0:T(8,128)S(1)} %copy-done.2), channel_id=1, source_target_pairs={{0,1},{1,0},{2,3},{3,2},{4,5},{5,4},{6,7},{7,6},{8,9},{9,8},{10,11... | collective-permute-start | bytes 393224 | tf_op jit(solution)/shard_map/ppermute | solution.py:389
  12.8 4.4 %collective-permute-done.1 = s32[16,16,128]{2,1,0:T(8,128)S(1)} collective-permute-done((s32[16,16,128]{2,1,0:T(8,128)S(1)}, s32[16,16,128]{2,1,0:T(8,128)S(1)}, u32[]{:S(2)}, u32[]{:S(2)}) %collective-permute-start.1) | collective-permute-done | bytes 131104 | tf_op jit(solution)/shard_map/ppermute | solution.py:389
  17.2 0.0 collective-permute-done
  17.2 0.0 collective-permute-done.3
  17.2 0.0 collective-permute-done.2
  17.2 0.0 copy-done.1
  17.2 0.0 copy-start.3
  17.2 1.1 %gather_images.1 = (f32[32,128]{1,0:T(8,128)S(1)}, f32[3,256,128]{2,1,0:T(8,128)S(1)}, f32[7,2,8,128]{3,2,1,0:T(8,128)S(1)}, f32[7,2,8,128]{3,2,1,0:T(8,128)S(1)}) custom-call(f32[5,8,128]{2,1,0:T(8,128)S(1)} %get-tuple-element.22.info_ref, f32[3,256,128]{2,1,0:T(8,128)S(1)} %bitcast.19, f32[3,256,128]{2,1,0:T(8,128)S(1)} %bitcast.24, ...), custom_call_target="tpu_custom_call" | custom-call | tf_op jit(solution)/shard_map/gather_images/pallas_call | solution.py:455
  18.3 0.6 %collective-permute-start.4 = (f32[3,16,16,128]{3,2,1,0:T(8,128)S(1)}, f32[3,16,16,128]{3,2,1,0:T(8,128)S(1)}, u32[]{:S(2)}, u32[]{:S(2)}) collective-permute-start(f32[3,16,16,128]{3,2,1,0:T(8,128)S(1)} %bitcast.26), channel_id=1, source_target_pairs={{0,1},{1,0},{2,3},{3,2},{4,5},{5,4},{6,7},{7,6},{8,9},{9,8},{10,11... | collective-permute-start | bytes 1179656 | tf_op jit(solution)/shard_map/ppermute | solution.py:389
  18.9 0.0 collective-permute-start.5
  18.9 1.6 %collective-permute-start.6 = (f32[7,2,8,128]{3,2,1,0:T(8,128)S(1)}, f32[7,2,8,128]{3,2,1,0:T(8,128)S(1)}, u32[]{:S(2)}, u32[]{:S(2)}) collective-permute-start(f32[7,2,8,128]{3,2,1,0:T(8,128)S(1)} %get-tuple-element.32), channel_id=1, source_target_pairs={{2,4},{6,0},{4,2},{0,6},{3,5},{7,1},{5,3},{1,7},{10,12},{14,8},{12... | collective-permute-start | bytes 172040 | tf_op jit(solution)/shard_map/ppermute | solution.py:395
  20.5 0.0 copy-done.3
  20.5 1.0 %parameters.1.par = f32[3,32,2,8,128]{4,3,2,1,0:T(8,128)S(1)} custom-call(f32[5,8,128]{2,1,0:T(8,128)S(1)} %get-tuple-element.22.info_ref, s32[256,128]{1,0:T(8,128)S(1)} %bitcast.22, s32[256,128]{1,0:T(8,128)S(1)} %bitcast.28), custom_call_target="tpu_custom_call" | custom-call | tf_op jit(solution)/shard_map/parameters/pallas_call | solution.py:472
  21.5 0.0 collective-permute-done.5.one_ref
  21.5 1.0 %collective-permute-done.6.two_ref = f32[7,2,8,128]{3,2,1,0:T(8,128)S(1)} collective-permute-done((f32[7,2,8,128]{3,2,1,0:T(8,128)S(1)}, f32[7,2,8,128]{3,2,1,0:T(8,128)S(1)}, u32[]{:S(2)}, u32[]{:S(2)}) %collective-permute-start.6) | collective-permute-done | bytes 57376 | tf_op jit(solution)/shard_map/ppermute | solution.py:395
  22.5 1.6 %collective-permute-start.7 = (f32[2,7,2,8,128]{4,3,2,1,0:T(8,128)S(1)}, f32[2,7,2,8,128]{4,3,2,1,0:T(8,128)S(1)}, u32[]{:S(2)}, u32[]{:S(2)}) collective-permute-start(f32[2,7,2,8,128]{4,3,2,1,0:T(8,128)S(1)} %merge_strips.1.strips_ref), channel_id=1, source_target_pairs={{0,1},{1,0},{2,3},{3,2},{4,5},{5,4},{6,7},{7,6},{8,9},{9,8},{10,11... | collective-permute-start | bytes 344072 | tf_op jit(solution)/shard_map/ppermute | solution.py:389
  24.1 11.1 %all_to_all.11 = f32[32,1,128]{2,1,0:T(1,128)S(1)} all-to-all(f32[32,1,128]{2,1,0:T(1,128)S(1)} %bitcast.30), channel_id=1, replica_groups=mesh['img'=4,'gx'=4,'gy'=2] {'img','gx','gy'}, dimensions={0} | all-to-all | bytes 32768 | tf_op jit(solution)/shard_map/all_to_all | solution.py:490
  35.2 0.0 collective-permute-done.7.stripsp_ref
  35.2 0.0 collective-permute-done.4
  35.2 13.1 %evolve.1 = f32[3,256,128]{2,1,0:T(8,128)} custom-call(f32[5,8,128]{2,1,0:T(8,128)S(1)} %get-tuple-element.22.info_ref, f32[32,128]{1,0:T(8,128)S(1)} %bitcast.29, f32[3,256,128]{2,1,0:T(8,128)S(1)} %bitcast.20, f32[3,256,128]{2,1,0:T(8,128)S(1)} %bitcast.25, f32[3,256,128]{2,1,0:T(8,128)S(1)} %get-tuple-element.27.n_ref, f32[3,256,128]{2,1,0:T(8,128)S(1)} %bitcast.27, ...), custom_call_target="tpu_custom_call" | custom-call | tf_op jit(solution)/shard_map/evolve/pallas_call | solution.py:492
  (1 shorter events, 0.0 us)
Async XLA Ops:
  0.0 17.2 %collective-permute-start = (f32[3,16,16,128]{3,2,1,0:T(8,128)}, f32[3,16,16,128]{3,2,1,0:T(8,128)S(1)}, u32[]{:S(2)}, u32[]{:S(2)}) collective-permute-start(f32[3,16,16,128]{3,2,1,0:T(8,128)} %bitcast.15), channel_id=1, source_target_pairs={{0,1},{1,0},{2,3},{3,2},{4,5},{5,4},{6,7},{7,6},{8,9},{9,8},{10,11... | collective-permute-start | bytes 1179656 | tf_op jit(solution)/shard_map/ppermute | solution.py:389
  2.9 14.3 %collective-permute-start.3 = (f32[3,16,16,128]{3,2,1,0:T(8,128)}, f32[3,16,16,128]{3,2,1,0:T(8,128)S(1)}, u32[]{:S(2)}, u32[]{:S(2)}) collective-permute-start(f32[3,16,16,128]{3,2,1,0:T(8,128)} %bitcast.16), channel_id=1, source_target_pairs={{8,16},{16,8},{9,17},{17,9},{10,18},{18,10},{11,19},{19,11},{12,20... | collective-permute-start | bytes 1179656 | tf_op jit(solution)/shard_map/ppermute | solution.py:395
  3.6 13.6 %collective-permute-start.2 = (f32[3,16,16,128]{3,2,1,0:T(8,128)}, f32[3,16,16,128]{3,2,1,0:T(8,128)S(1)}, u32[]{:S(2)}, u32[]{:S(2)}) collective-permute-start(f32[3,16,16,128]{3,2,1,0:T(8,128)} %bitcast.17), channel_id=1, source_target_pairs={{0,8},{16,24},{8,0},{24,16},{1,9},{17,25},{9,1},{25,17},{2,10},{18... | collective-permute-start | bytes 1179656 | tf_op jit(solution)/shard_map/ppermute | solution.py:395
  8.1 0.7 %copy-start.7 = (f32[3]{0:T(128)S(1)}, f32[3]{0:T(128)}, u32[]{:S(2)}) copy-start(f32[3]{0:T(128)} %param.8) | copy-start | bytes 40
  8.1 0.7 %copy-start.4 = (s32[4]{0:T(128)S(1)}, s32[4]{0:T(128)}, u32[]{:S(2)}) copy-start(s32[4]{0:T(128)} %lower_ref.1) | copy-start | bytes 52
  8.1 0.7 %copy-start.5 = (f32[8]{0:T(128)S(1)}, f32[8]{0:T(128)}, u32[]{:S(2)}) copy-start(f32[8]{0:T(128)} %aniso_ref.1) | copy-start | bytes 100
  8.1 0.7 %copy-start.6 = (f32[8]{0:T(128)S(1)}, f32[8]{0:T(128)}, u32[]{:S(2)}) copy-start(f32[8]{0:T(128)} %damp_ref.1) | copy-start | bytes 100
  8.8 1.0 %copy-start = (f32[1,3,16,16,128]{4,3,2,1,0:T(8,128)S(1)}, f32[1,3,16,16,128]{4,3,2,1,0:T(8,128)}, u32[]{:S(2)}) copy-start(f32[1,3,16,16,128]{4,3,2,1,0:T(8,128)} %param.6) | copy-start | bytes 1179652
  9.8 0.9 %copy-start.2 = (s32[16,16,128]{2,1,0:T(8,128)S(1)}, s32[16,16,128]{2,1,0:T(8,128)}, u32[]{:S(2)}) copy-start(s32[16,16,128]{2,1,0:T(8,128)} %param.9) | copy-start | bytes 393220
  10.7 6.6 %copy-start.1 = (f32[1,3,16,16,128]{4,3,2,1,0:T(8,128)S(1)}, f32[1,3,16,16,128]{4,3,2,1,0:T(8,128)}, u32[]{:S(2)}) copy-start(f32[1,3,16,16,128]{4,3,2,1,0:T(8,128)} %param.6) | copy-start | bytes 1179652
  12.2 5.0 %collective-permute-start.1 = (s32[16,16,128]{2,1,0:T(8,128)S(1)}, s32[16,16,128]{2,1,0:T(8,128)S(1)}, u32[]{:S(2)}, u32[]{:S(2)}) collective-permute-start(s32[16,16,128]{2,1,0:T(8,128)S(1)} %copy-done.2), channel_id=1, source_target_pairs={{0,1},{1,0},{2,3},{3,2},{4,5},{5,4},{6,7},{7,6},{8,9},{9,8},{10,11... | collective-permute-start | bytes 393224 | tf_op jit(solution)/shard_map/ppermute | solution.py:389
  17.2 3.3 %copy-start.3 = (s32[16,16,128]{2,1,0:T(8,128)S(1)}, s32[16,16,128]{2,1,0:T(8,128)}, u32[]{:S(2)}) copy-start(s32[16,16,128]{2,1,0:T(8,128)} %param.9) | copy-start | bytes 393220
  18.3 16.9 %collective-permute-start.4 = (f32[3,16,16,128]{3,2,1,0:T(8,128)S(1)}, f32[3,16,16,128]{3,2,1,0:T(8,128)S(1)}, u32[]{:S(2)}, u32[]{:S(2)}) collective-permute-start(f32[3,16,16,128]{3,2,1,0:T(8,128)S(1)} %bitcast.26), channel_id=1, source_target_pairs={{0,1},{1,0},{2,3},{3,2},{4,5},{5,4},{6,7},{7,6},{8,9},{9,8},{10,11... | collective-permute-start | bytes 1179656 | tf_op jit(solution)/shard_map/ppermute | solution.py:389
  18.9 2.6 %collective-permute-start.5 = (f32[7,2,8,128]{3,2,1,0:T(8,128)S(1)}, f32[7,2,8,128]{3,2,1,0:T(8,128)S(1)}, u32[]{:S(2)}, u32[]{:S(2)}) collective-permute-start(f32[7,2,8,128]{3,2,1,0:T(8,128)S(1)} %get-tuple-element.28), channel_id=1, source_target_pairs={{0,2},{4,6},{2,0},{6,4},{1,3},{5,7},{3,1},{7,5},{8,10},{12,14},{10... | collective-permute-start | bytes 172040 | tf_op jit(solution)/shard_map/ppermute | solution.py:395
  18.9 3.6 %collective-permute-start.6 = (f32[7,2,8,128]{3,2,1,0:T(8,128)S(1)}, f32[7,2,8,128]{3,2,1,0:T(8,128)S(1)}, u32[]{:S(2)}, u32[]{:S(2)}) collective-permute-start(f32[7,2,8,128]{3,2,1,0:T(8,128)S(1)} %get-tuple-element.32), channel_id=1, source_target_pairs={{2,4},{6,0},{4,2},{0,6},{3,5},{7,1},{5,3},{1,7},{10,12},{14,8},{12... | collective-permute-start | bytes 172040 | tf_op jit(solution)/shard_map/ppermute | solution.py:395
  22.5 12.6 %collective-permute-start.7 = (f32[2,7,2,8,128]{4,3,2,1,0:T(8,128)S(1)}, f32[2,7,2,8,128]{4,3,2,1,0:T(8,128)S(1)}, u32[]{:S(2)}, u32[]{:S(2)}) collective-permute-start(f32[2,7,2,8,128]{4,3,2,1,0:T(8,128)S(1)} %merge_strips.1.strips_ref), channel_id=1, source_target_pairs={{0,1},{1,0},{2,3},{3,2},{4,5},{5,4},{6,7},{7,6},{8,9},{9,8},{10,11... | collective-permute-start | bytes 344072 | tf_op jit(solution)/shard_map/ppermute | solution.py:389

commit v20 on v19

--- a/solution.py
+++ b/solution.py
@@ -31,27 +31,35 @@
     return pl.ds(y + ny * t, SUB, stride=ny * tiles)
 
 
+def is_turned():
+    return (lax.axis_index("gx") & 1) == 1
+
+
+def rims(ny, y):
+    block = lane_iota() // DEPTH
+    turned = is_turned()
+    after = (y + 1) & (ny - 1)
+    return block == jnp.where(turned, after, y), block == jnp.where(turned, y, after), (DEPTH * (y + 1)) & (LANES - 1)
+
+
 def pack_kernel(
-    ny, tiles, regions, lower_ref, aniso_ref, damp_ref, share_ref, m_ref, reg_ref, left_ref, right_ref, info_ref
+    ny, tiles, regions, lower_ref, aniso_ref, damp_ref, share_ref, m_ref, reg_ref, one_ref, two_ref, info_ref
 ):
     here = lax.axis_index("img")
     lane = lane_iota()
-    block = lane // DEPTH
     def pack(i, carry):
         done = []
         for u in range(2):
             y = 2 * i + u
-            shift = (DEPTH * (y + 1)) & (LANES - 1)
-            left = block == ((y + 1) & (ny - 1))
-            right = block == y
+            one, two, shift = rims(ny, y)
             for t in range(tiles):
                 rows = rows_at(ny, tiles, y, t)
                 for c in range(COMPS + 1):
                     cells = m_ref[c, rows, :] if c < COMPS else reg_ref[rows, :].astype(jnp.float32)
-                    done.append((c, t, left, right, pltpu.roll(cells, shift, 1)))
-        for c, t, left, right, cells in done:
-            pltpu.store(left_ref.at[c, t], cells, mask=left)
-            pltpu.store(right_ref.at[c, t], cells, mask=right)
+                    done.append((c, t, one, two, pltpu.roll(cells, shift, 1)))
+        for c, t, one, two, cells in done:
+            pltpu.store(one_ref.at[c, t], cells, mask=one)
+            pltpu.store(two_ref.at[c, t], cells, mask=two)
         return carry
 
     table_a = jnp.zeros((SUB, LANES), jnp.float32)
@@ -73,11 +81,12 @@
     lax.fori_loop(0, ny // 2, pack, 0)
 
 
-def merge_kernel(one_ref, two_ref, out_ref):
-    turned = (lax.axis_index("gx") & 1) == 1
-    one, two = one_ref[...], two_ref[...]
-    out_ref[0] = jnp.where(turned, one, two)
-    out_ref[1] = jnp.where(turned, two, one)
+def merge_kernel(one_ref, two_ref, own_one_ref, own_two_ref, out_ref):
+    turned = is_turned()
+    for first, (one_ref, two_ref) in ((0, (one_ref, two_ref)), (COMPS, (own_one_ref, own_two_ref))):
+        one, two = one_ref[...], two_ref[...]
+        out_ref[0, first : first + one.shape[0]] = jnp.where(turned, one, two)
+        out_ref[1, first : first + one.shape[0]] = jnp.where(turned, two, one)
 
 
 def take_first(info_ref, here):
@@ -87,7 +96,7 @@
 
 
 def gather_kernel(
-    ny, tiles, info_ref, m_ref, first_ref, second_ref, own_left_ref, own_right_ref, part_ref, near_ref, one_ref, two_ref
+    ny, tiles, info_ref, m_ref, first_ref, second_ref, part_ref, near_ref, one_ref, two_ref
 ):
     here = lax.axis_index("img")
     pick, odd = take_first(info_ref, here)
@@ -114,19 +123,11 @@
     total = jnp.sum(functools.reduce(jnp.add, sums), axis=(0, 1), keepdims=True)
     slot = lax.broadcasted_iota(jnp.int32, part_ref.shape, 1)
     part_ref[...] = jnp.where((slot == here) & (here > 0), total, 0.0)
-    turned = (lax.axis_index("gx") & 1) == 1
-    one_ref[COMPS:] = jnp.where(turned, own_left_ref[...], own_right_ref[...])
-    two_ref[COMPS:] = jnp.where(turned, own_right_ref[...], own_left_ref[...])
-    block = lane_iota() // DEPTH
-
     def pack(i, carry):
         done = []
         for u in range(2):
             y = 2 * i + u
-            after = (y + 1) & (ny - 1)
-            one = block == jnp.where(turned, after, y)
-            two = block == jnp.where(turned, y, after)
-            shift = (DEPTH * (y + 1)) & (LANES - 1)
+            one, two, shift = rims(ny, y)
             for t in range(tiles):
                 for c in range(COMPS):
                     cells = pltpu.roll(near_ref[c, rows_at(ny, tiles, y, t), :], shift, 1)
@@ -433,7 +434,7 @@
     limit = pltpu.CompilerParams(vmem_limit_bytes=32 * 1024 * 1024)
     vreg = (SUB, LANES)
     packed = jax.ShapeDtypeStruct((comps + 1, tiles) + vreg, f32)
-    left, right, info = pl.pallas_call(
+    own_one, own_two, info = pl.pallas_call(
         functools.partial(pack_kernel, ny, tiles, anisotropy.shape[0]),
         out_shape=(packed, packed, jax.ShapeDtypeStruct((5,) + vreg, f32)),
         in_specs=[smem] * 3 + [vmem] * 3,
@@ -448,10 +449,12 @@
         own.reshape(flat),
         regions.reshape(flat[1:]),
     )
+    own_one = swapped(own_one, "gx", 0, True)
+    own_two = swapped(own_two, "gx", 1, True)
     late_regions, info = lax.optimization_barrier((regions, info))
     reg_p = around(late_regions, 1)
-    info, own_p, reg_p = lax.optimization_barrier((info, own_p, reg_p))
-    packed = jax.ShapeDtypeStruct((2 * comps + 1, tiles) + vreg, f32)
+    info, own_p, reg_p, own_one, own_two = lax.optimization_barrier((info, own_p, reg_p, own_one, own_two))
+    packed = jax.ShapeDtypeStruct((comps, tiles) + vreg, f32)
     part, near, one, two = pl.pallas_call(
         functools.partial(gather_kernel, ny, tiles),
         out_shape=(
@@ -460,11 +463,11 @@
             packed,
             packed,
         ),
-        in_specs=[vmem] * 6,
+        in_specs=[vmem] * 4,
         out_specs=(vmem,) * 4,
         compiler_params=limit,
         name="gather_images",
-    )(info, own.reshape(flat), first.reshape(flat), second.reshape(flat), left, right)
+    )(info, own.reshape(flat), first.reshape(flat), second.reshape(flat))
     near_p = around(near.reshape(own.shape), 2)
     one = swapped(one, "gx", 0, True)
     two = swapped(two, "gx", 1, True)
@@ -480,12 +483,12 @@
     one, par = lax.optimization_barrier((one, par))
     strips = pl.pallas_call(
         merge_kernel,
-        out_shape=jax.ShapeDtypeStruct((2,) + packed.shape, f32),
-        in_specs=[vmem] * 2,
+        out_shape=jax.ShapeDtypeStruct((2, 2 * comps + 1, tiles) + vreg, f32),
+        in_specs=[vmem] * 4,
         out_specs=vmem,
         compiler_params=limit,
         name="merge_strips",
-    )(one, two)
+    )(one, two, own_one, own_two)
     strips_p = around_strips(strips)
     squares = lax.all_to_all(part, ("img", "gx", "gy"), 0, 0, tiled=True)
 

time: 48.5 us -> 48.1 us (level)
  waiting for transfers between devices: 5.42 us -> 3.87 us
  starting transfers between devices: 12.4 us -> 13.7 us
    ppermute x4, waiting for transfers between devices: 4.44 us -> 0.01 us  [shifted(): return lax.ppermute(cells, axis, pairs)]
    ppermute x4 -> x6, waiting for transfers between devices: 0.98 us -> 3.86 us  [swapped(): return lax.ppermute(cells, axis, pairs + [(j, i) for i, j in pairs])]
    ppermute x4 -> x6, starting transfers between devices: 6.75 us -> 8.04 us  [swapped(): return lax.ppermute(cells, axis, pairs + [(j, i) for i, j in pairs])]
  transfers between devices with their start and end apart: 8 -> 10, of which waited for: 2 -> 3; matrix products, arithmetic and copies ran while one was open for 0% -> 0% of each run, Pallas kernels for 5% -> 5%
where the time goes in v20:
time: 48.1 us; the launch traced here: 47.9 us
  Pallas kernels  16.7 us (35%)
  starting transfers between devices  13.7 us (28%)
  blocking collectives  10.9 us (23%)
  waiting for transfers between devices  3.87 us (8%)
  local copies, waits for them, and re-layouts  2.61 us (5%)
    pallas_call x1, Pallas kernels, body(): pl.pallas_call(functools.partial(evolve_kernel, ny, tiles, images), out_s...  13.1 us
    all_to_all x1, blocking collectives, body(): squares = lax.all_to_all(part, ('img', 'gx', 'gy'), 0, 0, tiled=True)  10.9 us
    ppermute x6, starting transfers between devices, swapped(): return lax.ppermute(cells, axis, pairs + [(j, i) for i, j in pairs])  8.04 us
    ppermute x4, starting transfers between devices, shifted(): return lax.ppermute(cells, axis, pairs)  5.69 us
    ppermute x6, waiting for transfers between devices, swapped(): return lax.ppermute(cells, axis, pairs + [(j, i) for i, j in pairs])  3.86 us
    unnamed x16, local copies, waits for them, and re-layouts  2.61 us
    pallas_call x1, Pallas kernels, body(): pl.pallas_call(functools.partial(pack_kernel, ny, tiles, anisotropy.shape...  1.51 us
    pallas_call x1, Pallas kernels, body(): pl.pallas_call(functools.partial(gather_kernel, ny, tiles), out_shape=(ja...  1.06 us
  transfers between devices with their start and end apart: 10, of which 3 were waited for; matrix products, arithmetic and copies ran while one was open for 0% of the time, Pallas kernels for 5%

profile of v20, /device:TPU:0, one launch (start us, length us, event | category | flops | bytes accessed | tf_op | source)
XLA Modules:
  0.0 47.9 jit_solution(1474226094090851810)
XLA Ops:
  0.0 2.9 %collective-permute-start = (f32[3,16,16,128]{3,2,1,0:T(8,128)}, f32[3,16,16,128]{3,2,1,0:T(8,128)S(1)}, u32[]{:S(2)}, u32[]{:S(2)}) collective-permute-start(f32[3,16,16,128]{3,2,1,0:T(8,128)} %bitcast.15), channel_id=1, source_target_pairs={{0,1},{1,0},{2,3},{3,2},{4,5},{5,4},{6,7},{7,6},{8,9},{9,8},{10,11... | collective-permute-start | bytes 1179656 | tf_op jit(solution)/shard_map/ppermute | solution.py:390
  2.9 0.7 %collective-permute-start.5 = (f32[3,16,16,128]{3,2,1,0:T(8,128)}, f32[3,16,16,128]{3,2,1,0:T(8,128)S(1)}, u32[]{:S(2)}, u32[]{:S(2)}) collective-permute-start(f32[3,16,16,128]{3,2,1,0:T(8,128)} %bitcast.16), channel_id=1, source_target_pairs={{8,16},{16,8},{9,17},{17,9},{10,18},{18,10},{11,19},{19,11},{12,20... | collective-permute-start | bytes 1179656 | tf_op jit(solution)/shard_map/ppermute | solution.py:396
  3.6 4.4 %collective-permute-start.4 = (f32[3,16,16,128]{3,2,1,0:T(8,128)}, f32[3,16,16,128]{3,2,1,0:T(8,128)S(1)}, u32[]{:S(2)}, u32[]{:S(2)}) collective-permute-start(f32[3,16,16,128]{3,2,1,0:T(8,128)} %bitcast.17), channel_id=1, source_target_pairs={{0,8},{16,24},{8,0},{24,16},{1,9},{17,25},{9,1},{25,17},{2,10},{18... | collective-permute-start | bytes 1179656 | tf_op jit(solution)/shard_map/ppermute | solution.py:396
  8.1 0.0 copy-start.7
  8.1 0.0 copy-start.4
  8.1 0.0 copy-start.5
  8.1 0.0 copy-start.6
  8.1 0.6 %copy-done.7 = f32[3]{0:T(128)S(1)} copy-done((f32[3]{0:T(128)S(1)}, f32[3]{0:T(128)}, u32[]{:S(2)}) %copy-start.7) | copy-done | bytes 36
  8.7 0.0 copy-done.4
  8.7 0.0 copy-done.5
  8.7 0.0 copy-done.6
  8.8 0.0 copy-start
  8.8 1.0 %copy-done = f32[1,3,16,16,128]{4,3,2,1,0:T(8,128)S(1)} copy-done((f32[1,3,16,16,128]{4,3,2,1,0:T(8,128)S(1)}, f32[1,3,16,16,128]{4,3,2,1,0:T(8,128)}, u32[]{:S(2)}) %copy-start) | copy-done | bytes 393240
  9.8 0.0 copy-start.2
  9.8 0.9 %copy-done.2 = s32[16,16,128]{2,1,0:T(8,128)S(1)} copy-done((s32[16,16,128]{2,1,0:T(8,128)S(1)}, s32[16,16,128]{2,1,0:T(8,128)}, u32[]{:S(2)}) %copy-start.2) | copy-done | bytes 131096
  10.7 0.0 copy-start.1
  10.7 1.5 %pack_strips.1 = (f32[4,2,8,128]{3,2,1,0:T(8,128)S(1)}, f32[4,2,8,128]{3,2,1,0:T(8,128)S(1)}, f32[5,8,128]{2,1,0:T(8,128)S(1)}) custom-call(s32[4]{0:T(128)S(1)} %copy-done.4, f32[8]{0:T(128)S(1)} %copy-done.5, f32[8]{0:T(128)S(1)} %copy-done.6, f32[1,3]{1,0:T(1,128)S(1)} %bitcast.31, f32[3,256,128]{2,1,0:T(8,128)S(1)} %bitcast.18, s32[256,128]{1,0:T(8,128)S(1)} %bitcast.21), custom_call_target="tpu_custom_call" | custom-call | tf_op jit(solution)/shard_map/pack_strips/pallas_call | solution.py:437
  12.2 0.6 %collective-permute-start.1 = (s32[16,16,128]{2,1,0:T(8,128)S(1)}, s32[16,16,128]{2,1,0:T(8,128)S(1)}, u32[]{:S(2)}, u32[]{:S(2)}) collective-permute-start(s32[16,16,128]{2,1,0:T(8,128)S(1)} %copy-done.2), channel_id=1, source_target_pairs={{0,1},{1,0},{2,3},{3,2},{4,5},{5,4},{6,7},{7,6},{8,9},{9,8},{10,11... | collective-permute-start | bytes 393224 | tf_op jit(solution)/shard_map/ppermute | solution.py:390
  12.8 0.0 collective-permute-start.2
  12.8 1.2 %collective-permute-done.2.own_one_ref = f32[4,2,8,128]{3,2,1,0:T(8,128)S(1)} collective-permute-done((f32[4,2,8,128]{3,2,1,0:T(8,128)S(1)}, f32[4,2,8,128]{3,2,1,0:T(8,128)S(1)}, u32[]{:S(2)}, u32[]{:S(2)}) %collective-permute-start.2) | collective-permute-done | bytes 32800 | tf_op jit(solution)/shard_map/ppermute | solution.py:396
  14.0 1.3 %collective-permute-start.3 = (f32[4,2,8,128]{3,2,1,0:T(8,128)S(1)}, f32[4,2,8,128]{3,2,1,0:T(8,128)S(1)}, u32[]{:S(2)}, u32[]{:S(2)}) collective-permute-start(f32[4,2,8,128]{3,2,1,0:T(8,128)S(1)} %get-tuple-element.25), channel_id=1, source_target_pairs={{2,4},{6,0},{4,2},{0,6},{3,5},{7,1},{5,3},{1,7},{10,12},{14,8},{12... | collective-permute-start | bytes 98312 | tf_op jit(solution)/shard_map/ppermute | solution.py:396
  15.3 2.1 %collective-permute-done.3.own_two_ref = f32[4,2,8,128]{3,2,1,0:T(8,128)S(1)} collective-permute-done((f32[4,2,8,128]{3,2,1,0:T(8,128)S(1)}, f32[4,2,8,128]{3,2,1,0:T(8,128)S(1)}, u32[]{:S(2)}, u32[]{:S(2)}) %collective-permute-start.3) | collective-permute-done | bytes 32800 | tf_op jit(solution)/shard_map/ppermute | solution.py:396
  17.3 0.0 collective-permute-done.1
  17.3 0.0 collective-permute-done
  17.3 0.0 collective-permute-done.5
  17.4 0.0 collective-permute-done.4
  17.4 0.0 copy-done.1
  17.4 0.0 copy-start.3
  17.4 1.1 %gather_images.1 = (f32[32,128]{1,0:T(8,128)S(1)}, f32[3,256,128]{2,1,0:T(8,128)S(1)}, f32[3,2,8,128]{3,2,1,0:T(8,128)S(1)}, f32[3,2,8,128]{3,2,1,0:T(8,128)S(1)}) custom-call(f32[5,8,128]{2,1,0:T(8,128)S(1)} %get-tuple-element.26.info_ref, f32[3,256,128]{2,1,0:T(8,128)S(1)} %bitcast.19, f32[3,256,128]{2,1,0:T(8,128)S(1)} %bitcast.24, ...), custom_call_target="tpu_custom_call" | custom-call | tf_op jit(solution)/shard_map/gather_images/pallas_call | solution.py:458
  18.4 1.6 %collective-permute-start.6 = (f32[3,16,16,128]{3,2,1,0:T(8,128)S(1)}, f32[3,16,16,128]{3,2,1,0:T(8,128)S(1)}, u32[]{:S(2)}, u32[]{:S(2)}) collective-permute-start(f32[3,16,16,128]{3,2,1,0:T(8,128)S(1)} %bitcast.26), channel_id=1, source_target_pairs={{0,1},{1,0},{2,3},{3,2},{4,5},{5,4},{6,7},{7,6},{8,9},{9,8},{10,11... | collective-permute-start | bytes 1179656 | tf_op jit(solution)/shard_map/ppermute | solution.py:390
  20.0 0.0 collective-permute-start.7
  20.0 1.6 %collective-permute-start.8 = (f32[3,2,8,128]{3,2,1,0:T(8,128)S(1)}, f32[3,2,8,128]{3,2,1,0:T(8,128)S(1)}, u32[]{:S(2)}, u32[]{:S(2)}) collective-permute-start(f32[3,2,8,128]{3,2,1,0:T(8,128)S(1)} %get-tuple-element.34), channel_id=1, source_target_pairs={{2,4},{6,0},{4,2},{0,6},{3,5},{7,1},{5,3},{1,7},{10,12},{14,8},{12... | collective-permute-start | bytes 73736 | tf_op jit(solution)/shard_map/ppermute | solution.py:396
  21.6 0.0 copy-done.3
  21.6 1.0 %parameters.1.par = f32[3,32,2,8,128]{4,3,2,1,0:T(8,128)S(1)} custom-call(f32[5,8,128]{2,1,0:T(8,128)S(1)} %get-tuple-element.26.info_ref, s32[256,128]{1,0:T(8,128)S(1)} %bitcast.22, s32[256,128]{1,0:T(8,128)S(1)} %bitcast.28), custom_call_target="tpu_custom_call" | custom-call | tf_op jit(solution)/shard_map/parameters/pallas_call | solution.py:475
  22.7 0.0 collective-permute-done.7.one_ref
  22.7 0.6 %collective-permute-done.8.two_ref = f32[3,2,8,128]{3,2,1,0:T(8,128)S(1)} collective-permute-done((f32[3,2,8,128]{3,2,1,0:T(8,128)S(1)}, f32[3,2,8,128]{3,2,1,0:T(8,128)S(1)}, u32[]{:S(2)}, u32[]{:S(2)}) %collective-permute-start.8) | collective-permute-done | bytes 24608 | tf_op jit(solution)/shard_map/ppermute | solution.py:396
  23.3 0.6 %collective-permute-start.9 = (f32[2,7,2,8,128]{4,3,2,1,0:T(8,128)S(1)}, f32[2,7,2,8,128]{4,3,2,1,0:T(8,128)S(1)}, u32[]{:S(2)}, u32[]{:S(2)}) collective-permute-start(f32[2,7,2,8,128]{4,3,2,1,0:T(8,128)S(1)} %merge_strips.1.strips_ref), channel_id=1, source_target_pairs={{0,1},{1,0},{2,3},{3,2},{4,5},{5,4},{6,7},{7,6},{8,9},{9,8},{10,11... | collective-permute-start | bytes 344072 | tf_op jit(solution)/shard_map/ppermute | solution.py:390
  23.9 10.9 %all_to_all.11 = f32[32,1,128]{2,1,0:T(1,128)S(1)} all-to-all(f32[32,1,128]{2,1,0:T(1,128)S(1)} %bitcast.30), channel_id=1, replica_groups=mesh['img'=4,'gx'=4,'gy'=2] {'img','gx','gy'}, dimensions={0} | all-to-all | bytes 32768 | tf_op jit(solution)/shard_map/all_to_all | solution.py:493
  34.8 0.0 collective-permute-done.9.stripsp_ref
  34.8 0.0 collective-permute-done.6
  34.8 13.1 %evolve.1 = f32[3,256,128]{2,1,0:T(8,128)} custom-call(f32[5,8,128]{2,1,0:T(8,128)S(1)} %get-tuple-element.26.info_ref, f32[32,128]{1,0:T(8,128)S(1)} %bitcast.29, f32[3,256,128]{2,1,0:T(8,128)S(1)} %bitcast.20, f32[3,256,128]{2,1,0:T(8,128)S(1)} %bitcast.25, f32[3,256,128]{2,1,0:T(8,128)S(1)} %get-tuple-element.29.n_ref, f32[3,256,128]{2,1,0:T(8,128)S(1)} %bitcast.27, ...), custom_call_target="tpu_custom_call" | custom-call | tf_op jit(solution)/shard_map/evolve/pallas_call | solution.py:495
  (1 shorter events, 0.0 us)
Async XLA Ops:
  0.0 17.3 %collective-permute-start = (f32[3,16,16,128]{3,2,1,0:T(8,128)}, f32[3,16,16,128]{3,2,1,0:T(8,128)S(1)}, u32[]{:S(2)}, u32[]{:S(2)}) collective-permute-start(f32[3,16,16,128]{3,2,1,0:T(8,128)} %bitcast.15), channel_id=1, source_target_pairs={{0,1},{1,0},{2,3},{3,2},{4,5},{5,4},{6,7},{7,6},{8,9},{9,8},{10,11... | collective-permute-start | bytes 1179656 | tf_op jit(solution)/shard_map/ppermute | solution.py:390
  2.9 14.4 %collective-permute-start.5 = (f32[3,16,16,128]{3,2,1,0:T(8,128)}, f32[3,16,16,128]{3,2,1,0:T(8,128)S(1)}, u32[]{:S(2)}, u32[]{:S(2)}) collective-permute-start(f32[3,16,16,128]{3,2,1,0:T(8,128)} %bitcast.16), channel_id=1, source_target_pairs={{8,16},{16,8},{9,17},{17,9},{10,18},{18,10},{11,19},{19,11},{12,20... | collective-permute-start | bytes 1179656 | tf_op jit(solution)/shard_map/ppermute | solution.py:396
  3.6 13.7 %collective-permute-start.4 = (f32[3,16,16,128]{3,2,1,0:T(8,128)}, f32[3,16,16,128]{3,2,1,0:T(8,128)S(1)}, u32[]{:S(2)}, u32[]{:S(2)}) collective-permute-start(f32[3,16,16,128]{3,2,1,0:T(8,128)} %bitcast.17), channel_id=1, source_target_pairs={{0,8},{16,24},{8,0},{24,16},{1,9},{17,25},{9,1},{25,17},{2,10},{18... | collective-permute-start | bytes 1179656 | tf_op jit(solution)/shard_map/ppermute | solution.py:396
  8.1 0.7 %copy-start.7 = (f32[3]{0:T(128)S(1)}, f32[3]{0:T(128)}, u32[]{:S(2)}) copy-start(f32[3]{0:T(128)} %param.8) | copy-start | bytes 40
  8.1 0.7 %copy-start.4 = (s32[4]{0:T(128)S(1)}, s32[4]{0:T(128)}, u32[]{:S(2)}) copy-start(s32[4]{0:T(128)} %lower_ref.1) | copy-start | bytes 52
  8.1 0.7 %copy-start.5 = (f32[8]{0:T(128)S(1)}, f32[8]{0:T(128)}, u32[]{:S(2)}) copy-start(f32[8]{0:T(128)} %aniso_ref.1) | copy-start | bytes 100
  8.1 0.7 %copy-start.6 = (f32[8]{0:T(128)S(1)}, f32[8]{0:T(128)}, u32[]{:S(2)}) copy-start(f32[8]{0:T(128)} %damp_ref.1) | copy-start | bytes 100
  8.8 1.0 %copy-start = (f32[1,3,16,16,128]{4,3,2,1,0:T(8,128)S(1)}, f32[1,3,16,16,128]{4,3,2,1,0:T(8,128)}, u32[]{:S(2)}) copy-start(f32[1,3,16,16,128]{4,3,2,1,0:T(8,128)} %param.6) | copy-start | bytes 1179652
  9.8 0.9 %copy-start.2 = (s32[16,16,128]{2,1,0:T(8,128)S(1)}, s32[16,16,128]{2,1,0:T(8,128)}, u32[]{:S(2)}) copy-start(s32[16,16,128]{2,1,0:T(8,128)} %param.9) | copy-start | bytes 393220
  10.7 6.7 %copy-start.1 = (f32[1,3,16,16,128]{4,3,2,1,0:T(8,128)S(1)}, f32[1,3,16,16,128]{4,3,2,1,0:T(8,128)}, u32[]{:S(2)}) copy-start(f32[1,3,16,16,128]{4,3,2,1,0:T(8,128)} %param.6) | copy-start | bytes 1179652
  12.2 5.2 %collective-permute-start.1 = (s32[16,16,128]{2,1,0:T(8,128)S(1)}, s32[16,16,128]{2,1,0:T(8,128)S(1)}, u32[]{:S(2)}, u32[]{:S(2)}) collective-permute-start(s32[16,16,128]{2,1,0:T(8,128)S(1)} %copy-done.2), channel_id=1, source_target_pairs={{0,1},{1,0},{2,3},{3,2},{4,5},{5,4},{6,7},{7,6},{8,9},{9,8},{10,11... | collective-permute-start | bytes 393224 | tf_op jit(solution)/shard_map/ppermute | solution.py:390
  12.8 1.2 %collective-permute-start.2 = (f32[4,2,8,128]{3,2,1,0:T(8,128)S(1)}, f32[4,2,8,128]{3,2,1,0:T(8,128)S(1)}, u32[]{:S(2)}, u32[]{:S(2)}) collective-permute-start(f32[4,2,8,128]{3,2,1,0:T(8,128)S(1)} %get-tuple-element.24), channel_id=1, source_target_pairs={{0,2},{4,6},{2,0},{6,4},{1,3},{5,7},{3,1},{7,5},{8,10},{12,14},{10... | collective-permute-start | bytes 98312 | tf_op jit(solution)/shard_map/ppermute | solution.py:396
  14.0 3.3 %collective-permute-start.3 = (f32[4,2,8,128]{3,2,1,0:T(8,128)S(1)}, f32[4,2,8,128]{3,2,1,0:T(8,128)S(1)}, u32[]{:S(2)}, u32[]{:S(2)}) collective-permute-start(f32[4,2,8,128]{3,2,1,0:T(8,128)S(1)} %get-tuple-element.25), channel_id=1, source_target_pairs={{2,4},{6,0},{4,2},{0,6},{3,5},{7,1},{5,3},{1,7},{10,12},{14,8},{12... | collective-permute-start | bytes 98312 | tf_op jit(solution)/shard_map/ppermute | solution.py:396
  17.4 4.3 %copy-start.3 = (s32[16,16,128]{2,1,0:T(8,128)S(1)}, s32[16,16,128]{2,1,0:T(8,128)}, u32[]{:S(2)}) copy-start(s32[16,16,128]{2,1,0:T(8,128)} %param.9) | copy-start | bytes 393220
  18.4 16.4 %collective-permute-start.6 = (f32[3,16,16,128]{3,2,1,0:T(8,128)S(1)}, f32[3,16,16,128]{3,2,1,0:T(8,128)S(1)}, u32[]{:S(2)}, u32[]{:S(2)}) collective-permute-start(f32[3,16,16,128]{3,2,1,0:T(8,128)S(1)} %bitcast.26), channel_id=1, source_target_pairs={{0,1},{1,0},{2,3},{3,2},{4,5},{5,4},{6,7},{7,6},{8,9},{9,8},{10,11... | collective-permute-start | bytes 1179656 | tf_op jit(solution)/shard_map/ppermute | solution.py:390
  20.0 2.7 %collective-permute-start.7 = (f32[3,2,8,128]{3,2,1,0:T(8,128)S(1)}, f32[3,2,8,128]{3,2,1,0:T(8,128)S(1)}, u32[]{:S(2)}, u32[]{:S(2)}) collective-permute-start(f32[3,2,8,128]{3,2,1,0:T(8,128)S(1)} %get-tuple-element.30), channel_id=1, source_target_pairs={{0,2},{4,6},{2,0},{6,4},{1,3},{5,7},{3,1},{7,5},{8,10},{12,14},{10... | collective-permute-start | bytes 73736 | tf_op jit(solution)/shard_map/ppermute | solution.py:396
  20.0 3.3 %collective-permute-start.8 = (f32[3,2,8,128]{3,2,1,0:T(8,128)S(1)}, f32[3,2,8,128]{3,2,1,0:T(8,128)S(1)}, u32[]{:S(2)}, u32[]{:S(2)}) collective-permute-start(f32[3,2,8,128]{3,2,1,0:T(8,128)S(1)} %get-tuple-element.34), channel_id=1, source_target_pairs={{2,4},{6,0},{4,2},{0,6},{3,5},{7,1},{5,3},{1,7},{10,12},{14,8},{12... | collective-permute-start | bytes 73736 | tf_op jit(solution)/shard_map/ppermute | solution.py:396
  23.3 11.5 %collective-permute-start.9 = (f32[2,7,2,8,128]{4,3,2,1,0:T(8,128)S(1)}, f32[2,7,2,8,128]{4,3,2,1,0:T(8,128)S(1)}, u32[]{:S(2)}, u32[]{:S(2)}) collective-permute-start(f32[2,7,2,8,128]{4,3,2,1,0:T(8,128)S(1)} %merge_strips.1.strips_ref), channel_id=1, source_target_pairs={{0,1},{1,0},{2,3},{3,2},{4,5},{5,4},{6,7},{7,6},{8,9},{9,8},{10,11... | collective-permute-start | bytes 344072 | tf_op jit(solution)/shard_map/ppermute | solution.py:390

commit v21 on v20

--- a/solution.py
+++ b/solution.py
@@ -42,25 +42,34 @@
     return block == jnp.where(turned, after, y), block == jnp.where(turned, y, after), (DEPTH * (y + 1)) & (LANES - 1)
 
 
-def pack_kernel(
-    ny, tiles, regions, lower_ref, aniso_ref, damp_ref, share_ref, m_ref, reg_ref, one_ref, two_ref, info_ref
-):
-    here = lax.axis_index("img")
-    lane = lane_iota()
+def pack_rows(ny, tiles, one_ref, two_ref, comps, cells_at):
     def pack(i, carry):
         done = []
         for u in range(2):
             y = 2 * i + u
             one, two, shift = rims(ny, y)
             for t in range(tiles):
-                rows = rows_at(ny, tiles, y, t)
-                for c in range(COMPS + 1):
-                    cells = m_ref[c, rows, :] if c < COMPS else reg_ref[rows, :].astype(jnp.float32)
+                for c in range(comps):
+                    cells = cells_at(c, rows_at(ny, tiles, y, t))
                     done.append((c, t, one, two, pltpu.roll(cells, shift, 1)))
         for c, t, one, two, cells in done:
             pltpu.store(one_ref.at[c, t], cells, mask=one)
             pltpu.store(two_ref.at[c, t], cells, mask=two)
         return carry
+
+    lax.fori_loop(0, ny // 2, pack, 0)
+
+
+def pack_kernel(ny, tiles, m_ref, one_ref, two_ref):
+    pack_rows(ny, tiles, one_ref, two_ref, COMPS, lambda c, rows: m_ref[c, rows, :])
+
+
+def info_kernel(
+    ny, tiles, regions, lower_ref, aniso_ref, damp_ref, share_ref, reg_ref, one_ref, two_ref, info_ref
+):
+    here = lax.axis_index("img")
+    lane = lane_iota()
+    pack_rows(ny, tiles, one_ref, two_ref, 1, lambda c, rows: reg_ref[rows, :].astype(jnp.float32))
 
     table_a = jnp.zeros((SUB, LANES), jnp.float32)
     table_d = jnp.zeros((SUB, LANES), jnp.float32)
@@ -78,12 +87,10 @@
     info_ref[3] = jnp.broadcast_to(target, (SUB, LANES))
     info_ref[4] = jnp.full((SUB, LANES), lower_ref[here].astype(jnp.float32))
 
-    lax.fori_loop(0, ny // 2, pack, 0)
-
 
 def merge_kernel(one_ref, two_ref, own_one_ref, own_two_ref, out_ref):
     turned = is_turned()
-    for first, (one_ref, two_ref) in ((0, (one_ref, two_ref)), (COMPS, (own_one_ref, own_two_ref))):
+    for first, (one_ref, two_ref) in ((0, (one_ref, two_ref)), (COMPS + 1, (own_one_ref, own_two_ref))):
         one, two = one_ref[...], two_ref[...]
         out_ref[0, first : first + one.shape[0]] = jnp.where(turned, one, two)
         out_ref[1, first : first + one.shape[0]] = jnp.where(turned, two, one)
@@ -96,7 +103,7 @@
 
 
 def gather_kernel(
-    ny, tiles, info_ref, m_ref, first_ref, second_ref, part_ref, near_ref, one_ref, two_ref
+    ny, tiles, info_ref, m_ref, first_ref, second_ref, reg_one_ref, reg_two_ref, part_ref, near_ref, one_ref, two_ref
 ):
     here = lax.axis_index("img")
     pick, odd = take_first(info_ref, here)
@@ -123,21 +130,9 @@
     total = jnp.sum(functools.reduce(jnp.add, sums), axis=(0, 1), keepdims=True)
     slot = lax.broadcasted_iota(jnp.int32, part_ref.shape, 1)
     part_ref[...] = jnp.where((slot == here) & (here > 0), total, 0.0)
-    def pack(i, carry):
-        done = []
-        for u in range(2):
-            y = 2 * i + u
-            one, two, shift = rims(ny, y)
-            for t in range(tiles):
-                for c in range(COMPS):
-                    cells = pltpu.roll(near_ref[c, rows_at(ny, tiles, y, t), :], shift, 1)
-                    done.append((c, t, one, two, cells))
-        for c, t, one, two, cells in done:
-            pltpu.store(one_ref.at[c, t], cells, mask=one)
-            pltpu.store(two_ref.at[c, t], cells, mask=two)
-        return carry
-
-    lax.fori_loop(0, ny // 2, pack, 0)
+    one_ref[COMPS:] = reg_one_ref[...]
+    two_ref[COMPS:] = reg_two_ref[...]
+    pack_rows(ny, tiles, one_ref, two_ref, COMPS, lambda c, rows: near_ref[c, rows, :])
 
 
 def turn(m, h, a2, b, sc):
@@ -255,9 +250,9 @@
         for g, cells in enumerate((strips_ref, stripsp_ref)):
             for side in range(2):
                 v = normal(
-                    [w_own * cells[side, COMPS + c, t] + w_near * cells[side, c, t] for c in range(COMPS)]
+                    [w_own * cells[side, COMPS + 1 + c, t] + w_near * cells[side, c, t] for c in range(COMPS)]
                 )
-                done.append((side, g, v, look_up(info_ref, cells[side, 2 * COMPS, t].astype(jnp.int32))))
+                done.append((side, g, v, look_up(info_ref, cells[side, COMPS, t].astype(jnp.int32))))
         for side, g, v, p in done:
             for c in range(COMPS):
                 strip0[c, side, g, t] = v[c]
@@ -433,41 +428,41 @@
     f32 = jnp.float32
     limit = pltpu.CompilerParams(vmem_limit_bytes=32 * 1024 * 1024)
     vreg = (SUB, LANES)
-    packed = jax.ShapeDtypeStruct((comps + 1, tiles) + vreg, f32)
-    own_one, own_two, info = pl.pallas_call(
-        functools.partial(pack_kernel, ny, tiles, anisotropy.shape[0]),
-        out_shape=(packed, packed, jax.ShapeDtypeStruct((5,) + vreg, f32)),
-        in_specs=[smem] * 3 + [vmem] * 3,
+    packed = [jax.ShapeDtypeStruct((count, tiles) + vreg, f32) for count in range(comps + 2)]
+    own_one, own_two = pl.pallas_call(
+        functools.partial(pack_kernel, ny, tiles),
+        out_shape=(packed[comps],) * 2,
+        in_specs=[vmem],
+        out_specs=(vmem,) * 2,
+        compiler_params=limit,
+        name="pack_strips",
+    )(own.reshape(flat))
+    own_one = swapped(own_one, "gx", 0, True)
+    own_two = swapped(own_two, "gx", 1, True)
+    reg_one, reg_two, info = pl.pallas_call(
+        functools.partial(info_kernel, ny, tiles, anisotropy.shape[0]),
+        out_shape=(packed[1], packed[1], jax.ShapeDtypeStruct((5,) + vreg, f32)),
+        in_specs=[smem] * 3 + [vmem] * 2,
         out_specs=(vmem,) * 3,
         compiler_params=limit,
-        name="pack_strips",
-    )(
-        lower_image,
-        anisotropy,
-        damping,
-        image_weights.reshape(1, -1),
-        own.reshape(flat),
-        regions.reshape(flat[1:]),
-    )
-    own_one = swapped(own_one, "gx", 0, True)
-    own_two = swapped(own_two, "gx", 1, True)
-    late_regions, info = lax.optimization_barrier((regions, info))
+        name="small_arguments",
+    )(lower_image, anisotropy, damping, image_weights.reshape(1, -1), regions.reshape(flat[1:]))
+    late_regions, own_one = lax.optimization_barrier((regions, own_one))
     reg_p = around(late_regions, 1)
     info, own_p, reg_p, own_one, own_two = lax.optimization_barrier((info, own_p, reg_p, own_one, own_two))
-    packed = jax.ShapeDtypeStruct((comps, tiles) + vreg, f32)
     part, near, one, two = pl.pallas_call(
         functools.partial(gather_kernel, ny, tiles),
         out_shape=(
             jax.ShapeDtypeStruct((devices, LANES), f32),
             jax.ShapeDtypeStruct(flat, f32),
-            packed,
-            packed,
+            packed[comps + 1],
+            packed[comps + 1],
         ),
-        in_specs=[vmem] * 4,
+        in_specs=[vmem] * 6,
         out_specs=(vmem,) * 4,
         compiler_params=limit,
         name="gather_images",
-    )(info, own.reshape(flat), first.reshape(flat), second.reshape(flat))
+    )(info, own.reshape(flat), first.reshape(flat), second.reshape(flat), reg_one, reg_two)
     near_p = around(near.reshape(own.shape), 2)
     one = swapped(one, "gx", 0, True)
     two = swapped(two, "gx", 1, True)

time: 48.1 us -> 48.2 us (level)
  waiting for transfers between devices: 3.87 us -> 3.29 us
  Pallas kernels: 16.7 us -> 17.2 us
  blocking collectives: 10.9 us -> 11.4 us
    ppermute x6, waiting for transfers between devices: 3.86 us -> 1.9 us  [swapped(): return lax.ppermute(cells, axis, pairs + [(j, i) for i, j in pairs])]
    ppermute x4, waiting for transfers between devices: 0.01 us -> 1.4 us  [shifted(): return lax.ppermute(cells, axis, pairs)]
    pallas_call x1 -> x2, Pallas kernels: 1.51 us -> 2.04 us  [the longest x1 1.25 us: body(): pl.pallas_call(functools.partial(info_kernel, ny, tiles, anisotropy.shape...]
  transfers between devices with their start and end apart: 10 -> 10, of which waited for: 3 -> 3; matrix products, arithmetic and copies ran while one was open for 0% -> 0% of each run, Pallas kernels for 5% -> 6%
where the time goes in v21:
time: 48.2 us; the launch traced here: 48 us
  Pallas kernels  17.2 us (36%)
  starting transfers between devices  13.5 us (28%)
  blocking collectives  11.4 us (24%)
  waiting for transfers between devices  3.29 us (7%)
  local copies, waits for them, and re-layouts  2.63 us (5%)
    pallas_call x1, Pallas kernels, body(): pl.pallas_call(functools.partial(evolve_kernel, ny, tiles, images), out_s...  13.1 us
    all_to_all x1, blocking collectives, body(): squares = lax.all_to_all(part, ('img', 'gx', 'gy'), 0, 0, tiled=True)  11.4 us
    ppermute x6, starting transfers between devices, swapped(): return lax.ppermute(cells, axis, pairs + [(j, i) for i, j in pairs])  7.83 us
    ppermute x4, starting transfers between devices, shifted(): return lax.ppermute(cells, axis, pairs)  5.63 us
    unnamed x16, local copies, waits for them, and re-layouts  2.63 us
    ppermute x6, waiting for transfers between devices, swapped(): return lax.ppermute(cells, axis, pairs + [(j, i) for i, j in pairs])  1.9 us
    ppermute x4, waiting for transfers between devices, shifted(): return lax.ppermute(cells, axis, pairs)  1.4 us
    pallas_call x1, Pallas kernels, body(): pl.pallas_call(functools.partial(info_kernel, ny, tiles, anisotropy.shape...  1.25 us
  transfers between devices with their start and end apart: 10, of which 3 were waited for; matrix products, arithmetic and copies ran while one was open for 0% of the time, Pallas kernels for 6%

profile of v21, /device:TPU:0, one launch (start us, length us, event | category | flops | bytes accessed | tf_op | source)
XLA Modules:
  0.0 48.0 jit_solution(4950587274229545734)
XLA Ops:
  0.0 2.9 %collective-permute-start = (f32[3,16,16,128]{3,2,1,0:T(8,128)}, f32[3,16,16,128]{3,2,1,0:T(8,128)S(1)}, u32[]{:S(2)}, u32[]{:S(2)}) collective-permute-start(f32[3,16,16,128]{3,2,1,0:T(8,128)} %bitcast.15), channel_id=1, source_target_pairs={{0,1},{1,0},{2,3},{3,2},{4,5},{5,4},{6,7},{7,6},{8,9},{9,8},{10,11... | collective-permute-start | bytes 1179656 | tf_op jit(solution)/shard_map/ppermute | solution.py:385
  2.9 0.7 %collective-permute-start.5 = (f32[3,16,16,128]{3,2,1,0:T(8,128)}, f32[3,16,16,128]{3,2,1,0:T(8,128)S(1)}, u32[]{:S(2)}, u32[]{:S(2)}) collective-permute-start(f32[3,16,16,128]{3,2,1,0:T(8,128)} %bitcast.16), channel_id=1, source_target_pairs={{8,16},{16,8},{9,17},{17,9},{10,18},{18,10},{11,19},{19,11},{12,20... | collective-permute-start | bytes 1179656 | tf_op jit(solution)/shard_map/ppermute | solution.py:391
  3.6 4.4 %collective-permute-start.4 = (f32[3,16,16,128]{3,2,1,0:T(8,128)}, f32[3,16,16,128]{3,2,1,0:T(8,128)S(1)}, u32[]{:S(2)}, u32[]{:S(2)}) collective-permute-start(f32[3,16,16,128]{3,2,1,0:T(8,128)} %bitcast.17), channel_id=1, source_target_pairs={{0,8},{16,24},{8,0},{24,16},{1,9},{17,25},{9,1},{25,17},{2,10},{18... | collective-permute-start | bytes 1179656 | tf_op jit(solution)/shard_map/ppermute | solution.py:391
  8.1 0.0 copy-start
  8.1 1.0 %copy-done = f32[1,3,16,16,128]{4,3,2,1,0:T(8,128)S(1)} copy-done((f32[1,3,16,16,128]{4,3,2,1,0:T(8,128)S(1)}, f32[1,3,16,16,128]{4,3,2,1,0:T(8,128)}, u32[]{:S(2)}) %copy-start) | copy-done | bytes 393240
  9.1 0.0 copy-start.1
  9.1 0.8 %pack_strips.1 = (f32[3,2,8,128]{3,2,1,0:T(8,128)S(1)}, f32[3,2,8,128]{3,2,1,0:T(8,128)S(1)}) custom-call(f32[3,256,128]{2,1,0:T(8,128)S(1)} %bitcast.18), custom_call_target="tpu_custom_call" | custom-call | tf_op jit(solution)/shard_map/pack_strips/pallas_call | solution.py:432
  9.9 0.0 copy-start.7
  9.9 0.1 collective-permute-start.1
  10.0 1.2 %collective-permute-done.1.own_one_ref = f32[3,2,8,128]{3,2,1,0:T(8,128)S(1)} collective-permute-done((f32[3,2,8,128]{3,2,1,0:T(8,128)S(1)}, f32[3,2,8,128]{3,2,1,0:T(8,128)S(1)}, u32[]{:S(2)}, u32[]{:S(2)}) %collective-permute-start.1) | collective-permute-done | bytes 24608 | tf_op jit(solution)/shard_map/ppermute | solution.py:391
  11.2 0.5 %collective-permute-start.2 = (s32[16,16,128]{2,1,0:T(8,128)}, s32[16,16,128]{2,1,0:T(8,128)S(1)}, u32[]{:S(2)}, u32[]{:S(2)}) collective-permute-start(s32[16,16,128]{2,1,0:T(8,128)} %param.9), channel_id=1, source_target_pairs={{0,1},{1,0},{2,3},{3,2},{4,5},{5,4},{6,7},{7,6},{8,9},{9,8},{10,11... | collective-permute-start | bytes 393224 | tf_op jit(solution)/shard_map/ppermute | solution.py:385
  11.7 1.0 %collective-permute-start.3 = (f32[3,2,8,128]{3,2,1,0:T(8,128)S(1)}, f32[3,2,8,128]{3,2,1,0:T(8,128)S(1)}, u32[]{:S(2)}, u32[]{:S(2)}) collective-permute-start(f32[3,2,8,128]{3,2,1,0:T(8,128)S(1)} %get-tuple-element.27), channel_id=1, source_target_pairs={{2,4},{6,0},{4,2},{0,6},{3,5},{7,1},{5,3},{1,7},{10,12},{14,8},{12... | collective-permute-start | bytes 73736 | tf_op jit(solution)/shard_map/ppermute | solution.py:391
  12.7 0.0 copy-start.4
  12.7 0.0 copy-start.5
  12.7 0.0 copy-start.6
  12.7 0.0 copy-done.7
  12.7 0.6 %copy-done.4 = s32[4]{0:T(128)S(1)} copy-done((s32[4]{0:T(128)S(1)}, s32[4]{0:T(128)}, u32[]{:S(2)}) %copy-start.4) | copy-done | bytes 40
  13.4 0.0 copy-done.5
  13.4 0.0 copy-done.6
  13.4 0.0 copy-start.2
  13.4 0.9 %copy-done.2 = s32[16,16,128]{2,1,0:T(8,128)S(1)} copy-done((s32[16,16,128]{2,1,0:T(8,128)S(1)}, s32[16,16,128]{2,1,0:T(8,128)}, u32[]{:S(2)}) %copy-start.2) | copy-done | bytes 131096
  14.3 1.2 %small_arguments.1 = (f32[1,2,8,128]{3,2,1,0:T(8,128)S(1)}, f32[1,2,8,128]{3,2,1,0:T(8,128)S(1)}, f32[5,8,128]{2,1,0:T(8,128)S(1)}) custom-call(s32[4]{0:T(128)S(1)} %copy-done.4, f32[8]{0:T(128)S(1)} %copy-done.5, f32[8]{0:T(128)S(1)} %copy-done.6, f32[1,3]{1,0:T(1,128)S(1)} %bitcast.31, s32[256,128]{1,0:T(8,128)S(1)} %bitcast.21), custom_call_target="tpu_custom_call" | custom-call | tf_op jit(solution)/shard_map/small_arguments/pallas_call | solution.py:442
  15.5 0.0 collective-permute-done.3.own_two_ref
  15.5 1.4 %collective-permute-done.2 = s32[16,16,128]{2,1,0:T(8,128)S(1)} collective-permute-done((s32[16,16,128]{2,1,0:T(8,128)}, s32[16,16,128]{2,1,0:T(8,128)S(1)}, u32[]{:S(2)}, u32[]{:S(2)}) %collective-permute-start.2) | collective-permute-done | bytes 131104 | tf_op jit(solution)/shard_map/ppermute | solution.py:385
  16.9 0.0 collective-permute-done
  16.9 0.0 collective-permute-done.5
  16.9 0.0 collective-permute-done.4
  16.9 0.0 copy-done.1
  17.0 0.0 copy-start.3
  17.0 1.1 %gather_images.1 = (f32[32,128]{1,0:T(8,128)S(1)}, f32[3,256,128]{2,1,0:T(8,128)S(1)}, f32[4,2,8,128]{3,2,1,0:T(8,128)S(1)}, f32[4,2,8,128]{3,2,1,0:T(8,128)S(1)}) custom-call(f32[5,8,128]{2,1,0:T(8,128)S(1)} %get-tuple-element.28.info_ref, f32[3,256,128]{2,1,0:T(8,128)S(1)} %bitcast.19, f32[3,256,128]{2,1,0:T(8,128)S(1)} %bitcast.24, ...), custom_call_target="tpu_custom_call" | custom-call | tf_op jit(solution)/shard_map/gather_images/pallas_call | solution.py:453
  18.0 0.6 %collective-permute-start.6 = (f32[3,16,16,128]{3,2,1,0:T(8,128)S(1)}, f32[3,16,16,128]{3,2,1,0:T(8,128)S(1)}, u32[]{:S(2)}, u32[]{:S(2)}) collective-permute-start(f32[3,16,16,128]{3,2,1,0:T(8,128)S(1)} %bitcast.26), channel_id=1, source_target_pairs={{0,1},{1,0},{2,3},{3,2},{4,5},{5,4},{6,7},{7,6},{8,9},{9,8},{10,11... | collective-permute-start | bytes 1179656 | tf_op jit(solution)/shard_map/ppermute | solution.py:385
  18.6 0.0 collective-permute-start.7
  18.6 1.6 %collective-permute-start.8 = (f32[4,2,8,128]{3,2,1,0:T(8,128)S(1)}, f32[4,2,8,128]{3,2,1,0:T(8,128)S(1)}, u32[]{:S(2)}, u32[]{:S(2)}) collective-permute-start(f32[4,2,8,128]{3,2,1,0:T(8,128)S(1)} %get-tuple-element.38), channel_id=1, source_target_pairs={{2,4},{6,0},{4,2},{0,6},{3,5},{7,1},{5,3},{1,7},{10,12},{14,8},{12... | collective-permute-start | bytes 98312 | tf_op jit(solution)/shard_map/ppermute | solution.py:391
  20.3 0.0 copy-done.3
  20.3 1.0 %parameters.1.par = f32[3,32,2,8,128]{4,3,2,1,0:T(8,128)S(1)} custom-call(f32[5,8,128]{2,1,0:T(8,128)S(1)} %get-tuple-element.28.info_ref, s32[256,128]{1,0:T(8,128)S(1)} %bitcast.22, s32[256,128]{1,0:T(8,128)S(1)} %bitcast.28), custom_call_target="tpu_custom_call" | custom-call | tf_op jit(solution)/shard_map/parameters/pallas_call | solution.py:470
  21.3 0.0 collective-permute-done.7.one_ref
  21.3 0.7 %collective-permute-done.8.two_ref = f32[4,2,8,128]{3,2,1,0:T(8,128)S(1)} collective-permute-done((f32[4,2,8,128]{3,2,1,0:T(8,128)S(1)}, f32[4,2,8,128]{3,2,1,0:T(8,128)S(1)}, u32[]{:S(2)}, u32[]{:S(2)}) %collective-permute-start.8) | collective-permute-done | bytes 32800 | tf_op jit(solution)/shard_map/ppermute | solution.py:391
  22.0 1.6 %collective-permute-start.9 = (f32[2,7,2,8,128]{4,3,2,1,0:T(8,128)S(1)}, f32[2,7,2,8,128]{4,3,2,1,0:T(8,128)S(1)}, u32[]{:S(2)}, u32[]{:S(2)}) collective-permute-start(f32[2,7,2,8,128]{4,3,2,1,0:T(8,128)S(1)} %merge_strips.1.strips_ref), channel_id=1, source_target_pairs={{0,1},{1,0},{2,3},{3,2},{4,5},{5,4},{6,7},{7,6},{8,9},{9,8},{10,11... | collective-permute-start | bytes 344072 | tf_op jit(solution)/shard_map/ppermute | solution.py:385
  23.5 11.4 %all_to_all.11 = f32[32,1,128]{2,1,0:T(1,128)S(1)} all-to-all(f32[32,1,128]{2,1,0:T(1,128)S(1)} %bitcast.30), channel_id=1, replica_groups=mesh['img'=4,'gx'=4,'gy'=2] {'img','gx','gy'}, dimensions={0} | all-to-all | bytes 32768 | tf_op jit(solution)/shard_map/all_to_all | solution.py:488
  34.9 0.0 collective-permute-done.9.stripsp_ref
  34.9 0.0 collective-permute-done.6
  34.9 13.1 %evolve.1 = f32[3,256,128]{2,1,0:T(8,128)} custom-call(f32[5,8,128]{2,1,0:T(8,128)S(1)} %get-tuple-element.28.info_ref, f32[32,128]{1,0:T(8,128)S(1)} %bitcast.29, f32[3,256,128]{2,1,0:T(8,128)S(1)} %bitcast.20, f32[3,256,128]{2,1,0:T(8,128)S(1)} %bitcast.25, f32[3,256,128]{2,1,0:T(8,128)S(1)} %get-tuple-element.33.n_ref, f32[3,256,128]{2,1,0:T(8,128)S(1)} %bitcast.27, ...), custom_call_target="tpu_custom_call" | custom-call | tf_op jit(solution)/shard_map/evolve/pallas_call | solution.py:490
  (1 shorter events, 0.0 us)
Async XLA Ops:
  0.0 16.9 %collective-permute-start = (f32[3,16,16,128]{3,2,1,0:T(8,128)}, f32[3,16,16,128]{3,2,1,0:T(8,128)S(1)}, u32[]{:S(2)}, u32[]{:S(2)}) collective-permute-start(f32[3,16,16,128]{3,2,1,0:T(8,128)} %bitcast.15), channel_id=1, source_target_pairs={{0,1},{1,0},{2,3},{3,2},{4,5},{5,4},{6,7},{7,6},{8,9},{9,8},{10,11... | collective-permute-start | bytes 1179656 | tf_op jit(solution)/shard_map/ppermute | solution.py:385
  2.9 14.0 %collective-permute-start.5 = (f32[3,16,16,128]{3,2,1,0:T(8,128)}, f32[3,16,16,128]{3,2,1,0:T(8,128)S(1)}, u32[]{:S(2)}, u32[]{:S(2)}) collective-permute-start(f32[3,16,16,128]{3,2,1,0:T(8,128)} %bitcast.16), channel_id=1, source_target_pairs={{8,16},{16,8},{9,17},{17,9},{10,18},{18,10},{11,19},{19,11},{12,20... | collective-permute-start | bytes 1179656 | tf_op jit(solution)/shard_map/ppermute | solution.py:391
  3.6 13.3 %collective-permute-start.4 = (f32[3,16,16,128]{3,2,1,0:T(8,128)}, f32[3,16,16,128]{3,2,1,0:T(8,128)S(1)}, u32[]{:S(2)}, u32[]{:S(2)}) collective-permute-start(f32[3,16,16,128]{3,2,1,0:T(8,128)} %bitcast.17), channel_id=1, source_target_pairs={{0,8},{16,24},{8,0},{24,16},{1,9},{17,25},{9,1},{25,17},{2,10},{18... | collective-permute-start | bytes 1179656 | tf_op jit(solution)/shard_map/ppermute | solution.py:391
  8.1 1.0 %copy-start = (f32[1,3,16,16,128]{4,3,2,1,0:T(8,128)S(1)}, f32[1,3,16,16,128]{4,3,2,1,0:T(8,128)}, u32[]{:S(2)}) copy-start(f32[1,3,16,16,128]{4,3,2,1,0:T(8,128)} %param.6) | copy-start | bytes 1179652
  9.1 7.9 %copy-start.1 = (f32[1,3,16,16,128]{4,3,2,1,0:T(8,128)S(1)}, f32[1,3,16,16,128]{4,3,2,1,0:T(8,128)}, u32[]{:S(2)}) copy-start(f32[1,3,16,16,128]{4,3,2,1,0:T(8,128)} %param.6) | copy-start | bytes 1179652
  9.9 2.8 %copy-start.7 = (f32[3]{0:T(128)S(1)}, f32[3]{0:T(128)}, u32[]{:S(2)}) copy-start(f32[3]{0:T(128)} %param.8) | copy-start | bytes 40
  9.9 1.3 %collective-permute-start.1 = (f32[3,2,8,128]{3,2,1,0:T(8,128)S(1)}, f32[3,2,8,128]{3,2,1,0:T(8,128)S(1)}, u32[]{:S(2)}, u32[]{:S(2)}) collective-permute-start(f32[3,2,8,128]{3,2,1,0:T(8,128)S(1)} %get-tuple-element.24), channel_id=1, source_target_pairs={{0,2},{4,6},{2,0},{6,4},{1,3},{5,7},{3,1},{7,5},{8,10},{12,14},{10... | collective-permute-start | bytes 73736 | tf_op jit(solution)/shard_map/ppermute | solution.py:391
  11.2 5.8 %collective-permute-start.2 = (s32[16,16,128]{2,1,0:T(8,128)}, s32[16,16,128]{2,1,0:T(8,128)S(1)}, u32[]{:S(2)}, u32[]{:S(2)}) collective-permute-start(s32[16,16,128]{2,1,0:T(8,128)} %param.9), channel_id=1, source_target_pairs={{0,1},{1,0},{2,3},{3,2},{4,5},{5,4},{6,7},{7,6},{8,9},{9,8},{10,11... | collective-permute-start | bytes 393224 | tf_op jit(solution)/shard_map/ppermute | solution.py:385
  11.7 3.9 %collective-permute-start.3 = (f32[3,2,8,128]{3,2,1,0:T(8,128)S(1)}, f32[3,2,8,128]{3,2,1,0:T(8,128)S(1)}, u32[]{:S(2)}, u32[]{:S(2)}) collective-permute-start(f32[3,2,8,128]{3,2,1,0:T(8,128)S(1)} %get-tuple-element.27), channel_id=1, source_target_pairs={{2,4},{6,0},{4,2},{0,6},{3,5},{7,1},{5,3},{1,7},{10,12},{14,8},{12... | collective-permute-start | bytes 73736 | tf_op jit(solution)/shard_map/ppermute | solution.py:391
  12.7 0.7 %copy-start.4 = (s32[4]{0:T(128)S(1)}, s32[4]{0:T(128)}, u32[]{:S(2)}) copy-start(s32[4]{0:T(128)} %lower_ref.1) | copy-start | bytes 52
  12.7 0.7 %copy-start.5 = (f32[8]{0:T(128)S(1)}, f32[8]{0:T(128)}, u32[]{:S(2)}) copy-start(f32[8]{0:T(128)} %aniso_ref.1) | copy-start | bytes 100
  12.7 0.7 %copy-start.6 = (f32[8]{0:T(128)S(1)}, f32[8]{0:T(128)}, u32[]{:S(2)}) copy-start(f32[8]{0:T(128)} %damp_ref.1) | copy-start | bytes 100
  13.4 0.9 %copy-start.2 = (s32[16,16,128]{2,1,0:T(8,128)S(1)}, s32[16,16,128]{2,1,0:T(8,128)}, u32[]{:S(2)}) copy-start(s32[16,16,128]{2,1,0:T(8,128)} %param.9) | copy-start | bytes 393220
  17.0 3.3 %copy-start.3 = (s32[16,16,128]{2,1,0:T(8,128)S(1)}, s32[16,16,128]{2,1,0:T(8,128)}, u32[]{:S(2)}) copy-start(s32[16,16,128]{2,1,0:T(8,128)} %param.9) | copy-start | bytes 393220
  18.0 16.9 %collective-permute-start.6 = (f32[3,16,16,128]{3,2,1,0:T(8,128)S(1)}, f32[3,16,16,128]{3,2,1,0:T(8,128)S(1)}, u32[]{:S(2)}, u32[]{:S(2)}) collective-permute-start(f32[3,16,16,128]{3,2,1,0:T(8,128)S(1)} %bitcast.26), channel_id=1, source_target_pairs={{0,1},{1,0},{2,3},{3,2},{4,5},{5,4},{6,7},{7,6},{8,9},{9,8},{10,11... | collective-permute-start | bytes 1179656 | tf_op jit(solution)/shard_map/ppermute | solution.py:385
  18.6 2.6 %collective-permute-start.7 = (f32[4,2,8,128]{3,2,1,0:T(8,128)S(1)}, f32[4,2,8,128]{3,2,1,0:T(8,128)S(1)}, u32[]{:S(2)}, u32[]{:S(2)}) collective-permute-start(f32[4,2,8,128]{3,2,1,0:T(8,128)S(1)} %get-tuple-element.34), channel_id=1, source_target_pairs={{0,2},{4,6},{2,0},{6,4},{1,3},{5,7},{3,1},{7,5},{8,10},{12,14},{10... | collective-permute-start | bytes 98312 | tf_op jit(solution)/shard_map/ppermute | solution.py:391
  18.6 3.3 %collective-permute-start.8 = (f32[4,2,8,128]{3,2,1,0:T(8,128)S(1)}, f32[4,2,8,128]{3,2,1,0:T(8,128)S(1)}, u32[]{:S(2)}, u32[]{:S(2)}) collective-permute-start(f32[4,2,8,128]{3,2,1,0:T(8,128)S(1)} %get-tuple-element.38), channel_id=1, source_target_pairs={{2,4},{6,0},{4,2},{0,6},{3,5},{7,1},{5,3},{1,7},{10,12},{14,8},{12... | collective-permute-start | bytes 98312 | tf_op jit(solution)/shard_map/ppermute | solution.py:391
  22.0 12.9 %collective-permute-start.9 = (f32[2,7,2,8,128]{4,3,2,1,0:T(8,128)S(1)}, f32[2,7,2,8,128]{4,3,2,1,0:T(8,128)S(1)}, u32[]{:S(2)}, u32[]{:S(2)}) collective-permute-start(f32[2,7,2,8,128]{4,3,2,1,0:T(8,128)S(1)} %merge_strips.1.strips_ref), channel_id=1, source_target_pairs={{0,1},{1,0},{2,3},{3,2},{4,5},{5,4},{6,7},{7,6},{8,9},{9,8},{10,11... | collective-permute-start | bytes 344072 | tf_op jit(solution)/shard_map/ppermute | solution.py:385

commit v22 on v20

--- a/solution.py
+++ b/solution.py
@@ -16,7 +16,7 @@
 SUB = 8
 LANES = 128
 COMPS = 3
-ROWS = 4
+ROWS = 8
 
 
 def lane_iota():
@@ -363,7 +363,7 @@
                     pltpu.store(edge.at[c, r // ny, t], ends[c], mask=mask)
             return carry
 
-        lax.fori_loop(0, count // ROWS, rows, 0)
+        lax.fori_loop(0, (count + ROWS - 1) // ROWS, rows, 0)
 
     def step(i, carry):
         for state in range(2):

time: 48.1 us -> 47 us (0.977)
  Pallas kernels: 16.7 us -> 15.6 us
    pallas_call x1, Pallas kernels: 13.1 us -> 12 us  [body(): pl.pallas_call(functools.partial(evolve_kernel, ny, tiles, images), out_s...]
where the time goes in v22:
time: 47 us; the launch traced here: 46.8 us
  Pallas kernels  15.6 us (33%)
  starting transfers between devices  13.7 us (29%)
  blocking collectives  10.9 us (23%)
  waiting for transfers between devices  3.87 us (8%)
  local copies, waits for them, and re-layouts  2.61 us (6%)
    pallas_call x1, Pallas kernels, body(): pl.pallas_call(functools.partial(evolve_kernel, ny, tiles, images), out_s...  12 us
    all_to_all x1, blocking collectives, body(): squares = lax.all_to_all(part, ('img', 'gx', 'gy'), 0, 0, tiled=True)  10.9 us
    ppermute x6, starting transfers between devices, swapped(): return lax.ppermute(cells, axis, pairs + [(j, i) for i, j in pairs])  8.04 us
    ppermute x4, starting transfers between devices, shifted(): return lax.ppermute(cells, axis, pairs)  5.69 us
    ppermute x6, waiting for transfers between devices, swapped(): return lax.ppermute(cells, axis, pairs + [(j, i) for i, j in pairs])  3.86 us
    unnamed x16, local copies, waits for them, and re-layouts  2.61 us
    pallas_call x1, Pallas kernels, body(): pl.pallas_call(functools.partial(pack_kernel, ny, tiles, anisotropy.shape...  1.51 us
    pallas_call x1, Pallas kernels, body(): pl.pallas_call(functools.partial(gather_kernel, ny, tiles), out_shape=(ja...  1.06 us
  transfers between devices with their start and end apart: 10, of which 3 were waited for; matrix products, arithmetic and copies ran while one was open for 0% of the time, Pallas kernels for 5%

profile of v22, /device:TPU:0, one launch (start us, length us, event | category | flops | bytes accessed | tf_op | source)
XLA Modules:
  0.0 46.8 jit_solution(6033508949604243348)
XLA Ops:
  0.0 2.9 %collective-permute-start = (f32[3,16,16,128]{3,2,1,0:T(8,128)}, f32[3,16,16,128]{3,2,1,0:T(8,128)S(1)}, u32[]{:S(2)}, u32[]{:S(2)}) collective-permute-start(f32[3,16,16,128]{3,2,1,0:T(8,128)} %bitcast.15), channel_id=1, source_target_pairs={{0,1},{1,0},{2,3},{3,2},{4,5},{5,4},{6,7},{7,6},{8,9},{9,8},{10,11... | collective-permute-start | bytes 1179656 | tf_op jit(solution)/shard_map/ppermute | solution.py:390
  2.9 0.7 %collective-permute-start.5 = (f32[3,16,16,128]{3,2,1,0:T(8,128)}, f32[3,16,16,128]{3,2,1,0:T(8,128)S(1)}, u32[]{:S(2)}, u32[]{:S(2)}) collective-permute-start(f32[3,16,16,128]{3,2,1,0:T(8,128)} %bitcast.16), channel_id=1, source_target_pairs={{8,16},{16,8},{9,17},{17,9},{10,18},{18,10},{11,19},{19,11},{12,20... | collective-permute-start | bytes 1179656 | tf_op jit(solution)/shard_map/ppermute | solution.py:396
  3.6 4.4 %collective-permute-start.4 = (f32[3,16,16,128]{3,2,1,0:T(8,128)}, f32[3,16,16,128]{3,2,1,0:T(8,128)S(1)}, u32[]{:S(2)}, u32[]{:S(2)}) collective-permute-start(f32[3,16,16,128]{3,2,1,0:T(8,128)} %bitcast.17), channel_id=1, source_target_pairs={{0,8},{16,24},{8,0},{24,16},{1,9},{17,25},{9,1},{25,17},{2,10},{18... | collective-permute-start | bytes 1179656 | tf_op jit(solution)/shard_map/ppermute | solution.py:396
  8.1 0.0 copy-start.7
  8.1 0.0 copy-start.4
  8.1 0.0 copy-start.5
  8.1 0.0 copy-start.6
  8.1 0.6 %copy-done.7 = f32[3]{0:T(128)S(1)} copy-done((f32[3]{0:T(128)S(1)}, f32[3]{0:T(128)}, u32[]{:S(2)}) %copy-start.7) | copy-done | bytes 36
  8.7 0.0 copy-done.4
  8.7 0.0 copy-done.5
  8.7 0.0 copy-done.6
  8.8 0.0 copy-start
  8.8 1.0 %copy-done = f32[1,3,16,16,128]{4,3,2,1,0:T(8,128)S(1)} copy-done((f32[1,3,16,16,128]{4,3,2,1,0:T(8,128)S(1)}, f32[1,3,16,16,128]{4,3,2,1,0:T(8,128)}, u32[]{:S(2)}) %copy-start) | copy-done | bytes 393240
  9.8 0.0 copy-start.2
  9.8 0.9 %copy-done.2 = s32[16,16,128]{2,1,0:T(8,128)S(1)} copy-done((s32[16,16,128]{2,1,0:T(8,128)S(1)}, s32[16,16,128]{2,1,0:T(8,128)}, u32[]{:S(2)}) %copy-start.2) | copy-done | bytes 131096
  10.7 0.0 copy-start.1
  10.7 1.5 %pack_strips.1 = (f32[4,2,8,128]{3,2,1,0:T(8,128)S(1)}, f32[4,2,8,128]{3,2,1,0:T(8,128)S(1)}, f32[5,8,128]{2,1,0:T(8,128)S(1)}) custom-call(s32[4]{0:T(128)S(1)} %copy-done.4, f32[8]{0:T(128)S(1)} %copy-done.5, f32[8]{0:T(128)S(1)} %copy-done.6, f32[1,3]{1,0:T(1,128)S(1)} %bitcast.31, f32[3,256,128]{2,1,0:T(8,128)S(1)} %bitcast.18, s32[256,128]{1,0:T(8,128)S(1)} %bitcast.21), custom_call_target="tpu_custom_call" | custom-call | tf_op jit(solution)/shard_map/pack_strips/pallas_call | solution.py:437
  12.2 0.6 %collective-permute-start.1 = (s32[16,16,128]{2,1,0:T(8,128)S(1)}, s32[16,16,128]{2,1,0:T(8,128)S(1)}, u32[]{:S(2)}, u32[]{:S(2)}) collective-permute-start(s32[16,16,128]{2,1,0:T(8,128)S(1)} %copy-done.2), channel_id=1, source_target_pairs={{0,1},{1,0},{2,3},{3,2},{4,5},{5,4},{6,7},{7,6},{8,9},{9,8},{10,11... | collective-permute-start | bytes 393224 | tf_op jit(solution)/shard_map/ppermute | solution.py:390
  12.8 0.0 collective-permute-start.2
  12.8 1.2 %collective-permute-done.2.own_one_ref = f32[4,2,8,128]{3,2,1,0:T(8,128)S(1)} collective-permute-done((f32[4,2,8,128]{3,2,1,0:T(8,128)S(1)}, f32[4,2,8,128]{3,2,1,0:T(8,128)S(1)}, u32[]{:S(2)}, u32[]{:S(2)}) %collective-permute-start.2) | collective-permute-done | bytes 32800 | tf_op jit(solution)/shard_map/ppermute | solution.py:396
  14.0 1.3 %collective-permute-start.3 = (f32[4,2,8,128]{3,2,1,0:T(8,128)S(1)}, f32[4,2,8,128]{3,2,1,0:T(8,128)S(1)}, u32[]{:S(2)}, u32[]{:S(2)}) collective-permute-start(f32[4,2,8,128]{3,2,1,0:T(8,128)S(1)} %get-tuple-element.25), channel_id=1, source_target_pairs={{2,4},{6,0},{4,2},{0,6},{3,5},{7,1},{5,3},{1,7},{10,12},{14,8},{12... | collective-permute-start | bytes 98312 | tf_op jit(solution)/shard_map/ppermute | solution.py:396
  15.3 2.1 %collective-permute-done.3.own_two_ref = f32[4,2,8,128]{3,2,1,0:T(8,128)S(1)} collective-permute-done((f32[4,2,8,128]{3,2,1,0:T(8,128)S(1)}, f32[4,2,8,128]{3,2,1,0:T(8,128)S(1)}, u32[]{:S(2)}, u32[]{:S(2)}) %collective-permute-start.3) | collective-permute-done | bytes 32800 | tf_op jit(solution)/shard_map/ppermute | solution.py:396
  17.3 0.0 collective-permute-done.1
  17.3 0.0 collective-permute-done
  17.3 0.0 collective-permute-done.5
  17.4 0.0 collective-permute-done.4
  17.4 0.0 copy-done.1
  17.4 0.0 copy-start.3
  17.4 1.1 %gather_images.1 = (f32[32,128]{1,0:T(8,128)S(1)}, f32[3,256,128]{2,1,0:T(8,128)S(1)}, f32[3,2,8,128]{3,2,1,0:T(8,128)S(1)}, f32[3,2,8,128]{3,2,1,0:T(8,128)S(1)}) custom-call(f32[5,8,128]{2,1,0:T(8,128)S(1)} %get-tuple-element.26.info_ref, f32[3,256,128]{2,1,0:T(8,128)S(1)} %bitcast.19, f32[3,256,128]{2,1,0:T(8,128)S(1)} %bitcast.24, ...), custom_call_target="tpu_custom_call" | custom-call | tf_op jit(solution)/shard_map/gather_images/pallas_call | solution.py:458
  18.4 1.6 %collective-permute-start.6 = (f32[3,16,16,128]{3,2,1,0:T(8,128)S(1)}, f32[3,16,16,128]{3,2,1,0:T(8,128)S(1)}, u32[]{:S(2)}, u32[]{:S(2)}) collective-permute-start(f32[3,16,16,128]{3,2,1,0:T(8,128)S(1)} %bitcast.26), channel_id=1, source_target_pairs={{0,1},{1,0},{2,3},{3,2},{4,5},{5,4},{6,7},{7,6},{8,9},{9,8},{10,11... | collective-permute-start | bytes 1179656 | tf_op jit(solution)/shard_map/ppermute | solution.py:390
  20.0 0.0 collective-permute-start.7
  20.0 1.6 %collective-permute-start.8 = (f32[3,2,8,128]{3,2,1,0:T(8,128)S(1)}, f32[3,2,8,128]{3,2,1,0:T(8,128)S(1)}, u32[]{:S(2)}, u32[]{:S(2)}) collective-permute-start(f32[3,2,8,128]{3,2,1,0:T(8,128)S(1)} %get-tuple-element.34), channel_id=1, source_target_pairs={{2,4},{6,0},{4,2},{0,6},{3,5},{7,1},{5,3},{1,7},{10,12},{14,8},{12... | collective-permute-start | bytes 73736 | tf_op jit(solution)/shard_map/ppermute | solution.py:396
  21.6 0.0 copy-done.3
  21.6 1.0 %parameters.1.par = f32[3,32,2,8,128]{4,3,2,1,0:T(8,128)S(1)} custom-call(f32[5,8,128]{2,1,0:T(8,128)S(1)} %get-tuple-element.26.info_ref, s32[256,128]{1,0:T(8,128)S(1)} %bitcast.22, s32[256,128]{1,0:T(8,128)S(1)} %bitcast.28), custom_call_target="tpu_custom_call" | custom-call | tf_op jit(solution)/shard_map/parameters/pallas_call | solution.py:475
  22.7 0.0 collective-permute-done.7.one_ref
  22.7 0.6 %collective-permute-done.8.two_ref = f32[3,2,8,128]{3,2,1,0:T(8,128)S(1)} collective-permute-done((f32[3,2,8,128]{3,2,1,0:T(8,128)S(1)}, f32[3,2,8,128]{3,2,1,0:T(8,128)S(1)}, u32[]{:S(2)}, u32[]{:S(2)}) %collective-permute-start.8) | collective-permute-done | bytes 24608 | tf_op jit(solution)/shard_map/ppermute | solution.py:396
  23.3 0.6 %collective-permute-start.9 = (f32[2,7,2,8,128]{4,3,2,1,0:T(8,128)S(1)}, f32[2,7,2,8,128]{4,3,2,1,0:T(8,128)S(1)}, u32[]{:S(2)}, u32[]{:S(2)}) collective-permute-start(f32[2,7,2,8,128]{4,3,2,1,0:T(8,128)S(1)} %merge_strips.1.strips_ref), channel_id=1, source_target_pairs={{0,1},{1,0},{2,3},{3,2},{4,5},{5,4},{6,7},{7,6},{8,9},{9,8},{10,11... | collective-permute-start | bytes 344072 | tf_op jit(solution)/shard_map/ppermute | solution.py:390
  23.9 10.9 %all_to_all.11 = f32[32,1,128]{2,1,0:T(1,128)S(1)} all-to-all(f32[32,1,128]{2,1,0:T(1,128)S(1)} %bitcast.30), channel_id=1, replica_groups=mesh['img'=4,'gx'=4,'gy'=2] {'img','gx','gy'}, dimensions={0} | all-to-all | bytes 32768 | tf_op jit(solution)/shard_map/all_to_all | solution.py:493
  34.8 0.0 collective-permute-done.9.stripsp_ref
  34.8 0.0 collective-permute-done.6
  34.8 12.0 %evolve.1 = f32[3,256,128]{2,1,0:T(8,128)} custom-call(f32[5,8,128]{2,1,0:T(8,128)S(1)} %get-tuple-element.26.info_ref, f32[32,128]{1,0:T(8,128)S(1)} %bitcast.29, f32[3,256,128]{2,1,0:T(8,128)S(1)} %bitcast.20, f32[3,256,128]{2,1,0:T(8,128)S(1)} %bitcast.25, f32[3,256,128]{2,1,0:T(8,128)S(1)} %get-tuple-element.29.n_ref, f32[3,256,128]{2,1,0:T(8,128)S(1)} %bitcast.27, ...), custom_call_target="tpu_custom_call" | custom-call | tf_op jit(solution)/shard_map/evolve/pallas_call | solution.py:495
  (1 shorter events, 0.0 us)
Async XLA Ops:
  0.0 17.3 %collective-permute-start = (f32[3,16,16,128]{3,2,1,0:T(8,128)}, f32[3,16,16,128]{3,2,1,0:T(8,128)S(1)}, u32[]{:S(2)}, u32[]{:S(2)}) collective-permute-start(f32[3,16,16,128]{3,2,1,0:T(8,128)} %bitcast.15), channel_id=1, source_target_pairs={{0,1},{1,0},{2,3},{3,2},{4,5},{5,4},{6,7},{7,6},{8,9},{9,8},{10,11... | collective-permute-start | bytes 1179656 | tf_op jit(solution)/shard_map/ppermute | solution.py:390
  2.9 14.4 %collective-permute-start.5 = (f32[3,16,16,128]{3,2,1,0:T(8,128)}, f32[3,16,16,128]{3,2,1,0:T(8,128)S(1)}, u32[]{:S(2)}, u32[]{:S(2)}) collective-permute-start(f32[3,16,16,128]{3,2,1,0:T(8,128)} %bitcast.16), channel_id=1, source_target_pairs={{8,16},{16,8},{9,17},{17,9},{10,18},{18,10},{11,19},{19,11},{12,20... | collective-permute-start | bytes 1179656 | tf_op jit(solution)/shard_map/ppermute | solution.py:396
  3.6 13.7 %collective-permute-start.4 = (f32[3,16,16,128]{3,2,1,0:T(8,128)}, f32[3,16,16,128]{3,2,1,0:T(8,128)S(1)}, u32[]{:S(2)}, u32[]{:S(2)}) collective-permute-start(f32[3,16,16,128]{3,2,1,0:T(8,128)} %bitcast.17), channel_id=1, source_target_pairs={{0,8},{16,24},{8,0},{24,16},{1,9},{17,25},{9,1},{25,17},{2,10},{18... | collective-permute-start | bytes 1179656 | tf_op jit(solution)/shard_map/ppermute | solution.py:396
  8.1 0.7 %copy-start.7 = (f32[3]{0:T(128)S(1)}, f32[3]{0:T(128)}, u32[]{:S(2)}) copy-start(f32[3]{0:T(128)} %param.8) | copy-start | bytes 40
  8.1 0.7 %copy-start.4 = (s32[4]{0:T(128)S(1)}, s32[4]{0:T(128)}, u32[]{:S(2)}) copy-start(s32[4]{0:T(128)} %lower_ref.1) | copy-start | bytes 52
  8.1 0.7 %copy-start.5 = (f32[8]{0:T(128)S(1)}, f32[8]{0:T(128)}, u32[]{:S(2)}) copy-start(f32[8]{0:T(128)} %aniso_ref.1) | copy-start | bytes 100
  8.1 0.7 %copy-start.6 = (f32[8]{0:T(128)S(1)}, f32[8]{0:T(128)}, u32[]{:S(2)}) copy-start(f32[8]{0:T(128)} %damp_ref.1) | copy-start | bytes 100
  8.8 1.0 %copy-start = (f32[1,3,16,16,128]{4,3,2,1,0:T(8,128)S(1)}, f32[1,3,16,16,128]{4,3,2,1,0:T(8,128)}, u32[]{:S(2)}) copy-start(f32[1,3,16,16,128]{4,3,2,1,0:T(8,128)} %param.6) | copy-start | bytes 1179652
  9.8 0.9 %copy-start.2 = (s32[16,16,128]{2,1,0:T(8,128)S(1)}, s32[16,16,128]{2,1,0:T(8,128)}, u32[]{:S(2)}) copy-start(s32[16,16,128]{2,1,0:T(8,128)} %param.9) | copy-start | bytes 393220
  10.7 6.7 %copy-start.1 = (f32[1,3,16,16,128]{4,3,2,1,0:T(8,128)S(1)}, f32[1,3,16,16,128]{4,3,2,1,0:T(8,128)}, u32[]{:S(2)}) copy-start(f32[1,3,16,16,128]{4,3,2,1,0:T(8,128)} %param.6) | copy-start | bytes 1179652
  12.2 5.2 %collective-permute-start.1 = (s32[16,16,128]{2,1,0:T(8,128)S(1)}, s32[16,16,128]{2,1,0:T(8,128)S(1)}, u32[]{:S(2)}, u32[]{:S(2)}) collective-permute-start(s32[16,16,128]{2,1,0:T(8,128)S(1)} %copy-done.2), channel_id=1, source_target_pairs={{0,1},{1,0},{2,3},{3,2},{4,5},{5,4},{6,7},{7,6},{8,9},{9,8},{10,11... | collective-permute-start | bytes 393224 | tf_op jit(solution)/shard_map/ppermute | solution.py:390
  12.8 1.2 %collective-permute-start.2 = (f32[4,2,8,128]{3,2,1,0:T(8,128)S(1)}, f32[4,2,8,128]{3,2,1,0:T(8,128)S(1)}, u32[]{:S(2)}, u32[]{:S(2)}) collective-permute-start(f32[4,2,8,128]{3,2,1,0:T(8,128)S(1)} %get-tuple-element.24), channel_id=1, source_target_pairs={{0,2},{4,6},{2,0},{6,4},{1,3},{5,7},{3,1},{7,5},{8,10},{12,14},{10... | collective-permute-start | bytes 98312 | tf_op jit(solution)/shard_map/ppermute | solution.py:396
  14.0 3.3 %collective-permute-start.3 = (f32[4,2,8,128]{3,2,1,0:T(8,128)S(1)}, f32[4,2,8,128]{3,2,1,0:T(8,128)S(1)}, u32[]{:S(2)}, u32[]{:S(2)}) collective-permute-start(f32[4,2,8,128]{3,2,1,0:T(8,128)S(1)} %get-tuple-element.25), channel_id=1, source_target_pairs={{2,4},{6,0},{4,2},{0,6},{3,5},{7,1},{5,3},{1,7},{10,12},{14,8},{12... | collective-permute-start | bytes 98312 | tf_op jit(solution)/shard_map/ppermute | solution.py:396
  17.4 4.3 %copy-start.3 = (s32[16,16,128]{2,1,0:T(8,128)S(1)}, s32[16,16,128]{2,1,0:T(8,128)}, u32[]{:S(2)}) copy-start(s32[16,16,128]{2,1,0:T(8,128)} %param.9) | copy-start | bytes 393220
  18.4 16.4 %collective-permute-start.6 = (f32[3,16,16,128]{3,2,1,0:T(8,128)S(1)}, f32[3,16,16,128]{3,2,1,0:T(8,128)S(1)}, u32[]{:S(2)}, u32[]{:S(2)}) collective-permute-start(f32[3,16,16,128]{3,2,1,0:T(8,128)S(1)} %bitcast.26), channel_id=1, source_target_pairs={{0,1},{1,0},{2,3},{3,2},{4,5},{5,4},{6,7},{7,6},{8,9},{9,8},{10,11... | collective-permute-start | bytes 1179656 | tf_op jit(solution)/shard_map/ppermute | solution.py:390
  20.0 2.7 %collective-permute-start.7 = (f32[3,2,8,128]{3,2,1,0:T(8,128)S(1)}, f32[3,2,8,128]{3,2,1,0:T(8,128)S(1)}, u32[]{:S(2)}, u32[]{:S(2)}) collective-permute-start(f32[3,2,8,128]{3,2,1,0:T(8,128)S(1)} %get-tuple-element.30), channel_id=1, source_target_pairs={{0,2},{4,6},{2,0},{6,4},{1,3},{5,7},{3,1},{7,5},{8,10},{12,14},{10... | collective-permute-start | bytes 73736 | tf_op jit(solution)/shard_map/ppermute | solution.py:396
  20.0 3.3 %collective-permute-start.8 = (f32[3,2,8,128]{3,2,1,0:T(8,128)S(1)}, f32[3,2,8,128]{3,2,1,0:T(8,128)S(1)}, u32[]{:S(2)}, u32[]{:S(2)}) collective-permute-start(f32[3,2,8,128]{3,2,1,0:T(8,128)S(1)} %get-tuple-element.34), channel_id=1, source_target_pairs={{2,4},{6,0},{4,2},{0,6},{3,5},{7,1},{5,3},{1,7},{10,12},{14,8},{12... | collective-permute-start | bytes 73736 | tf_op jit(solution)/shard_map/ppermute | solution.py:396
  23.3 11.5 %collective-permute-start.9 = (f32[2,7,2,8,128]{4,3,2,1,0:T(8,128)S(1)}, f32[2,7,2,8,128]{4,3,2,1,0:T(8,128)S(1)}, u32[]{:S(2)}, u32[]{:S(2)}) collective-permute-start(f32[2,7,2,8,128]{4,3,2,1,0:T(8,128)S(1)} %merge_strips.1.strips_ref), channel_id=1, source_target_pairs={{0,1},{1,0},{2,3},{3,2},{4,5},{5,4},{6,7},{7,6},{8,9},{9,8},{10,11... | collective-permute-start | bytes 344072 | tf_op jit(solution)/shard_map/ppermute | solution.py:390

commit v23 on v22

--- a/solution.py
+++ b/solution.py
@@ -16,7 +16,7 @@
 SUB = 8
 LANES = 128
 COMPS = 3
-ROWS = 8
+ROWS = 10
 
 
 def lane_iota():
@@ -100,7 +100,7 @@
 ):
     here = lax.axis_index("img")
     pick, odd = take_first(info_ref, here)
-    chunks = 4
+    chunks = 8
     depth = m_ref.shape[1]
 
     def squares(i, sums):
@@ -113,20 +113,20 @@
                 two = second_ref[c, pl.ds(start, SUB), :]
                 done.append((c, start, jnp.where(pick, one, two)))
                 diff = m_ref[c, pl.ds(start, SUB), :] - jnp.where(odd, one, two)
-                sums[c + COMPS * u] = sums[c + COMPS * u] + diff * diff
+                sums[c + COMPS * (u % 4)] = sums[c + COMPS * (u % 4)] + diff * diff
         for c, start, cells in done:
             near_ref[c, pl.ds(start, SUB), :] = cells
         return tuple(sums)
 
     zero = jnp.zeros((SUB, LANES), jnp.float32)
-    sums = lax.fori_loop(0, depth // (chunks * SUB), squares, (zero,) * (chunks * COMPS))
+    sums = lax.fori_loop(0, depth // (chunks * SUB), squares, (zero,) * (4 * COMPS))
     total = jnp.sum(functools.reduce(jnp.add, sums), axis=(0, 1), keepdims=True)
     slot = lax.broadcasted_iota(jnp.int32, part_ref.shape, 1)
     part_ref[...] = jnp.where((slot == here) & (here > 0), total, 0.0)
     def pack(i, carry):
         done = []
-        for u in range(2):
-            y = 2 * i + u
+        for u in range(4):
+            y = 4 * i + u
             one, two, shift = rims(ny, y)
             for t in range(tiles):
                 for c in range(COMPS):
@@ -137,7 +137,7 @@
             pltpu.store(two_ref.at[c, t], cells, mask=two)
         return carry
 
-    lax.fori_loop(0, ny // 2, pack, 0)
+    lax.fori_loop(0, ny // 4, pack, 0)
 
 
 def turn(m, h, a2, b, sc):
@@ -232,7 +232,7 @@
 
     def fill(i, carry):
         done = []
-        for k in (2 * i, 2 * i + 1):
+        for k in [4 * i + u for u in range(4)]:
             for g, (own, near) in enumerate(((m_ref, n_ref), (mp_ref, np_ref))):
                 for t in range(tiles):
                     rows = rows_at(ny, tiles, k, t)
@@ -245,7 +245,7 @@
                 main0[c, r, t] = v[c]
         return carry
 
-    lax.fori_loop(0, ny // 2, fill, 0)
+    lax.fori_loop(0, ny // 4, fill, 0)
 
     def seam_of(left, right):
         return jnp.where(head_lane, pltpu.roll(left, 1, 1), pltpu.roll(right, LANES - 1, 1))
@@ -367,7 +367,7 @@
 
     def step(i, carry):
         for state in range(2):
-            margin = DEPTH - 2 * state - 2 * i
+            margin = DEPTH - 1 - state - 2 * i
             main_rows(state, -margin, ny + 2 * margin)
             strip_rows(state)
         return carry

time: 47 us -> 46.3 us (0.985)
  Pallas kernels: 15.6 us -> 14.9 us
  transfers between devices with their start and end apart: 10 -> 10, of which waited for: 3 -> 3; matrix products, arithmetic and copies ran while one was open for 0% -> 0% of each run, Pallas kernels for 5% -> 6%
where the time goes in v23:
time: 46.3 us; the launch traced here: 46.1 us
  Pallas kernels  14.9 us (32%)
  starting transfers between devices  13.7 us (30%)
  blocking collectives  10.9 us (24%)
  waiting for transfers between devices  3.87 us (8%)
  local copies, waits for them, and re-layouts  2.61 us (6%)
    pallas_call x1, Pallas kernels, body(): pl.pallas_call(functools.partial(evolve_kernel, ny, tiles, images), out_s...  11.6 us
    all_to_all x1, blocking collectives, body(): squares = lax.all_to_all(part, ('img', 'gx', 'gy'), 0, 0, tiled=True)  10.9 us
    ppermute x6, starting transfers between devices, swapped(): return lax.ppermute(cells, axis, pairs + [(j, i) for i, j in pairs])  8.04 us
    ppermute x4, starting transfers between devices, shifted(): return lax.ppermute(cells, axis, pairs)  5.69 us
    ppermute x6, waiting for transfers between devices, swapped(): return lax.ppermute(cells, axis, pairs + [(j, i) for i, j in pairs])  3.86 us
    unnamed x16, local copies, waits for them, and re-layouts  2.61 us
    pallas_call x1, Pallas kernels, body(): pl.pallas_call(functools.partial(pack_kernel, ny, tiles, anisotropy.shape...  1.51 us
    pallas_call x1, Pallas kernels, body(): pl.pallas_call(functools.partial(look_up_kernel, ny, tiles), out_shape=ja...  1.01 us
  transfers between devices with their start and end apart: 10, of which 3 were waited for; matrix products, arithmetic and copies ran while one was open for 0% of the time, Pallas kernels for 6%

profile of v23, /device:TPU:0, one launch (start us, length us, event | category | flops | bytes accessed | tf_op | source)
XLA Modules:
  0.0 46.1 jit_solution(8707147123872553734)
XLA Ops:
  0.0 2.9 %collective-permute-start = (f32[3,16,16,128]{3,2,1,0:T(8,128)}, f32[3,16,16,128]{3,2,1,0:T(8,128)S(1)}, u32[]{:S(2)}, u32[]{:S(2)}) collective-permute-start(f32[3,16,16,128]{3,2,1,0:T(8,128)} %bitcast.15), channel_id=1, source_target_pairs={{0,1},{1,0},{2,3},{3,2},{4,5},{5,4},{6,7},{7,6},{8,9},{9,8},{10,11... | collective-permute-start | bytes 1179656 | tf_op jit(solution)/shard_map/ppermute | solution.py:390
  2.9 0.7 %collective-permute-start.5 = (f32[3,16,16,128]{3,2,1,0:T(8,128)}, f32[3,16,16,128]{3,2,1,0:T(8,128)S(1)}, u32[]{:S(2)}, u32[]{:S(2)}) collective-permute-start(f32[3,16,16,128]{3,2,1,0:T(8,128)} %bitcast.16), channel_id=1, source_target_pairs={{8,16},{16,8},{9,17},{17,9},{10,18},{18,10},{11,19},{19,11},{12,20... | collective-permute-start | bytes 1179656 | tf_op jit(solution)/shard_map/ppermute | solution.py:396
  3.6 4.4 %collective-permute-start.4 = (f32[3,16,16,128]{3,2,1,0:T(8,128)}, f32[3,16,16,128]{3,2,1,0:T(8,128)S(1)}, u32[]{:S(2)}, u32[]{:S(2)}) collective-permute-start(f32[3,16,16,128]{3,2,1,0:T(8,128)} %bitcast.17), channel_id=1, source_target_pairs={{0,8},{16,24},{8,0},{24,16},{1,9},{17,25},{9,1},{25,17},{2,10},{18... | collective-permute-start | bytes 1179656 | tf_op jit(solution)/shard_map/ppermute | solution.py:396
  8.1 0.0 copy-start.7
  8.1 0.0 copy-start.4
  8.1 0.0 copy-start.5
  8.1 0.0 copy-start.6
  8.1 0.6 %copy-done.7 = f32[3]{0:T(128)S(1)} copy-done((f32[3]{0:T(128)S(1)}, f32[3]{0:T(128)}, u32[]{:S(2)}) %copy-start.7) | copy-done | bytes 36
  8.7 0.0 copy-done.4
  8.7 0.0 copy-done.5
  8.7 0.0 copy-done.6
  8.8 0.0 copy-start
  8.8 1.0 %copy-done = f32[1,3,16,16,128]{4,3,2,1,0:T(8,128)S(1)} copy-done((f32[1,3,16,16,128]{4,3,2,1,0:T(8,128)S(1)}, f32[1,3,16,16,128]{4,3,2,1,0:T(8,128)}, u32[]{:S(2)}) %copy-start) | copy-done | bytes 393240
  9.8 0.0 copy-start.2
  9.8 0.9 %copy-done.2 = s32[16,16,128]{2,1,0:T(8,128)S(1)} copy-done((s32[16,16,128]{2,1,0:T(8,128)S(1)}, s32[16,16,128]{2,1,0:T(8,128)}, u32[]{:S(2)}) %copy-start.2) | copy-done | bytes 131096
  10.7 0.0 copy-start.1
  10.7 1.5 %pack_strips.1 = (f32[4,2,8,128]{3,2,1,0:T(8,128)S(1)}, f32[4,2,8,128]{3,2,1,0:T(8,128)S(1)}, f32[5,8,128]{2,1,0:T(8,128)S(1)}) custom-call(s32[4]{0:T(128)S(1)} %copy-done.4, f32[8]{0:T(128)S(1)} %copy-done.5, f32[8]{0:T(128)S(1)} %copy-done.6, f32[1,3]{1,0:T(1,128)S(1)} %bitcast.31, f32[3,256,128]{2,1,0:T(8,128)S(1)} %bitcast.18, s32[256,128]{1,0:T(8,128)S(1)} %bitcast.21), custom_call_target="tpu_custom_call" | custom-call | tf_op jit(solution)/shard_map/pack_strips/pallas_call | solution.py:437
  12.2 0.6 %collective-permute-start.1 = (s32[16,16,128]{2,1,0:T(8,128)S(1)}, s32[16,16,128]{2,1,0:T(8,128)S(1)}, u32[]{:S(2)}, u32[]{:S(2)}) collective-permute-start(s32[16,16,128]{2,1,0:T(8,128)S(1)} %copy-done.2), channel_id=1, source_target_pairs={{0,1},{1,0},{2,3},{3,2},{4,5},{5,4},{6,7},{7,6},{8,9},{9,8},{10,11... | collective-permute-start | bytes 393224 | tf_op jit(solution)/shard_map/ppermute | solution.py:390
  12.8 0.0 collective-permute-start.2
  12.8 1.2 %collective-permute-done.2.own_one_ref = f32[4,2,8,128]{3,2,1,0:T(8,128)S(1)} collective-permute-done((f32[4,2,8,128]{3,2,1,0:T(8,128)S(1)}, f32[4,2,8,128]{3,2,1,0:T(8,128)S(1)}, u32[]{:S(2)}, u32[]{:S(2)}) %collective-permute-start.2) | collective-permute-done | bytes 32800 | tf_op jit(solution)/shard_map/ppermute | solution.py:396
  14.0 1.3 %collective-permute-start.3 = (f32[4,2,8,128]{3,2,1,0:T(8,128)S(1)}, f32[4,2,8,128]{3,2,1,0:T(8,128)S(1)}, u32[]{:S(2)}, u32[]{:S(2)}) collective-permute-start(f32[4,2,8,128]{3,2,1,0:T(8,128)S(1)} %get-tuple-element.25), channel_id=1, source_target_pairs={{2,4},{6,0},{4,2},{0,6},{3,5},{7,1},{5,3},{1,7},{10,12},{14,8},{12... | collective-permute-start | bytes 98312 | tf_op jit(solution)/shard_map/ppermute | solution.py:396
  15.3 2.1 %collective-permute-done.3.own_two_ref = f32[4,2,8,128]{3,2,1,0:T(8,128)S(1)} collective-permute-done((f32[4,2,8,128]{3,2,1,0:T(8,128)S(1)}, f32[4,2,8,128]{3,2,1,0:T(8,128)S(1)}, u32[]{:S(2)}, u32[]{:S(2)}) %collective-permute-start.3) | collective-permute-done | bytes 32800 | tf_op jit(solution)/shard_map/ppermute | solution.py:396
  17.3 0.0 collective-permute-done.1
  17.3 0.0 collective-permute-done
  17.3 0.0 collective-permute-done.5
  17.4 0.0 collective-permute-done.4
  17.4 0.0 copy-done.1
  17.4 0.0 copy-start.3
  17.4 0.7 %gather_images.1 = (f32[32,128]{1,0:T(8,128)S(1)}, f32[3,256,128]{2,1,0:T(8,128)S(1)}, f32[3,2,8,128]{3,2,1,0:T(8,128)S(1)}, f32[3,2,8,128]{3,2,1,0:T(8,128)S(1)}) custom-call(f32[5,8,128]{2,1,0:T(8,128)S(1)} %get-tuple-element.26.info_ref, f32[3,256,128]{2,1,0:T(8,128)S(1)} %bitcast.19, f32[3,256,128]{2,1,0:T(8,128)S(1)} %bitcast.24, ...), custom_call_target="tpu_custom_call" | custom-call | tf_op jit(solution)/shard_map/gather_images/pallas_call | solution.py:458
  18.1 1.6 %collective-permute-start.6 = (f32[3,16,16,128]{3,2,1,0:T(8,128)S(1)}, f32[3,16,16,128]{3,2,1,0:T(8,128)S(1)}, u32[]{:S(2)}, u32[]{:S(2)}) collective-permute-start(f32[3,16,16,128]{3,2,1,0:T(8,128)S(1)} %bitcast.26), channel_id=1, source_target_pairs={{0,1},{1,0},{2,3},{3,2},{4,5},{5,4},{6,7},{7,6},{8,9},{9,8},{10,11... | collective-permute-start | bytes 1179656 | tf_op jit(solution)/shard_map/ppermute | solution.py:390
  19.7 0.0 collective-permute-start.7
  19.7 1.6 %collective-permute-start.8 = (f32[3,2,8,128]{3,2,1,0:T(8,128)S(1)}, f32[3,2,8,128]{3,2,1,0:T(8,128)S(1)}, u32[]{:S(2)}, u32[]{:S(2)}) collective-permute-start(f32[3,2,8,128]{3,2,1,0:T(8,128)S(1)} %get-tuple-element.34), channel_id=1, source_target_pairs={{2,4},{6,0},{4,2},{0,6},{3,5},{7,1},{5,3},{1,7},{10,12},{14,8},{12... | collective-permute-start | bytes 73736 | tf_op jit(solution)/shard_map/ppermute | solution.py:396
  21.3 0.0 copy-done.3
  21.3 1.0 %parameters.1.par = f32[3,32,2,8,128]{4,3,2,1,0:T(8,128)S(1)} custom-call(f32[5,8,128]{2,1,0:T(8,128)S(1)} %get-tuple-element.26.info_ref, s32[256,128]{1,0:T(8,128)S(1)} %bitcast.22, s32[256,128]{1,0:T(8,128)S(1)} %bitcast.28), custom_call_target="tpu_custom_call" | custom-call | tf_op jit(solution)/shard_map/parameters/pallas_call | solution.py:475
  22.3 0.0 collective-permute-done.7.one_ref
  22.3 0.6 %collective-permute-done.8.two_ref = f32[3,2,8,128]{3,2,1,0:T(8,128)S(1)} collective-permute-done((f32[3,2,8,128]{3,2,1,0:T(8,128)S(1)}, f32[3,2,8,128]{3,2,1,0:T(8,128)S(1)}, u32[]{:S(2)}, u32[]{:S(2)}) %collective-permute-start.8) | collective-permute-done | bytes 24608 | tf_op jit(solution)/shard_map/ppermute | solution.py:396
  23.0 0.6 %collective-permute-start.9 = (f32[2,7,2,8,128]{4,3,2,1,0:T(8,128)S(1)}, f32[2,7,2,8,128]{4,3,2,1,0:T(8,128)S(1)}, u32[]{:S(2)}, u32[]{:S(2)}) collective-permute-start(f32[2,7,2,8,128]{4,3,2,1,0:T(8,128)S(1)} %merge_strips.1.strips_ref), channel_id=1, source_target_pairs={{0,1},{1,0},{2,3},{3,2},{4,5},{5,4},{6,7},{7,6},{8,9},{9,8},{10,11... | collective-permute-start | bytes 344072 | tf_op jit(solution)/shard_map/ppermute | solution.py:390
  23.6 10.9 %all_to_all.11 = f32[32,1,128]{2,1,0:T(1,128)S(1)} all-to-all(f32[32,1,128]{2,1,0:T(1,128)S(1)} %bitcast.30), channel_id=1, replica_groups=mesh['img'=4,'gx'=4,'gy'=2] {'img','gx','gy'}, dimensions={0} | all-to-all | bytes 32768 | tf_op jit(solution)/shard_map/all_to_all | solution.py:493
  34.5 0.0 collective-permute-done.9.stripsp_ref
  34.5 0.0 collective-permute-done.6
  34.5 11.6 %evolve.1 = f32[3,256,128]{2,1,0:T(8,128)} custom-call(f32[5,8,128]{2,1,0:T(8,128)S(1)} %get-tuple-element.26.info_ref, f32[32,128]{1,0:T(8,128)S(1)} %bitcast.29, f32[3,256,128]{2,1,0:T(8,128)S(1)} %bitcast.20, f32[3,256,128]{2,1,0:T(8,128)S(1)} %bitcast.25, f32[3,256,128]{2,1,0:T(8,128)S(1)} %get-tuple-element.29.n_ref, f32[3,256,128]{2,1,0:T(8,128)S(1)} %bitcast.27, ...), custom_call_target="tpu_custom_call" | custom-call | tf_op jit(solution)/shard_map/evolve/pallas_call | solution.py:495
  (1 shorter events, 0.0 us)
Async XLA Ops:
  0.0 17.3 %collective-permute-start = (f32[3,16,16,128]{3,2,1,0:T(8,128)}, f32[3,16,16,128]{3,2,1,0:T(8,128)S(1)}, u32[]{:S(2)}, u32[]{:S(2)}) collective-permute-start(f32[3,16,16,128]{3,2,1,0:T(8,128)} %bitcast.15), channel_id=1, source_target_pairs={{0,1},{1,0},{2,3},{3,2},{4,5},{5,4},{6,7},{7,6},{8,9},{9,8},{10,11... | collective-permute-start | bytes 1179656 | tf_op jit(solution)/shard_map/ppermute | solution.py:390
  2.9 14.4 %collective-permute-start.5 = (f32[3,16,16,128]{3,2,1,0:T(8,128)}, f32[3,16,16,128]{3,2,1,0:T(8,128)S(1)}, u32[]{:S(2)}, u32[]{:S(2)}) collective-permute-start(f32[3,16,16,128]{3,2,1,0:T(8,128)} %bitcast.16), channel_id=1, source_target_pairs={{8,16},{16,8},{9,17},{17,9},{10,18},{18,10},{11,19},{19,11},{12,20... | collective-permute-start | bytes 1179656 | tf_op jit(solution)/shard_map/ppermute | solution.py:396
  3.6 13.7 %collective-permute-start.4 = (f32[3,16,16,128]{3,2,1,0:T(8,128)}, f32[3,16,16,128]{3,2,1,0:T(8,128)S(1)}, u32[]{:S(2)}, u32[]{:S(2)}) collective-permute-start(f32[3,16,16,128]{3,2,1,0:T(8,128)} %bitcast.17), channel_id=1, source_target_pairs={{0,8},{16,24},{8,0},{24,16},{1,9},{17,25},{9,1},{25,17},{2,10},{18... | collective-permute-start | bytes 1179656 | tf_op jit(solution)/shard_map/ppermute | solution.py:396
  8.1 0.7 %copy-start.7 = (f32[3]{0:T(128)S(1)}, f32[3]{0:T(128)}, u32[]{:S(2)}) copy-start(f32[3]{0:T(128)} %param.8) | copy-start | bytes 40
  8.1 0.7 %copy-start.4 = (s32[4]{0:T(128)S(1)}, s32[4]{0:T(128)}, u32[]{:S(2)}) copy-start(s32[4]{0:T(128)} %lower_ref.1) | copy-start | bytes 52
  8.1 0.7 %copy-start.5 = (f32[8]{0:T(128)S(1)}, f32[8]{0:T(128)}, u32[]{:S(2)}) copy-start(f32[8]{0:T(128)} %aniso_ref.1) | copy-start | bytes 100
  8.1 0.7 %copy-start.6 = (f32[8]{0:T(128)S(1)}, f32[8]{0:T(128)}, u32[]{:S(2)}) copy-start(f32[8]{0:T(128)} %damp_ref.1) | copy-start | bytes 100
  8.8 1.0 %copy-start = (f32[1,3,16,16,128]{4,3,2,1,0:T(8,128)S(1)}, f32[1,3,16,16,128]{4,3,2,1,0:T(8,128)}, u32[]{:S(2)}) copy-start(f32[1,3,16,16,128]{4,3,2,1,0:T(8,128)} %param.6) | copy-start | bytes 1179652
  9.8 0.9 %copy-start.2 = (s32[16,16,128]{2,1,0:T(8,128)S(1)}, s32[16,16,128]{2,1,0:T(8,128)}, u32[]{:S(2)}) copy-start(s32[16,16,128]{2,1,0:T(8,128)} %param.9) | copy-start | bytes 393220
  10.7 6.7 %copy-start.1 = (f32[1,3,16,16,128]{4,3,2,1,0:T(8,128)S(1)}, f32[1,3,16,16,128]{4,3,2,1,0:T(8,128)}, u32[]{:S(2)}) copy-start(f32[1,3,16,16,128]{4,3,2,1,0:T(8,128)} %param.6) | copy-start | bytes 1179652
  12.2 5.2 %collective-permute-start.1 = (s32[16,16,128]{2,1,0:T(8,128)S(1)}, s32[16,16,128]{2,1,0:T(8,128)S(1)}, u32[]{:S(2)}, u32[]{:S(2)}) collective-permute-start(s32[16,16,128]{2,1,0:T(8,128)S(1)} %copy-done.2), channel_id=1, source_target_pairs={{0,1},{1,0},{2,3},{3,2},{4,5},{5,4},{6,7},{7,6},{8,9},{9,8},{10,11... | collective-permute-start | bytes 393224 | tf_op jit(solution)/shard_map/ppermute | solution.py:390
  12.8 1.2 %collective-permute-start.2 = (f32[4,2,8,128]{3,2,1,0:T(8,128)S(1)}, f32[4,2,8,128]{3,2,1,0:T(8,128)S(1)}, u32[]{:S(2)}, u32[]{:S(2)}) collective-permute-start(f32[4,2,8,128]{3,2,1,0:T(8,128)S(1)} %get-tuple-element.24), channel_id=1, source_target_pairs={{0,2},{4,6},{2,0},{6,4},{1,3},{5,7},{3,1},{7,5},{8,10},{12,14},{10... | collective-permute-start | bytes 98312 | tf_op jit(solution)/shard_map/ppermute | solution.py:396
  14.0 3.3 %collective-permute-start.3 = (f32[4,2,8,128]{3,2,1,0:T(8,128)S(1)}, f32[4,2,8,128]{3,2,1,0:T(8,128)S(1)}, u32[]{:S(2)}, u32[]{:S(2)}) collective-permute-start(f32[4,2,8,128]{3,2,1,0:T(8,128)S(1)} %get-tuple-element.25), channel_id=1, source_target_pairs={{2,4},{6,0},{4,2},{0,6},{3,5},{7,1},{5,3},{1,7},{10,12},{14,8},{12... | collective-permute-start | bytes 98312 | tf_op jit(solution)/shard_map/ppermute | solution.py:396
  17.4 3.9 %copy-start.3 = (s32[16,16,128]{2,1,0:T(8,128)S(1)}, s32[16,16,128]{2,1,0:T(8,128)}, u32[]{:S(2)}) copy-start(s32[16,16,128]{2,1,0:T(8,128)} %param.9) | copy-start | bytes 393220
  18.1 16.4 %collective-permute-start.6 = (f32[3,16,16,128]{3,2,1,0:T(8,128)S(1)}, f32[3,16,16,128]{3,2,1,0:T(8,128)S(1)}, u32[]{:S(2)}, u32[]{:S(2)}) collective-permute-start(f32[3,16,16,128]{3,2,1,0:T(8,128)S(1)} %bitcast.26), channel_id=1, source_target_pairs={{0,1},{1,0},{2,3},{3,2},{4,5},{5,4},{6,7},{7,6},{8,9},{9,8},{10,11... | collective-permute-start | bytes 1179656 | tf_op jit(solution)/shard_map/ppermute | solution.py:390
  19.7 2.7 %collective-permute-start.7 = (f32[3,2,8,128]{3,2,1,0:T(8,128)S(1)}, f32[3,2,8,128]{3,2,1,0:T(8,128)S(1)}, u32[]{:S(2)}, u32[]{:S(2)}) collective-permute-start(f32[3,2,8,128]{3,2,1,0:T(8,128)S(1)} %get-tuple-element.30), channel_id=1, source_target_pairs={{0,2},{4,6},{2,0},{6,4},{1,3},{5,7},{3,1},{7,5},{8,10},{12,14},{10... | collective-permute-start | bytes 73736 | tf_op jit(solution)/shard_map/ppermute | solution.py:396
  19.7 3.3 %collective-permute-start.8 = (f32[3,2,8,128]{3,2,1,0:T(8,128)S(1)}, f32[3,2,8,128]{3,2,1,0:T(8,128)S(1)}, u32[]{:S(2)}, u32[]{:S(2)}) collective-permute-start(f32[3,2,8,128]{3,2,1,0:T(8,128)S(1)} %get-tuple-element.34), channel_id=1, source_target_pairs={{2,4},{6,0},{4,2},{0,6},{3,5},{7,1},{5,3},{1,7},{10,12},{14,8},{12... | collective-permute-start | bytes 73736 | tf_op jit(solution)/shard_map/ppermute | solution.py:396
  23.0 11.5 %collective-permute-start.9 = (f32[2,7,2,8,128]{4,3,2,1,0:T(8,128)S(1)}, f32[2,7,2,8,128]{4,3,2,1,0:T(8,128)S(1)}, u32[]{:S(2)}, u32[]{:S(2)}) collective-permute-start(f32[2,7,2,8,128]{4,3,2,1,0:T(8,128)S(1)} %merge_strips.1.strips_ref), channel_id=1, source_target_pairs={{0,1},{1,0},{2,3},{3,2},{4,5},{5,4},{6,7},{7,6},{8,9},{9,8},{10,11... | collective-permute-start | bytes 344072 | tf_op jit(solution)/shard_map/ppermute | solution.py:390

commit v24 on v23

--- a/solution.py
+++ b/solution.py
@@ -375,13 +375,13 @@
     lax.fori_loop(0, STEPS, step, 0)
 
     def hand_out(i, carry):
-        for k in (2 * i, 2 * i + 1):
+        for k in [4 * i + u for u in range(4)]:
             for t in range(tiles):
                 for c in range(COMPS):
                     out_ref[c, rows_at(ny, tiles, k, t), :] = main0[c, k, t]
         return carry
 
-    lax.fori_loop(0, ny // 2, hand_out, 0)
+    lax.fori_loop(0, ny // 4, hand_out, 0)
 
 
 def shifted(cells, axis, step, closed):
@@ -449,8 +449,8 @@
         own.reshape(flat),
         regions.reshape(flat[1:]),
     )
+    own_two = swapped(own_two, "gx", 1, True)
     own_one = swapped(own_one, "gx", 0, True)
-    own_two = swapped(own_two, "gx", 1, True)
     late_regions, info = lax.optimization_barrier((regions, info))
     reg_p = around(late_regions, 1)
     info, own_p, reg_p, own_one, own_two = lax.optimization_barrier((info, own_p, reg_p, own_one, own_two))
@@ -469,7 +469,6 @@
         name="gather_images",
     )(info, own.reshape(flat), first.reshape(flat), second.reshape(flat))
     near_p = around(near.reshape(own.shape), 2)
-    one = swapped(one, "gx", 0, True)
     two = swapped(two, "gx", 1, True)
     window = ny + 2 * DEPTH
     par = pl.pallas_call(
@@ -481,6 +480,7 @@
         name="parameters",
     )(info, regions.reshape(flat[1:]), reg_p.reshape(flat[1:]))
     one, par = lax.optimization_barrier((one, par))
+    one = swapped(one, "gx", 0, True)
     strips = pl.pallas_call(
         merge_kernel,
         out_shape=jax.ShapeDtypeStruct((2, 2 * comps + 1, tiles) + vreg, f32),

time: 46.3 us -> 46.4 us (level)
  transfers between devices with their start and end apart: 10 -> 10, of which waited for: 3 -> 4; matrix products, arithmetic and copies ran while one was open for 0% -> 0% of each run, Pallas kernels for 6% -> 6%
where the time goes in v24:
time: 46.4 us; the launch traced here: 46.2 us
  Pallas kernels  14.9 us (32%)
  starting transfers between devices  13.8 us (30%)
  blocking collectives  10.7 us (23%)
  waiting for transfers between devices  4.13 us (9%)
  local copies, waits for them, and re-layouts  2.61 us (6%)
    pallas_call x1, Pallas kernels, body(): pl.pallas_call(functools.partial(evolve_kernel, ny, tiles, images), out_s...  11.6 us
    all_to_all x1, blocking collectives, body(): squares = lax.all_to_all(part, ('img', 'gx', 'gy'), 0, 0, tiled=True)  10.7 us
    ppermute x6, starting transfers between devices, swapped(): return lax.ppermute(cells, axis, pairs + [(j, i) for i, j in pairs])  8.1 us
    ppermute x4, starting transfers between devices, shifted(): return lax.ppermute(cells, axis, pairs)  5.69 us
    ppermute x6, waiting for transfers between devices, swapped(): return lax.ppermute(cells, axis, pairs + [(j, i) for i, j in pairs])  4.12 us
    unnamed x16, local copies, waits for them, and re-layouts  2.61 us
    pallas_call x1, Pallas kernels, body(): pl.pallas_call(functools.partial(pack_kernel, ny, tiles, anisotropy.shape...  1.51 us
    pallas_call x1, Pallas kernels, body(): pl.pallas_call(functools.partial(look_up_kernel, ny, tiles), out_shape=ja...  1.01 us
  transfers between devices with their start and end apart: 10, of which 4 were waited for; matrix products, arithmetic and copies ran while one was open for 0% of the time, Pallas kernels for 6%

profile of v24, /device:TPU:0, one launch (start us, length us, event | category | flops | bytes accessed | tf_op | source)
XLA Modules:
  0.0 46.2 jit_solution(2308139529368209145)
XLA Ops:
  0.0 2.9 %collective-permute-start = (f32[3,16,16,128]{3,2,1,0:T(8,128)}, f32[3,16,16,128]{3,2,1,0:T(8,128)S(1)}, u32[]{:S(2)}, u32[]{:S(2)}) collective-permute-start(f32[3,16,16,128]{3,2,1,0:T(8,128)} %bitcast.15), channel_id=1, source_target_pairs={{0,1},{1,0},{2,3},{3,2},{4,5},{5,4},{6,7},{7,6},{8,9},{9,8},{10,11... | collective-permute-start | bytes 1179656 | tf_op jit(solution)/shard_map/ppermute | solution.py:390
  2.9 0.7 %collective-permute-start.5 = (f32[3,16,16,128]{3,2,1,0:T(8,128)}, f32[3,16,16,128]{3,2,1,0:T(8,128)S(1)}, u32[]{:S(2)}, u32[]{:S(2)}) collective-permute-start(f32[3,16,16,128]{3,2,1,0:T(8,128)} %bitcast.16), channel_id=1, source_target_pairs={{8,16},{16,8},{9,17},{17,9},{10,18},{18,10},{11,19},{19,11},{12,20... | collective-permute-start | bytes 1179656 | tf_op jit(solution)/shard_map/ppermute | solution.py:396
  3.6 4.4 %collective-permute-start.4 = (f32[3,16,16,128]{3,2,1,0:T(8,128)}, f32[3,16,16,128]{3,2,1,0:T(8,128)S(1)}, u32[]{:S(2)}, u32[]{:S(2)}) collective-permute-start(f32[3,16,16,128]{3,2,1,0:T(8,128)} %bitcast.17), channel_id=1, source_target_pairs={{0,8},{16,24},{8,0},{24,16},{1,9},{17,25},{9,1},{25,17},{2,10},{18... | collective-permute-start | bytes 1179656 | tf_op jit(solution)/shard_map/ppermute | solution.py:396
  8.1 0.0 copy-start.7
  8.1 0.0 copy-start.4
  8.1 0.0 copy-start.5
  8.1 0.0 copy-start.6
  8.1 0.6 %copy-done.7 = f32[3]{0:T(128)S(1)} copy-done((f32[3]{0:T(128)S(1)}, f32[3]{0:T(128)}, u32[]{:S(2)}) %copy-start.7) | copy-done | bytes 36
  8.7 0.0 copy-done.4
  8.7 0.0 copy-done.5
  8.7 0.0 copy-done.6
  8.8 0.0 copy-start
  8.8 1.0 %copy-done = f32[1,3,16,16,128]{4,3,2,1,0:T(8,128)S(1)} copy-done((f32[1,3,16,16,128]{4,3,2,1,0:T(8,128)S(1)}, f32[1,3,16,16,128]{4,3,2,1,0:T(8,128)}, u32[]{:S(2)}) %copy-start) | copy-done | bytes 393240
  9.8 0.0 copy-start.2
  9.8 0.9 %copy-done.2 = s32[16,16,128]{2,1,0:T(8,128)S(1)} copy-done((s32[16,16,128]{2,1,0:T(8,128)S(1)}, s32[16,16,128]{2,1,0:T(8,128)}, u32[]{:S(2)}) %copy-start.2) | copy-done | bytes 131096
  10.7 0.0 copy-start.1
  10.7 1.5 %pack_strips.1 = (f32[4,2,8,128]{3,2,1,0:T(8,128)S(1)}, f32[4,2,8,128]{3,2,1,0:T(8,128)S(1)}, f32[5,8,128]{2,1,0:T(8,128)S(1)}) custom-call(s32[4]{0:T(128)S(1)} %copy-done.4, f32[8]{0:T(128)S(1)} %copy-done.5, f32[8]{0:T(128)S(1)} %copy-done.6, f32[1,3]{1,0:T(1,128)S(1)} %bitcast.31, f32[3,256,128]{2,1,0:T(8,128)S(1)} %bitcast.18, s32[256,128]{1,0:T(8,128)S(1)} %bitcast.21), custom_call_target="tpu_custom_call" | custom-call | tf_op jit(solution)/shard_map/pack_strips/pallas_call | solution.py:437
  12.2 0.6 %collective-permute-start.1 = (s32[16,16,128]{2,1,0:T(8,128)S(1)}, s32[16,16,128]{2,1,0:T(8,128)S(1)}, u32[]{:S(2)}, u32[]{:S(2)}) collective-permute-start(s32[16,16,128]{2,1,0:T(8,128)S(1)} %copy-done.2), channel_id=1, source_target_pairs={{0,1},{1,0},{2,3},{3,2},{4,5},{5,4},{6,7},{7,6},{8,9},{9,8},{10,11... | collective-permute-start | bytes 393224 | tf_op jit(solution)/shard_map/ppermute | solution.py:390
  12.8 0.0 collective-permute-start.2
  12.8 1.2 %collective-permute-done.2.own_one_ref = f32[4,2,8,128]{3,2,1,0:T(8,128)S(1)} collective-permute-done((f32[4,2,8,128]{3,2,1,0:T(8,128)S(1)}, f32[4,2,8,128]{3,2,1,0:T(8,128)S(1)}, u32[]{:S(2)}, u32[]{:S(2)}) %collective-permute-start.2) | collective-permute-done | bytes 32800 | tf_op jit(solution)/shard_map/ppermute | solution.py:396
  14.0 1.3 %collective-permute-start.3 = (f32[4,2,8,128]{3,2,1,0:T(8,128)S(1)}, f32[4,2,8,128]{3,2,1,0:T(8,128)S(1)}, u32[]{:S(2)}, u32[]{:S(2)}) collective-permute-start(f32[4,2,8,128]{3,2,1,0:T(8,128)S(1)} %get-tuple-element.25), channel_id=1, source_target_pairs={{2,4},{6,0},{4,2},{0,6},{3,5},{7,1},{5,3},{1,7},{10,12},{14,8},{12... | collective-permute-start | bytes 98312 | tf_op jit(solution)/shard_map/ppermute | solution.py:396
  15.3 2.1 %collective-permute-done.3.own_two_ref = f32[4,2,8,128]{3,2,1,0:T(8,128)S(1)} collective-permute-done((f32[4,2,8,128]{3,2,1,0:T(8,128)S(1)}, f32[4,2,8,128]{3,2,1,0:T(8,128)S(1)}, u32[]{:S(2)}, u32[]{:S(2)}) %collective-permute-start.3) | collective-permute-done | bytes 32800 | tf_op jit(solution)/shard_map/ppermute | solution.py:396
  17.3 0.0 collective-permute-done.1
  17.3 0.0 collective-permute-done
  17.3 0.0 collective-permute-done.5
  17.4 0.0 collective-permute-done.4
  17.4 0.0 copy-done.1
  17.4 0.0 copy-start.3
  17.4 0.7 %gather_images.1 = (f32[32,128]{1,0:T(8,128)S(1)}, f32[3,256,128]{2,1,0:T(8,128)S(1)}, f32[3,2,8,128]{3,2,1,0:T(8,128)S(1)}, f32[3,2,8,128]{3,2,1,0:T(8,128)S(1)}) custom-call(f32[5,8,128]{2,1,0:T(8,128)S(1)} %get-tuple-element.26.info_ref, f32[3,256,128]{2,1,0:T(8,128)S(1)} %bitcast.19, f32[3,256,128]{2,1,0:T(8,128)S(1)} %bitcast.24, ...), custom_call_target="tpu_custom_call" | custom-call | tf_op jit(solution)/shard_map/gather_images/pallas_call | solution.py:458
  18.1 1.6 %collective-permute-start.6 = (f32[3,16,16,128]{3,2,1,0:T(8,128)S(1)}, f32[3,16,16,128]{3,2,1,0:T(8,128)S(1)}, u32[]{:S(2)}, u32[]{:S(2)}) collective-permute-start(f32[3,16,16,128]{3,2,1,0:T(8,128)S(1)} %bitcast.26), channel_id=1, source_target_pairs={{0,1},{1,0},{2,3},{3,2},{4,5},{5,4},{6,7},{7,6},{8,9},{9,8},{10,11... | collective-permute-start | bytes 1179656 | tf_op jit(solution)/shard_map/ppermute | solution.py:390
  19.7 1.0 %collective-permute-start.8 = (f32[3,2,8,128]{3,2,1,0:T(8,128)S(1)}, f32[3,2,8,128]{3,2,1,0:T(8,128)S(1)}, u32[]{:S(2)}, u32[]{:S(2)}) collective-permute-start(f32[3,2,8,128]{3,2,1,0:T(8,128)S(1)} %get-tuple-element.34), channel_id=1, source_target_pairs={{2,4},{6,0},{4,2},{0,6},{3,5},{7,1},{5,3},{1,7},{10,12},{14,8},{12... | collective-permute-start | bytes 73736 | tf_op jit(solution)/shard_map/ppermute | solution.py:396
  20.7 0.0 copy-done.3
  20.7 1.0 %parameters.1.par = f32[3,32,2,8,128]{4,3,2,1,0:T(8,128)S(1)} custom-call(f32[5,8,128]{2,1,0:T(8,128)S(1)} %get-tuple-element.26.info_ref, s32[256,128]{1,0:T(8,128)S(1)} %bitcast.22, s32[256,128]{1,0:T(8,128)S(1)} %bitcast.28), custom_call_target="tpu_custom_call" | custom-call | tf_op jit(solution)/shard_map/parameters/pallas_call | solution.py:474
  21.7 0.7 %collective-permute-start.7 = (f32[3,2,8,128]{3,2,1,0:T(8,128)S(1)}, f32[3,2,8,128]{3,2,1,0:T(8,128)S(1)}, u32[]{:S(2)}, u32[]{:S(2)}) collective-permute-start(f32[3,2,8,128]{3,2,1,0:T(8,128)S(1)} %get-tuple-element.33), channel_id=1, source_target_pairs={{0,2},{4,6},{2,0},{6,4},{1,3},{5,7},{3,1},{7,5},{8,10},{12,14},{10... | collective-permute-start | bytes 73736 | tf_op jit(solution)/shard_map/ppermute | solution.py:396
  22.4 0.7 %collective-permute-done.8.two_ref = f32[3,2,8,128]{3,2,1,0:T(8,128)S(1)} collective-permute-done((f32[3,2,8,128]{3,2,1,0:T(8,128)S(1)}, f32[3,2,8,128]{3,2,1,0:T(8,128)S(1)}, u32[]{:S(2)}, u32[]{:S(2)}) %collective-permute-start.8) | collective-permute-done | bytes 24608 | tf_op jit(solution)/shard_map/ppermute | solution.py:396
  23.1 0.1 collective-permute-done.7.one_ref
  23.3 0.6 %collective-permute-start.9 = (f32[2,7,2,8,128]{4,3,2,1,0:T(8,128)S(1)}, f32[2,7,2,8,128]{4,3,2,1,0:T(8,128)S(1)}, u32[]{:S(2)}, u32[]{:S(2)}) collective-permute-start(f32[2,7,2,8,128]{4,3,2,1,0:T(8,128)S(1)} %merge_strips.1.strips_ref), channel_id=1, source_target_pairs={{0,1},{1,0},{2,3},{3,2},{4,5},{5,4},{6,7},{7,6},{8,9},{9,8},{10,11... | collective-permute-start | bytes 344072 | tf_op jit(solution)/shard_map/ppermute | solution.py:390
  23.9 10.7 %all_to_all.11 = f32[32,1,128]{2,1,0:T(1,128)S(1)} all-to-all(f32[32,1,128]{2,1,0:T(1,128)S(1)} %bitcast.30), channel_id=1, replica_groups=mesh['img'=4,'gx'=4,'gy'=2] {'img','gx','gy'}, dimensions={0} | all-to-all | bytes 32768 | tf_op jit(solution)/shard_map/all_to_all | solution.py:493
  34.6 0.0 collective-permute-done.9.stripsp_ref
  34.6 0.0 collective-permute-done.6
  34.6 11.6 %evolve.1 = f32[3,256,128]{2,1,0:T(8,128)} custom-call(f32[5,8,128]{2,1,0:T(8,128)S(1)} %get-tuple-element.26.info_ref, f32[32,128]{1,0:T(8,128)S(1)} %bitcast.29, f32[3,256,128]{2,1,0:T(8,128)S(1)} %bitcast.20, f32[3,256,128]{2,1,0:T(8,128)S(1)} %bitcast.25, f32[3,256,128]{2,1,0:T(8,128)S(1)} %get-tuple-element.29.n_ref, f32[3,256,128]{2,1,0:T(8,128)S(1)} %bitcast.27, ...), custom_call_target="tpu_custom_call" | custom-call | tf_op jit(solution)/shard_map/evolve/pallas_call | solution.py:495
  (1 shorter events, 0.0 us)
Async XLA Ops:
  0.0 17.3 %collective-permute-start = (f32[3,16,16,128]{3,2,1,0:T(8,128)}, f32[3,16,16,128]{3,2,1,0:T(8,128)S(1)}, u32[]{:S(2)}, u32[]{:S(2)}) collective-permute-start(f32[3,16,16,128]{3,2,1,0:T(8,128)} %bitcast.15), channel_id=1, source_target_pairs={{0,1},{1,0},{2,3},{3,2},{4,5},{5,4},{6,7},{7,6},{8,9},{9,8},{10,11... | collective-permute-start | bytes 1179656 | tf_op jit(solution)/shard_map/ppermute | solution.py:390
  2.9 14.4 %collective-permute-start.5 = (f32[3,16,16,128]{3,2,1,0:T(8,128)}, f32[3,16,16,128]{3,2,1,0:T(8,128)S(1)}, u32[]{:S(2)}, u32[]{:S(2)}) collective-permute-start(f32[3,16,16,128]{3,2,1,0:T(8,128)} %bitcast.16), channel_id=1, source_target_pairs={{8,16},{16,8},{9,17},{17,9},{10,18},{18,10},{11,19},{19,11},{12,20... | collective-permute-start | bytes 1179656 | tf_op jit(solution)/shard_map/ppermute | solution.py:396
  3.6 13.7 %collective-permute-start.4 = (f32[3,16,16,128]{3,2,1,0:T(8,128)}, f32[3,16,16,128]{3,2,1,0:T(8,128)S(1)}, u32[]{:S(2)}, u32[]{:S(2)}) collective-permute-start(f32[3,16,16,128]{3,2,1,0:T(8,128)} %bitcast.17), channel_id=1, source_target_pairs={{0,8},{16,24},{8,0},{24,16},{1,9},{17,25},{9,1},{25,17},{2,10},{18... | collective-permute-start | bytes 1179656 | tf_op jit(solution)/shard_map/ppermute | solution.py:396
  8.1 0.7 %copy-start.7 = (f32[3]{0:T(128)S(1)}, f32[3]{0:T(128)}, u32[]{:S(2)}) copy-start(f32[3]{0:T(128)} %param.8) | copy-start | bytes 40
  8.1 0.7 %copy-start.4 = (s32[4]{0:T(128)S(1)}, s32[4]{0:T(128)}, u32[]{:S(2)}) copy-start(s32[4]{0:T(128)} %lower_ref.1) | copy-start | bytes 52
  8.1 0.7 %copy-start.5 = (f32[8]{0:T(128)S(1)}, f32[8]{0:T(128)}, u32[]{:S(2)}) copy-start(f32[8]{0:T(128)} %aniso_ref.1) | copy-start | bytes 100
  8.1 0.7 %copy-start.6 = (f32[8]{0:T(128)S(1)}, f32[8]{0:T(128)}, u32[]{:S(2)}) copy-start(f32[8]{0:T(128)} %damp_ref.1) | copy-start | bytes 100
  8.8 1.0 %copy-start = (f32[1,3,16,16,128]{4,3,2,1,0:T(8,128)S(1)}, f32[1,3,16,16,128]{4,3,2,1,0:T(8,128)}, u32[]{:S(2)}) copy-start(f32[1,3,16,16,128]{4,3,2,1,0:T(8,128)} %param.6) | copy-start | bytes 1179652
  9.8 0.9 %copy-start.2 = (s32[16,16,128]{2,1,0:T(8,128)S(1)}, s32[16,16,128]{2,1,0:T(8,128)}, u32[]{:S(2)}) copy-start(s32[16,16,128]{2,1,0:T(8,128)} %param.9) | copy-start | bytes 393220
  10.7 6.7 %copy-start.1 = (f32[1,3,16,16,128]{4,3,2,1,0:T(8,128)S(1)}, f32[1,3,16,16,128]{4,3,2,1,0:T(8,128)}, u32[]{:S(2)}) copy-start(f32[1,3,16,16,128]{4,3,2,1,0:T(8,128)} %param.6) | copy-start | bytes 1179652
  12.2 5.2 %collective-permute-start.1 = (s32[16,16,128]{2,1,0:T(8,128)S(1)}, s32[16,16,128]{2,1,0:T(8,128)S(1)}, u32[]{:S(2)}, u32[]{:S(2)}) collective-permute-start(s32[16,16,128]{2,1,0:T(8,128)S(1)} %copy-done.2), channel_id=1, source_target_pairs={{0,1},{1,0},{2,3},{3,2},{4,5},{5,4},{6,7},{7,6},{8,9},{9,8},{10,11... | collective-permute-start | bytes 393224 | tf_op jit(solution)/shard_map/ppermute | solution.py:390
  12.8 1.2 %collective-permute-start.2 = (f32[4,2,8,128]{3,2,1,0:T(8,128)S(1)}, f32[4,2,8,128]{3,2,1,0:T(8,128)S(1)}, u32[]{:S(2)}, u32[]{:S(2)}) collective-permute-start(f32[4,2,8,128]{3,2,1,0:T(8,128)S(1)} %get-tuple-element.24), channel_id=1, source_target_pairs={{0,2},{4,6},{2,0},{6,4},{1,3},{5,7},{3,1},{7,5},{8,10},{12,14},{10... | collective-permute-start | bytes 98312 | tf_op jit(solution)/shard_map/ppermute | solution.py:396
  14.0 3.3 %collective-permute-start.3 = (f32[4,2,8,128]{3,2,1,0:T(8,128)S(1)}, f32[4,2,8,128]{3,2,1,0:T(8,128)S(1)}, u32[]{:S(2)}, u32[]{:S(2)}) collective-permute-start(f32[4,2,8,128]{3,2,1,0:T(8,128)S(1)} %get-tuple-element.25), channel_id=1, source_target_pairs={{2,4},{6,0},{4,2},{0,6},{3,5},{7,1},{5,3},{1,7},{10,12},{14,8},{12... | collective-permute-start | bytes 98312 | tf_op jit(solution)/shard_map/ppermute | solution.py:396
  17.4 3.3 %copy-start.3 = (s32[16,16,128]{2,1,0:T(8,128)S(1)}, s32[16,16,128]{2,1,0:T(8,128)}, u32[]{:S(2)}) copy-start(s32[16,16,128]{2,1,0:T(8,128)} %param.9) | copy-start | bytes 393220
  18.1 16.5 %collective-permute-start.6 = (f32[3,16,16,128]{3,2,1,0:T(8,128)S(1)}, f32[3,16,16,128]{3,2,1,0:T(8,128)S(1)}, u32[]{:S(2)}, u32[]{:S(2)}) collective-permute-start(f32[3,16,16,128]{3,2,1,0:T(8,128)S(1)} %bitcast.26), channel_id=1, source_target_pairs={{0,1},{1,0},{2,3},{3,2},{4,5},{5,4},{6,7},{7,6},{8,9},{9,8},{10,11... | collective-permute-start | bytes 1179656 | tf_op jit(solution)/shard_map/ppermute | solution.py:390
  19.7 3.4 %collective-permute-start.8 = (f32[3,2,8,128]{3,2,1,0:T(8,128)S(1)}, f32[3,2,8,128]{3,2,1,0:T(8,128)S(1)}, u32[]{:S(2)}, u32[]{:S(2)}) collective-permute-start(f32[3,2,8,128]{3,2,1,0:T(8,128)S(1)} %get-tuple-element.34), channel_id=1, source_target_pairs={{2,4},{6,0},{4,2},{0,6},{3,5},{7,1},{5,3},{1,7},{10,12},{14,8},{12... | collective-permute-start | bytes 73736 | tf_op jit(solution)/shard_map/ppermute | solution.py:396
  21.7 1.5 %collective-permute-start.7 = (f32[3,2,8,128]{3,2,1,0:T(8,128)S(1)}, f32[3,2,8,128]{3,2,1,0:T(8,128)S(1)}, u32[]{:S(2)}, u32[]{:S(2)}) collective-permute-start(f32[3,2,8,128]{3,2,1,0:T(8,128)S(1)} %get-tuple-element.33), channel_id=1, source_target_pairs={{0,2},{4,6},{2,0},{6,4},{1,3},{5,7},{3,1},{7,5},{8,10},{12,14},{10... | collective-permute-start | bytes 73736 | tf_op jit(solution)/shard_map/ppermute | solution.py:396
  23.3 11.3 %collective-permute-start.9 = (f32[2,7,2,8,128]{4,3,2,1,0:T(8,128)S(1)}, f32[2,7,2,8,128]{4,3,2,1,0:T(8,128)S(1)}, u32[]{:S(2)}, u32[]{:S(2)}) collective-permute-start(f32[2,7,2,8,128]{4,3,2,1,0:T(8,128)S(1)} %merge_strips.1.strips_ref), channel_id=1, source_target_pairs={{0,1},{1,0},{2,3},{3,2},{4,5},{5,4},{6,7},{7,6},{8,9},{9,8},{10,11... | collective-permute-start | bytes 344072 | tf_op jit(solution)/shard_map/ppermute | solution.py:390

commit v25 on v21

--- a/solution.py
+++ b/solution.py
@@ -16,7 +16,7 @@
 SUB = 8
 LANES = 128
 COMPS = 3
-ROWS = 4
+ROWS = 10
 
 
 def lane_iota():
@@ -45,8 +45,8 @@
 def pack_rows(ny, tiles, one_ref, two_ref, comps, cells_at):
     def pack(i, carry):
         done = []
-        for u in range(2):
-            y = 2 * i + u
+        for u in range(4):
+            y = 4 * i + u
             one, two, shift = rims(ny, y)
             for t in range(tiles):
                 for c in range(comps):
@@ -57,7 +57,7 @@
             pltpu.store(two_ref.at[c, t], cells, mask=two)
         return carry
 
-    lax.fori_loop(0, ny // 2, pack, 0)
+    lax.fori_loop(0, ny // 4, pack, 0)
 
 
 def pack_kernel(ny, tiles, m_ref, one_ref, two_ref):
@@ -107,7 +107,7 @@
 ):
     here = lax.axis_index("img")
     pick, odd = take_first(info_ref, here)
-    chunks = 4
+    chunks = 8
     depth = m_ref.shape[1]
 
     def squares(i, sums):
@@ -120,13 +120,13 @@
                 two = second_ref[c, pl.ds(start, SUB), :]
                 done.append((c, start, jnp.where(pick, one, two)))
                 diff = m_ref[c, pl.ds(start, SUB), :] - jnp.where(odd, one, two)
-                sums[c + COMPS * u] = sums[c + COMPS * u] + diff * diff
+                sums[c + COMPS * (u % 4)] = sums[c + COMPS * (u % 4)] + diff * diff
         for c, start, cells in done:
             near_ref[c, pl.ds(start, SUB), :] = cells
         return tuple(sums)
 
     zero = jnp.zeros((SUB, LANES), jnp.float32)
-    sums = lax.fori_loop(0, depth // (chunks * SUB), squares, (zero,) * (chunks * COMPS))
+    sums = lax.fori_loop(0, depth // (chunks * SUB), squares, (zero,) * (4 * COMPS))
     total = jnp.sum(functools.reduce(jnp.add, sums), axis=(0, 1), keepdims=True)
     slot = lax.broadcasted_iota(jnp.int32, part_ref.shape, 1)
     part_ref[...] = jnp.where((slot == here) & (here > 0), total, 0.0)
@@ -227,7 +227,7 @@
 
     def fill(i, carry):
         done = []
-        for k in (2 * i, 2 * i + 1):
+        for k in [4 * i + u for u in range(4)]:
             for g, (own, near) in enumerate(((m_ref, n_ref), (mp_ref, np_ref))):
                 for t in range(tiles):
                     rows = rows_at(ny, tiles, k, t)
@@ -240,7 +240,7 @@
                 main0[c, r, t] = v[c]
         return carry
 
-    lax.fori_loop(0, ny // 2, fill, 0)
+    lax.fori_loop(0, ny // 4, fill, 0)
 
     def seam_of(left, right):
         return jnp.where(head_lane, pltpu.roll(left, 1, 1), pltpu.roll(right, LANES - 1, 1))
@@ -358,11 +358,11 @@
                     pltpu.store(edge.at[c, r // ny, t], ends[c], mask=mask)
             return carry
 
-        lax.fori_loop(0, count // ROWS, rows, 0)
+        lax.fori_loop(0, (count + ROWS - 1) // ROWS, rows, 0)
 
     def step(i, carry):
         for state in range(2):
-            margin = DEPTH - 2 * state - 2 * i
+            margin = DEPTH - 1 - state - 2 * i
             main_rows(state, -margin, ny + 2 * margin)
             strip_rows(state)
         return carry

time: 48.2 us -> 46.4 us (0.963)
  Pallas kernels: 17.2 us -> 14.8 us
    pallas_call x1, Pallas kernels: 13.1 us -> 11.6 us  [body(): pl.pallas_call(functools.partial(evolve_kernel, ny, tiles, images), out_s...]
  transfers between devices with their start and end apart: 10 -> 10, of which waited for: 3 -> 4; matrix products, arithmetic and copies ran while one was open for 0% -> 0% of each run, Pallas kernels for 6% -> 5%
where the time goes in v25:
time: 46.4 us; the launch traced here: 46.2 us
  Pallas kernels  14.8 us (32%)
  starting transfers between devices  13.5 us (29%)
  blocking collectives  11.5 us (25%)
  waiting for transfers between devices  3.76 us (8%)
  local copies, waits for them, and re-layouts  2.62 us (6%)
    pallas_call x1, Pallas kernels, body(): pl.pallas_call(functools.partial(evolve_kernel, ny, tiles, images), out_s...  11.6 us
    all_to_all x1, blocking collectives, body(): squares = lax.all_to_all(part, ('img', 'gx', 'gy'), 0, 0, tiled=True)  11.5 us
    ppermute x6, starting transfers between devices, swapped(): return lax.ppermute(cells, axis, pairs + [(j, i) for i, j in pairs])  7.83 us
    ppermute x4, starting transfers between devices, shifted(): return lax.ppermute(cells, axis, pairs)  5.63 us
    unnamed x16, local copies, waits for them, and re-layouts  2.62 us
    ppermute x6, waiting for transfers between devices, swapped(): return lax.ppermute(cells, axis, pairs + [(j, i) for i, j in pairs])  2.07 us
    ppermute x4, waiting for transfers between devices, shifted(): return lax.ppermute(cells, axis, pairs)  1.69 us
    pallas_call x1, Pallas kernels, body(): pl.pallas_call(functools.partial(look_up_kernel, ny, tiles), out_shape=ja...  0.98 us
  transfers between devices with their start and end apart: 10, of which 4 were waited for; matrix products, arithmetic and copies ran while one was open for 0% of the time, Pallas kernels for 5%

profile of v25, /device:TPU:0, one launch (start us, length us, event | category | flops | bytes accessed | tf_op | source)
XLA Modules:
  0.0 46.2 jit_solution(1100149599022901302)
XLA Ops:
  0.0 2.9 %collective-permute-start = (f32[3,16,16,128]{3,2,1,0:T(8,128)}, f32[3,16,16,128]{3,2,1,0:T(8,128)S(1)}, u32[]{:S(2)}, u32[]{:S(2)}) collective-permute-start(f32[3,16,16,128]{3,2,1,0:T(8,128)} %bitcast.15), channel_id=1, source_target_pairs={{0,1},{1,0},{2,3},{3,2},{4,5},{5,4},{6,7},{7,6},{8,9},{9,8},{10,11... | collective-permute-start | bytes 1179656 | tf_op jit(solution)/shard_map/ppermute | solution.py:385
  2.9 0.7 %collective-permute-start.5 = (f32[3,16,16,128]{3,2,1,0:T(8,128)}, f32[3,16,16,128]{3,2,1,0:T(8,128)S(1)}, u32[]{:S(2)}, u32[]{:S(2)}) collective-permute-start(f32[3,16,16,128]{3,2,1,0:T(8,128)} %bitcast.16), channel_id=1, source_target_pairs={{8,16},{16,8},{9,17},{17,9},{10,18},{18,10},{11,19},{19,11},{12,20... | collective-permute-start | bytes 1179656 | tf_op jit(solution)/shard_map/ppermute | solution.py:391
  3.6 4.4 %collective-permute-start.4 = (f32[3,16,16,128]{3,2,1,0:T(8,128)}, f32[3,16,16,128]{3,2,1,0:T(8,128)S(1)}, u32[]{:S(2)}, u32[]{:S(2)}) collective-permute-start(f32[3,16,16,128]{3,2,1,0:T(8,128)} %bitcast.17), channel_id=1, source_target_pairs={{0,8},{16,24},{8,0},{24,16},{1,9},{17,25},{9,1},{25,17},{2,10},{18... | collective-permute-start | bytes 1179656 | tf_op jit(solution)/shard_map/ppermute | solution.py:391
  8.1 0.0 copy-start
  8.1 1.0 %copy-done = f32[1,3,16,16,128]{4,3,2,1,0:T(8,128)S(1)} copy-done((f32[1,3,16,16,128]{4,3,2,1,0:T(8,128)S(1)}, f32[1,3,16,16,128]{4,3,2,1,0:T(8,128)}, u32[]{:S(2)}) %copy-start) | copy-done | bytes 393240
  9.1 0.0 copy-start.1
  9.1 0.5 %pack_strips.1 = (f32[3,2,8,128]{3,2,1,0:T(8,128)S(1)}, f32[3,2,8,128]{3,2,1,0:T(8,128)S(1)}) custom-call(f32[3,256,128]{2,1,0:T(8,128)S(1)} %bitcast.18), custom_call_target="tpu_custom_call" | custom-call | tf_op jit(solution)/shard_map/pack_strips/pallas_call | solution.py:432
  9.6 0.0 copy-start.7
  9.6 0.1 collective-permute-start.1
  9.7 1.2 %collective-permute-done.1.own_one_ref = f32[3,2,8,128]{3,2,1,0:T(8,128)S(1)} collective-permute-done((f32[3,2,8,128]{3,2,1,0:T(8,128)S(1)}, f32[3,2,8,128]{3,2,1,0:T(8,128)S(1)}, u32[]{:S(2)}, u32[]{:S(2)}) %collective-permute-start.1) | collective-permute-done | bytes 24608 | tf_op jit(solution)/shard_map/ppermute | solution.py:391
  10.9 0.5 %collective-permute-start.2 = (s32[16,16,128]{2,1,0:T(8,128)}, s32[16,16,128]{2,1,0:T(8,128)S(1)}, u32[]{:S(2)}, u32[]{:S(2)}) collective-permute-start(s32[16,16,128]{2,1,0:T(8,128)} %param.9), channel_id=1, source_target_pairs={{0,1},{1,0},{2,3},{3,2},{4,5},{5,4},{6,7},{7,6},{8,9},{9,8},{10,11... | collective-permute-start | bytes 393224 | tf_op jit(solution)/shard_map/ppermute | solution.py:385
  11.4 1.0 %collective-permute-start.3 = (f32[3,2,8,128]{3,2,1,0:T(8,128)S(1)}, f32[3,2,8,128]{3,2,1,0:T(8,128)S(1)}, u32[]{:S(2)}, u32[]{:S(2)}) collective-permute-start(f32[3,2,8,128]{3,2,1,0:T(8,128)S(1)} %get-tuple-element.27), channel_id=1, source_target_pairs={{2,4},{6,0},{4,2},{0,6},{3,5},{7,1},{5,3},{1,7},{10,12},{14,8},{12... | collective-permute-start | bytes 73736 | tf_op jit(solution)/shard_map/ppermute | solution.py:391
  12.4 0.0 copy-start.4
  12.4 0.0 copy-start.5
  12.4 0.0 copy-start.6
  12.4 0.0 copy-done.7
  12.4 0.6 %copy-done.4 = s32[4]{0:T(128)S(1)} copy-done((s32[4]{0:T(128)S(1)}, s32[4]{0:T(128)}, u32[]{:S(2)}) %copy-start.4) | copy-done | bytes 40
  13.1 0.0 copy-done.5
  13.1 0.0 copy-done.6
  13.1 0.0 copy-start.2
  13.1 0.9 %copy-done.2 = s32[16,16,128]{2,1,0:T(8,128)S(1)} copy-done((s32[16,16,128]{2,1,0:T(8,128)S(1)}, s32[16,16,128]{2,1,0:T(8,128)}, u32[]{:S(2)}) %copy-start.2) | copy-done | bytes 131096
  14.0 1.0 %small_arguments.1 = (f32[1,2,8,128]{3,2,1,0:T(8,128)S(1)}, f32[1,2,8,128]{3,2,1,0:T(8,128)S(1)}, f32[5,8,128]{2,1,0:T(8,128)S(1)}) custom-call(s32[4]{0:T(128)S(1)} %copy-done.4, f32[8]{0:T(128)S(1)} %copy-done.5, f32[8]{0:T(128)S(1)} %copy-done.6, f32[1,3]{1,0:T(1,128)S(1)} %bitcast.31, s32[256,128]{1,0:T(8,128)S(1)} %bitcast.21), custom_call_target="tpu_custom_call" | custom-call | tf_op jit(solution)/shard_map/small_arguments/pallas_call | solution.py:442
  15.0 0.0 collective-permute-done.3.own_two_ref
  15.0 1.7 %collective-permute-done.2 = s32[16,16,128]{2,1,0:T(8,128)S(1)} collective-permute-done((s32[16,16,128]{2,1,0:T(8,128)}, s32[16,16,128]{2,1,0:T(8,128)S(1)}, u32[]{:S(2)}, u32[]{:S(2)}) %collective-permute-start.2) | collective-permute-done | bytes 131104 | tf_op jit(solution)/shard_map/ppermute | solution.py:385
  16.6 0.0 collective-permute-done
  16.6 0.0 collective-permute-done.5
  16.6 0.2 collective-permute-done.4
  16.8 0.0 copy-done.1
  16.8 0.0 copy-start.3
  16.8 0.7 %gather_images.1 = (f32[32,128]{1,0:T(8,128)S(1)}, f32[3,256,128]{2,1,0:T(8,128)S(1)}, f32[4,2,8,128]{3,2,1,0:T(8,128)S(1)}, f32[4,2,8,128]{3,2,1,0:T(8,128)S(1)}) custom-call(f32[5,8,128]{2,1,0:T(8,128)S(1)} %get-tuple-element.28.info_ref, f32[3,256,128]{2,1,0:T(8,128)S(1)} %bitcast.19, f32[3,256,128]{2,1,0:T(8,128)S(1)} %bitcast.24, ...), custom_call_target="tpu_custom_call" | custom-call | tf_op jit(solution)/shard_map/gather_images/pallas_call | solution.py:453
  17.6 0.6 %collective-permute-start.6 = (f32[3,16,16,128]{3,2,1,0:T(8,128)S(1)}, f32[3,16,16,128]{3,2,1,0:T(8,128)S(1)}, u32[]{:S(2)}, u32[]{:S(2)}) collective-permute-start(f32[3,16,16,128]{3,2,1,0:T(8,128)S(1)} %bitcast.26), channel_id=1, source_target_pairs={{0,1},{1,0},{2,3},{3,2},{4,5},{5,4},{6,7},{7,6},{8,9},{9,8},{10,11... | collective-permute-start | bytes 1179656 | tf_op jit(solution)/shard_map/ppermute | solution.py:385
  18.2 0.0 collective-permute-start.7
  18.2 1.6 %collective-permute-start.8 = (f32[4,2,8,128]{3,2,1,0:T(8,128)S(1)}, f32[4,2,8,128]{3,2,1,0:T(8,128)S(1)}, u32[]{:S(2)}, u32[]{:S(2)}) collective-permute-start(f32[4,2,8,128]{3,2,1,0:T(8,128)S(1)} %get-tuple-element.38), channel_id=1, source_target_pairs={{2,4},{6,0},{4,2},{0,6},{3,5},{7,1},{5,3},{1,7},{10,12},{14,8},{12... | collective-permute-start | bytes 98312 | tf_op jit(solution)/shard_map/ppermute | solution.py:391
  19.8 0.0 copy-done.3
  19.8 1.0 %parameters.1.par = f32[3,32,2,8,128]{4,3,2,1,0:T(8,128)S(1)} custom-call(f32[5,8,128]{2,1,0:T(8,128)S(1)} %get-tuple-element.28.info_ref, s32[256,128]{1,0:T(8,128)S(1)} %bitcast.22, s32[256,128]{1,0:T(8,128)S(1)} %bitcast.28), custom_call_target="tpu_custom_call" | custom-call | tf_op jit(solution)/shard_map/parameters/pallas_call | solution.py:470
  20.8 0.0 collective-permute-done.7.one_ref
  20.8 0.7 %collective-permute-done.8.two_ref = f32[4,2,8,128]{3,2,1,0:T(8,128)S(1)} collective-permute-done((f32[4,2,8,128]{3,2,1,0:T(8,128)S(1)}, f32[4,2,8,128]{3,2,1,0:T(8,128)S(1)}, u32[]{:S(2)}, u32[]{:S(2)}) %collective-permute-start.8) | collective-permute-done | bytes 32800 | tf_op jit(solution)/shard_map/ppermute | solution.py:391
  21.5 1.6 %collective-permute-start.9 = (f32[2,7,2,8,128]{4,3,2,1,0:T(8,128)S(1)}, f32[2,7,2,8,128]{4,3,2,1,0:T(8,128)S(1)}, u32[]{:S(2)}, u32[]{:S(2)}) collective-permute-start(f32[2,7,2,8,128]{4,3,2,1,0:T(8,128)S(1)} %merge_strips.1.strips_ref), channel_id=1, source_target_pairs={{0,1},{1,0},{2,3},{3,2},{4,5},{5,4},{6,7},{7,6},{8,9},{9,8},{10,11... | collective-permute-start | bytes 344072 | tf_op jit(solution)/shard_map/ppermute | solution.py:385
  23.1 11.5 %all_to_all.11 = f32[32,1,128]{2,1,0:T(1,128)S(1)} all-to-all(f32[32,1,128]{2,1,0:T(1,128)S(1)} %bitcast.30), channel_id=1, replica_groups=mesh['img'=4,'gx'=4,'gy'=2] {'img','gx','gy'}, dimensions={0} | all-to-all | bytes 32768 | tf_op jit(solution)/shard_map/all_to_all | solution.py:488
  34.6 0.0 collective-permute-done.9.stripsp_ref
  34.6 0.0 collective-permute-done.6
  34.6 11.6 %evolve.1 = f32[3,256,128]{2,1,0:T(8,128)} custom-call(f32[5,8,128]{2,1,0:T(8,128)S(1)} %get-tuple-element.28.info_ref, f32[32,128]{1,0:T(8,128)S(1)} %bitcast.29, f32[3,256,128]{2,1,0:T(8,128)S(1)} %bitcast.20, f32[3,256,128]{2,1,0:T(8,128)S(1)} %bitcast.25, f32[3,256,128]{2,1,0:T(8,128)S(1)} %get-tuple-element.33.n_ref, f32[3,256,128]{2,1,0:T(8,128)S(1)} %bitcast.27, ...), custom_call_target="tpu_custom_call" | custom-call | tf_op jit(solution)/shard_map/evolve/pallas_call | solution.py:490
  (1 shorter events, 0.0 us)
Async XLA Ops:
  0.0 16.6 %collective-permute-start = (f32[3,16,16,128]{3,2,1,0:T(8,128)}, f32[3,16,16,128]{3,2,1,0:T(8,128)S(1)}, u32[]{:S(2)}, u32[]{:S(2)}) collective-permute-start(f32[3,16,16,128]{3,2,1,0:T(8,128)} %bitcast.15), channel_id=1, source_target_pairs={{0,1},{1,0},{2,3},{3,2},{4,5},{5,4},{6,7},{7,6},{8,9},{9,8},{10,11... | collective-permute-start | bytes 1179656 | tf_op jit(solution)/shard_map/ppermute | solution.py:385
  2.9 13.7 %collective-permute-start.5 = (f32[3,16,16,128]{3,2,1,0:T(8,128)}, f32[3,16,16,128]{3,2,1,0:T(8,128)S(1)}, u32[]{:S(2)}, u32[]{:S(2)}) collective-permute-start(f32[3,16,16,128]{3,2,1,0:T(8,128)} %bitcast.16), channel_id=1, source_target_pairs={{8,16},{16,8},{9,17},{17,9},{10,18},{18,10},{11,19},{19,11},{12,20... | collective-permute-start | bytes 1179656 | tf_op jit(solution)/shard_map/ppermute | solution.py:391
  3.6 13.2 %collective-permute-start.4 = (f32[3,16,16,128]{3,2,1,0:T(8,128)}, f32[3,16,16,128]{3,2,1,0:T(8,128)S(1)}, u32[]{:S(2)}, u32[]{:S(2)}) collective-permute-start(f32[3,16,16,128]{3,2,1,0:T(8,128)} %bitcast.17), channel_id=1, source_target_pairs={{0,8},{16,24},{8,0},{24,16},{1,9},{17,25},{9,1},{25,17},{2,10},{18... | collective-permute-start | bytes 1179656 | tf_op jit(solution)/shard_map/ppermute | solution.py:391
  8.1 1.0 %copy-start = (f32[1,3,16,16,128]{4,3,2,1,0:T(8,128)S(1)}, f32[1,3,16,16,128]{4,3,2,1,0:T(8,128)}, u32[]{:S(2)}) copy-start(f32[1,3,16,16,128]{4,3,2,1,0:T(8,128)} %param.6) | copy-start | bytes 1179652
  9.1 7.7 %copy-start.1 = (f32[1,3,16,16,128]{4,3,2,1,0:T(8,128)S(1)}, f32[1,3,16,16,128]{4,3,2,1,0:T(8,128)}, u32[]{:S(2)}) copy-start(f32[1,3,16,16,128]{4,3,2,1,0:T(8,128)} %param.6) | copy-start | bytes 1179652
  9.6 2.8 %copy-start.7 = (f32[3]{0:T(128)S(1)}, f32[3]{0:T(128)}, u32[]{:S(2)}) copy-start(f32[3]{0:T(128)} %param.8) | copy-start | bytes 40
  9.6 1.3 %collective-permute-start.1 = (f32[3,2,8,128]{3,2,1,0:T(8,128)S(1)}, f32[3,2,8,128]{3,2,1,0:T(8,128)S(1)}, u32[]{:S(2)}, u32[]{:S(2)}) collective-permute-start(f32[3,2,8,128]{3,2,1,0:T(8,128)S(1)} %get-tuple-element.24), channel_id=1, source_target_pairs={{0,2},{4,6},{2,0},{6,4},{1,3},{5,7},{3,1},{7,5},{8,10},{12,14},{10... | collective-permute-start | bytes 73736 | tf_op jit(solution)/shard_map/ppermute | solution.py:391
  10.9 5.8 %collective-permute-start.2 = (s32[16,16,128]{2,1,0:T(8,128)}, s32[16,16,128]{2,1,0:T(8,128)S(1)}, u32[]{:S(2)}, u32[]{:S(2)}) collective-permute-start(s32[16,16,128]{2,1,0:T(8,128)} %param.9), channel_id=1, source_target_pairs={{0,1},{1,0},{2,3},{3,2},{4,5},{5,4},{6,7},{7,6},{8,9},{9,8},{10,11... | collective-permute-start | bytes 393224 | tf_op jit(solution)/shard_map/ppermute | solution.py:385
  11.4 3.6 %collective-permute-start.3 = (f32[3,2,8,128]{3,2,1,0:T(8,128)S(1)}, f32[3,2,8,128]{3,2,1,0:T(8,128)S(1)}, u32[]{:S(2)}, u32[]{:S(2)}) collective-permute-start(f32[3,2,8,128]{3,2,1,0:T(8,128)S(1)} %get-tuple-element.27), channel_id=1, source_target_pairs={{2,4},{6,0},{4,2},{0,6},{3,5},{7,1},{5,3},{1,7},{10,12},{14,8},{12... | collective-permute-start | bytes 73736 | tf_op jit(solution)/shard_map/ppermute | solution.py:391
  12.4 0.7 %copy-start.4 = (s32[4]{0:T(128)S(1)}, s32[4]{0:T(128)}, u32[]{:S(2)}) copy-start(s32[4]{0:T(128)} %lower_ref.1) | copy-start | bytes 52
  12.4 0.7 %copy-start.5 = (f32[8]{0:T(128)S(1)}, f32[8]{0:T(128)}, u32[]{:S(2)}) copy-start(f32[8]{0:T(128)} %aniso_ref.1) | copy-start | bytes 100
  12.4 0.7 %copy-start.6 = (f32[8]{0:T(128)S(1)}, f32[8]{0:T(128)}, u32[]{:S(2)}) copy-start(f32[8]{0:T(128)} %damp_ref.1) | copy-start | bytes 100
  13.1 0.9 %copy-start.2 = (s32[16,16,128]{2,1,0:T(8,128)S(1)}, s32[16,16,128]{2,1,0:T(8,128)}, u32[]{:S(2)}) copy-start(s32[16,16,128]{2,1,0:T(8,128)} %param.9) | copy-start | bytes 393220
  16.8 3.0 %copy-start.3 = (s32[16,16,128]{2,1,0:T(8,128)S(1)}, s32[16,16,128]{2,1,0:T(8,128)}, u32[]{:S(2)}) copy-start(s32[16,16,128]{2,1,0:T(8,128)} %param.9) | copy-start | bytes 393220
  17.6 17.0 %collective-permute-start.6 = (f32[3,16,16,128]{3,2,1,0:T(8,128)S(1)}, f32[3,16,16,128]{3,2,1,0:T(8,128)S(1)}, u32[]{:S(2)}, u32[]{:S(2)}) collective-permute-start(f32[3,16,16,128]{3,2,1,0:T(8,128)S(1)} %bitcast.26), channel_id=1, source_target_pairs={{0,1},{1,0},{2,3},{3,2},{4,5},{5,4},{6,7},{7,6},{8,9},{9,8},{10,11... | collective-permute-start | bytes 1179656 | tf_op jit(solution)/shard_map/ppermute | solution.py:385
  18.2 2.6 %collective-permute-start.7 = (f32[4,2,8,128]{3,2,1,0:T(8,128)S(1)}, f32[4,2,8,128]{3,2,1,0:T(8,128)S(1)}, u32[]{:S(2)}, u32[]{:S(2)}) collective-permute-start(f32[4,2,8,128]{3,2,1,0:T(8,128)S(1)} %get-tuple-element.34), channel_id=1, source_target_pairs={{0,2},{4,6},{2,0},{6,4},{1,3},{5,7},{3,1},{7,5},{8,10},{12,14},{10... | collective-permute-start | bytes 98312 | tf_op jit(solution)/shard_map/ppermute | solution.py:391
  18.2 3.3 %collective-permute-start.8 = (f32[4,2,8,128]{3,2,1,0:T(8,128)S(1)}, f32[4,2,8,128]{3,2,1,0:T(8,128)S(1)}, u32[]{:S(2)}, u32[]{:S(2)}) collective-permute-start(f32[4,2,8,128]{3,2,1,0:T(8,128)S(1)} %get-tuple-element.38), channel_id=1, source_target_pairs={{2,4},{6,0},{4,2},{0,6},{3,5},{7,1},{5,3},{1,7},{10,12},{14,8},{12... | collective-permute-start | bytes 98312 | tf_op jit(solution)/shard_map/ppermute | solution.py:391
  21.5 13.1 %collective-permute-start.9 = (f32[2,7,2,8,128]{4,3,2,1,0:T(8,128)S(1)}, f32[2,7,2,8,128]{4,3,2,1,0:T(8,128)S(1)}, u32[]{:S(2)}, u32[]{:S(2)}) collective-permute-start(f32[2,7,2,8,128]{4,3,2,1,0:T(8,128)S(1)} %merge_strips.1.strips_ref), channel_id=1, source_target_pairs={{0,1},{1,0},{2,3},{3,2},{4,5},{5,4},{6,7},{7,6},{8,9},{9,8},{10,11... | collective-permute-start | bytes 344072 | tf_op jit(solution)/shard_map/ppermute | solution.py:385

commit v26 on v23

--- a/solution.py
+++ b/solution.py
@@ -232,7 +232,7 @@
 
     def fill(i, carry):
         done = []
-        for k in [4 * i + u for u in range(4)]:
+        for k in [8 * i + u for u in range(8)]:
             for g, (own, near) in enumerate(((m_ref, n_ref), (mp_ref, np_ref))):
                 for t in range(tiles):
                     rows = rows_at(ny, tiles, k, t)
@@ -245,7 +245,7 @@
                 main0[c, r, t] = v[c]
         return carry
 
-    lax.fori_loop(0, ny // 4, fill, 0)
+    lax.fori_loop(0, ny // 8, fill, 0)
 
     def seam_of(left, right):
         return jnp.where(head_lane, pltpu.roll(left, 1, 1), pltpu.roll(right, LANES - 1, 1))
@@ -375,13 +375,13 @@
     lax.fori_loop(0, STEPS, step, 0)
 
     def hand_out(i, carry):
-        for k in (2 * i, 2 * i + 1):
+        for k in [8 * i + u for u in range(8)]:
             for t in range(tiles):
                 for c in range(COMPS):
                     out_ref[c, rows_at(ny, tiles, k, t), :] = main0[c, k, t]
         return carry
 
-    lax.fori_loop(0, ny // 2, hand_out, 0)
+    lax.fori_loop(0, ny // 8, hand_out, 0)
 
 
 def shifted(cells, axis, step, closed):

time: 46.3 us -> 46.3 us (level)
  no operation moved by 1% of the time
where the time goes in v26:
time: 46.3 us; the launch traced here: 46.1 us
  Pallas kernels  14.8 us (32%)
  starting transfers between devices  13.7 us (30%)
  blocking collectives  10.9 us (24%)
  waiting for transfers between devices  3.87 us (8%)
  local copies, waits for them, and re-layouts  2.61 us (6%)
    pallas_call x1, Pallas kernels, body(): pl.pallas_call(functools.partial(evolve_kernel, ny, tiles, images), out_s...  11.6 us
    all_to_all x1, blocking collectives, body(): squares = lax.all_to_all(part, ('img', 'gx', 'gy'), 0, 0, tiled=True)  10.9 us
    ppermute x6, starting transfers between devices, swapped(): return lax.ppermute(cells, axis, pairs + [(j, i) for i, j in pairs])  8.04 us
    ppermute x4, starting transfers between devices, shifted(): return lax.ppermute(cells, axis, pairs)  5.69 us
    ppermute x6, waiting for transfers between devices, swapped(): return lax.ppermute(cells, axis, pairs + [(j, i) for i, j in pairs])  3.86 us
    unnamed x16, local copies, waits for them, and re-layouts  2.61 us
    pallas_call x1, Pallas kernels, body(): pl.pallas_call(functools.partial(pack_kernel, ny, tiles, anisotropy.shape...  1.51 us
    pallas_call x1, Pallas kernels, body(): pl.pallas_call(functools.partial(look_up_kernel, ny, tiles), out_shape=ja...  1.01 us
  transfers between devices with their start and end apart: 10, of which 3 were waited for; matrix products, arithmetic and copies ran while one was open for 0% of the time, Pallas kernels for 6%

profile of v26, /device:TPU:0, one launch (start us, length us, event | category | flops | bytes accessed | tf_op | source)
XLA Modules:
  0.0 46.1 jit_solution(14183209724371991305)
XLA Ops:
  0.0 2.9 %collective-permute-start = (f32[3,16,16,128]{3,2,1,0:T(8,128)}, f32[3,16,16,128]{3,2,1,0:T(8,128)S(1)}, u32[]{:S(2)}, u32[]{:S(2)}) collective-permute-start(f32[3,16,16,128]{3,2,1,0:T(8,128)} %bitcast.15), channel_id=1, source_target_pairs={{0,1},{1,0},{2,3},{3,2},{4,5},{5,4},{6,7},{7,6},{8,9},{9,8},{10,11... | collective-permute-start | bytes 1179656 | tf_op jit(solution)/shard_map/ppermute | solution.py:390
  2.9 0.7 %collective-permute-start.5 = (f32[3,16,16,128]{3,2,1,0:T(8,128)}, f32[3,16,16,128]{3,2,1,0:T(8,128)S(1)}, u32[]{:S(2)}, u32[]{:S(2)}) collective-permute-start(f32[3,16,16,128]{3,2,1,0:T(8,128)} %bitcast.16), channel_id=1, source_target_pairs={{8,16},{16,8},{9,17},{17,9},{10,18},{18,10},{11,19},{19,11},{12,20... | collective-permute-start | bytes 1179656 | tf_op jit(solution)/shard_map/ppermute | solution.py:396
  3.6 4.4 %collective-permute-start.4 = (f32[3,16,16,128]{3,2,1,0:T(8,128)}, f32[3,16,16,128]{3,2,1,0:T(8,128)S(1)}, u32[]{:S(2)}, u32[]{:S(2)}) collective-permute-start(f32[3,16,16,128]{3,2,1,0:T(8,128)} %bitcast.17), channel_id=1, source_target_pairs={{0,8},{16,24},{8,0},{24,16},{1,9},{17,25},{9,1},{25,17},{2,10},{18... | collective-permute-start | bytes 1179656 | tf_op jit(solution)/shard_map/ppermute | solution.py:396
  8.1 0.0 copy-start.7
  8.1 0.0 copy-start.4
  8.1 0.0 copy-start.5
  8.1 0.0 copy-start.6
  8.1 0.6 %copy-done.7 = f32[3]{0:T(128)S(1)} copy-done((f32[3]{0:T(128)S(1)}, f32[3]{0:T(128)}, u32[]{:S(2)}) %copy-start.7) | copy-done | bytes 36
  8.7 0.0 copy-done.4
  8.7 0.0 copy-done.5
  8.7 0.0 copy-done.6
  8.8 0.0 copy-start
  8.8 1.0 %copy-done = f32[1,3,16,16,128]{4,3,2,1,0:T(8,128)S(1)} copy-done((f32[1,3,16,16,128]{4,3,2,1,0:T(8,128)S(1)}, f32[1,3,16,16,128]{4,3,2,1,0:T(8,128)}, u32[]{:S(2)}) %copy-start) | copy-done | bytes 393240
  9.8 0.0 copy-start.2
  9.8 0.9 %copy-done.2 = s32[16,16,128]{2,1,0:T(8,128)S(1)} copy-done((s32[16,16,128]{2,1,0:T(8,128)S(1)}, s32[16,16,128]{2,1,0:T(8,128)}, u32[]{:S(2)}) %copy-start.2) | copy-done | bytes 131096
  10.7 0.0 copy-start.1
  10.7 1.5 %pack_strips.1 = (f32[4,2,8,128]{3,2,1,0:T(8,128)S(1)}, f32[4,2,8,128]{3,2,1,0:T(8,128)S(1)}, f32[5,8,128]{2,1,0:T(8,128)S(1)}) custom-call(s32[4]{0:T(128)S(1)} %copy-done.4, f32[8]{0:T(128)S(1)} %copy-done.5, f32[8]{0:T(128)S(1)} %copy-done.6, f32[1,3]{1,0:T(1,128)S(1)} %bitcast.31, f32[3,256,128]{2,1,0:T(8,128)S(1)} %bitcast.18, s32[256,128]{1,0:T(8,128)S(1)} %bitcast.21), custom_call_target="tpu_custom_call" | custom-call | tf_op jit(solution)/shard_map/pack_strips/pallas_call | solution.py:437
  12.2 0.6 %collective-permute-start.1 = (s32[16,16,128]{2,1,0:T(8,128)S(1)}, s32[16,16,128]{2,1,0:T(8,128)S(1)}, u32[]{:S(2)}, u32[]{:S(2)}) collective-permute-start(s32[16,16,128]{2,1,0:T(8,128)S(1)} %copy-done.2), channel_id=1, source_target_pairs={{0,1},{1,0},{2,3},{3,2},{4,5},{5,4},{6,7},{7,6},{8,9},{9,8},{10,11... | collective-permute-start | bytes 393224 | tf_op jit(solution)/shard_map/ppermute | solution.py:390
  12.8 0.0 collective-permute-start.2
  12.8 1.2 %collective-permute-done.2.own_one_ref = f32[4,2,8,128]{3,2,1,0:T(8,128)S(1)} collective-permute-done((f32[4,2,8,128]{3,2,1,0:T(8,128)S(1)}, f32[4,2,8,128]{3,2,1,0:T(8,128)S(1)}, u32[]{:S(2)}, u32[]{:S(2)}) %collective-permute-start.2) | collective-permute-done | bytes 32800 | tf_op jit(solution)/shard_map/ppermute | solution.py:396
  14.0 1.3 %collective-permute-start.3 = (f32[4,2,8,128]{3,2,1,0:T(8,128)S(1)}, f32[4,2,8,128]{3,2,1,0:T(8,128)S(1)}, u32[]{:S(2)}, u32[]{:S(2)}) collective-permute-start(f32[4,2,8,128]{3,2,1,0:T(8,128)S(1)} %get-tuple-element.25), channel_id=1, source_target_pairs={{2,4},{6,0},{4,2},{0,6},{3,5},{7,1},{5,3},{1,7},{10,12},{14,8},{12... | collective-permute-start | bytes 98312 | tf_op jit(solution)/shard_map/ppermute | solution.py:396
  15.3 2.1 %collective-permute-done.3.own_two_ref = f32[4,2,8,128]{3,2,1,0:T(8,128)S(1)} collective-permute-done((f32[4,2,8,128]{3,2,1,0:T(8,128)S(1)}, f32[4,2,8,128]{3,2,1,0:T(8,128)S(1)}, u32[]{:S(2)}, u32[]{:S(2)}) %collective-permute-start.3) | collective-permute-done | bytes 32800 | tf_op jit(solution)/shard_map/ppermute | solution.py:396
  17.3 0.0 collective-permute-done.1
  17.3 0.0 collective-permute-done
  17.3 0.0 collective-permute-done.5
  17.4 0.0 collective-permute-done.4
  17.4 0.0 copy-done.1
  17.4 0.0 copy-start.3
  17.4 0.7 %gather_images.1 = (f32[32,128]{1,0:T(8,128)S(1)}, f32[3,256,128]{2,1,0:T(8,128)S(1)}, f32[3,2,8,128]{3,2,1,0:T(8,128)S(1)}, f32[3,2,8,128]{3,2,1,0:T(8,128)S(1)}) custom-call(f32[5,8,128]{2,1,0:T(8,128)S(1)} %get-tuple-element.26.info_ref, f32[3,256,128]{2,1,0:T(8,128)S(1)} %bitcast.19, f32[3,256,128]{2,1,0:T(8,128)S(1)} %bitcast.24, ...), custom_call_target="tpu_custom_call" | custom-call | tf_op jit(solution)/shard_map/gather_images/pallas_call | solution.py:458
  18.1 1.6 %collective-permute-start.6 = (f32[3,16,16,128]{3,2,1,0:T(8,128)S(1)}, f32[3,16,16,128]{3,2,1,0:T(8,128)S(1)}, u32[]{:S(2)}, u32[]{:S(2)}) collective-permute-start(f32[3,16,16,128]{3,2,1,0:T(8,128)S(1)} %bitcast.26), channel_id=1, source_target_pairs={{0,1},{1,0},{2,3},{3,2},{4,5},{5,4},{6,7},{7,6},{8,9},{9,8},{10,11... | collective-permute-start | bytes 1179656 | tf_op jit(solution)/shard_map/ppermute | solution.py:390
  19.7 0.0 collective-permute-start.7
  19.7 1.6 %collective-permute-start.8 = (f32[3,2,8,128]{3,2,1,0:T(8,128)S(1)}, f32[3,2,8,128]{3,2,1,0:T(8,128)S(1)}, u32[]{:S(2)}, u32[]{:S(2)}) collective-permute-start(f32[3,2,8,128]{3,2,1,0:T(8,128)S(1)} %get-tuple-element.34), channel_id=1, source_target_pairs={{2,4},{6,0},{4,2},{0,6},{3,5},{7,1},{5,3},{1,7},{10,12},{14,8},{12... | collective-permute-start | bytes 73736 | tf_op jit(solution)/shard_map/ppermute | solution.py:396
  21.3 0.0 copy-done.3
  21.3 1.0 %parameters.1.par = f32[3,32,2,8,128]{4,3,2,1,0:T(8,128)S(1)} custom-call(f32[5,8,128]{2,1,0:T(8,128)S(1)} %get-tuple-element.26.info_ref, s32[256,128]{1,0:T(8,128)S(1)} %bitcast.22, s32[256,128]{1,0:T(8,128)S(1)} %bitcast.28), custom_call_target="tpu_custom_call" | custom-call | tf_op jit(solution)/shard_map/parameters/pallas_call | solution.py:475
  22.3 0.0 collective-permute-done.7.one_ref
  22.3 0.6 %collective-permute-done.8.two_ref = f32[3,2,8,128]{3,2,1,0:T(8,128)S(1)} collective-permute-done((f32[3,2,8,128]{3,2,1,0:T(8,128)S(1)}, f32[3,2,8,128]{3,2,1,0:T(8,128)S(1)}, u32[]{:S(2)}, u32[]{:S(2)}) %collective-permute-start.8) | collective-permute-done | bytes 24608 | tf_op jit(solution)/shard_map/ppermute | solution.py:396
  23.0 0.6 %collective-permute-start.9 = (f32[2,7,2,8,128]{4,3,2,1,0:T(8,128)S(1)}, f32[2,7,2,8,128]{4,3,2,1,0:T(8,128)S(1)}, u32[]{:S(2)}, u32[]{:S(2)}) collective-permute-start(f32[2,7,2,8,128]{4,3,2,1,0:T(8,128)S(1)} %merge_strips.1.strips_ref), channel_id=1, source_target_pairs={{0,1},{1,0},{2,3},{3,2},{4,5},{5,4},{6,7},{7,6},{8,9},{9,8},{10,11... | collective-permute-start | bytes 344072 | tf_op jit(solution)/shard_map/ppermute | solution.py:390
  23.6 10.9 %all_to_all.11 = f32[32,1,128]{2,1,0:T(1,128)S(1)} all-to-all(f32[32,1,128]{2,1,0:T(1,128)S(1)} %bitcast.30), channel_id=1, replica_groups=mesh['img'=4,'gx'=4,'gy'=2] {'img','gx','gy'}, dimensions={0} | all-to-all | bytes 32768 | tf_op jit(solution)/shard_map/all_to_all | solution.py:493
  34.5 0.0 collective-permute-done.9.stripsp_ref
  34.5 0.0 collective-permute-done.6
  34.5 11.6 %evolve.1 = f32[3,256,128]{2,1,0:T(8,128)} custom-call(f32[5,8,128]{2,1,0:T(8,128)S(1)} %get-tuple-element.26.info_ref, f32[32,128]{1,0:T(8,128)S(1)} %bitcast.29, f32[3,256,128]{2,1,0:T(8,128)S(1)} %bitcast.20, f32[3,256,128]{2,1,0:T(8,128)S(1)} %bitcast.25, f32[3,256,128]{2,1,0:T(8,128)S(1)} %get-tuple-element.29.n_ref, f32[3,256,128]{2,1,0:T(8,128)S(1)} %bitcast.27, ...), custom_call_target="tpu_custom_call" | custom-call | tf_op jit(solution)/shard_map/evolve/pallas_call | solution.py:495
  (1 shorter events, 0.0 us)
Async XLA Ops:
  0.0 17.3 %collective-permute-start = (f32[3,16,16,128]{3,2,1,0:T(8,128)}, f32[3,16,16,128]{3,2,1,0:T(8,128)S(1)}, u32[]{:S(2)}, u32[]{:S(2)}) collective-permute-start(f32[3,16,16,128]{3,2,1,0:T(8,128)} %bitcast.15), channel_id=1, source_target_pairs={{0,1},{1,0},{2,3},{3,2},{4,5},{5,4},{6,7},{7,6},{8,9},{9,8},{10,11... | collective-permute-start | bytes 1179656 | tf_op jit(solution)/shard_map/ppermute | solution.py:390
  2.9 14.4 %collective-permute-start.5 = (f32[3,16,16,128]{3,2,1,0:T(8,128)}, f32[3,16,16,128]{3,2,1,0:T(8,128)S(1)}, u32[]{:S(2)}, u32[]{:S(2)}) collective-permute-start(f32[3,16,16,128]{3,2,1,0:T(8,128)} %bitcast.16), channel_id=1, source_target_pairs={{8,16},{16,8},{9,17},{17,9},{10,18},{18,10},{11,19},{19,11},{12,20... | collective-permute-start | bytes 1179656 | tf_op jit(solution)/shard_map/ppermute | solution.py:396
  3.6 13.7 %collective-permute-start.4 = (f32[3,16,16,128]{3,2,1,0:T(8,128)}, f32[3,16,16,128]{3,2,1,0:T(8,128)S(1)}, u32[]{:S(2)}, u32[]{:S(2)}) collective-permute-start(f32[3,16,16,128]{3,2,1,0:T(8,128)} %bitcast.17), channel_id=1, source_target_pairs={{0,8},{16,24},{8,0},{24,16},{1,9},{17,25},{9,1},{25,17},{2,10},{18... | collective-permute-start | bytes 1179656 | tf_op jit(solution)/shard_map/ppermute | solution.py:396
  8.1 0.7 %copy-start.7 = (f32[3]{0:T(128)S(1)}, f32[3]{0:T(128)}, u32[]{:S(2)}) copy-start(f32[3]{0:T(128)} %param.8) | copy-start | bytes 40
  8.1 0.7 %copy-start.4 = (s32[4]{0:T(128)S(1)}, s32[4]{0:T(128)}, u32[]{:S(2)}) copy-start(s32[4]{0:T(128)} %lower_ref.1) | copy-start | bytes 52
  8.1 0.7 %copy-start.5 = (f32[8]{0:T(128)S(1)}, f32[8]{0:T(128)}, u32[]{:S(2)}) copy-start(f32[8]{0:T(128)} %aniso_ref.1) | copy-start | bytes 100
  8.1 0.7 %copy-start.6 = (f32[8]{0:T(128)S(1)}, f32[8]{0:T(128)}, u32[]{:S(2)}) copy-start(f32[8]{0:T(128)} %damp_ref.1) | copy-start | bytes 100
  8.8 1.0 %copy-start = (f32[1,3,16,16,128]{4,3,2,1,0:T(8,128)S(1)}, f32[1,3,16,16,128]{4,3,2,1,0:T(8,128)}, u32[]{:S(2)}) copy-start(f32[1,3,16,16,128]{4,3,2,1,0:T(8,128)} %param.6) | copy-start | bytes 1179652
  9.8 0.9 %copy-start.2 = (s32[16,16,128]{2,1,0:T(8,128)S(1)}, s32[16,16,128]{2,1,0:T(8,128)}, u32[]{:S(2)}) copy-start(s32[16,16,128]{2,1,0:T(8,128)} %param.9) | copy-start | bytes 393220
  10.7 6.7 %copy-start.1 = (f32[1,3,16,16,128]{4,3,2,1,0:T(8,128)S(1)}, f32[1,3,16,16,128]{4,3,2,1,0:T(8,128)}, u32[]{:S(2)}) copy-start(f32[1,3,16,16,128]{4,3,2,1,0:T(8,128)} %param.6) | copy-start | bytes 1179652
  12.2 5.2 %collective-permute-start.1 = (s32[16,16,128]{2,1,0:T(8,128)S(1)}, s32[16,16,128]{2,1,0:T(8,128)S(1)}, u32[]{:S(2)}, u32[]{:S(2)}) collective-permute-start(s32[16,16,128]{2,1,0:T(8,128)S(1)} %copy-done.2), channel_id=1, source_target_pairs={{0,1},{1,0},{2,3},{3,2},{4,5},{5,4},{6,7},{7,6},{8,9},{9,8},{10,11... | collective-permute-start | bytes 393224 | tf_op jit(solution)/shard_map/ppermute | solution.py:390
  12.8 1.2 %collective-permute-start.2 = (f32[4,2,8,128]{3,2,1,0:T(8,128)S(1)}, f32[4,2,8,128]{3,2,1,0:T(8,128)S(1)}, u32[]{:S(2)}, u32[]{:S(2)}) collective-permute-start(f32[4,2,8,128]{3,2,1,0:T(8,128)S(1)} %get-tuple-element.24), channel_id=1, source_target_pairs={{0,2},{4,6},{2,0},{6,4},{1,3},{5,7},{3,1},{7,5},{8,10},{12,14},{10... | collective-permute-start | bytes 98312 | tf_op jit(solution)/shard_map/ppermute | solution.py:396
  14.0 3.3 %collective-permute-start.3 = (f32[4,2,8,128]{3,2,1,0:T(8,128)S(1)}, f32[4,2,8,128]{3,2,1,0:T(8,128)S(1)}, u32[]{:S(2)}, u32[]{:S(2)}) collective-permute-start(f32[4,2,8,128]{3,2,1,0:T(8,128)S(1)} %get-tuple-element.25), channel_id=1, source_target_pairs={{2,4},{6,0},{4,2},{0,6},{3,5},{7,1},{5,3},{1,7},{10,12},{14,8},{12... | collective-permute-start | bytes 98312 | tf_op jit(solution)/shard_map/ppermute | solution.py:396
  17.4 3.9 %copy-start.3 = (s32[16,16,128]{2,1,0:T(8,128)S(1)}, s32[16,16,128]{2,1,0:T(8,128)}, u32[]{:S(2)}) copy-start(s32[16,16,128]{2,1,0:T(8,128)} %param.9) | copy-start | bytes 393220
  18.1 16.4 %collective-permute-start.6 = (f32[3,16,16,128]{3,2,1,0:T(8,128)S(1)}, f32[3,16,16,128]{3,2,1,0:T(8,128)S(1)}, u32[]{:S(2)}, u32[]{:S(2)}) collective-permute-start(f32[3,16,16,128]{3,2,1,0:T(8,128)S(1)} %bitcast.26), channel_id=1, source_target_pairs={{0,1},{1,0},{2,3},{3,2},{4,5},{5,4},{6,7},{7,6},{8,9},{9,8},{10,11... | collective-permute-start | bytes 1179656 | tf_op jit(solution)/shard_map/ppermute | solution.py:390
  19.7 2.7 %collective-permute-start.7 = (f32[3,2,8,128]{3,2,1,0:T(8,128)S(1)}, f32[3,2,8,128]{3,2,1,0:T(8,128)S(1)}, u32[]{:S(2)}, u32[]{:S(2)}) collective-permute-start(f32[3,2,8,128]{3,2,1,0:T(8,128)S(1)} %get-tuple-element.30), channel_id=1, source_target_pairs={{0,2},{4,6},{2,0},{6,4},{1,3},{5,7},{3,1},{7,5},{8,10},{12,14},{10... | collective-permute-start | bytes 73736 | tf_op jit(solution)/shard_map/ppermute | solution.py:396
  19.7 3.3 %collective-permute-start.8 = (f32[3,2,8,128]{3,2,1,0:T(8,128)S(1)}, f32[3,2,8,128]{3,2,1,0:T(8,128)S(1)}, u32[]{:S(2)}, u32[]{:S(2)}) collective-permute-start(f32[3,2,8,128]{3,2,1,0:T(8,128)S(1)} %get-tuple-element.34), channel_id=1, source_target_pairs={{2,4},{6,0},{4,2},{0,6},{3,5},{7,1},{5,3},{1,7},{10,12},{14,8},{12... | collective-permute-start | bytes 73736 | tf_op jit(solution)/shard_map/ppermute | solution.py:396
  23.0 11.5 %collective-permute-start.9 = (f32[2,7,2,8,128]{4,3,2,1,0:T(8,128)S(1)}, f32[2,7,2,8,128]{4,3,2,1,0:T(8,128)S(1)}, u32[]{:S(2)}, u32[]{:S(2)}) collective-permute-start(f32[2,7,2,8,128]{4,3,2,1,0:T(8,128)S(1)} %merge_strips.1.strips_ref), channel_id=1, source_target_pairs={{0,1},{1,0},{2,3},{3,2},{4,5},{5,4},{6,7},{7,6},{8,9},{9,8},{10,11... | collective-permute-start | bytes 344072 | tf_op jit(solution)/shard_map/ppermute | solution.py:390

commit v27 on v23

--- a/solution.py
+++ b/solution.py
@@ -100,7 +100,7 @@
 ):
     here = lax.axis_index("img")
     pick, odd = take_first(info_ref, here)
-    chunks = 8
+    chunks = 16
     depth = m_ref.shape[1]
 
     def squares(i, sums):
@@ -125,8 +125,8 @@
     part_ref[...] = jnp.where((slot == here) & (here > 0), total, 0.0)
     def pack(i, carry):
         done = []
-        for u in range(4):
-            y = 4 * i + u
+        for u in range(8):
+            y = 8 * i + u
             one, two, shift = rims(ny, y)
             for t in range(tiles):
                 for c in range(COMPS):
@@ -137,7 +137,7 @@
             pltpu.store(two_ref.at[c, t], cells, mask=two)
         return carry
 
-    lax.fori_loop(0, ny // 4, pack, 0)
+    lax.fori_loop(0, ny // 8, pack, 0)
 
 
 def turn(m, h, a2, b, sc):

time: 46.3 us -> 46.2 us (level)
  no operation moved by 1% of the time
where the time goes in v27:
time: 46.2 us; the launch traced here: 46 us
  Pallas kernels  14.7 us (32%)
  starting transfers between devices  13.7 us (30%)
  blocking collectives  10.9 us (24%)
  waiting for transfers between devices  3.87 us (8%)
  local copies, waits for them, and re-layouts  2.61 us (6%)
    pallas_call x1, Pallas kernels, body(): pl.pallas_call(functools.partial(evolve_kernel, ny, tiles, images), out_s...  11.6 us
    all_to_all x1, blocking collectives, body(): squares = lax.all_to_all(part, ('img', 'gx', 'gy'), 0, 0, tiled=True)  10.9 us
    ppermute x6, starting transfers between devices, swapped(): return lax.ppermute(cells, axis, pairs + [(j, i) for i, j in pairs])  8.04 us
    ppermute x4, starting transfers between devices, shifted(): return lax.ppermute(cells, axis, pairs)  5.69 us
    ppermute x6, waiting for transfers between devices, swapped(): return lax.ppermute(cells, axis, pairs + [(j, i) for i, j in pairs])  3.86 us
    unnamed x16, local copies, waits for them, and re-layouts  2.61 us
    pallas_call x1, Pallas kernels, body(): pl.pallas_call(functools.partial(pack_kernel, ny, tiles, anisotropy.shape...  1.51 us
    pallas_call x1, Pallas kernels, body(): pl.pallas_call(functools.partial(look_up_kernel, ny, tiles), out_shape=ja...  1.01 us
  transfers between devices with their start and end apart: 10, of which 3 were waited for; matrix products, arithmetic and copies ran while one was open for 0% of the time, Pallas kernels for 6%

profile of v27, /device:TPU:0, one launch (start us, length us, event | category | flops | bytes accessed | tf_op | source)
XLA Modules:
  0.0 46.0 jit_solution(4092367460190409980)
XLA Ops:
  0.0 2.9 %collective-permute-start = (f32[3,16,16,128]{3,2,1,0:T(8,128)}, f32[3,16,16,128]{3,2,1,0:T(8,128)S(1)}, u32[]{:S(2)}, u32[]{:S(2)}) collective-permute-start(f32[3,16,16,128]{3,2,1,0:T(8,128)} %bitcast.15), channel_id=1, source_target_pairs={{0,1},{1,0},{2,3},{3,2},{4,5},{5,4},{6,7},{7,6},{8,9},{9,8},{10,11... | collective-permute-start | bytes 1179656 | tf_op jit(solution)/shard_map/ppermute | solution.py:390
  2.9 0.7 %collective-permute-start.5 = (f32[3,16,16,128]{3,2,1,0:T(8,128)}, f32[3,16,16,128]{3,2,1,0:T(8,128)S(1)}, u32[]{:S(2)}, u32[]{:S(2)}) collective-permute-start(f32[3,16,16,128]{3,2,1,0:T(8,128)} %bitcast.16), channel_id=1, source_target_pairs={{8,16},{16,8},{9,17},{17,9},{10,18},{18,10},{11,19},{19,11},{12,20... | collective-permute-start | bytes 1179656 | tf_op jit(solution)/shard_map/ppermute | solution.py:396
  3.6 4.4 %collective-permute-start.4 = (f32[3,16,16,128]{3,2,1,0:T(8,128)}, f32[3,16,16,128]{3,2,1,0:T(8,128)S(1)}, u32[]{:S(2)}, u32[]{:S(2)}) collective-permute-start(f32[3,16,16,128]{3,2,1,0:T(8,128)} %bitcast.17), channel_id=1, source_target_pairs={{0,8},{16,24},{8,0},{24,16},{1,9},{17,25},{9,1},{25,17},{2,10},{18... | collective-permute-start | bytes 1179656 | tf_op jit(solution)/shard_map/ppermute | solution.py:396
  8.1 0.0 copy-start.7
  8.1 0.0 copy-start.4
  8.1 0.0 copy-start.5
  8.1 0.0 copy-start.6
  8.1 0.6 %copy-done.7 = f32[3]{0:T(128)S(1)} copy-done((f32[3]{0:T(128)S(1)}, f32[3]{0:T(128)}, u32[]{:S(2)}) %copy-start.7) | copy-done | bytes 36
  8.7 0.0 copy-done.4
  8.7 0.0 copy-done.5
  8.7 0.0 copy-done.6
  8.8 0.0 copy-start
  8.8 1.0 %copy-done = f32[1,3,16,16,128]{4,3,2,1,0:T(8,128)S(1)} copy-done((f32[1,3,16,16,128]{4,3,2,1,0:T(8,128)S(1)}, f32[1,3,16,16,128]{4,3,2,1,0:T(8,128)}, u32[]{:S(2)}) %copy-start) | copy-done | bytes 393240
  9.8 0.0 copy-start.2
  9.8 0.9 %copy-done.2 = s32[16,16,128]{2,1,0:T(8,128)S(1)} copy-done((s32[16,16,128]{2,1,0:T(8,128)S(1)}, s32[16,16,128]{2,1,0:T(8,128)}, u32[]{:S(2)}) %copy-start.2) | copy-done | bytes 131096
  10.7 0.0 copy-start.1
  10.7 1.5 %pack_strips.1 = (f32[4,2,8,128]{3,2,1,0:T(8,128)S(1)}, f32[4,2,8,128]{3,2,1,0:T(8,128)S(1)}, f32[5,8,128]{2,1,0:T(8,128)S(1)}) custom-call(s32[4]{0:T(128)S(1)} %copy-done.4, f32[8]{0:T(128)S(1)} %copy-done.5, f32[8]{0:T(128)S(1)} %copy-done.6, f32[1,3]{1,0:T(1,128)S(1)} %bitcast.31, f32[3,256,128]{2,1,0:T(8,128)S(1)} %bitcast.18, s32[256,128]{1,0:T(8,128)S(1)} %bitcast.21), custom_call_target="tpu_custom_call" | custom-call | tf_op jit(solution)/shard_map/pack_strips/pallas_call | solution.py:437
  12.2 0.6 %collective-permute-start.1 = (s32[16,16,128]{2,1,0:T(8,128)S(1)}, s32[16,16,128]{2,1,0:T(8,128)S(1)}, u32[]{:S(2)}, u32[]{:S(2)}) collective-permute-start(s32[16,16,128]{2,1,0:T(8,128)S(1)} %copy-done.2), channel_id=1, source_target_pairs={{0,1},{1,0},{2,3},{3,2},{4,5},{5,4},{6,7},{7,6},{8,9},{9,8},{10,11... | collective-permute-start | bytes 393224 | tf_op jit(solution)/shard_map/ppermute | solution.py:390
  12.8 0.0 collective-permute-start.2
  12.8 1.2 %collective-permute-done.2.own_one_ref = f32[4,2,8,128]{3,2,1,0:T(8,128)S(1)} collective-permute-done((f32[4,2,8,128]{3,2,1,0:T(8,128)S(1)}, f32[4,2,8,128]{3,2,1,0:T(8,128)S(1)}, u32[]{:S(2)}, u32[]{:S(2)}) %collective-permute-start.2) | collective-permute-done | bytes 32800 | tf_op jit(solution)/shard_map/ppermute | solution.py:396
  14.0 1.3 %collective-permute-start.3 = (f32[4,2,8,128]{3,2,1,0:T(8,128)S(1)}, f32[4,2,8,128]{3,2,1,0:T(8,128)S(1)}, u32[]{:S(2)}, u32[]{:S(2)}) collective-permute-start(f32[4,2,8,128]{3,2,1,0:T(8,128)S(1)} %get-tuple-element.25), channel_id=1, source_target_pairs={{2,4},{6,0},{4,2},{0,6},{3,5},{7,1},{5,3},{1,7},{10,12},{14,8},{12... | collective-permute-start | bytes 98312 | tf_op jit(solution)/shard_map/ppermute | solution.py:396
  15.3 2.1 %collective-permute-done.3.own_two_ref = f32[4,2,8,128]{3,2,1,0:T(8,128)S(1)} collective-permute-done((f32[4,2,8,128]{3,2,1,0:T(8,128)S(1)}, f32[4,2,8,128]{3,2,1,0:T(8,128)S(1)}, u32[]{:S(2)}, u32[]{:S(2)}) %collective-permute-start.3) | collective-permute-done | bytes 32800 | tf_op jit(solution)/shard_map/ppermute | solution.py:396
  17.3 0.0 collective-permute-done.1
  17.3 0.0 collective-permute-done
  17.3 0.0 collective-permute-done.5
  17.4 0.0 collective-permute-done.4
  17.4 0.0 copy-done.1
  17.4 0.0 copy-start.3
  17.4 0.6 %gather_images.1 = (f32[32,128]{1,0:T(8,128)S(1)}, f32[3,256,128]{2,1,0:T(8,128)S(1)}, f32[3,2,8,128]{3,2,1,0:T(8,128)S(1)}, f32[3,2,8,128]{3,2,1,0:T(8,128)S(1)}) custom-call(f32[5,8,128]{2,1,0:T(8,128)S(1)} %get-tuple-element.26.info_ref, f32[3,256,128]{2,1,0:T(8,128)S(1)} %bitcast.19, f32[3,256,128]{2,1,0:T(8,128)S(1)} %bitcast.24, ...), custom_call_target="tpu_custom_call" | custom-call | tf_op jit(solution)/shard_map/gather_images/pallas_call | solution.py:458
  18.0 1.6 %collective-permute-start.6 = (f32[3,16,16,128]{3,2,1,0:T(8,128)S(1)}, f32[3,16,16,128]{3,2,1,0:T(8,128)S(1)}, u32[]{:S(2)}, u32[]{:S(2)}) collective-permute-start(f32[3,16,16,128]{3,2,1,0:T(8,128)S(1)} %bitcast.26), channel_id=1, source_target_pairs={{0,1},{1,0},{2,3},{3,2},{4,5},{5,4},{6,7},{7,6},{8,9},{9,8},{10,11... | collective-permute-start | bytes 1179656 | tf_op jit(solution)/shard_map/ppermute | solution.py:390
  19.5 0.0 collective-permute-start.7
  19.5 1.6 %collective-permute-start.8 = (f32[3,2,8,128]{3,2,1,0:T(8,128)S(1)}, f32[3,2,8,128]{3,2,1,0:T(8,128)S(1)}, u32[]{:S(2)}, u32[]{:S(2)}) collective-permute-start(f32[3,2,8,128]{3,2,1,0:T(8,128)S(1)} %get-tuple-element.34), channel_id=1, source_target_pairs={{2,4},{6,0},{4,2},{0,6},{3,5},{7,1},{5,3},{1,7},{10,12},{14,8},{12... | collective-permute-start | bytes 73736 | tf_op jit(solution)/shard_map/ppermute | solution.py:396
  21.1 0.0 copy-done.3
  21.2 1.0 %parameters.1.par = f32[3,32,2,8,128]{4,3,2,1,0:T(8,128)S(1)} custom-call(f32[5,8,128]{2,1,0:T(8,128)S(1)} %get-tuple-element.26.info_ref, s32[256,128]{1,0:T(8,128)S(1)} %bitcast.22, s32[256,128]{1,0:T(8,128)S(1)} %bitcast.28), custom_call_target="tpu_custom_call" | custom-call | tf_op jit(solution)/shard_map/parameters/pallas_call | solution.py:475
  22.2 0.0 collective-permute-done.7.one_ref
  22.2 0.6 %collective-permute-done.8.two_ref = f32[3,2,8,128]{3,2,1,0:T(8,128)S(1)} collective-permute-done((f32[3,2,8,128]{3,2,1,0:T(8,128)S(1)}, f32[3,2,8,128]{3,2,1,0:T(8,128)S(1)}, u32[]{:S(2)}, u32[]{:S(2)}) %collective-permute-start.8) | collective-permute-done | bytes 24608 | tf_op jit(solution)/shard_map/ppermute | solution.py:396
  22.8 0.6 %collective-permute-start.9 = (f32[2,7,2,8,128]{4,3,2,1,0:T(8,128)S(1)}, f32[2,7,2,8,128]{4,3,2,1,0:T(8,128)S(1)}, u32[]{:S(2)}, u32[]{:S(2)}) collective-permute-start(f32[2,7,2,8,128]{4,3,2,1,0:T(8,128)S(1)} %merge_strips.1.strips_ref), channel_id=1, source_target_pairs={{0,1},{1,0},{2,3},{3,2},{4,5},{5,4},{6,7},{7,6},{8,9},{9,8},{10,11... | collective-permute-start | bytes 344072 | tf_op jit(solution)/shard_map/ppermute | solution.py:390
  23.4 10.9 %all_to_all.11 = f32[32,1,128]{2,1,0:T(1,128)S(1)} all-to-all(f32[32,1,128]{2,1,0:T(1,128)S(1)} %bitcast.30), channel_id=1, replica_groups=mesh['img'=4,'gx'=4,'gy'=2] {'img','gx','gy'}, dimensions={0} | all-to-all | bytes 32768 | tf_op jit(solution)/shard_map/all_to_all | solution.py:493
  34.3 0.0 collective-permute-done.9.stripsp_ref
  34.3 0.0 collective-permute-done.6
  34.3 11.6 %evolve.1 = f32[3,256,128]{2,1,0:T(8,128)} custom-call(f32[5,8,128]{2,1,0:T(8,128)S(1)} %get-tuple-element.26.info_ref, f32[32,128]{1,0:T(8,128)S(1)} %bitcast.29, f32[3,256,128]{2,1,0:T(8,128)S(1)} %bitcast.20, f32[3,256,128]{2,1,0:T(8,128)S(1)} %bitcast.25, f32[3,256,128]{2,1,0:T(8,128)S(1)} %get-tuple-element.29.n_ref, f32[3,256,128]{2,1,0:T(8,128)S(1)} %bitcast.27, ...), custom_call_target="tpu_custom_call" | custom-call | tf_op jit(solution)/shard_map/evolve/pallas_call | solution.py:495
  (1 shorter events, 0.0 us)
Async XLA Ops:
  0.0 17.3 %collective-permute-start = (f32[3,16,16,128]{3,2,1,0:T(8,128)}, f32[3,16,16,128]{3,2,1,0:T(8,128)S(1)}, u32[]{:S(2)}, u32[]{:S(2)}) collective-permute-start(f32[3,16,16,128]{3,2,1,0:T(8,128)} %bitcast.15), channel_id=1, source_target_pairs={{0,1},{1,0},{2,3},{3,2},{4,5},{5,4},{6,7},{7,6},{8,9},{9,8},{10,11... | collective-permute-start | bytes 1179656 | tf_op jit(solution)/shard_map/ppermute | solution.py:390
  2.9 14.4 %collective-permute-start.5 = (f32[3,16,16,128]{3,2,1,0:T(8,128)}, f32[3,16,16,128]{3,2,1,0:T(8,128)S(1)}, u32[]{:S(2)}, u32[]{:S(2)}) collective-permute-start(f32[3,16,16,128]{3,2,1,0:T(8,128)} %bitcast.16), channel_id=1, source_target_pairs={{8,16},{16,8},{9,17},{17,9},{10,18},{18,10},{11,19},{19,11},{12,20... | collective-permute-start | bytes 1179656 | tf_op jit(solution)/shard_map/ppermute | solution.py:396
  3.6 13.7 %collective-permute-start.4 = (f32[3,16,16,128]{3,2,1,0:T(8,128)}, f32[3,16,16,128]{3,2,1,0:T(8,128)S(1)}, u32[]{:S(2)}, u32[]{:S(2)}) collective-permute-start(f32[3,16,16,128]{3,2,1,0:T(8,128)} %bitcast.17), channel_id=1, source_target_pairs={{0,8},{16,24},{8,0},{24,16},{1,9},{17,25},{9,1},{25,17},{2,10},{18... | collective-permute-start | bytes 1179656 | tf_op jit(solution)/shard_map/ppermute | solution.py:396
  8.1 0.7 %copy-start.7 = (f32[3]{0:T(128)S(1)}, f32[3]{0:T(128)}, u32[]{:S(2)}) copy-start(f32[3]{0:T(128)} %param.8) | copy-start | bytes 40
  8.1 0.7 %copy-start.4 = (s32[4]{0:T(128)S(1)}, s32[4]{0:T(128)}, u32[]{:S(2)}) copy-start(s32[4]{0:T(128)} %lower_ref.1) | copy-start | bytes 52
  8.1 0.7 %copy-start.5 = (f32[8]{0:T(128)S(1)}, f32[8]{0:T(128)}, u32[]{:S(2)}) copy-start(f32[8]{0:T(128)} %aniso_ref.1) | copy-start | bytes 100
  8.1 0.7 %copy-start.6 = (f32[8]{0:T(128)S(1)}, f32[8]{0:T(128)}, u32[]{:S(2)}) copy-start(f32[8]{0:T(128)} %damp_ref.1) | copy-start | bytes 100
  8.8 1.0 %copy-start = (f32[1,3,16,16,128]{4,3,2,1,0:T(8,128)S(1)}, f32[1,3,16,16,128]{4,3,2,1,0:T(8,128)}, u32[]{:S(2)}) copy-start(f32[1,3,16,16,128]{4,3,2,1,0:T(8,128)} %param.6) | copy-start | bytes 1179652
  9.8 0.9 %copy-start.2 = (s32[16,16,128]{2,1,0:T(8,128)S(1)}, s32[16,16,128]{2,1,0:T(8,128)}, u32[]{:S(2)}) copy-start(s32[16,16,128]{2,1,0:T(8,128)} %param.9) | copy-start | bytes 393220
  10.7 6.7 %copy-start.1 = (f32[1,3,16,16,128]{4,3,2,1,0:T(8,128)S(1)}, f32[1,3,16,16,128]{4,3,2,1,0:T(8,128)}, u32[]{:S(2)}) copy-start(f32[1,3,16,16,128]{4,3,2,1,0:T(8,128)} %param.6) | copy-start | bytes 1179652
  12.2 5.2 %collective-permute-start.1 = (s32[16,16,128]{2,1,0:T(8,128)S(1)}, s32[16,16,128]{2,1,0:T(8,128)S(1)}, u32[]{:S(2)}, u32[]{:S(2)}) collective-permute-start(s32[16,16,128]{2,1,0:T(8,128)S(1)} %copy-done.2), channel_id=1, source_target_pairs={{0,1},{1,0},{2,3},{3,2},{4,5},{5,4},{6,7},{7,6},{8,9},{9,8},{10,11... | collective-permute-start | bytes 393224 | tf_op jit(solution)/shard_map/ppermute | solution.py:390
  12.8 1.2 %collective-permute-start.2 = (f32[4,2,8,128]{3,2,1,0:T(8,128)S(1)}, f32[4,2,8,128]{3,2,1,0:T(8,128)S(1)}, u32[]{:S(2)}, u32[]{:S(2)}) collective-permute-start(f32[4,2,8,128]{3,2,1,0:T(8,128)S(1)} %get-tuple-element.24), channel_id=1, source_target_pairs={{0,2},{4,6},{2,0},{6,4},{1,3},{5,7},{3,1},{7,5},{8,10},{12,14},{10... | collective-permute-start | bytes 98312 | tf_op jit(solution)/shard_map/ppermute | solution.py:396
  14.0 3.3 %collective-permute-start.3 = (f32[4,2,8,128]{3,2,1,0:T(8,128)S(1)}, f32[4,2,8,128]{3,2,1,0:T(8,128)S(1)}, u32[]{:S(2)}, u32[]{:S(2)}) collective-permute-start(f32[4,2,8,128]{3,2,1,0:T(8,128)S(1)} %get-tuple-element.25), channel_id=1, source_target_pairs={{2,4},{6,0},{4,2},{0,6},{3,5},{7,1},{5,3},{1,7},{10,12},{14,8},{12... | collective-permute-start | bytes 98312 | tf_op jit(solution)/shard_map/ppermute | solution.py:396
  17.4 3.8 %copy-start.3 = (s32[16,16,128]{2,1,0:T(8,128)S(1)}, s32[16,16,128]{2,1,0:T(8,128)}, u32[]{:S(2)}) copy-start(s32[16,16,128]{2,1,0:T(8,128)} %param.9) | copy-start | bytes 393220
  18.0 16.4 %collective-permute-start.6 = (f32[3,16,16,128]{3,2,1,0:T(8,128)S(1)}, f32[3,16,16,128]{3,2,1,0:T(8,128)S(1)}, u32[]{:S(2)}, u32[]{:S(2)}) collective-permute-start(f32[3,16,16,128]{3,2,1,0:T(8,128)S(1)} %bitcast.26), channel_id=1, source_target_pairs={{0,1},{1,0},{2,3},{3,2},{4,5},{5,4},{6,7},{7,6},{8,9},{9,8},{10,11... | collective-permute-start | bytes 1179656 | tf_op jit(solution)/shard_map/ppermute | solution.py:390
  19.5 2.7 %collective-permute-start.7 = (f32[3,2,8,128]{3,2,1,0:T(8,128)S(1)}, f32[3,2,8,128]{3,2,1,0:T(8,128)S(1)}, u32[]{:S(2)}, u32[]{:S(2)}) collective-permute-start(f32[3,2,8,128]{3,2,1,0:T(8,128)S(1)} %get-tuple-element.30), channel_id=1, source_target_pairs={{0,2},{4,6},{2,0},{6,4},{1,3},{5,7},{3,1},{7,5},{8,10},{12,14},{10... | collective-permute-start | bytes 73736 | tf_op jit(solution)/shard_map/ppermute | solution.py:396
  19.5 3.3 %collective-permute-start.8 = (f32[3,2,8,128]{3,2,1,0:T(8,128)S(1)}, f32[3,2,8,128]{3,2,1,0:T(8,128)S(1)}, u32[]{:S(2)}, u32[]{:S(2)}) collective-permute-start(f32[3,2,8,128]{3,2,1,0:T(8,128)S(1)} %get-tuple-element.34), channel_id=1, source_target_pairs={{2,4},{6,0},{4,2},{0,6},{3,5},{7,1},{5,3},{1,7},{10,12},{14,8},{12... | collective-permute-start | bytes 73736 | tf_op jit(solution)/shard_map/ppermute | solution.py:396
  22.8 11.5 %collective-permute-start.9 = (f32[2,7,2,8,128]{4,3,2,1,0:T(8,128)S(1)}, f32[2,7,2,8,128]{4,3,2,1,0:T(8,128)S(1)}, u32[]{:S(2)}, u32[]{:S(2)}) collective-permute-start(f32[2,7,2,8,128]{4,3,2,1,0:T(8,128)S(1)} %merge_strips.1.strips_ref), channel_id=1, source_target_pairs={{0,1},{1,0},{2,3},{3,2},{4,5},{5,4},{6,7},{7,6},{8,9},{9,8},{10,11... | collective-permute-start | bytes 344072 | tf_op jit(solution)/shard_map/ppermute | solution.py:390
